TPU v7x, 256 devices: a whole 4x4x8 slice. The times are simulated.
256 devices in a mesh: row: 8 (over y, core), col: 32 (over z, x).
Axes of the slice: x: 4, y: 4, z: 8, core: 2. Of those that a mesh axis runs over, the one named last changes fastest.
Arguments:
- object_field: float32 [2, 1024, 4096], P(None, 'row', 'col'), may hold values from -3 to 3
- probe_field: float32 [2, 256, 256], replicated, may hold values from -3 to 3
- intensity: float32 [8, 32, 8, 256, 256], P('row', 'col'), may hold values from 0.05 to 1
- scan_offsets: int32 [8, 32, 8, 2], P('row', 'col'), may hold values from -128 to 0
- pattern_counts: int32 [8, 32], P('row', 'col'), may hold values from 1 to 8, as said below
Outputs:
- new_object: float32 [2, 1024, 4096], P(None, 'row', 'col')
- new_probe: float32 [2, 256, 256], replicated
Inputs may be any that keep to these rules, and one draw needn't show every extreme that they name: `pattern_counts`: some region has 8 live slots in every draw.
All inputs are finite; a program needn't handle non-finite values.
Results may differ from a plain program's by a relative error of at most 0.0025.
The roundings to bfloat16 on the way count: a program that leaves them out, or rounds other values in their place, can miss the bound.
Values sent between devices are 32-bit elements; how exact they have to be, the bound alone decides.
No kernel may reach another device: no remote copies, remote signals or barrier semaphores. Data moves between devices by JAX's collectives and lax.ppermute only.
A program may use at most 64 MiB of HBM per device.

v0:
```python
import jax
import jax.numpy as jnp
from jax import lax
from jax.sharding import PartitionSpec as P

ITERS = 2


def passed_along(value, axis, steps):
    count = lax.axis_size(axis)
    leading, last = (max(0, -steps), min(count, count - steps))
    return lax.ppermute(value, axis, [(source, source + steps) for source in range(leading, last)])


def extended_2(block, sides, width):
    for axis, dim in sides:
        count = lax.axis_size(axis)
        forward = [(i, i + 1) for i in range(count - 1)]
        backward = [(target, source) for source, target in forward]
        low = lax.ppermute(
            lax.slice_in_dim(block, block.shape[dim] - width, None, axis=dim), axis, forward
        )
        high = lax.ppermute(lax.slice_in_dim(block, 0, width, axis=dim), axis, backward)
        block = jnp.concatenate([low, block, high], axis=dim)
    return block


def dft_tables(length):
    index = jnp.arange(length, dtype=jnp.int32)
    product = index[:, None] * index[None, :] % length
    angle = 2.0 * jnp.pi / length * product.astype(jnp.float32)
    factor = 1.0 / jnp.sqrt(jnp.float32(length))
    return (
        (jnp.cos(angle) * factor).astype(jnp.bfloat16),
        (jnp.sin(angle) * factor).astype(jnp.bfloat16),
    )


def left_section(real_part, imag_part, cos_table, sin_table, sign_value):
    width = real_part.shape[1]
    joined = jnp.concatenate([real_part, imag_part], axis=1)
    first = jnp.dot(cos_table, joined, preferred_element_type=jnp.float32)
    second = jnp.dot(sin_table, joined, preferred_element_type=jnp.float32)
    return (
        first[:, :width] + sign_value * second[:, width:],
        first[:, width:] - sign_value * second[:, :width],
    )


def right_section(real_part, imag_part, cos_table, sin_table, sign_value):
    height = real_part.shape[0]
    joined = jnp.concatenate([real_part, imag_part], axis=0)
    first = jnp.dot(joined, cos_table, preferred_element_type=jnp.float32)
    second = jnp.dot(joined, sin_table, preferred_element_type=jnp.float32)
    return (
        first[:height] + sign_value * second[height:],
        first[height:] - sign_value * second[:height],
    )


def transform(real_part, imag_part, cos_table, sin_table, sign_value):
    mid_real, mid_imag = left_section(
        real_part.astype(jnp.bfloat16),
        imag_part.astype(jnp.bfloat16),
        cos_table,
        sin_table,
        sign_value,
    )
    return right_section(
        mid_real.astype(jnp.bfloat16),
        mid_imag.astype(jnp.bfloat16),
        cos_table,
        sin_table,
        sign_value,
    )


def pattern_terms(window, probe, pattern, weight, cos_table, sin_table):
    wave_real = probe[0] * window[0] - probe[1] * window[1]
    wave_imag = probe[0] * window[1] + probe[1] * window[0]
    far_real, far_imag = transform(wave_real, wave_imag, cos_table, sin_table, 1.0)
    misfit = (far_real * far_real + far_imag * far_imag - pattern) * weight
    back_real, back_imag = transform(
        misfit * far_real, misfit * far_imag, cos_table, sin_table, -1.0
    )
    object_term = jnp.stack(
        [probe[0] * back_real + probe[1] * back_imag, probe[0] * back_imag - probe[1] * back_real]
    )
    probe_term = jnp.stack(
        [
            window[0] * back_real + window[1] * back_imag,
            window[0] * back_imag - window[1] * back_real,
        ]
    )
    return (object_term, probe_term)


def margins_direct(grad_ext, region):
    width = lax.axis_size("col")
    column = lax.axis_index("col")
    total = grad_ext[:, region : 2 * region, region : 2 * region]
    moves = [
        (row_step, col_step)
        for row_step in (-1, 0, 1)
        for col_step in (-1, 0, 1)
        if row_step != 0 or col_step != 0
    ]
    for row_step, col_step in moves:
        piece = grad_ext[
            :,
            (1 - row_step) * region : (2 - row_step) * region,
            (1 - col_step) * region : (2 - col_step) * region,
        ]
        arrived = passed_along(piece, ("row", "col"), -(row_step * width + col_step))
        inside = ((column + col_step >= 0) & (column + col_step < width)).astype(jnp.float32)
        total = total + inside * arrived
    return total


def body(object_field, probe_field, intensity, scan_offsets, pattern_counts):
    region = object_field.shape[1]
    length = probe_field.shape[1]
    slots = intensity.shape[2]
    cos_table, sin_table = dft_tables(length)
    patterns = intensity.reshape(slots, length, length)
    offsets = scan_offsets.reshape(slots, 2)
    weights = (jnp.arange(slots, dtype=jnp.int32) < pattern_counts.reshape(())).astype(jnp.float32)
    start_row = offsets[:, 0] + region
    start_col = offsets[:, 1] + region
    for step in range(ITERS):
        extended = extended_2(object_field, (("row", 1), ("col", 2)), region)
        probe_now = probe_field

        def visit(carry, item):
            grad_ext, grad_probe = carry
            row_start, col_start, pattern, weight = item
            anchor = jnp.zeros((), jnp.int32)
            window = lax.dynamic_slice(
                extended, (anchor, row_start, col_start), (2, length, length)
            )
            object_term, probe_term = pattern_terms(
                window, probe_now, pattern, weight, cos_table, sin_table
            )
            current = lax.dynamic_slice(
                grad_ext, (anchor, row_start, col_start), (2, length, length)
            )
            grad_ext = lax.dynamic_update_slice(
                grad_ext, current + object_term, (anchor, row_start, col_start)
            )
            return ((grad_ext, grad_probe + probe_term), None)

        start = (jnp.zeros_like(extended), jnp.zeros_like(probe_field))
        (grad_ext, grad_probe), unused = lax.scan(
            visit, start, (start_row, start_col, patterns, weights)
        )
        own_grad = margins_direct(grad_ext, region)
        peak = jnp.max(probe_now[0] * probe_now[0] + probe_now[1] * probe_now[1]) + 1e-06
        object_field = object_field - own_grad / peak
        summed = lax.psum(grad_probe, ("row", "col"))
        spread = jnp.sqrt(jnp.sum(summed * summed) / summed.size + 1e-06)
        probe_field = probe_now - 0.3 * summed / spread
    return (object_field, probe_field)


def solution(mesh):
    in_specs = (
        P(None, "row", "col"),
        P(),
        P("row", "col", None, None, None),
        P("row", "col", None, None),
        P("row", "col"),
    )
    out_specs = (P(None, "row", "col"), P())
    return jax.shard_map(body, mesh=mesh, in_specs=in_specs, out_specs=out_specs, check_vma=False)
```

profile of v0, /device:TPU:1, one launch (start us, length us, event | category | flops | bytes accessed | tf_op | source)
XLA Modules:
  0.0 1037.2 jit_solution(3132421256174582590)
XLA Ops:
  7.2 4.6 collective-permute-start
  27.8 4.1 collective-permute-done.3
  33.2 202.8 %while.28 = (s32[]{:T(128)}, f32[2,384,384]{2,1,0:T(8,128)}, f32[2,256,256]{2,1,0:T(8,128)}, s32[8]{0:T(128)S(1)}, s32[8]{0:T(128)S(1)}, /*index=5*/f32[2,256,25...) while((s32[]{:T(128)}, f32[2,384,384]{2,1,0:T(8,128)}, ...), condition=%wide.region_1.2_spmd.clone.clone, body=%wide.region_0.1_spmd.clone.clone.sunk | while | flops 553058304 | bytes 20709684 | solution.py:153
  52.3 6.3 dynamic_update_slice.12
  78.0 5.9 dynamic_update_slice.12
  103.2 6.3 dynamic_update_slice.12
  128.8 6.1 dynamic_update_slice.12
  154.1 6.2 dynamic_update_slice.12
  179.6 6.2 dynamic_update_slice.12
  205.0 5.4 dynamic_update_slice.12
  229.7 6.3 dynamic_update_slice.12
  240.7 7.6 collective-permute-start.4
  248.2 3.6 collective-permute-start.5
  251.9 11.8 %collective-permute-start.6 = (f32[2,128,128]{2,1,0:T(8,128)S(1)}, f32[2,128,128]{2,1,0:T(8,128)S(1)}, u32[]{:S(2)}, u32[]{:S(2)}) collective-permute-start(f32[2,128,128]{2,1,0:T(8,128)S(1)} %get-tuple-element.371), channel_id=1, source_target_pairs={{0,31},{1,32},{2,33},{3,34},{4,35},{5,36},{6,37},{7,38},{8,39},{9,... | collective-permute-start | bytes 393224 | tf_op jit(solution)/shard_map/ppermute | solution.py:12
  265.7 7.0 collective-permute-start.8
  276.0 5.7 collective-permute-done.9
  282.7 4.6 collective-permute-start.12
  289.3 4.7 collective-permute-done.13
  296.7 233.4 %all-reduce.3.cloned.1.call-done = f32[2,256,256]{2,1,0:T(8,128)} async-done(((f32[2,256,256]{2,1,0:T(8,128)}), f32[2,256,256]{2,1,0:T(8,128)}) %all-reduce.3.cloned.1.call-update) | async-done | bytes 524304 | tf_op jit(solution)/shard_map/psum | solution.py:159
  534.9 206.7 %while.29 = (s32[]{:T(128)}, f32[2,384,384]{2,1,0:T(8,128)}, f32[2,256,256]{2,1,0:T(8,128)}, s32[8]{0:T(128)S(1)}, s32[8]{0:T(128)S(1)}, /*index=5*/f32[2,256,25...) while((s32[]{:T(128)}, f32[2,384,384]{2,1,0:T(8,128)}, ...), condition=%wide.region_6.7_spmd.clone.clone, body=%wide.region_5.6_spmd.clone.clone.sunk | while | flops 553058304 | bytes 20709684 | solution.py:153
  554.5 6.3 dynamic_update_slice.13
  580.6 5.9 dynamic_update_slice.13
  606.3 6.3 dynamic_update_slice.13
  632.4 6.1 dynamic_update_slice.13
  658.3 6.1 dynamic_update_slice.13
  684.2 6.1 dynamic_update_slice.13
  710.1 5.3 dynamic_update_slice.13
  735.3 6.3 dynamic_update_slice.13
  742.9 6.5 collective-permute-start.16
  751.4 7.7 collective-permute-start.18
  761.1 7.0 collective-permute-start.20
  782.2 243.9 %all-reduce.5.cloned.1.call-done = f32[2,256,256]{2,1,0:T(8,128)} async-done(((f32[2,256,256]{2,1,0:T(8,128)}), f32[2,256,256]{2,1,0:T(8,128)}) %all-reduce.5.cloned.1.call-update) | async-done | bytes 524304 | tf_op jit(solution)/shard_map/psum | solution.py:159
  (357 shorter events, 310.8 us)
Async XLA Ops:
  7.2 522.9 %all-reduce.3.cloned.1.call-start = ((), (), s32[]{:S(2)}) async-start(), calls=%async_computation | async-start | bytes 1048576 | tf_op jit(solution)/shard_map/psum | solution.py:159
  7.2 6.8 collective-permute-start
  11.8 6.5 collective-permute-start.1
  18.3 9.5 collective-permute-start.2
  21.5 10.4 %collective-permute-start.3 = (f32[2,384,128]{2,1,0:T(8,128)S(1)}, f32[2,384,128]{2,1,0:T(8,128)S(1)}, u32[]{:S(2)}, u32[]{:S(2)}) collective-permute-start(f32[2,384,128]{2,1,0:T(8,128)S(1)} %constant_dynamic-update-slice_fusion), channel_id=1, source_target_pairs={{1,0},{2,1},{3,2},{4,3},{5,4},{6,5},{7,6},{8,7},{9,8},{10,9},{11,1... | collective-permute-start | bytes 1179656 | tf_op jit(solution)/shard_map/ppermute | solution.py:23
  22.8 3.6 copy-start.2
  32.0 1.2 copy-start
  236.0 45.7 %copy-start.1 = (f32[2,128,128]{2,1,0:T(8,128)S(1)}, f32[2,128,128]{2,1,0:T(8,128)}, u32[]{:S(2)}) copy-start(f32[2,128,128]{2,1,0:T(8,128)} %param.9) | copy-start | bytes 393220
  237.4 26.3 %collective-permute-start.10 = (f32[2,128,128]{2,1,0:T(8,128)S(1)}, f32[2,128,128]{2,1,0:T(8,128)S(1)}, u32[]{:S(2)}, u32[]{:S(2)}) collective-permute-start(f32[2,128,128]{2,1,0:T(8,128)S(1)} %get-tuple-element.374), channel_id=1, source_target_pairs={{32,0},{33,1},{34,2},{35,3},{36,4},{37,5},{38,6},{39,7},{40,8},{41... | collective-permute-start | bytes 393224 | tf_op jit(solution)/shard_map/ppermute | solution.py:12
  239.4 26.3 %collective-permute-start.11 = (f32[2,128,128]{2,1,0:T(8,128)S(1)}, f32[2,128,128]{2,1,0:T(8,128)S(1)}, u32[]{:S(2)}, u32[]{:S(2)}) collective-permute-start(f32[2,128,128]{2,1,0:T(8,128)S(1)} %get-tuple-element.373), channel_id=1, source_target_pairs={{33,0},{34,1},{35,2},{36,3},{37,4},{38,5},{39,6},{40,7},{41,8},{42... | collective-permute-start | bytes 393224 | tf_op jit(solution)/shard_map/ppermute | solution.py:12
  240.7 32.0 %collective-permute-start.4 = (f32[2,128,128]{2,1,0:T(8,128)S(1)}, f32[2,128,128]{2,1,0:T(8,128)S(1)}, u32[]{:S(2)}, u32[]{:S(2)}) collective-permute-start(f32[2,128,128]{2,1,0:T(8,128)S(1)} %get-tuple-element.368), channel_id=1, source_target_pairs={{0,33},{1,34},{2,35},{3,36},{4,37},{5,38},{6,39},{7,40},{8,41},{9,... | collective-permute-start | bytes 393224 | tf_op jit(solution)/shard_map/ppermute | solution.py:12
  248.2 27.8 %collective-permute-start.5 = (f32[2,128,128]{2,1,0:T(8,128)S(1)}, f32[2,128,128]{2,1,0:T(8,128)S(1)}, u32[]{:S(2)}, u32[]{:S(2)}) collective-permute-start(f32[2,128,128]{2,1,0:T(8,128)S(1)} %get-tuple-element.372), channel_id=1, source_target_pairs={{0,32},{1,33},{2,34},{3,35},{4,36},{5,37},{6,38},{7,39},{8,40},{9,... | collective-permute-start | bytes 393224 | tf_op jit(solution)/shard_map/ppermute | solution.py:12
  251.9 24.1 %collective-permute-start.6 = (f32[2,128,128]{2,1,0:T(8,128)S(1)}, f32[2,128,128]{2,1,0:T(8,128)S(1)}, u32[]{:S(2)}, u32[]{:S(2)}) collective-permute-start(f32[2,128,128]{2,1,0:T(8,128)S(1)} %get-tuple-element.371), channel_id=1, source_target_pairs={{0,31},{1,32},{2,33},{3,34},{4,35},{5,36},{6,37},{7,38},{8,39},{9,... | collective-permute-start | bytes 393224 | tf_op jit(solution)/shard_map/ppermute | solution.py:12
  263.7 12.3 %collective-permute-start.7 = (f32[2,128,128]{2,1,0:T(8,128)S(1)}, f32[2,128,128]{2,1,0:T(8,128)S(1)}, u32[]{:S(2)}, u32[]{:S(2)}) collective-permute-start(f32[2,128,128]{2,1,0:T(8,128)S(1)} %get-tuple-element.370), channel_id=1, source_target_pairs={{0,1},{1,2},{2,3},{3,4},{4,5},{5,6},{6,7},{7,8},{8,9},{9,10},{10,1... | collective-permute-start | bytes 393224 | tf_op jit(solution)/shard_map/ppermute | solution.py:12
  265.7 10.3 collective-permute-start.8
  272.7 9.0 collective-permute-start.9
  275.9 750.1 %all-reduce.5.cloned.1.call-start = ((), (), s32[]{:S(2)}) async-start(), calls=%async_computation.1 | async-start | bytes 1048576 | tf_op jit(solution)/shard_map/psum | solution.py:159
  282.7 6.6 collective-permute-start.12
  287.3 6.7 collective-permute-start.13
  294.1 239.6 %collective-permute-start.14 = (f32[2,384,128]{2,1,0:T(8,128)S(1)}, f32[2,384,128]{2,1,0:T(8,128)S(1)}, u32[]{:S(2)}, u32[]{:S(2)}) collective-permute-start(f32[2,384,128]{2,1,0:T(8,128)S(1)} %pad_maximum_fusion.26), channel_id=1, source_target_pairs={{0,1},{1,2},{2,3},{3,4},{4,5},{5,6},{6,7},{7,8},{8,9},{9,10},{10,1... | collective-permute-start | bytes 1179656 | tf_op jit(solution)/shard_map/ppermute | solution.py:20
  295.4 238.3 %collective-permute-start.15 = (f32[2,384,128]{2,1,0:T(8,128)S(1)}, f32[2,384,128]{2,1,0:T(8,128)S(1)}, u32[]{:S(2)}, u32[]{:S(2)}) collective-permute-start(f32[2,384,128]{2,1,0:T(8,128)S(1)} %pad_maximum_fusion.26), channel_id=1, source_target_pairs={{1,0},{2,1},{3,2},{4,3},{5,4},{6,5},{7,6},{8,7},{9,8},{10,9},{11,1... | collective-permute-start | bytes 1179656 | tf_op jit(solution)/shard_map/ppermute | solution.py:23
  742.9 25.1 %collective-permute-start.16 = (f32[2,128,128]{2,1,0:T(8,128)S(1)}, f32[2,128,128]{2,1,0:T(8,128)S(1)}, u32[]{:S(2)}, u32[]{:S(2)}) collective-permute-start(f32[2,128,128]{2,1,0:T(8,128)S(1)} %get-tuple-element.360), channel_id=1, source_target_pairs={{0,33},{1,34},{2,35},{3,36},{4,37},{5,38},{6,39},{7,40},{8,41},{9,... | collective-permute-start | bytes 393224 | tf_op jit(solution)/shard_map/ppermute | solution.py:12
  749.4 20.6 %collective-permute-start.17 = (f32[2,128,128]{2,1,0:T(8,128)S(1)}, f32[2,128,128]{2,1,0:T(8,128)S(1)}, u32[]{:S(2)}, u32[]{:S(2)}) collective-permute-start(f32[2,128,128]{2,1,0:T(8,128)S(1)} %get-tuple-element.364), channel_id=1, source_target_pairs={{0,32},{1,33},{2,34},{3,35},{4,36},{5,37},{6,38},{7,39},{8,40},{9,... | collective-permute-start | bytes 393224 | tf_op jit(solution)/shard_map/ppermute | solution.py:12
  751.4 20.5 %collective-permute-start.18 = (f32[2,128,128]{2,1,0:T(8,128)S(1)}, f32[2,128,128]{2,1,0:T(8,128)S(1)}, u32[]{:S(2)}, u32[]{:S(2)}) collective-permute-start(f32[2,128,128]{2,1,0:T(8,128)S(1)} %get-tuple-element.363), channel_id=1, source_target_pairs={{0,31},{1,32},{2,33},{3,34},{4,35},{5,36},{6,37},{7,38},{8,39},{9,... | collective-permute-start | bytes 393224 | tf_op jit(solution)/shard_map/ppermute | solution.py:12
  759.2 15.4 %collective-permute-start.19 = (f32[2,128,128]{2,1,0:T(8,128)S(1)}, f32[2,128,128]{2,1,0:T(8,128)S(1)}, u32[]{:S(2)}, u32[]{:S(2)}) collective-permute-start(f32[2,128,128]{2,1,0:T(8,128)S(1)} %get-tuple-element.362), channel_id=1, source_target_pairs={{0,1},{1,2},{2,3},{3,4},{4,5},{5,6},{6,7},{7,8},{8,9},{9,10},{10,1... | collective-permute-start | bytes 393224 | tf_op jit(solution)/shard_map/ppermute | solution.py:12
  761.1 13.5 %collective-permute-start.20 = (f32[2,128,128]{2,1,0:T(8,128)S(1)}, f32[2,128,128]{2,1,0:T(8,128)S(1)}, u32[]{:S(2)}, u32[]{:S(2)}) collective-permute-start(f32[2,128,128]{2,1,0:T(8,128)S(1)} %get-tuple-element.361), channel_id=1, source_target_pairs={{1,0},{2,1},{3,2},{4,3},{5,4},{6,5},{7,6},{8,7},{9,8},{10,9},{11,1... | collective-permute-start | bytes 393224 | tf_op jit(solution)/shard_map/ppermute | solution.py:12
  768.1 9.0 collective-permute-start.21
  770.0 7.1 collective-permute-start.22
  771.9 8.6 collective-permute-start.23
Sparse Core Ops, SparseCore 0:
  276.1 253.9 all-reduce.2
  773.4 252.5 all-reduce.4
where the time goes:
time: 1040 us
  waiting for transfers between devices  503 us (48%)
  matrix products  148 us (14%)
  local copies, waits for them, and re-layouts  134 us (13%)
  other arithmetic  87.8 us (8%)
  starting transfers between devices  87.5 us (8%)
  loops' own time  59.6 us (6%)
  between operations  17.8 us (2%)
    psum x2, waiting for transfers between devices, body(): summed = lax.psum(grad_probe, ('row', 'col'))  477 us
    dynamic_update_slice x16, local copies, waits for them, and re-layouts, visit(): lax.dynamic_update_slice(grad_ext, current + object_term, (anchor, row_st...  96.9 us
    ppermute x16, starting transfers between devices, passed_along(): lax.ppermute(value, axis, [(source, source + steps) for source in range(l...  67.3 us
    another operation x2, loops' own time, body(): lax.scan(visit, start, (start_row, start_col, patterns, weights))  59.6 us
    dot_general x32, matrix products, right_section(): second = jnp.dot(joined, sin_table, preferred_element_type=jnp.float32)  38.1 us
    dot_general x32, matrix products, right_section(): first = jnp.dot(joined, cos_table, preferred_element_type=jnp.float32)  37.6 us
    add x16, other arithmetic, visit(): current + object_term  36.5 us
    dot_general x32, matrix products, left_section(): second = jnp.dot(sin_table, joined, preferred_element_type=jnp.float32)  36.2 us
  transfers between devices with their start and end apart: 26, of which 10 were waited for; matrix products, arithmetic and copies ran while one was open for 1% of the time, Pallas kernels for 0%

commit v1 on v0

v1 whole, which is shorter than its diff:
```python
import jax
import jax.numpy as jnp
import numpy as np
from jax import lax
from jax.experimental import pallas as pl
from jax.experimental.pallas import tpu as pltpu
from jax.sharding import Mesh, PartitionSpec as P

ROW = ("y", "core")
COL = ("z", "x")
PLANE = ("y", "core", "x")
LANES = 128
F32 = jnp.float32


def dft_tables(length):
    index = jnp.arange(length, dtype=jnp.int32)
    product = index[:, None] * index[None, :] % length
    angle = 2.0 * jnp.pi / length * product.astype(F32)
    factor = 1.0 / jnp.sqrt(F32(length))
    cos_table = (jnp.cos(angle) * factor).astype(jnp.bfloat16)
    sin_table = (jnp.sin(angle) * factor).astype(jnp.bfloat16)
    forward = jnp.block([[cos_table, sin_table], [-sin_table, cos_table]])
    inverse = jnp.block([[cos_table, -sin_table], [sin_table, cos_table]])
    return forward, inverse


def dot(a, b):
    return jnp.dot(a, b, preferred_element_type=F32)


def transform(real_part, imag_part, left, right):
    size = real_part.shape[0]
    mid = dot(left, jnp.concatenate([real_part, imag_part], axis=0).astype(jnp.bfloat16))
    mid = mid.astype(jnp.bfloat16)
    out = dot(jnp.concatenate([mid[:size], mid[size:]], axis=1), right)
    return out[:, :size], out[:, size:]


def updated_probe(probe, total):
    mean = jnp.sum(total * total, keepdims=True) / total.size
    return probe - 0.3 * total / jnp.sqrt(mean + 1e-06)


def patterns_loop(count_ref, offset_ref, pattern_ref, forward_ref, inverse_ref, probe, ext, gobj, gprobe):
    size = pattern_ref.shape[1]
    region = size // 2
    tiles = size // 8
    gobj[...] = jnp.zeros_like(gobj)
    gprobe[...] = jnp.zeros_like(gprobe)

    def visit(k, carry):
        row = offset_ref[k, 0] + region
        col = offset_ref[k, 1] + region
        tile = jnp.minimum(row // 8, region // 8 - 1)
        sub = row - tile * 8
        sub_id = lax.broadcasted_iota(jnp.int32, (1, 8, LANES), 1)
        lane_id = lax.broadcasted_iota(jnp.int32, (1, 8, LANES), 2)

        def window(part):
            pieces = [
                pltpu.roll(
                    ext[part, pl.ds(tile, tiles + 1), :, v * LANES : (v + 1) * LANES],
                    lax.rem(LANES - col, LANES),
                    2,
                )
                for v in range(3)
            ]
            halves = []
            for v in range(2):
                x = jnp.where(lane_id < LANES - col, pieces[v], pieces[v + 1])
                x = pltpu.roll(x, lax.rem(8 - sub, 8), 1)
                halves.append(jnp.where(sub_id < 8 - sub, x[:tiles], x[1:]).reshape(size, LANES))
            return jnp.concatenate(halves, axis=1)

        def place(part, value):
            zero = jnp.zeros((1, 8, LANES), F32)
            rolled = []
            for v in range(2):
                x = value[:, v * LANES : (v + 1) * LANES].reshape(tiles, 8, LANES)
                x = pltpu.roll(x, lax.rem(sub, 8), 1)
                x = jnp.where(
                    sub_id < sub,
                    jnp.concatenate([zero, x], axis=0),
                    jnp.concatenate([x, zero], axis=0),
                )
                rolled.append(pltpu.roll(x, lax.rem(col, LANES), 2))
            inside = lane_id < col
            pieces = [
                jnp.where(inside, 0.0, rolled[0]),
                jnp.where(inside, rolled[0], rolled[1]),
                jnp.where(inside, rolled[1], 0.0),
            ]
            for v in range(3):
                gobj[part, pl.ds(tile, tiles + 1), :, v * LANES : (v + 1) * LANES] += pieces[v]

        def add_probe(part, value):
            for v in range(2):
                gprobe[part, v] += value[:, v * LANES : (v + 1) * LANES]

        def probe_part(part):
            return jnp.concatenate([probe[part, 0], probe[part, 1]], axis=1)

        win_real, win_imag = window(0), window(1)
        probe_real, probe_imag = probe_part(0), probe_part(1)
        far_real, far_imag = transform(
            probe_real * win_real - probe_imag * win_imag,
            probe_real * win_imag + probe_imag * win_real,
            forward_ref[...],
            inverse_ref[...],
        )
        misfit = far_real * far_real + far_imag * far_imag - pattern_ref[k]
        back_real, back_imag = transform(
            misfit * far_real, misfit * far_imag, inverse_ref[...], forward_ref[...]
        )
        add_probe(0, win_real * back_real + win_imag * back_imag)
        add_probe(1, win_real * back_imag - win_imag * back_real)
        place(0, probe_real * back_real + probe_imag * back_imag)
        place(1, probe_real * back_imag - probe_imag * back_real)
        return carry

    lax.fori_loop(0, count_ref[0], visit, 0)


def load_object(ext, strip_refs):
    rows = LANES // 8
    for i, ref in enumerate(strip_refs):
        for j in range(3):
            for part in range(2):
                ext[part, i * rows : (i + 1) * rows, :, j * LANES : (j + 1) * LANES] = ref[j, part]


def store_gradient(gobj, strip_refs):
    rows = LANES // 8
    for i, ref in enumerate(strip_refs):
        for j in range(3):
            for part in range(2):
                ref[j, part] = gobj[part, i * rows : (i + 1) * rows, :, j * LANES : (j + 1) * LANES]


def peak_of(probe):
    power = probe[0] * probe[0] + probe[1] * probe[1]
    return jnp.max(power, keepdims=True).reshape(1, 1) + 1e-06


def first_kernel(
    count_ref, offset_ref, pattern_ref, forward_ref, inverse_ref, above_ref, own_ref, below_ref, start_ref,
    up_ref, mid_ref, down_ref, gprobe_ref, peak_ref, probe_ref,
    ext, gobj,
):
    for part in range(2):
        for v in range(2):
            probe_ref[part, v] = start_ref[part, :, v * LANES : (v + 1) * LANES]
    peak_ref[...] = jnp.broadcast_to(peak_of(probe_ref[...]), peak_ref.shape)
    load_object(ext, (above_ref, own_ref, below_ref))
    patterns_loop(count_ref, offset_ref, pattern_ref, forward_ref, inverse_ref, probe_ref, ext, gobj, gprobe_ref)
    store_gradient(gobj, (up_ref, mid_ref, down_ref))


def second_kernel(
    count_ref, offset_ref, pattern_ref, forward_ref, inverse_ref, above_ref, own_ref, below_ref, start_ref, total_ref,
    up_ref, mid_ref, down_ref, gprobe_ref, peak_ref, probe_ref,
    ext, gobj,
):
    probe_ref[...] = updated_probe(start_ref[...], total_ref[...])
    peak_ref[...] = jnp.broadcast_to(peak_of(probe_ref[...]), peak_ref.shape)
    load_object(ext, (above_ref, own_ref, below_ref))
    patterns_loop(count_ref, offset_ref, pattern_ref, forward_ref, inverse_ref, probe_ref, ext, gobj, gprobe_ref)
    store_gradient(gobj, (up_ref, mid_ref, down_ref))


def gradients(kernel, count, offsets, patterns, tables, strips, *probes):
    size = patterns.shape[1]
    vmem = pl.BlockSpec(memory_space=pltpu.VMEM)
    smem = pl.BlockSpec(memory_space=pltpu.SMEM)
    strip = jax.ShapeDtypeStruct((3, 2, LANES // 8, 8, LANES), F32)
    halves = jax.ShapeDtypeStruct((2, 2, size, LANES), F32)
    return pl.pallas_call(
        kernel,
        out_shape=(strip, strip, strip, halves, jax.ShapeDtypeStruct((8, LANES), F32), halves),
        in_specs=[smem, smem] + [vmem] * (6 + len(probes)),
        out_specs=(vmem,) * 6,
        scratch_shapes=[pltpu.VMEM((2, 48, 8, 3 * LANES), F32), pltpu.VMEM((2, 48, 8, 3 * LANES), F32)],
        compiler_params=pltpu.CompilerParams(vmem_limit_bytes=40 * 1024 * 1024),
    )(count, offsets, patterns, *tables, *strips, *probes)


def small_call(kernel, out_shapes, *args):
    vmem = pl.BlockSpec(memory_space=pltpu.VMEM)
    return pl.pallas_call(
        kernel,
        out_shape=tuple(jax.ShapeDtypeStruct(shape, F32) for shape in out_shapes),
        in_specs=[vmem] * len(args),
        out_specs=(vmem,) * len(out_shapes),
        compiler_params=pltpu.CompilerParams(vmem_limit_bytes=24 * 1024 * 1024),
    )(*args)


def sum_copies_kernel(in_ref, out_ref):
    total = in_ref[0]
    for i in range(1, in_ref.shape[0]):
        total = total + in_ref[i]
    for i in range(out_ref.shape[0]):
        out_ref[i] = total


def sum_copies(value, copies):
    return small_call(sum_copies_kernel, [(copies,) + value.shape[1:]], value)[0]


def exchange(value, axes):
    return lax.all_to_all(value, axes, 0, 0, tiled=True)


def shifted(value, axes, step):
    count = lax.axis_size(axes)
    return lax.ppermute(value, axes, [(i, i + step) for i in range(count) if 0 <= i + step < count])


def final_probe_kernel(probe_ref, total_ref, out_ref):
    new = updated_probe(probe_ref[...], total_ref[...])
    for part in range(2):
        for v in range(2):
            out_ref[part, :, v * LANES : (v + 1) * LANES] = new[part, v]


def total_over_devices(gprobe):
    shape = gprobe.shape
    plane = lax.axis_size(PLANE)
    chunks = gprobe.reshape(plane, -1, LANES)
    shares = sum_copies(exchange(chunks, PLANE), lax.axis_size("z"))
    shares = sum_copies(exchange(shares, "z"), plane)
    return exchange(shares, PLANE).reshape(shape)


def body(object_field, probe_field, intensity, scan_offsets, pattern_counts):
    size = probe_field.shape[1]
    slots = intensity.shape[2]
    patterns = intensity.reshape(slots, size, size)
    offsets = scan_offsets.reshape(slots, 2)
    count = pattern_counts.reshape(1)
    tables = dft_tables(size)
    col = lax.axis_index(COL)
    cols = lax.axis_size(COL)

    block = (2, LANES // 8, 8, LANES)
    own = object_field.reshape(block)
    strip = jnp.stack([shifted(own, COL, 1), own, shifted(own, COL, -1)])
    strips = (shifted(strip, ROW, 1), strip, shifted(strip, ROW, -1))
    up, mid, down, gprobe, peak, probe = gradients(
        first_kernel, count, offsets, patterns, tables, strips, probe_field
    )
    total = total_over_devices(gprobe)
    mid = mid + shifted(up, ROW, -1) + shifted(down, ROW, 1)
    left, right = shifted(mid[1:], COL, 1), shifted(mid[:2], COL, -1)
    far_left, far_right = shifted(mid[2], COL, 2), shifted(mid[0], COL, -2)
    peak = peak[0, 0]
    grads = jnp.stack(
        [
            jnp.where(col > 0, left[0] + far_left + mid[0], 0.0),
            mid[1] + left[1] + right[0],
            jnp.where(col < cols - 1, right[1] + far_right + mid[2], 0.0),
        ]
    )
    strip = strip - grads / peak
    strips = (shifted(strip, ROW, 1), strip, shifted(strip, ROW, -1))
    up, mid, down, gprobe, peak, probe = gradients(
        second_kernel, count, offsets, patterns, tables, strips, probe, total
    )
    total = total_over_devices(gprobe)
    mid = mid + shifted(up, ROW, -1) + shifted(down, ROW, 1)
    grad = mid[1] + shifted(mid[2], COL, 1) + shifted(mid[0], COL, -1)
    new_object = strip[1] - grad / peak[0, 0]
    new_probe = small_call(final_probe_kernel, [probe_field.shape], probe, total)[0]
    return (new_object.reshape(object_field.shape), new_probe)


def solution(mesh):
    split = Mesh(mesh.devices.reshape(4, 2, 8, 4), ("y", "core", "z", "x"))
    in_specs = (
        P(None, ROW, COL),
        P(),
        P(ROW, COL, None, None, None),
        P(ROW, COL, None, None),
        P(ROW, COL),
    )
    out_specs = (P(None, ROW, COL), P())
    return jax.shard_map(body, mesh=split, in_specs=in_specs, out_specs=out_specs, check_vma=False)
```

time: 1040 us -> 194 us (0.19)
  waiting for transfers between devices: 503 us -> 33.8 us
  matrix products: 148 us -> 0 us
  local copies, waits for them, and re-layouts: 134 us -> 15.1 us
  other arithmetic: 87.8 us -> 10.6 us
  loops' own time: 59.6 us -> 0 us
  starting transfers between devices: 87.5 us -> 119 us
  between operations: 17.8 us -> 1.65 us
  Pallas kernels: 0 us -> 12.5 us
    psum x2 -> x0, waiting for transfers between devices: 477 us -> none  [body(): summed = lax.psum(grad_probe, ('row', 'col'))]
    dot_general x128 -> x0, matrix products: 148 us -> none  [the longest x32 38.1 us: right_section(): second = jnp.dot(joined, sin_table, preferred_element_type=jnp.float32)]
    dynamic_update_slice x16 -> x0, local copies, waits for them, and re-layouts: 96.9 us -> none  [visit(): lax.dynamic_update_slice(grad_ext, current + object_term, (anchor, row_st...]
    all_to_all x0 -> x6, starting transfers between devices: none -> 65.4 us  [exchange(): return lax.all_to_all(value, axes, 0, 0, tiled=True)]
    another operation x2 -> x0, loops' own time: 59.6 us -> none  [body(): lax.scan(visit, start, (start_row, start_col, patterns, weights))]
    add x17 -> x2, other arithmetic: 36.5 us -> 1.27 us  [body(): mid = mid + shifted(up, ROW, -1) + shifted(down, ROW, 1)]
    ppermute x24 -> x16, starting transfers between devices: 87.4 us -> 53.1 us  [shifted(): lax.ppermute(value, axes, [(i, i + step) for i in range(count) if 0 <= i...]
    convert_element_type x65 -> x1, other arithmetic: 32.7 us -> 1.11 us  [dft_tables(): sin_table = (jnp.sin(angle) * factor).astype(jnp.bfloat16)]
  transfers between devices with their start and end apart: 26 -> 22, of which waited for: 10 -> 10; matrix products, arithmetic and copies ran while one was open for 1% -> 6% of each run, Pallas kernels for 0% -> 1%
where the time goes in v1:
time: 194 us; the launch traced here: 192 us
  starting transfers between devices  119 us (61%)
  waiting for transfers between devices  33.8 us (17%)
  local copies, waits for them, and re-layouts  15.1 us (8%)
  Pallas kernels  12.5 us (6%)
  other arithmetic  10.6 us (5%)
    all_to_all x6, starting transfers between devices, exchange(): return lax.all_to_all(value, axes, 0, 0, tiled=True)  65.4 us
    ppermute x16, starting transfers between devices, shifted(): lax.ppermute(value, axes, [(i, i + step) for i in range(count) if 0 <= i...  53.1 us
    all_to_all x6, waiting for transfers between devices, exchange(): return lax.all_to_all(value, axes, 0, 0, tiled=True)  20.3 us
    ppermute x16, waiting for transfers between devices, shifted(): lax.ppermute(value, axes, [(i, i + step) for i in range(count) if 0 <= i...  13.5 us
    unnamed x42, local copies, waits for them, and re-layouts  12.4 us
    pallas_call x2, Pallas kernels, gradients(): pl.pallas_call(kernel, out_shape=(strip, strip, strip, halves, jax.ShapeD...  7.92 us
    pallas_call x5, Pallas kernels, small_call(): pl.pallas_call(kernel, out_shape=tuple((jax.ShapeDtypeStruct(shape, F32)...  4.54 us
  transfers between devices with their start and end apart: 22, of which 10 were waited for; matrix products, arithmetic and copies ran while one was open for 6% of the time, Pallas kernels for 1%

profile of v1, /device:TPU:1, one launch (start us, length us, event | category | flops | bytes accessed | tf_op | source)
XLA Modules:
  0.0 192.2 jit_solution(8086394048935907971)
XLA Ops:
  0.6 1.4 collective-permute-start.1
  2.1 4.6 %collective-permute-start = (f32[2,16,8,128]{3,2,1,0:T(8,128)}, f32[2,16,8,128]{3,2,1,0:T(8,128)S(1)}, u32[]{:S(2)}, u32[]{:S(2)}) collective-permute-start(f32[2,16,8,128]{3,2,1,0:T(8,128)} %bitcast.75), channel_id=1, source_target_pairs={{0,1},{1,2},{2,3},{3,4},{4,5},{5,6},{6,7},{7,8},{8,9},{9,10},{10,1... | collective-permute-start | bytes 393224 | tf_op jit(solution)/shard_map/ppermute | solution.py:217
  7.3 1.6 collective-permute-done
  9.9 5.7 %collective-permute-start.3 = (f32[3,2,16,8,128]{4,3,2,1,0:T(8,128)S(1)}, f32[3,2,16,8,128]{4,3,2,1,0:T(8,128)}, u32[]{:S(2)}, u32[]{:S(2)}) collective-permute-start(f32[3,2,16,8,128]{4,3,2,1,0:T(8,128)S(1)} %pad_maximum_fusion.4.own_ref), channel_id=1, source_target_pairs={{32,0},{64,32},{96,64},{128,96},{160,128},{192,160},{224,192},{33,... | collective-permute-start | bytes 1179656 | tf_op jit(solution)/shard_map/ppermute | solution.py:217
  15.6 1.9 collective-permute-start.2
  22.2 4.2 %shard_map.68 = (f32[3,2,16,8,128]{4,3,2,1,0:T(8,128)}, f32[3,2,16,8,128]{4,3,2,1,0:T(8,128)S(1)}, f32[3,2,16,8,128]{4,3,2,1,0:T(8,128)}, f32[2,2,256,128]{3,2,1...) custom-call(s32[1]{0:T(128)} %bitcast.67.count_ref, s32[8,2]{1,0:T(8,128)S(1)} %copy.7.offset_ref, ...), custom_call_target="tpu_custom_call" | custom-call | tf_op jit(solution)/shard_map/pallas_call | solution.py:178
  28.8 13.6 %collective-permute-start.4 = (f32[3,2,16,8,128]{4,3,2,1,0:T(8,128)}, f32[3,2,16,8,128]{4,3,2,1,0:T(8,128)S(1)}, u32[]{:S(2)}, u32[]{:S(2)}) collective-permute-start(f32[3,2,16,8,128]{4,3,2,1,0:T(8,128)} %get-tuple-element.15), channel_id=1, source_target_pairs={{32,0},{64,32},{96,64},{128,96},{160,128},{192,160},{224,192},{33,... | collective-permute-start | bytes 1179656 | tf_op jit(solution)/shard_map/ppermute | solution.py:217
  42.4 2.4 %collective-permute-start.5 = (f32[3,2,16,8,128]{4,3,2,1,0:T(8,128)}, f32[3,2,16,8,128]{4,3,2,1,0:T(8,128)}, u32[]{:S(2)}, u32[]{:S(2)}) collective-permute-start(f32[3,2,16,8,128]{4,3,2,1,0:T(8,128)} %get-tuple-element.16), channel_id=1, source_target_pairs={{0,32},{32,64},{64,96},{96,128},{128,160},{160,192},{192,224},{1,3... | collective-permute-start | bytes 1179656 | tf_op jit(solution)/shard_map/ppermute | solution.py:217
  44.9 12.1 %all-to-all-start = ((f32[32,32,128]{2,1,0:T(8,128)}), f32[32,32,128]{2,1,0:T(8,128)}, u32[]{:S(2)}, u32[]{:S(2)}) async-start(f32[32,32,128]{2,1,0:T(8,128)} %bitcast.72), calls=%async_computation | async-start | bytes 1048576 | tf_op jit(solution)/shard_map/all_to_all | solution.py:212
  59.8 3.3 %collective-permute-start.6 = (f32[2,2,16,8,128]{4,3,2,1,0:T(8,128)}, f32[2,2,16,8,128]{4,3,2,1,0:T(8,128)S(1)}, u32[]{:S(2)}, u32[]{:S(2)}) collective-permute-start(f32[2,2,16,8,128]{4,3,2,1,0:T(8,128)} %get-tuple-element.33), channel_id=1, source_target_pairs={{0,1},{1,2},{2,3},{3,4},{4,5},{5,6},{6,7},{7,8},{8,9},{9,10},{10,1... | collective-permute-start | bytes 786440 | tf_op jit(solution)/shard_map/ppermute | solution.py:217
  64.4 4.0 %all-to-all-done.in_ref = f32[32,32,128]{2,1,0:T(8,128)} async-done(((f32[32,32,128]{2,1,0:T(8,128)}), f32[32,32,128]{2,1,0:T(8,128)}, u32[]{:S(2)}, u32[]{:S(2)}) %all-to-all-start) | async-done | bytes 524320 | tf_op jit(solution)/shard_map/all_to_all | solution.py:212
  68.4 1.7 shard_map.69
  70.1 9.9 %all-to-all-start.1 = ((f32[8,32,128]{2,1,0:T(8,128)}), f32[8,32,128]{2,1,0:T(8,128)S(1)}, u32[]{:S(2)}, u32[]{:S(2)}) async-start(f32[8,32,128]{2,1,0:T(8,128)} %shard_map.69), calls=%async_computation.1 | async-start | bytes 262144 | tf_op jit(solution)/shard_map/all_to_all | solution.py:212
  80.0 1.9 slice_bitcast_fusion.6
  81.9 1.9 %collective-permute-start.7 = (f32[2,16,8,128]{3,2,1,0:T(8,128)}, f32[2,16,8,128]{3,2,1,0:T(8,128)}, u32[]{:S(2)}, u32[]{:S(2)}) collective-permute-start(f32[2,16,8,128]{3,2,1,0:T(8,128)} %get-tuple-element.30), channel_id=1, source_target_pairs={{0,2},{1,3},{2,4},{3,5},{4,6},{5,7},{6,8},{7,9},{8,10},{9,11},{10,... | collective-permute-start | bytes 393224 | tf_op jit(solution)/shard_map/ppermute | solution.py:217
  85.7 2.9 %all-to-all-done.1.in_ref = f32[8,32,128]{2,1,0:T(8,128)S(1)} async-done(((f32[8,32,128]{2,1,0:T(8,128)}), f32[8,32,128]{2,1,0:T(8,128)S(1)}, u32[]{:S(2)}, u32[]{:S(2)}) %all-to-all-start.1) | async-done | bytes 131104 | tf_op jit(solution)/shard_map/all_to_all | solution.py:212
  89.4 8.3 %all-to-all-start.2 = ((f32[32,32,128]{2,1,0:T(8,128)}), f32[32,32,128]{2,1,0:T(8,128)}, u32[]{:S(2)}, u32[]{:S(2)}) async-start(f32[32,32,128]{2,1,0:T(8,128)} %copy-done.1), calls=%async_computation.2 | async-start | bytes 1048576 | tf_op jit(solution)/shard_map/all_to_all | solution.py:212
  98.9 1.8 fusion.2.own_ref
  100.7 2.2 %collective-permute-start.11 = (f32[3,2,16,8,128]{4,3,2,1,0:T(8,128)S(1)}, f32[3,2,16,8,128]{4,3,2,1,0:T(8,128)S(1)}, u32[]{:S(2)}, u32[]{:S(2)}) collective-permute-start(f32[3,2,16,8,128]{4,3,2,1,0:T(8,128)S(1)} %fusion.2.own_ref), channel_id=1, source_target_pairs={{32,0},{64,32},{96,64},{128,96},{160,128},{192,160},{224,192},{33,... | collective-permute-start | bytes 1179656 | tf_op jit(solution)/shard_map/ppermute | solution.py:217
  102.9 3.3 %collective-permute-start.10 = (f32[3,2,16,8,128]{4,3,2,1,0:T(8,128)S(1)}, f32[3,2,16,8,128]{4,3,2,1,0:T(8,128)S(1)}, u32[]{:S(2)}, u32[]{:S(2)}) collective-permute-start(f32[3,2,16,8,128]{4,3,2,1,0:T(8,128)S(1)} %fusion.2.own_ref), channel_id=1, source_target_pairs={{0,32},{32,64},{64,96},{96,128},{128,160},{160,192},{192,224},{1,3... | collective-permute-start | bytes 1179656 | tf_op jit(solution)/shard_map/ppermute | solution.py:217
  106.3 4.9 %collective-permute-done.11.below_ref = f32[3,2,16,8,128]{4,3,2,1,0:T(8,128)S(1)} collective-permute-done((f32[3,2,16,8,128]{4,3,2,1,0:T(8,128)S(1)}, f32[3,2,16,8,128]{4,3,2,1,0:T(8,128)S(1)}, u32[]{:S(2)}, u32[]{:S(2)}) %collective-permute-start.11) | collective-permute-done | bytes 393248 | tf_op jit(solution)/shard_map/ppermute | solution.py:217
  115.8 3.7 %shard_map.71 = (f32[3,2,16,8,128]{4,3,2,1,0:T(8,128)S(1)}, f32[3,2,16,8,128]{4,3,2,1,0:T(8,128)S(1)}, f32[3,2,16,8,128]{4,3,2,1,0:T(8,128)S(1)}, f32[2,2,256,12...) custom-call(s32[1]{0:T(128)} %bitcast.68.count_ref, s32[8,2]{1,0:T(8,128)S(1)} %copy.7.offset_ref, ...), custom_call_target="tpu_custom_call" | custom-call | tf_op jit(solution)/shard_map/pallas_call | solution.py:178
  123.4 20.8 %all-to-all-start.3 = ((f32[32,32,128]{2,1,0:T(8,128)}), f32[32,32,128]{2,1,0:T(8,128)S(1)}, u32[]{:S(2)}, u32[]{:S(2)}) async-start(f32[32,32,128]{2,1,0:T(8,128)} %bitcast.73), calls=%async_computation.3 | async-start | bytes 1048576 | tf_op jit(solution)/shard_map/all_to_all | solution.py:212
  144.2 2.1 %collective-permute-start.12 = (f32[3,2,16,8,128]{4,3,2,1,0:T(8,128)}, f32[3,2,16,8,128]{4,3,2,1,0:T(8,128)S(1)}, u32[]{:S(2)}, u32[]{:S(2)}) collective-permute-start(f32[3,2,16,8,128]{4,3,2,1,0:T(8,128)} %copy-done.17), channel_id=1, source_target_pairs={{32,0},{64,32},{96,64},{128,96},{160,128},{192,160},{224,192},{33,... | collective-permute-start | bytes 1179656 | tf_op jit(solution)/shard_map/ppermute | solution.py:217
  146.3 3.4 %collective-permute-start.13 = (f32[3,2,16,8,128]{4,3,2,1,0:T(8,128)}, f32[3,2,16,8,128]{4,3,2,1,0:T(8,128)S(1)}, u32[]{:S(2)}, u32[]{:S(2)}) collective-permute-start(f32[3,2,16,8,128]{4,3,2,1,0:T(8,128)} %copy-done.16), channel_id=1, source_target_pairs={{0,32},{32,64},{64,96},{96,128},{128,160},{160,192},{192,224},{1,3... | collective-permute-start | bytes 1179656 | tf_op jit(solution)/shard_map/ppermute | solution.py:217
  149.7 5.8 %all-to-all-done.3.in_ref = f32[32,32,128]{2,1,0:T(8,128)S(1)} async-done(((f32[32,32,128]{2,1,0:T(8,128)}), f32[32,32,128]{2,1,0:T(8,128)S(1)}, u32[]{:S(2)}, u32[]{:S(2)}) %all-to-all-start.3) | async-done | bytes 524320 | tf_op jit(solution)/shard_map/all_to_all | solution.py:212
  156.3 8.4 %all-to-all-start.4 = ((f32[8,32,128]{2,1,0:T(8,128)}), f32[8,32,128]{2,1,0:T(8,128)S(1)}, u32[]{:S(2)}, u32[]{:S(2)}) async-start(f32[8,32,128]{2,1,0:T(8,128)} %shard_map.72), calls=%async_computation.4 | async-start | bytes 262144 | tf_op jit(solution)/shard_map/all_to_all | solution.py:212
  164.8 7.7 %all-to-all-done.4.in_ref = f32[8,32,128]{2,1,0:T(8,128)S(1)} async-done(((f32[8,32,128]{2,1,0:T(8,128)}), f32[8,32,128]{2,1,0:T(8,128)S(1)}, u32[]{:S(2)}, u32[]{:S(2)}) %all-to-all-start.4) | async-done | bytes 131104 | tf_op jit(solution)/shard_map/all_to_all | solution.py:212
  173.3 6.0 %all-to-all-start.5 = ((f32[32,32,128]{2,1,0:T(8,128)}), f32[32,32,128]{2,1,0:T(8,128)S(1)}, u32[]{:S(2)}, u32[]{:S(2)}) async-start(f32[32,32,128]{2,1,0:T(8,128)} %shard_map.73), calls=%async_computation.5 | async-start | bytes 1048576 | tf_op jit(solution)/shard_map/all_to_all | solution.py:212
  179.3 3.3 %collective-permute-start.14 = (f32[2,16,8,128]{3,2,1,0:T(8,128)S(1)}, f32[2,16,8,128]{3,2,1,0:T(8,128)S(1)}, u32[]{:S(2)}, u32[]{:S(2)}) collective-permute-start(f32[2,16,8,128]{3,2,1,0:T(8,128)S(1)} %get-tuple-element.26), channel_id=1, source_target_pairs={{0,1},{1,2},{2,3},{3,4},{4,5},{5,6},{6,7},{7,8},{8,9},{9,10},{10,1... | collective-permute-start | bytes 393224 | tf_op jit(solution)/shard_map/ppermute | solution.py:217
  184.5 3.5 %collective-permute-done.14 = f32[2,16,8,128]{3,2,1,0:T(8,128)S(1)} collective-permute-done((f32[2,16,8,128]{3,2,1,0:T(8,128)S(1)}, f32[2,16,8,128]{3,2,1,0:T(8,128)S(1)}, u32[]{:S(2)}, u32[]{:S(2)}) %collective-permute-start.14) | collective-permute-done | bytes 131104 | tf_op jit(solution)/shard_map/ppermute | solution.py:217
  188.0 1.7 collective-permute-done.15
  (76 shorter events, 30.5 us)
Async XLA Ops:
  0.6 21.6 %copy-start = (f32[1,1,8,256,256]{4,3,2,1,0:T(8,128)S(1)}, f32[1,1,8,256,256]{4,3,2,1,0:T(8,128)}, u32[]{:S(2)}) copy-start(f32[1,1,8,256,256]{4,3,2,1,0:T(8,128)} %param.7) | copy-start | bytes 6291460
  0.6 6.6 %collective-permute-start.1 = (f32[2,16,8,128]{3,2,1,0:T(8,128)}, f32[2,16,8,128]{3,2,1,0:T(8,128)S(1)}, u32[]{:S(2)}, u32[]{:S(2)}) collective-permute-start(f32[2,16,8,128]{3,2,1,0:T(8,128)} %bitcast.74), channel_id=1, source_target_pairs={{1,0},{2,1},{3,2},{4,3},{5,4},{6,5},{7,6},{8,7},{9,8},{10,9},{11,1... | collective-permute-start | bytes 393224 | tf_op jit(solution)/shard_map/ppermute | solution.py:217
  2.1 6.8 %collective-permute-start = (f32[2,16,8,128]{3,2,1,0:T(8,128)}, f32[2,16,8,128]{3,2,1,0:T(8,128)S(1)}, u32[]{:S(2)}, u32[]{:S(2)}) collective-permute-start(f32[2,16,8,128]{3,2,1,0:T(8,128)} %bitcast.75), channel_id=1, source_target_pairs={{0,1},{1,2},{2,3},{3,4},{4,5},{5,6},{6,7},{7,8},{8,9},{9,10},{10,1... | collective-permute-start | bytes 393224 | tf_op jit(solution)/shard_map/ppermute | solution.py:217
  7.3 10.9 %copy-start.19 = (f32[2,16,8,128]{3,2,1,0:T(8,128)}, f32[2,16,8,128]{3,2,1,0:T(8,128)S(1)}, u32[]{:S(2)}) copy-start(f32[2,16,8,128]{3,2,1,0:T(8,128)S(1)} %collective-permute-done.1) | copy-start | bytes 393220
  8.9 12.1 %copy-start.20 = (f32[2,16,8,128]{3,2,1,0:T(8,128)}, f32[2,16,8,128]{3,2,1,0:T(8,128)S(1)}, u32[]{:S(2)}) copy-start(f32[2,16,8,128]{3,2,1,0:T(8,128)S(1)} %collective-permute-done) | copy-start | bytes 393220
  9.9 11.3 %collective-permute-start.3 = (f32[3,2,16,8,128]{4,3,2,1,0:T(8,128)S(1)}, f32[3,2,16,8,128]{4,3,2,1,0:T(8,128)}, u32[]{:S(2)}, u32[]{:S(2)}) collective-permute-start(f32[3,2,16,8,128]{4,3,2,1,0:T(8,128)S(1)} %pad_maximum_fusion.4.own_ref), channel_id=1, source_target_pairs={{32,0},{64,32},{96,64},{128,96},{160,128},{192,160},{224,192},{33,... | collective-permute-start | bytes 1179656 | tf_op jit(solution)/shard_map/ppermute | solution.py:217
  15.6 6.6 %collective-permute-start.2 = (f32[3,2,16,8,128]{4,3,2,1,0:T(8,128)S(1)}, f32[3,2,16,8,128]{4,3,2,1,0:T(8,128)}, u32[]{:S(2)}, u32[]{:S(2)}) collective-permute-start(f32[3,2,16,8,128]{4,3,2,1,0:T(8,128)S(1)} %pad_maximum_fusion.4.own_ref), channel_id=1, source_target_pairs={{0,32},{32,64},{64,96},{96,128},{128,160},{160,192},{192,224},{1,3... | collective-permute-start | bytes 1179656 | tf_op jit(solution)/shard_map/ppermute | solution.py:217
  18.9 3.3 %copy-start.2 = (f32[2,256,256]{2,1,0:T(8,128)S(1)}, f32[2,256,256]{2,1,0:T(8,128)}, u32[]{:S(2)}) copy-start(f32[2,256,256]{2,1,0:T(8,128)} %start_ref.1) | copy-start | bytes 1572868
  27.3 0.8 copy-start.7
  28.8 28.1 %collective-permute-start.4 = (f32[3,2,16,8,128]{4,3,2,1,0:T(8,128)}, f32[3,2,16,8,128]{4,3,2,1,0:T(8,128)S(1)}, u32[]{:S(2)}, u32[]{:S(2)}) collective-permute-start(f32[3,2,16,8,128]{4,3,2,1,0:T(8,128)} %get-tuple-element.15), channel_id=1, source_target_pairs={{32,0},{64,32},{96,64},{128,96},{160,128},{192,160},{224,192},{33,... | collective-permute-start | bytes 1179656 | tf_op jit(solution)/shard_map/ppermute | solution.py:217
  42.4 14.5 %collective-permute-start.5 = (f32[3,2,16,8,128]{4,3,2,1,0:T(8,128)}, f32[3,2,16,8,128]{4,3,2,1,0:T(8,128)}, u32[]{:S(2)}, u32[]{:S(2)}) collective-permute-start(f32[3,2,16,8,128]{4,3,2,1,0:T(8,128)} %get-tuple-element.16), channel_id=1, source_target_pairs={{0,32},{32,64},{64,96},{96,128},{128,160},{160,192},{192,224},{1,3... | collective-permute-start | bytes 1179656 | tf_op jit(solution)/shard_map/ppermute | solution.py:217
  44.9 23.5 %all-to-all-start = ((f32[32,32,128]{2,1,0:T(8,128)}), f32[32,32,128]{2,1,0:T(8,128)}, u32[]{:S(2)}, u32[]{:S(2)}) async-start(f32[32,32,128]{2,1,0:T(8,128)} %bitcast.72), calls=%async_computation | async-start | bytes 1048576 | tf_op jit(solution)/shard_map/all_to_all | solution.py:212
  59.8 20.2 %collective-permute-start.6 = (f32[2,2,16,8,128]{4,3,2,1,0:T(8,128)}, f32[2,2,16,8,128]{4,3,2,1,0:T(8,128)S(1)}, u32[]{:S(2)}, u32[]{:S(2)}) collective-permute-start(f32[2,2,16,8,128]{4,3,2,1,0:T(8,128)} %get-tuple-element.33), channel_id=1, source_target_pairs={{0,1},{1,2},{2,3},{3,4},{4,5},{5,6},{6,7},{7,8},{8,9},{9,10},{10,1... | collective-permute-start | bytes 786440 | tf_op jit(solution)/shard_map/ppermute | solution.py:217
  63.1 16.9 %collective-permute-start.8 = (f32[2,2,16,8,128]{4,3,2,1,0:T(8,128)}, f32[2,2,16,8,128]{4,3,2,1,0:T(8,128)}, u32[]{:S(2)}, u32[]{:S(2)}) collective-permute-start(f32[2,2,16,8,128]{4,3,2,1,0:T(8,128)} %get-tuple-element.34), channel_id=1, source_target_pairs={{1,0},{2,1},{3,2},{4,3},{5,4},{6,5},{7,6},{8,7},{9,8},{10,9},{11,1... | collective-permute-start | bytes 786440 | tf_op jit(solution)/shard_map/ppermute | solution.py:217
  70.1 18.4 %all-to-all-start.1 = ((f32[8,32,128]{2,1,0:T(8,128)}), f32[8,32,128]{2,1,0:T(8,128)S(1)}, u32[]{:S(2)}, u32[]{:S(2)}) async-start(f32[8,32,128]{2,1,0:T(8,128)} %shard_map.69), calls=%async_computation.1 | async-start | bytes 262144 | tf_op jit(solution)/shard_map/all_to_all | solution.py:212
  81.9 15.8 %collective-permute-start.7 = (f32[2,16,8,128]{3,2,1,0:T(8,128)}, f32[2,16,8,128]{3,2,1,0:T(8,128)}, u32[]{:S(2)}, u32[]{:S(2)}) collective-permute-start(f32[2,16,8,128]{3,2,1,0:T(8,128)} %get-tuple-element.30), channel_id=1, source_target_pairs={{0,2},{1,3},{2,4},{3,5},{4,6},{5,7},{6,8},{7,9},{8,10},{9,11},{10,... | collective-permute-start | bytes 393224 | tf_op jit(solution)/shard_map/ppermute | solution.py:217
  83.8 13.9 %collective-permute-start.9 = (f32[2,16,8,128]{3,2,1,0:T(8,128)}, f32[2,16,8,128]{3,2,1,0:T(8,128)}, u32[]{:S(2)}, u32[]{:S(2)}) collective-permute-start(f32[2,16,8,128]{3,2,1,0:T(8,128)} %get-tuple-element.32), channel_id=1, source_target_pairs={{2,0},{3,1},{4,2},{5,3},{6,4},{7,5},{8,6},{9,7},{10,8},{11,9},{12,... | collective-permute-start | bytes 393224 | tf_op jit(solution)/shard_map/ppermute | solution.py:217
  89.4 23.4 %all-to-all-start.2 = ((f32[32,32,128]{2,1,0:T(8,128)}), f32[32,32,128]{2,1,0:T(8,128)}, u32[]{:S(2)}, u32[]{:S(2)}) async-start(f32[32,32,128]{2,1,0:T(8,128)} %copy-done.1), calls=%async_computation.2 | async-start | bytes 1048576 | tf_op jit(solution)/shard_map/all_to_all | solution.py:212
  100.7 10.5 %collective-permute-start.11 = (f32[3,2,16,8,128]{4,3,2,1,0:T(8,128)S(1)}, f32[3,2,16,8,128]{4,3,2,1,0:T(8,128)S(1)}, u32[]{:S(2)}, u32[]{:S(2)}) collective-permute-start(f32[3,2,16,8,128]{4,3,2,1,0:T(8,128)S(1)} %fusion.2.own_ref), channel_id=1, source_target_pairs={{32,0},{64,32},{96,64},{128,96},{160,128},{192,160},{224,192},{33,... | collective-permute-start | bytes 1179656 | tf_op jit(solution)/shard_map/ppermute | solution.py:217
  102.9 9.1 %collective-permute-start.10 = (f32[3,2,16,8,128]{4,3,2,1,0:T(8,128)S(1)}, f32[3,2,16,8,128]{4,3,2,1,0:T(8,128)S(1)}, u32[]{:S(2)}, u32[]{:S(2)}) collective-permute-start(f32[3,2,16,8,128]{4,3,2,1,0:T(8,128)S(1)} %fusion.2.own_ref), channel_id=1, source_target_pairs={{0,32},{32,64},{64,96},{96,128},{128,160},{160,192},{192,224},{1,3... | collective-permute-start | bytes 1179656 | tf_op jit(solution)/shard_map/ppermute | solution.py:217
  112.8 1.0 copy-start.4
  113.8 1.0 copy-start.10
  114.8 1.0 copy-start.12
  123.4 41.3 %copy-start.14 = (f32[3,2,16,8,128]{4,3,2,1,0:T(8,128)S(1)}, f32[3,2,16,8,128]{4,3,2,1,0:T(8,128)}, u32[]{:S(2)}) copy-start(f32[3,2,16,8,128]{4,3,2,1,0:T(8,128)} %copy-done.13) | copy-start | bytes 1179652
  123.4 32.2 %all-to-all-start.3 = ((f32[32,32,128]{2,1,0:T(8,128)}), f32[32,32,128]{2,1,0:T(8,128)S(1)}, u32[]{:S(2)}, u32[]{:S(2)}) async-start(f32[32,32,128]{2,1,0:T(8,128)} %bitcast.73), calls=%async_computation.3 | async-start | bytes 1048576 | tf_op jit(solution)/shard_map/all_to_all | solution.py:212
  144.2 20.5 %collective-permute-start.12 = (f32[3,2,16,8,128]{4,3,2,1,0:T(8,128)}, f32[3,2,16,8,128]{4,3,2,1,0:T(8,128)S(1)}, u32[]{:S(2)}, u32[]{:S(2)}) collective-permute-start(f32[3,2,16,8,128]{4,3,2,1,0:T(8,128)} %copy-done.17), channel_id=1, source_target_pairs={{32,0},{64,32},{96,64},{128,96},{160,128},{192,160},{224,192},{33,... | collective-permute-start | bytes 1179656 | tf_op jit(solution)/shard_map/ppermute | solution.py:217
  146.3 18.4 %collective-permute-start.13 = (f32[3,2,16,8,128]{4,3,2,1,0:T(8,128)}, f32[3,2,16,8,128]{4,3,2,1,0:T(8,128)S(1)}, u32[]{:S(2)}, u32[]{:S(2)}) collective-permute-start(f32[3,2,16,8,128]{4,3,2,1,0:T(8,128)} %copy-done.16), channel_id=1, source_target_pairs={{0,32},{32,64},{64,96},{96,128},{128,160},{160,192},{192,224},{1,3... | collective-permute-start | bytes 1179656 | tf_op jit(solution)/shard_map/ppermute | solution.py:217
  156.3 16.2 %all-to-all-start.4 = ((f32[8,32,128]{2,1,0:T(8,128)}), f32[8,32,128]{2,1,0:T(8,128)S(1)}, u32[]{:S(2)}, u32[]{:S(2)}) async-start(f32[8,32,128]{2,1,0:T(8,128)} %shard_map.72), calls=%async_computation.4 | async-start | bytes 262144 | tf_op jit(solution)/shard_map/all_to_all | solution.py:212
  164.7 26.4 %copy-start.6 = (f32[2,2,256,128]{3,2,1,0:T(8,128)S(1)}, f32[2,2,256,128]{3,2,1,0:T(8,128)}, u32[]{:S(2)}) copy-start(f32[2,2,256,128]{3,2,1,0:T(8,128)} %copy-done.5) | copy-start | bytes 1572868
  173.3 17.7 %all-to-all-start.5 = ((f32[32,32,128]{2,1,0:T(8,128)}), f32[32,32,128]{2,1,0:T(8,128)S(1)}, u32[]{:S(2)}, u32[]{:S(2)}) async-start(f32[32,32,128]{2,1,0:T(8,128)} %shard_map.73), calls=%async_computation.5 | async-start | bytes 1048576 | tf_op jit(solution)/shard_map/all_to_all | solution.py:212
  179.3 8.7 %collective-permute-start.14 = (f32[2,16,8,128]{3,2,1,0:T(8,128)S(1)}, f32[2,16,8,128]{3,2,1,0:T(8,128)S(1)}, u32[]{:S(2)}, u32[]{:S(2)}) collective-permute-start(f32[2,16,8,128]{3,2,1,0:T(8,128)S(1)} %get-tuple-element.26), channel_id=1, source_target_pairs={{0,1},{1,2},{2,3},{3,4},{4,5},{5,6},{6,7},{7,8},{8,9},{9,10},{10,1... | collective-permute-start | bytes 393224 | tf_op jit(solution)/shard_map/ppermute | solution.py:217
  182.6 7.1 %collective-permute-start.15 = (f32[2,16,8,128]{3,2,1,0:T(8,128)S(1)}, f32[2,16,8,128]{3,2,1,0:T(8,128)S(1)}, u32[]{:S(2)}, u32[]{:S(2)}) collective-permute-start(f32[2,16,8,128]{3,2,1,0:T(8,128)S(1)} %get-tuple-element.27), channel_id=1, source_target_pairs={{1,0},{2,1},{3,2},{4,3},{5,4},{6,5},{7,6},{8,7},{9,8},{10,9},{11,1... | collective-permute-start | bytes 393224 | tf_op jit(solution)/shard_map/ppermute | solution.py:217
  (11 other events, 8.5 us)

commit v2 on v1

v2 whole, which is shorter than its diff:
```python
import functools

import jax
import jax.numpy as jnp
import numpy as np
from jax import lax
from jax.experimental import pallas as pl
from jax.experimental.pallas import tpu as pltpu
from jax.sharding import Mesh, PartitionSpec as P

ROW = ("y", "core")
COL = ("z", "x")
PLANE = ("y", "core", "x")
LANES = 128
TILES = 16
GROUP = 4
F32 = jnp.float32
VMEM_BYTES = 56 * 1024 * 1024


def dft_tables(length):
    index = np.arange(length, dtype=np.int64)
    angle = 2.0 * np.pi / length * (index[:, None] * index[None, :] % length)
    factor = 1.0 / np.sqrt(length)
    cos_table = (np.cos(angle) * factor).astype(np.float32)
    sin_table = (np.sin(angle) * factor).astype(np.float32)
    forward = np.block([[cos_table, sin_table], [-sin_table, cos_table]])
    inverse = np.block([[cos_table, -sin_table], [sin_table, cos_table]])
    return jnp.asarray(forward, jnp.bfloat16), jnp.asarray(inverse, jnp.bfloat16)


def place_of(axes):
    index = lax.axis_index(axes)
    odd = lax.rem(index, 2)
    at_end = (index == 0) | (index == lax.axis_size(axes) - 1)
    return index, (2 - 2 * odd, 1, 2 * odd), at_end


def paired(value, axes, side):
    count = lax.axis_size(axes)
    pairs = [(i, (i + (1 if (i + side // 2) % 2 == 0 else -1)) % count) for i in range(count)]
    return lax.ppermute(value, axes, pairs)


def paired_far(value, axes, phase):
    count = lax.axis_size(axes)
    pairs = [(i, (i + (2 if (i // 2 + phase) % 2 == 0 else -2)) % count) for i in range(count)]
    return lax.ppermute(value, axes, pairs)


def dot(a, b):
    return jnp.dot(a, b, preferred_element_type=F32)


def transform(reals, imags, left, right):
    size = reals[0].shape[0]
    columns = [jnp.concatenate(pair, axis=0).astype(jnp.bfloat16) for pair in zip(reals, imags)]
    mid = dot(left, jnp.concatenate(columns, axis=1)).astype(jnp.bfloat16)
    rows = [
        jnp.concatenate([mid[:size, i * size : (i + 1) * size], mid[size:, i * size : (i + 1) * size]], axis=1)
        for i in range(len(reals))
    ]
    out = dot(jnp.concatenate(rows, axis=0), right)
    return (
        [out[i * size : (i + 1) * size, :size] for i in range(len(reals))],
        [out[i * size : (i + 1) * size, size:] for i in range(len(reals))],
    )


def updated_probe(probe, total):
    mean = jnp.sum(total * total, keepdims=True) / total.size
    return probe - 0.3 * total / jnp.sqrt(mean + 1e-06)


def pattern_group(group, count, offset_ref, pattern, left, right, probe, ext, gobj, gprobe):
    size = pattern.shape[1]
    region = size // 2
    tiles = size // 8
    slots = [group * GROUP + i for i in range(GROUP)]
    sub_id = lax.broadcasted_iota(jnp.int32, (1, 8, LANES), 1)
    lane_id = lax.broadcasted_iota(jnp.int32, (1, 8, LANES), 2)

    def corner(slot):
        row = offset_ref[0, slot] + region
        col = offset_ref[1, slot] + region
        tile = jnp.minimum(row // 8, region // 8 - 1)
        return tile, row - tile * 8, col

    def window(part, at):
        tile, sub, col = at
        pieces = [
            pltpu.roll(ext[v, part, pl.ds(tile, tiles + 1)], lax.rem(LANES - col, LANES), 2) for v in range(3)
        ]
        halves = []
        for v in range(2):
            x = jnp.where(lane_id < LANES - col, pieces[v], pieces[v + 1])
            x = pltpu.roll(x, lax.rem(8 - sub, 8), 1)
            halves.append(jnp.where(sub_id < 8 - sub, x[:tiles], x[1:]).reshape(size, LANES))
        return jnp.concatenate(halves, axis=1)

    def add_object(part, value, at):
        tile, sub, col = at
        zero = jnp.zeros((1, 8, LANES), F32)
        rolled = []
        for v in range(2):
            x = value[:, v * LANES : (v + 1) * LANES].reshape(tiles, 8, LANES)
            x = pltpu.roll(x, lax.rem(sub, 8), 1)
            x = jnp.where(
                sub_id < sub, jnp.concatenate([zero, x], axis=0), jnp.concatenate([x, zero], axis=0)
            )
            rolled.append(pltpu.roll(x, lax.rem(col, LANES), 2))
        inside = lane_id < col
        gobj[0, part, pl.ds(tile, tiles + 1)] += jnp.where(inside, 0.0, rolled[0])
        gobj[1, part, pl.ds(tile, tiles + 1)] += jnp.where(inside, rolled[0], rolled[1])
        gobj[2, part, pl.ds(tile, tiles + 1)] += jnp.where(inside, rolled[1], 0.0)

    def add_probe(part, value):
        for v in range(2):
            gprobe[part, v] += value[:, v * LANES : (v + 1) * LANES]

    at = [corner(slot) for slot in slots]
    win_real = [window(0, a) for a in at]
    win_imag = [window(1, a) for a in at]
    probe_real = jnp.concatenate([probe[0, 0], probe[0, 1]], axis=1)
    probe_imag = jnp.concatenate([probe[1, 0], probe[1, 1]], axis=1)
    far_real, far_imag = transform(
        [probe_real * a - probe_imag * b for a, b in zip(win_real, win_imag)],
        [probe_real * b + probe_imag * a for a, b in zip(win_real, win_imag)],
        left[...],
        right[...],
    )
    misfit = [
        jnp.where(slot < count, a * a + b * b - pattern[slot], 0.0) for a, b, slot in zip(far_real, far_imag, slots)
    ]
    back_real, back_imag = transform(
        [m * a for m, a in zip(misfit, far_real)],
        [m * b for m, b in zip(misfit, far_imag)],
        right[...],
        left[...],
    )
    both = list(zip(win_real, win_imag, back_real, back_imag))
    add_probe(0, sum(a * c + b * d for a, b, c, d in both))
    add_probe(1, sum(a * d - b * c for a, b, c, d in both))
    for i in range(GROUP):
        add_object(0, probe_real * back_real[i] + probe_imag * back_imag[i], at[i])
        add_object(1, probe_real * back_imag[i] - probe_imag * back_real[i], at[i])


def gradient_kernel(
    first,
    count_ref, offset_ref, pattern_ref, left_ref, right_ref, own_ref, side0_ref, side2_ref, start_ref, total_ref,
    out0_ref, own_out_ref, out2_ref, gprobe_ref, probe_ref, peak_ref,
    pattern, left, right, probe, total, ext, gobj, gprobe,
    strip_sems, probe_sems, table_sems, pattern_sems, out_sems,
):
    row, row_places, row_end = place_of(ROW)
    col, col_places, col_end = place_of(COL)
    groups = pattern.shape[0] // GROUP
    count = count_ref[0]

    if first:
        probe_copies = [
            pltpu.make_async_copy(start_ref.at[:, :, pl.ds(v * LANES, LANES)], probe.at[:, v], probe_sems.at[v])
            for v in range(2)
        ]
    else:
        probe_copies = [
            pltpu.make_async_copy(total_ref, total, probe_sems.at[0]),
            pltpu.make_async_copy(start_ref, probe, probe_sems.at[1]),
        ]
    strip_copies = [
        pltpu.make_async_copy(
            ref.at[j],
            ext.at[col_places[j], :, pl.ds(row_places[i] * TILES, TILES)],
            strip_sems.at[i * 3 + j],
        )
        for i, ref in ((1, own_ref), (0, side0_ref), (2, side2_ref))
        for j in range(3)
    ]
    table_copies = [
        pltpu.make_async_copy(left_ref, left, table_sems.at[0]),
        pltpu.make_async_copy(right_ref, right, table_sems.at[1]),
    ]
    pattern_copies = [
        pltpu.make_async_copy(
            pattern_ref.at[pl.ds(g * GROUP, GROUP)], pattern.at[pl.ds(g * GROUP, GROUP)], pattern_sems.at[g]
        )
        for g in range(groups)
    ]
    for copy in probe_copies + strip_copies + table_copies + pattern_copies:
        copy.start()
    gobj[...] = jnp.zeros_like(gobj)
    gprobe[...] = jnp.zeros_like(gprobe)
    for copy in probe_copies:
        copy.wait()
    if not first:
        probe[...] = updated_probe(probe[...], total[...])
    power = probe[0] * probe[0] + probe[1] * probe[1]
    peak_ref[...] = jnp.broadcast_to(jnp.max(power, keepdims=True).reshape(1, 1) + 1e-06, peak_ref.shape)
    for copy in strip_copies:
        copy.wait()

    @pl.when(col_end)
    def _():
        ext[col_places[2]] = jnp.zeros(ext.shape[1:], F32)

    @pl.when(row_end)
    def _():
        ext[:, :, pl.ds(row_places[2] * TILES, TILES)] = jnp.zeros(ext.shape[:2] + (TILES, 8, LANES), F32)

    for copy in table_copies + pattern_copies:
        copy.wait()

    def visit(group, carry):
        pattern_group(group, count, offset_ref, pattern, left, right, probe, ext, gobj, gprobe)
        return carry

    lax.fori_loop(0, (count + GROUP - 1) // GROUP, visit, 0)

    out_copies = [
        pltpu.make_async_copy(gprobe, gprobe_ref, out_sems.at[9]),
        pltpu.make_async_copy(probe, probe_ref, out_sems.at[10]),
    ] + [
        pltpu.make_async_copy(
            gobj.at[col_places[j], :, pl.ds(row_places[i] * TILES, TILES)], ref.at[j], out_sems.at[i * 3 + j]
        )
        for i, ref in ((0, out0_ref), (2, out2_ref), (1, own_out_ref))
        for j in range(3)
    ]
    for copy in out_copies:
        copy.start()
    for copy in out_copies:
        copy.wait()


def gradients(first, count, offsets, patterns, tables, strips, probe, total):
    slots, size = patterns.shape[:2]
    vmem = pl.BlockSpec(memory_space=pltpu.VMEM)
    smem = pl.BlockSpec(memory_space=pltpu.SMEM)
    anywhere = pl.BlockSpec(memory_space=pl.ANY)
    hbm = pl.BlockSpec(memory_space=pltpu.HBM)
    strip = jax.ShapeDtypeStruct((3, 2, TILES, 8, LANES), F32)
    halves = jax.ShapeDtypeStruct((2, 2, size, LANES), F32)
    ext = pltpu.VMEM((3, 2, 3 * TILES, 8, LANES), F32)
    return pl.pallas_call(
        functools.partial(gradient_kernel, first),
        out_shape=(strip, strip, strip, halves, halves, jax.ShapeDtypeStruct((8, LANES), F32)),
        in_specs=[smem, smem] + [anywhere] * 8,
        out_specs=(hbm,) * 5 + (vmem,),
        scratch_shapes=[
            pltpu.VMEM(patterns.shape, F32),
            pltpu.VMEM(tables[0].shape, jnp.bfloat16),
            pltpu.VMEM(tables[1].shape, jnp.bfloat16),
            pltpu.VMEM(halves.shape, F32),
            pltpu.VMEM(halves.shape, F32),
            ext,
            ext,
            pltpu.VMEM(halves.shape, F32),
            pltpu.SemaphoreType.DMA((9,)),
            pltpu.SemaphoreType.DMA((2,)),
            pltpu.SemaphoreType.DMA((2,)),
            pltpu.SemaphoreType.DMA((slots // GROUP,)),
            pltpu.SemaphoreType.DMA((11,)),
        ],
        compiler_params=pltpu.CompilerParams(vmem_limit_bytes=VMEM_BYTES),
    )(count, offsets, patterns, *tables, *strips, probe, total)


def small_call(kernel, out_shapes, *args):
    vmem = pl.BlockSpec(memory_space=pltpu.VMEM)
    return pl.pallas_call(
        kernel,
        out_shape=tuple(jax.ShapeDtypeStruct(shape, F32) for shape in out_shapes),
        in_specs=[vmem] * len(args),
        out_specs=(vmem,) * len(out_shapes),
        compiler_params=pltpu.CompilerParams(vmem_limit_bytes=VMEM_BYTES),
    )(*args)


def sum_copies_kernel(in_ref, out_ref):
    total = in_ref[0]
    for i in range(1, in_ref.shape[0]):
        total = total + in_ref[i]
    for i in range(out_ref.shape[0]):
        out_ref[i] = total


def sum_copies(value, copies):
    return small_call(sum_copies_kernel, [(copies,) + value.shape[1:]], value)[0]


def exchange(value, axes):
    return lax.all_to_all(value, axes, 0, 0, tiled=True)


def total_over_devices(gprobe):
    shape = gprobe.shape
    plane = lax.axis_size(PLANE)
    chunks = gprobe.reshape(plane, -1, LANES)
    shares = sum_copies(exchange(chunks, PLANE), lax.axis_size("z"))
    shares = sum_copies(exchange(shares, "z"), plane)
    return exchange(shares, PLANE).reshape(shape)


def row_sum(own_ref, side0_ref, side2_ref, j):
    at_end = place_of(ROW)[2]
    return own_ref[j] + side0_ref[j] + jnp.where(at_end, 0.0, side2_ref[j])


def far_choice():
    index, places, at_end = place_of(COL)
    return lax.rem(index, 2) == lax.rem(index // 2, 2)


def rows_kernel(own_ref, side0_ref, side2_ref, sum_ref, near0_ref, near2_ref, far0_ref, far2_ref):
    side0, own, side2 = (row_sum(own_ref, side0_ref, side2_ref, j) for j in range(3))
    sum_ref[0], sum_ref[1], sum_ref[2] = side0, own, side2
    near0_ref[0], near0_ref[1] = own, side0
    near2_ref[0], near2_ref[1] = own, side2
    first = far_choice()
    far0_ref[...] = jnp.where(first, side0, side2)
    far2_ref[...] = jnp.where(first, side2, side0)


def update_kernel(strip_ref, sum_ref, near0_ref, near2_ref, far0_ref, far2_ref, peak_ref, out_ref):
    index, places, at_end = place_of(COL)
    inner = (index >= 2, index <= lax.axis_size(COL) - 3)
    odd = lax.rem(index, 2) == 1
    first = far_choice()
    far0 = jnp.where(first, far0_ref[...], far2_ref[...])
    far2 = jnp.where(first, far2_ref[...], far0_ref[...])
    reach0 = jnp.where(odd, inner[0].astype(jnp.int32), inner[1].astype(jnp.int32)) == 1
    reach2 = jnp.where(odd, inner[1].astype(jnp.int32), inner[0].astype(jnp.int32)) == 1
    peak = peak_ref[...]
    grad0 = sum_ref[0] + near0_ref[0] + jnp.where(reach0, far0, 0.0)
    grad = sum_ref[1] + near0_ref[1] + jnp.where(at_end, 0.0, near2_ref[1])
    grad2 = sum_ref[2] + near2_ref[0] + jnp.where(reach2, far2, 0.0)
    out_ref[0] = strip_ref[0] - grad0 / peak
    out_ref[1] = strip_ref[1] - grad / peak
    out_ref[2] = strip_ref[2] - grad2 / peak


def last_rows_kernel(own_ref, side0_ref, side2_ref, sum0_ref, sum1_ref, sum2_ref):
    for j, ref in enumerate((sum0_ref, sum1_ref, sum2_ref)):
        ref[...] = row_sum(own_ref, side0_ref, side2_ref, j)


def last_object_kernel(strip_ref, sum_ref, near0_ref, near2_ref, peak_ref, out_ref):
    at_end = place_of(COL)[2]
    grad = sum_ref[...] + near0_ref[...] + jnp.where(at_end, 0.0, near2_ref[...])
    out_ref[...] = strip_ref[1] - grad / peak_ref[...]


def last_probe_kernel(probe_ref, total_ref, out_ref):
    new = updated_probe(probe_ref[...], total_ref[...])
    for part in range(2):
        for v in range(2):
            out_ref[part, :, v * LANES : (v + 1) * LANES] = new[part, v]


def body(object_field, probe_field, intensity, scan_offsets, pattern_counts):
    size = probe_field.shape[1]
    slots = intensity.shape[2]
    patterns = intensity.reshape(slots, size, size)
    offsets = scan_offsets.reshape(slots, 2).T
    count = pattern_counts.reshape(1)
    tables = dft_tables(size)
    block = (2, TILES, 8, LANES)
    strip_shape = (3,) + block

    own = object_field.reshape(block)
    strip = jnp.stack([paired(own, COL, 0), own, paired(own, COL, 2)])
    strips = (strip, paired(strip, ROW, 0), paired(strip, ROW, 2))
    out0, mid, out2, gprobe, probe, peak = gradients(
        True, count, offsets, patterns, tables, strips, probe_field, probe_field
    )
    total = total_over_devices(gprobe)
    sums, near0, near2, far0, far2 = small_call(
        rows_kernel,
        [strip_shape, (2,) + block, (2,) + block, block, block],
        mid, paired(out0, ROW, 0), paired(out2, ROW, 2),
    )
    (strip,) = small_call(
        update_kernel,
        [strip_shape],
        strip, sums, paired(near0, COL, 0), paired(near2, COL, 2), paired_far(far0, COL, 0), paired_far(far2, COL, 1), peak,
    )
    strips = (strip, paired(strip, ROW, 0), paired(strip, ROW, 2))
    out0, mid, out2, gprobe, probe, peak = gradients(
        False, count, offsets, patterns, tables, strips, probe, total
    )
    total = total_over_devices(gprobe)
    sum0, sum1, sum2 = small_call(
        last_rows_kernel, [block] * 3, mid, paired(out0, ROW, 0), paired(out2, ROW, 2)
    )
    (new_object,) = small_call(
        last_object_kernel, [block], strip, sum1, paired(sum0, COL, 0), paired(sum2, COL, 2), peak
    )
    (new_probe,) = small_call(last_probe_kernel, [probe_field.shape], probe, total)
    return (new_object.reshape(object_field.shape), new_probe)


def solution(mesh):
    split = Mesh(mesh.devices.reshape(4, 2, 8, 4), ("y", "core", "z", "x"))
    in_specs = (
        P(None, ROW, COL),
        P(),
        P(ROW, COL, None, None, None),
        P(ROW, COL, None, None),
        P(ROW, COL),
    )
    out_specs = (P(None, ROW, COL), P())
    return jax.shard_map(body, mesh=split, in_specs=in_specs, out_specs=out_specs, check_vma=False)
```

time: 194 us -> 167 us (0.86)
  starting transfers between devices: 119 us -> 54.1 us
  Pallas kernels: 12.5 us -> 44.6 us
  blocking collectives: 0 us -> 16.6 us
  other arithmetic: 10.6 us -> 0.93 us
  local copies, waits for them, and re-layouts: 15.1 us -> 8.03 us
  waiting for transfers between devices: 33.8 us -> 40 us
    all_to_all x6 -> x5, starting transfers between devices: 65.4 us -> 26.2 us  [exchange(): return lax.all_to_all(value, axes, 0, 0, tiled=True)]
    ppermute x16, starting transfers between devices: 53.1 us -> 28 us  [the longest x14 24.1 us: paired(): return lax.ppermute(value, axes, pairs)]
    pallas_call x2, Pallas kernels: 7.92 us -> 26.9 us  [gradients(): pl.pallas_call(functools.partial(gradient_kernel, first), out_shape=(stri...]
    all_to_all x0 -> x1, blocking collectives: none -> 16.6 us  [exchange(): return lax.all_to_all(value, axes, 0, 0, tiled=True)]
    pallas_call x5 -> x9, Pallas kernels: 4.54 us -> 17.7 us  [small_call(): pl.pallas_call(kernel, out_shape=tuple((jax.ShapeDtypeStruct(shape, F32)...]
    ppermute x16, waiting for transfers between devices: 13.5 us -> 23.9 us  [the longest x14 23.3 us: paired(): return lax.ppermute(value, axes, pairs)]
    unnamed x42 -> x40, local copies, waits for them, and re-layouts: 12.4 us -> 8.03 us
    all_to_all x6 -> x5, waiting for transfers between devices: 20.3 us -> 16 us  [exchange(): return lax.all_to_all(value, axes, 0, 0, tiled=True)]
  transfers between devices with their start and end apart: 22 -> 21, of which waited for: 10 -> 9; matrix products, arithmetic and copies ran while one was open for 6% -> 0% of each run, Pallas kernels for 1% -> 8%
where the time goes in v2:
time: 167 us; the launch traced here: 166 us
  starting transfers between devices  54.1 us (32%)
  Pallas kernels  44.6 us (27%)
  waiting for transfers between devices  40 us (24%)
  blocking collectives  16.6 us (10%)
  local copies, waits for them, and re-layouts  8.03 us (5%)
    pallas_call x2, Pallas kernels, gradients(): pl.pallas_call(functools.partial(gradient_kernel, first), out_shape=(stri...  26.9 us
    all_to_all x5, starting transfers between devices, exchange(): return lax.all_to_all(value, axes, 0, 0, tiled=True)  26.2 us
    ppermute x14, starting transfers between devices, paired(): return lax.ppermute(value, axes, pairs)  24.1 us
    ppermute x14, waiting for transfers between devices, paired(): return lax.ppermute(value, axes, pairs)  23.3 us
    pallas_call x9, Pallas kernels, small_call(): pl.pallas_call(kernel, out_shape=tuple((jax.ShapeDtypeStruct(shape, F32)...  17.7 us
    all_to_all x1, blocking collectives, exchange(): return lax.all_to_all(value, axes, 0, 0, tiled=True)  16.6 us
    all_to_all x5, waiting for transfers between devices, exchange(): return lax.all_to_all(value, axes, 0, 0, tiled=True)  16 us
    unnamed x40, local copies, waits for them, and re-layouts  8.03 us
  transfers between devices with their start and end apart: 21, of which 9 were waited for; matrix products, arithmetic and copies ran while one was open for 0% of the time, Pallas kernels for 8%

profile of v2, /device:TPU:1, one launch (start us, length us, event | category | flops | bytes accessed | tf_op | source)
XLA Modules:
  0.0 165.8 jit_solution(11789635284388645024)
XLA Ops:
  0.6 8.7 %collective-permute-start.1 = (f32[2,16,8,128]{3,2,1,0:T(8,128)}, f32[2,16,8,128]{3,2,1,0:T(8,128)S(1)}, u32[]{:S(2)}, u32[]{:S(2)}) collective-permute-start(f32[2,16,8,128]{3,2,1,0:T(8,128)} %bitcast.23), channel_id=1, source_target_pairs={{0,31},{1,2},{2,1},{3,4},{4,3},{5,6},{6,5},{7,8},{8,7},{9,10},{10,... | collective-permute-start | bytes 393224 | tf_op jit(solution)/shard_map/ppermute | solution.py:42
  9.3 3.4 %collective-permute-done.1 = f32[2,16,8,128]{3,2,1,0:T(8,128)S(1)} collective-permute-done((f32[2,16,8,128]{3,2,1,0:T(8,128)}, f32[2,16,8,128]{3,2,1,0:T(8,128)S(1)}, u32[]{:S(2)}, u32[]{:S(2)}) %collective-permute-start.1) | collective-permute-done | bytes 131104 | tf_op jit(solution)/shard_map/ppermute | solution.py:42
  14.5 3.1 %collective-permute-start.3 = (f32[3,2,16,8,128]{4,3,2,1,0:T(8,128)S(1)}, f32[3,2,16,8,128]{4,3,2,1,0:T(8,128)S(1)}, u32[]{:S(2)}, u32[]{:S(2)}) collective-permute-start(f32[3,2,16,8,128]{4,3,2,1,0:T(8,128)S(1)} %pad_maximum_fusion.own_ref.strip_ref), channel_id=1, source_target_pairs={{0,224},{32,64},{64,32},{96,128},{128,96},{160,192},{192,160},{224... | collective-permute-start | bytes 1179656 | tf_op jit(solution)/shard_map/ppermute | solution.py:42
  18.4 5.0 %collective-permute-done.3.side2_ref = f32[3,2,16,8,128]{4,3,2,1,0:T(8,128)S(1)} collective-permute-done((f32[3,2,16,8,128]{4,3,2,1,0:T(8,128)S(1)}, f32[3,2,16,8,128]{4,3,2,1,0:T(8,128)S(1)}, u32[]{:S(2)}, u32[]{:S(2)}) %collective-permute-start.3) | collective-permute-done | bytes 393248 | tf_op jit(solution)/shard_map/ppermute | solution.py:42
  24.3 13.3 %shard_map.86 = (f32[3,2,16,8,128]{4,3,2,1,0:T(8,128)}, f32[3,2,16,8,128]{4,3,2,1,0:T(8,128)}, f32[3,2,16,8,128]{4,3,2,1,0:T(8,128)}, f32[2,2,256,128]{3,2,1,0:T...) custom-call(s32[1]{0:T(128)} %bitcast.14.count_ref, s32[2,8]{1,0:T(2,128)} %bitcast.28, f32[8,256,256]{2,1,0:T(8,128)} %bitcast.16, ...), custom_call_target="tpu_custom_call" | custom-call | tf_op jit(solution)/shard_map/pallas_call | solution.py:245
  37.6 4.8 %all-to-all-start = ((f32[32,32,128]{2,1,0:T(8,128)}), f32[32,32,128]{2,1,0:T(8,128)S(1)}, u32[]{:S(2)}, u32[]{:S(2)}) async-start(f32[32,32,128]{2,1,0:T(8,128)} %bitcast.20), calls=%async_computation | async-start | bytes 1048576 | tf_op jit(solution)/shard_map/all_to_all | solution.py:293
  42.8 1.5 collective-permute-start.5
  44.4 9.5 %all-to-all-done.in_ref = f32[32,32,128]{2,1,0:T(8,128)S(1)} async-done(((f32[32,32,128]{2,1,0:T(8,128)}), f32[32,32,128]{2,1,0:T(8,128)S(1)}, u32[]{:S(2)}, u32[]{:S(2)}) %all-to-all-start) | async-done | bytes 524320 | tf_op jit(solution)/shard_map/all_to_all | solution.py:293
  54.7 1.7 %shard_map.89 = f32[8,32,128]{2,1,0:T(8,128)} custom-call(f32[32,32,128]{2,1,0:T(8,128)} %copy-done.3), custom_call_target="tpu_custom_call" | custom-call | tf_op jit(solution)/shard_map/pallas_call | solution.py:271
  56.4 4.7 %all-to-all-start.1 = ((f32[8,32,128]{2,1,0:T(8,128)}), f32[8,32,128]{2,1,0:T(8,128)S(1)}, u32[]{:S(2)}, u32[]{:S(2)}) async-start(f32[8,32,128]{2,1,0:T(8,128)} %shard_map.89), calls=%async_computation.1 | async-start | bytes 262144 | tf_op jit(solution)/shard_map/all_to_all | solution.py:293
  62.0 2.3 %shard_map.87 = (f32[3,2,16,8,128]{4,3,2,1,0:T(8,128)}, f32[2,2,16,8,128]{4,3,2,1,0:T(8,128)}, f32[2,2,16,8,128]{4,3,2,1,0:T(8,128)}, f32[2,16,8,128]{3,2,1,0:T(8,128)}, f32[2,16,8,128]{3,2,1,0:T(8,128)}) custom-call(f32[3,2,16,8,128]{4,3,2,1,0:T(8,128)} %get-tuple-element.22.own_ref, f32[3,2,16,8,128]{4,3,2,1,0:T(8,128)} %copy-done.10, ...), custom_call_target="tpu_custom_call" | custom-call | tf_op jit(solution)/shard_map/pallas_call | solution.py:271
  64.6 3.3 %collective-permute-start.7 = (f32[2,2,16,8,128]{4,3,2,1,0:T(8,128)}, f32[2,2,16,8,128]{4,3,2,1,0:T(8,128)S(1)}, u32[]{:S(2)}, u32[]{:S(2)}) collective-permute-start(f32[2,2,16,8,128]{4,3,2,1,0:T(8,128)} %get-tuple-element.27), channel_id=1, source_target_pairs={{0,31},{1,2},{2,1},{3,4},{4,3},{5,6},{6,5},{7,8},{8,7},{9,10},{10,... | collective-permute-start | bytes 786440 | tf_op jit(solution)/shard_map/ppermute | solution.py:42
  67.9 3.9 %collective-permute-start.9 = (f32[2,16,8,128]{3,2,1,0:T(8,128)}, f32[2,16,8,128]{3,2,1,0:T(8,128)S(1)}, u32[]{:S(2)}, u32[]{:S(2)}) collective-permute-start(f32[2,16,8,128]{3,2,1,0:T(8,128)} %get-tuple-element.29), channel_id=1, source_target_pairs={{0,30},{1,31},{2,4},{3,5},{4,2},{5,3},{6,8},{7,9},{8,6},{9,7},{10,... | collective-permute-start | bytes 393224 | tf_op jit(solution)/shard_map/ppermute | solution.py:48
  72.5 1.8 %shard_map.90 = f32[32,32,128]{2,1,0:T(8,128)} custom-call(f32[8,32,128]{2,1,0:T(8,128)} %copy-done.4), custom_call_target="tpu_custom_call" | custom-call | tf_op jit(solution)/shard_map/pallas_call | solution.py:271
  74.2 6.1 %all-to-all-start.2 = ((f32[32,32,128]{2,1,0:T(8,128)}), f32[32,32,128]{2,1,0:T(8,128)S(1)}, u32[]{:S(2)}, u32[]{:S(2)}) async-start(f32[32,32,128]{2,1,0:T(8,128)} %shard_map.90), calls=%async_computation.2 | async-start | bytes 1048576 | tf_op jit(solution)/shard_map/all_to_all | solution.py:293
  81.9 2.2 %shard_map.88.own_ref.strip_ref = f32[3,2,16,8,128]{4,3,2,1,0:T(8,128)} custom-call(f32[3,2,16,8,128]{4,3,2,1,0:T(8,128)} %copy-done, f32[3,2,16,8,128]{4,3,2,1,0:T(8,128)} %get-tuple-element.25.sum_ref, f32[2,2,16,8,128]{4,3,2,1,0:T(8,128)} %copy-done.14, f32[2,2,16,8,128]{4,3,2,1,0:T(8,128)} %copy-done.15, f32[2,16,8,128]{3,2,1,0:T(8,128)} %copy-done.18, ...), custom_call_target="tpu_custom_call" | custom-call | tf_op jit(solution)/shard_map/pallas_call | solution.py:271
  84.1 1.8 %collective-permute-start.11 = (f32[3,2,16,8,128]{4,3,2,1,0:T(8,128)}, f32[3,2,16,8,128]{4,3,2,1,0:T(8,128)S(1)}, u32[]{:S(2)}, u32[]{:S(2)}) collective-permute-start(f32[3,2,16,8,128]{4,3,2,1,0:T(8,128)} %shard_map.88.own_ref.strip_ref), channel_id=1, source_target_pairs={{0,224},{32,64},{64,32},{96,128},{128,96},{160,192},{192,160},{224... | collective-permute-start | bytes 1179656 | tf_op jit(solution)/shard_map/ppermute | solution.py:42
  86.6 7.6 %collective-permute-done.11.side2_ref = f32[3,2,16,8,128]{4,3,2,1,0:T(8,128)S(1)} collective-permute-done((f32[3,2,16,8,128]{4,3,2,1,0:T(8,128)}, f32[3,2,16,8,128]{4,3,2,1,0:T(8,128)S(1)}, u32[]{:S(2)}, u32[]{:S(2)}) %collective-permute-start.11) | collective-permute-done | bytes 393248 | tf_op jit(solution)/shard_map/ppermute | solution.py:42
  95.3 13.6 %shard_map.91 = (f32[3,2,16,8,128]{4,3,2,1,0:T(8,128)}, f32[3,2,16,8,128]{4,3,2,1,0:T(8,128)}, f32[3,2,16,8,128]{4,3,2,1,0:T(8,128)}, f32[2,2,256,128]{3,2,1,0:T...) custom-call(s32[1]{0:T(128)} %bitcast.15.count_ref, s32[2,8]{1,0:T(2,128)} %bitcast.29, f32[8,256,256]{2,1,0:T(8,128)} %bitcast.17, ...), custom_call_target="tpu_custom_call" | custom-call | tf_op jit(solution)/shard_map/pallas_call | solution.py:245
  108.9 16.6 %all_to_all.30.in_ref = f32[32,32,128]{2,1,0:T(8,128)} all-to-all(f32[32,32,128]{2,1,0:T(8,128)} %bitcast.21), channel_id=1, replica_groups=mesh['y'=4,'core'=2,'z'=8,'x'=4] {'y','core','x'}, dimensions={0} | all-to-all | bytes 1048576 | tf_op jit(solution)/shard_map/all_to_all | solution.py:293
  125.5 1.7 %shard_map.94 = f32[8,32,128]{2,1,0:T(8,128)} custom-call(f32[32,32,128]{2,1,0:T(8,128)} %all_to_all.30.in_ref), custom_call_target="tpu_custom_call" | custom-call | tf_op jit(solution)/shard_map/pallas_call | solution.py:271
  127.3 4.5 %all-to-all-start.4 = ((f32[8,32,128]{2,1,0:T(8,128)}), f32[8,32,128]{2,1,0:T(8,128)S(1)}, u32[]{:S(2)}, u32[]{:S(2)}) async-start(f32[8,32,128]{2,1,0:T(8,128)} %shard_map.94), calls=%async_computation.4 | async-start | bytes 262144 | tf_op jit(solution)/shard_map/all_to_all | solution.py:293
  133.0 6.5 %all-to-all-done.4.in_ref = f32[8,32,128]{2,1,0:T(8,128)S(1)} async-done(((f32[8,32,128]{2,1,0:T(8,128)}), f32[8,32,128]{2,1,0:T(8,128)S(1)}, u32[]{:S(2)}, u32[]{:S(2)}) %all-to-all-start.4) | async-done | bytes 131104 | tf_op jit(solution)/shard_map/all_to_all | solution.py:293
  140.2 1.8 %shard_map.95 = f32[32,32,128]{2,1,0:T(8,128)} custom-call(f32[8,32,128]{2,1,0:T(8,128)} %copy-done.5), custom_call_target="tpu_custom_call" | custom-call | tf_op jit(solution)/shard_map/pallas_call | solution.py:271
  142.0 5.9 %all-to-all-start.5 = ((f32[32,32,128]{2,1,0:T(8,128)}), f32[32,32,128]{2,1,0:T(8,128)S(1)}, u32[]{:S(2)}, u32[]{:S(2)}) async-start(f32[32,32,128]{2,1,0:T(8,128)} %shard_map.95), calls=%async_computation.5 | async-start | bytes 1048576 | tf_op jit(solution)/shard_map/all_to_all | solution.py:293
  148.8 2.0 %shard_map.92 = (f32[2,16,8,128]{3,2,1,0:T(8,128)}, f32[2,16,8,128]{3,2,1,0:T(8,128)}, f32[2,16,8,128]{3,2,1,0:T(8,128)}) custom-call(f32[3,2,16,8,128]{4,3,2,1,0:T(8,128)} %get-tuple-element.33.own_ref, f32[3,2,16,8,128]{4,3,2,1,0:T(8,128)} %copy-done.11, f32[3,2,16,8,128]{4,3,2,1,0:T(8,128)} %copy-done.13), custom_call_target="tpu_custom_call" | custom-call | tf_op jit(solution)/shard_map/pallas_call | solution.py:271
  150.8 1.4 collective-permute-start.14
  152.2 1.6 collective-permute-start.15
  153.8 4.8 %collective-permute-done.14.near0_ref = f32[2,16,8,128]{3,2,1,0:T(8,128)S(1)} collective-permute-done((f32[2,16,8,128]{3,2,1,0:T(8,128)}, f32[2,16,8,128]{3,2,1,0:T(8,128)S(1)}, u32[]{:S(2)}, u32[]{:S(2)}) %collective-permute-start.14) | collective-permute-done | bytes 131104 | tf_op jit(solution)/shard_map/ppermute | solution.py:42
  158.6 1.5 collective-permute-done.15.near2_ref
  160.8 1.8 %shard_map.93 = f32[2,16,8,128]{3,2,1,0:T(8,128)} custom-call(f32[3,2,16,8,128]{4,3,2,1,0:T(8,128)} %shard_map.88.own_ref.strip_ref, f32[2,16,8,128]{3,2,1,0:T(8,128)} %get-tuple-element.36.sum_ref, f32[2,16,8,128]{3,2,1,0:T(8,128)} %copy-done.16, f32[2,16,8,128]{3,2,1,0:T(8,128)} %copy-done.17, f32[8,128]{1,0:T(8,128)} %get-tuple-element.39.peak_ref), custom_call_target="tpu_custom_call" | custom-call | tf_op jit(solution)/shard_map/pallas_call | solution.py:271
  163.4 2.4 %shard_map.96 = f32[2,256,256]{2,1,0:T(8,128)} custom-call(f32[2,2,256,128]{3,2,1,0:T(8,128)} %get-tuple-element.40.probe_ref, f32[2,2,256,128]{3,2,1,0:T(8,128)} %bitcast.19), custom_call_target="tpu_custom_call" | custom-call | tf_op jit(solution)/shard_map/pallas_call | solution.py:271
  (63 shorter events, 13.1 us)
Async XLA Ops:
  0.6 12.1 %collective-permute-start.1 = (f32[2,16,8,128]{3,2,1,0:T(8,128)}, f32[2,16,8,128]{3,2,1,0:T(8,128)S(1)}, u32[]{:S(2)}, u32[]{:S(2)}) collective-permute-start(f32[2,16,8,128]{3,2,1,0:T(8,128)} %bitcast.23), channel_id=1, source_target_pairs={{0,31},{1,2},{2,1},{3,4},{4,3},{5,6},{6,5},{7,8},{8,7},{9,10},{10,... | collective-permute-start | bytes 393224 | tf_op jit(solution)/shard_map/ppermute | solution.py:42
  9.3 4.3 %collective-permute-start = (f32[2,16,8,128]{3,2,1,0:T(8,128)}, f32[2,16,8,128]{3,2,1,0:T(8,128)S(1)}, u32[]{:S(2)}, u32[]{:S(2)}) collective-permute-start(f32[2,16,8,128]{3,2,1,0:T(8,128)} %bitcast.24), channel_id=1, source_target_pairs={{0,1},{1,0},{2,3},{3,2},{4,5},{5,4},{6,7},{7,6},{8,9},{9,8},{10,11... | collective-permute-start | bytes 393224 | tf_op jit(solution)/shard_map/ppermute | solution.py:42
  14.5 8.9 %copy-start = (f32[3,2,16,8,128]{4,3,2,1,0:T(8,128)}, f32[3,2,16,8,128]{4,3,2,1,0:T(8,128)S(1)}, u32[]{:S(2)}) copy-start(f32[3,2,16,8,128]{4,3,2,1,0:T(8,128)S(1)} %pad_maximum_fusion.own_ref.strip_ref) | copy-start | bytes 1179652
  14.5 8.9 %collective-permute-start.3 = (f32[3,2,16,8,128]{4,3,2,1,0:T(8,128)S(1)}, f32[3,2,16,8,128]{4,3,2,1,0:T(8,128)S(1)}, u32[]{:S(2)}, u32[]{:S(2)}) collective-permute-start(f32[3,2,16,8,128]{4,3,2,1,0:T(8,128)S(1)} %pad_maximum_fusion.own_ref.strip_ref), channel_id=1, source_target_pairs={{0,224},{32,64},{64,32},{96,128},{128,96},{160,192},{192,160},{224... | collective-permute-start | bytes 1179656 | tf_op jit(solution)/shard_map/ppermute | solution.py:42
  17.7 5.8 %collective-permute-start.2 = (f32[3,2,16,8,128]{4,3,2,1,0:T(8,128)S(1)}, f32[3,2,16,8,128]{4,3,2,1,0:T(8,128)S(1)}, u32[]{:S(2)}, u32[]{:S(2)}) collective-permute-start(f32[3,2,16,8,128]{4,3,2,1,0:T(8,128)S(1)} %pad_maximum_fusion.own_ref.strip_ref), channel_id=1, source_target_pairs={{0,32},{32,0},{64,96},{96,64},{128,160},{160,128},{192,224},{224,1... | collective-permute-start | bytes 1179656 | tf_op jit(solution)/shard_map/ppermute | solution.py:42
  23.4 0.9 copy-start.9
  37.6 16.2 %all-to-all-start = ((f32[32,32,128]{2,1,0:T(8,128)}), f32[32,32,128]{2,1,0:T(8,128)S(1)}, u32[]{:S(2)}, u32[]{:S(2)}) async-start(f32[32,32,128]{2,1,0:T(8,128)} %bitcast.20), calls=%async_computation | async-start | bytes 1048576 | tf_op jit(solution)/shard_map/all_to_all | solution.py:293
  42.5 18.7 %collective-permute-start.4 = (f32[3,2,16,8,128]{4,3,2,1,0:T(8,128)}, f32[3,2,16,8,128]{4,3,2,1,0:T(8,128)S(1)}, u32[]{:S(2)}, u32[]{:S(2)}) collective-permute-start(f32[3,2,16,8,128]{4,3,2,1,0:T(8,128)} %get-tuple-element.23), channel_id=1, source_target_pairs={{0,32},{32,0},{64,96},{96,64},{128,160},{160,128},{192,224},{224,1... | collective-permute-start | bytes 1179656 | tf_op jit(solution)/shard_map/ppermute | solution.py:42
  42.8 18.4 %collective-permute-start.5 = (f32[3,2,16,8,128]{4,3,2,1,0:T(8,128)}, f32[3,2,16,8,128]{4,3,2,1,0:T(8,128)S(1)}, u32[]{:S(2)}, u32[]{:S(2)}) collective-permute-start(f32[3,2,16,8,128]{4,3,2,1,0:T(8,128)} %get-tuple-element.24), channel_id=1, source_target_pairs={{0,224},{32,64},{64,32},{96,128},{128,96},{160,192},{192,160},{224... | collective-permute-start | bytes 1179656 | tf_op jit(solution)/shard_map/ppermute | solution.py:42
  53.9 0.8 copy-start.3
  56.4 15.4 %all-to-all-start.1 = ((f32[8,32,128]{2,1,0:T(8,128)}), f32[8,32,128]{2,1,0:T(8,128)S(1)}, u32[]{:S(2)}, u32[]{:S(2)}) async-start(f32[8,32,128]{2,1,0:T(8,128)} %shard_map.89), calls=%async_computation.1 | async-start | bytes 262144 | tf_op jit(solution)/shard_map/all_to_all | solution.py:293
  61.2 0.9 copy-start.12
  64.3 16.7 %collective-permute-start.6 = (f32[2,2,16,8,128]{4,3,2,1,0:T(8,128)}, f32[2,2,16,8,128]{4,3,2,1,0:T(8,128)S(1)}, u32[]{:S(2)}, u32[]{:S(2)}) collective-permute-start(f32[2,2,16,8,128]{4,3,2,1,0:T(8,128)} %get-tuple-element.26), channel_id=1, source_target_pairs={{0,1},{1,0},{2,3},{3,2},{4,5},{5,4},{6,7},{7,6},{8,9},{9,8},{10,11... | collective-permute-start | bytes 786440 | tf_op jit(solution)/shard_map/ppermute | solution.py:42
  64.6 16.5 %collective-permute-start.7 = (f32[2,2,16,8,128]{4,3,2,1,0:T(8,128)}, f32[2,2,16,8,128]{4,3,2,1,0:T(8,128)S(1)}, u32[]{:S(2)}, u32[]{:S(2)}) collective-permute-start(f32[2,2,16,8,128]{4,3,2,1,0:T(8,128)} %get-tuple-element.27), channel_id=1, source_target_pairs={{0,31},{1,2},{2,1},{3,4},{4,3},{5,6},{6,5},{7,8},{8,7},{9,10},{10,... | collective-permute-start | bytes 786440 | tf_op jit(solution)/shard_map/ppermute | solution.py:42
  67.9 13.1 %collective-permute-start.8 = (f32[2,16,8,128]{3,2,1,0:T(8,128)}, f32[2,16,8,128]{3,2,1,0:T(8,128)S(1)}, u32[]{:S(2)}, u32[]{:S(2)}) collective-permute-start(f32[2,16,8,128]{3,2,1,0:T(8,128)} %get-tuple-element.28), channel_id=1, source_target_pairs={{0,2},{1,3},{2,0},{3,1},{4,6},{5,7},{6,4},{7,5},{8,10},{9,11},{10,... | collective-permute-start | bytes 393224 | tf_op jit(solution)/shard_map/ppermute | solution.py:48
  67.9 13.1 %collective-permute-start.9 = (f32[2,16,8,128]{3,2,1,0:T(8,128)}, f32[2,16,8,128]{3,2,1,0:T(8,128)S(1)}, u32[]{:S(2)}, u32[]{:S(2)}) collective-permute-start(f32[2,16,8,128]{3,2,1,0:T(8,128)} %get-tuple-element.29), channel_id=1, source_target_pairs={{0,30},{1,31},{2,4},{3,5},{4,2},{5,3},{6,8},{7,9},{8,6},{9,7},{10,... | collective-permute-start | bytes 393224 | tf_op jit(solution)/shard_map/ppermute | solution.py:48
  74.2 20.0 %all-to-all-start.2 = ((f32[32,32,128]{2,1,0:T(8,128)}), f32[32,32,128]{2,1,0:T(8,128)S(1)}, u32[]{:S(2)}, u32[]{:S(2)}) async-start(f32[32,32,128]{2,1,0:T(8,128)} %shard_map.90), calls=%async_computation.2 | async-start | bytes 1048576 | tf_op jit(solution)/shard_map/all_to_all | solution.py:293
  81.1 0.8 copy-start.14
  81.1 0.8 copy-start.15
  84.1 10.1 %collective-permute-start.11 = (f32[3,2,16,8,128]{4,3,2,1,0:T(8,128)}, f32[3,2,16,8,128]{4,3,2,1,0:T(8,128)S(1)}, u32[]{:S(2)}, u32[]{:S(2)}) collective-permute-start(f32[3,2,16,8,128]{4,3,2,1,0:T(8,128)} %shard_map.88.own_ref.strip_ref), channel_id=1, source_target_pairs={{0,224},{32,64},{64,32},{96,128},{128,96},{160,192},{192,160},{224... | collective-permute-start | bytes 1179656 | tf_op jit(solution)/shard_map/ppermute | solution.py:42
  85.9 8.3 %collective-permute-start.10 = (f32[3,2,16,8,128]{4,3,2,1,0:T(8,128)}, f32[3,2,16,8,128]{4,3,2,1,0:T(8,128)S(1)}, u32[]{:S(2)}, u32[]{:S(2)}) collective-permute-start(f32[3,2,16,8,128]{4,3,2,1,0:T(8,128)} %shard_map.88.own_ref.strip_ref), channel_id=1, source_target_pairs={{0,32},{32,0},{64,96},{96,64},{128,160},{160,128},{192,224},{224,1... | collective-permute-start | bytes 1179656 | tf_op jit(solution)/shard_map/ppermute | solution.py:42
  94.2 0.9 copy-start.7
  94.2 1.0 copy-start.1
  127.3 12.3 %all-to-all-start.4 = ((f32[8,32,128]{2,1,0:T(8,128)}), f32[8,32,128]{2,1,0:T(8,128)S(1)}, u32[]{:S(2)}, u32[]{:S(2)}) async-start(f32[8,32,128]{2,1,0:T(8,128)} %shard_map.94), calls=%async_computation.4 | async-start | bytes 262144 | tf_op jit(solution)/shard_map/all_to_all | solution.py:293
  131.8 16.1 %collective-permute-start.12 = (f32[3,2,16,8,128]{4,3,2,1,0:T(8,128)}, f32[3,2,16,8,128]{4,3,2,1,0:T(8,128)S(1)}, u32[]{:S(2)}, u32[]{:S(2)}) collective-permute-start(f32[3,2,16,8,128]{4,3,2,1,0:T(8,128)} %get-tuple-element.34), channel_id=1, source_target_pairs={{0,32},{32,0},{64,96},{96,64},{128,160},{160,128},{192,224},{224,1... | collective-permute-start | bytes 1179656 | tf_op jit(solution)/shard_map/ppermute | solution.py:42
  132.6 15.3 %collective-permute-start.13 = (f32[3,2,16,8,128]{4,3,2,1,0:T(8,128)}, f32[3,2,16,8,128]{4,3,2,1,0:T(8,128)S(1)}, u32[]{:S(2)}, u32[]{:S(2)}) collective-permute-start(f32[3,2,16,8,128]{4,3,2,1,0:T(8,128)} %get-tuple-element.35), channel_id=1, source_target_pairs={{0,224},{32,64},{64,32},{96,128},{128,96},{160,192},{192,160},{224... | collective-permute-start | bytes 1179656 | tf_op jit(solution)/shard_map/ppermute | solution.py:42
  142.0 20.6 %all-to-all-start.5 = ((f32[32,32,128]{2,1,0:T(8,128)}), f32[32,32,128]{2,1,0:T(8,128)S(1)}, u32[]{:S(2)}, u32[]{:S(2)}) async-start(f32[32,32,128]{2,1,0:T(8,128)} %shard_map.95), calls=%async_computation.5 | async-start | bytes 1048576 | tf_op jit(solution)/shard_map/all_to_all | solution.py:293
  148.0 0.8 copy-start.13
  150.8 7.8 %collective-permute-start.14 = (f32[2,16,8,128]{3,2,1,0:T(8,128)}, f32[2,16,8,128]{3,2,1,0:T(8,128)S(1)}, u32[]{:S(2)}, u32[]{:S(2)}) collective-permute-start(f32[2,16,8,128]{3,2,1,0:T(8,128)} %get-tuple-element.37), channel_id=1, source_target_pairs={{0,1},{1,0},{2,3},{3,2},{4,5},{5,4},{6,7},{7,6},{8,9},{9,8},{10,11... | collective-permute-start | bytes 393224 | tf_op jit(solution)/shard_map/ppermute | solution.py:42
  152.2 7.9 %collective-permute-start.15 = (f32[2,16,8,128]{3,2,1,0:T(8,128)}, f32[2,16,8,128]{3,2,1,0:T(8,128)S(1)}, u32[]{:S(2)}, u32[]{:S(2)}) collective-permute-start(f32[2,16,8,128]{3,2,1,0:T(8,128)} %get-tuple-element.38), channel_id=1, source_target_pairs={{0,31},{1,2},{2,1},{3,4},{4,3},{5,6},{6,5},{7,8},{8,7},{9,10},{10,... | collective-permute-start | bytes 393224 | tf_op jit(solution)/shard_map/ppermute | solution.py:42
  158.6 1.5 copy-start.16
  162.6 0.8 copy-start.2
  (9 other events, 6.3 us)

commit v3 on v2

v3 whole, which is shorter than its diff:
```python
import functools

import jax
import jax.numpy as jnp
import numpy as np
from jax import lax
from jax.experimental import pallas as pl
from jax.experimental.pallas import tpu as pltpu
from jax.sharding import Mesh, PartitionSpec as P

ROW = ("y", "core")
COL = ("z", "x")
PLANE = ("y", "x")
LANES = 128
TILES = 16
GROUP = 4
F32 = jnp.float32
VMEM_BYTES = 50 * 1024 * 1024


def dft_tables(length):
    index = np.arange(length, dtype=np.int64)
    angle = 2.0 * np.pi / length * (index[:, None] * index[None, :] % length)
    factor = 1.0 / np.sqrt(length)
    cos_table = (np.cos(angle) * factor).astype(np.float32)
    sin_table = (np.sin(angle) * factor).astype(np.float32)
    forward = np.block([[cos_table, sin_table], [-sin_table, cos_table]])
    inverse = np.block([[cos_table, -sin_table], [sin_table, cos_table]])
    return jnp.asarray(forward, jnp.bfloat16), jnp.asarray(inverse, jnp.bfloat16)


def place_of(axes):
    index = lax.axis_index(axes)
    odd = lax.rem(index, 2)
    at_end = (index == 0) | (index == lax.axis_size(axes) - 1)
    return index, (2 - 2 * odd, 1, 2 * odd), at_end


def paired(value, axes, side):
    count = lax.axis_size(axes)
    pairs = [(i, (i + (1 if (i + side // 2) % 2 == 0 else -1)) % count) for i in range(count)]
    return lax.ppermute(value, axes, pairs)


def paired_far(value, axes, phase):
    count = lax.axis_size(axes)
    pairs = [(i, (i + (2 if (i // 2 + phase) % 2 == 0 else -2)) % count) for i in range(count)]
    return lax.ppermute(value, axes, pairs)


def dot(a, b):
    return jnp.dot(a, b, preferred_element_type=F32)


def transform(reals, imags, left, right):
    size = reals[0].shape[0]
    columns = [jnp.concatenate(pair, axis=0).astype(jnp.bfloat16) for pair in zip(reals, imags)]
    mid = dot(left, jnp.concatenate(columns, axis=1)).astype(jnp.bfloat16)
    rows = [
        jnp.concatenate([mid[:size, i * size : (i + 1) * size], mid[size:, i * size : (i + 1) * size]], axis=1)
        for i in range(len(reals))
    ]
    out = dot(jnp.concatenate(rows, axis=0), right)
    return (
        [out[i * size : (i + 1) * size, :size] for i in range(len(reals))],
        [out[i * size : (i + 1) * size, size:] for i in range(len(reals))],
    )


def updated_probe(probe, total):
    mean = jnp.sum(total * total, keepdims=True) / total.size
    return probe - 0.3 * total / jnp.sqrt(mean + 1e-06)


def pattern_group(group, count, slots_ref, pattern, pattern_copy, left, right, probe, ext, gobj, keep, send):
    size = pattern.shape[1]
    region = size // 2
    tiles = size // 8
    slots = [group * GROUP + i for i in range(GROUP)]
    sub_id = lax.broadcasted_iota(jnp.int32, (1, 8, LANES), 1)
    lane_id = lax.broadcasted_iota(jnp.int32, (1, 8, LANES), 2)

    def corner(slot):
        row = slots_ref[0, slot] + region
        col = slots_ref[1, slot] + region
        tile = jnp.minimum(row // 8, region // 8 - 1)
        return tile, row - tile * 8, col

    def window(part, at):
        tile, sub, col = at
        pieces = [
            pltpu.roll(ext[v, part, pl.ds(tile, tiles + 1)], lax.rem(LANES - col, LANES), 2) for v in range(3)
        ]
        halves = []
        for v in range(2):
            x = jnp.where(lane_id < LANES - col, pieces[v], pieces[v + 1])
            x = pltpu.roll(x, lax.rem(8 - sub, 8), 1)
            halves.append(jnp.where(sub_id < 8 - sub, x[:tiles], x[1:]).reshape(size, LANES))
        return jnp.concatenate(halves, axis=1)

    def add_object(part, value, at):
        tile, sub, col = at
        zero = jnp.zeros((1, 8, LANES), F32)
        rolled = []
        for v in range(2):
            x = value[:, v * LANES : (v + 1) * LANES].reshape(tiles, 8, LANES)
            x = pltpu.roll(x, lax.rem(sub, 8), 1)
            x = jnp.where(
                sub_id < sub, jnp.concatenate([zero, x], axis=0), jnp.concatenate([x, zero], axis=0)
            )
            rolled.append(pltpu.roll(x, lax.rem(col, LANES), 2))
        inside = lane_id < col
        gobj[0, part, pl.ds(tile, tiles + 1)] += jnp.where(inside, 0.0, rolled[0])
        gobj[1, part, pl.ds(tile, tiles + 1)] += jnp.where(inside, rolled[0], rolled[1])
        gobj[2, part, pl.ds(tile, tiles + 1)] += jnp.where(inside, rolled[1], 0.0)

    def add_probe(real, imag):
        first = lax.axis_index("core") == 0
        for v in range(2):
            lanes = slice(v * LANES, (v + 1) * LANES)
            keep[v] += jnp.where(first, real[:, lanes], imag[:, lanes])
            send[v] += jnp.where(first, imag[:, lanes], real[:, lanes])

    at = [corner(slot) for slot in slots]
    win_real = [window(0, a) for a in at]
    win_imag = [window(1, a) for a in at]
    probe_real = jnp.concatenate([probe[0, 0], probe[0, 1]], axis=1)
    probe_imag = jnp.concatenate([probe[1, 0], probe[1, 1]], axis=1)
    far_real, far_imag = transform(
        [probe_real * a - probe_imag * b for a, b in zip(win_real, win_imag)],
        [probe_real * b + probe_imag * a for a, b in zip(win_real, win_imag)],
        left[...],
        right[...],
    )
    pattern_copy(group).wait()
    misfit = [
        jnp.where(slot < count, a * a + b * b - pattern[slot], 0.0) for a, b, slot in zip(far_real, far_imag, slots)
    ]
    back_real, back_imag = transform(
        [m * a for m, a in zip(misfit, far_real)],
        [m * b for m, b in zip(misfit, far_imag)],
        right[...],
        left[...],
    )
    both = list(zip(win_real, win_imag, back_real, back_imag))
    add_probe(sum(a * c + b * d for a, b, c, d in both), sum(a * d - b * c for a, b, c, d in both))
    for i in range(GROUP):
        add_object(0, probe_real * back_real[i] + probe_imag * back_imag[i], at[i])
        add_object(1, probe_real * back_imag[i] - probe_imag * back_real[i], at[i])


def gradient_kernel(
    first,
    slots_ref, pattern_ref, left_ref, right_ref, own_ref, side0_ref, side2_ref, start_ref, mine_ref, other_ref,
    out0_ref, own_out_ref, out2_ref, probe_ref, rows_ref, keep, send, peak_ref,
    pattern, left, right, probe, total, ext, gobj,
    strip_sems, probe_sems, table_sems, pattern_sems, rows_sems, out_sems,
):
    row, row_places, row_end = place_of(ROW)
    col, col_places, col_end = place_of(COL)
    core = lax.axis_index("core")
    count = slots_ref[2, 0]
    groups = pattern.shape[0] // GROUP

    def block(ref, row_order, col_order):
        return ref.at[col_places[col_order], :, pl.ds(row_places[row_order] * TILES, TILES)]

    def pattern_copy(group):
        slots = pl.ds(group * GROUP, GROUP)
        return pltpu.make_async_copy(pattern_ref.at[slots], pattern.at[slots], pattern_sems.at[group])

    if first:
        probe_copies = [
            pltpu.make_async_copy(start_ref.at[:, :, pl.ds(v * LANES, LANES)], probe.at[:, v], probe_sems.at[v])
            for v in range(2)
        ]
    else:
        probe_copies = [
            pltpu.make_async_copy(mine_ref, total.at[core], probe_sems.at[0]),
            pltpu.make_async_copy(other_ref, total.at[1 - core], probe_sems.at[1]),
            pltpu.make_async_copy(start_ref, probe, probe_sems.at[2]),
        ]
    strip_copies = [
        pltpu.make_async_copy(
            ref.at[j], block(ext, i, j) if first else block(ext, j, i), strip_sems.at[i * 3 + j]
        )
        for i, ref in ((1, own_ref), (0, side0_ref), (2, side2_ref))
        for j in range(3)
    ]
    table_copies = [
        pltpu.make_async_copy(left_ref, left, table_sems.at[0]),
        pltpu.make_async_copy(right_ref, right, table_sems.at[1]),
    ]
    for copy in probe_copies + strip_copies + table_copies:
        copy.start()
    for group in range(groups):
        pattern_copy(group).start()
    gobj[...] = jnp.zeros_like(gobj)
    keep[...] = jnp.zeros_like(keep)
    send[...] = jnp.zeros_like(send)
    for copy in probe_copies:
        copy.wait()
    if not first:
        probe[...] = updated_probe(probe[...], total[...])
    power = probe[0] * probe[0] + probe[1] * probe[1]
    peak_ref[...] = jnp.broadcast_to(jnp.max(power, keepdims=True).reshape(1, 1) + 1e-06, peak_ref.shape)
    for copy in strip_copies:
        copy.wait()

    @pl.when(col_end)
    def _():
        ext[col_places[2]] = jnp.zeros(ext.shape[1:], F32)

    @pl.when(row_end)
    def _():
        ext[:, :, pl.ds(row_places[2] * TILES, TILES)] = jnp.zeros(ext.shape[:2] + (TILES, 8, LANES), F32)

    side_copies = [pltpu.make_async_copy(probe, probe_ref, rows_sems.at[3])] + [
        pltpu.make_async_copy(block(ext, i, 1), rows_ref.at[i], rows_sems.at[i]) for i in range(3)
    ]
    for copy in side_copies:
        copy.start()
    for copy in table_copies:
        copy.wait()

    def visit(group, carry):
        pattern_group(
            group, count, slots_ref, pattern, pattern_copy, left, right, probe, ext, gobj, keep, send
        )
        return carry

    live_groups = (count + GROUP - 1) // GROUP
    lax.fori_loop(0, live_groups, visit, 0)

    out_copies = [
        pltpu.make_async_copy(block(gobj, j, i) if first else block(gobj, i, j), ref.at[j], out_sems.at[i * 3 + j])
        for i, ref in ((0, out0_ref), (2, out2_ref), (1, own_out_ref))
        for j in range(3)
    ]
    for copy in out_copies:
        copy.start()
    for group in range(1, groups):

        @pl.when(group >= live_groups)
        def _():
            pattern_copy(group).wait()

    for copy in side_copies + out_copies:
        copy.wait()


def gradients(first, live_slots, patterns, tables, strips, *probes):
    slots, size = patterns.shape[:2]
    vmem = pl.BlockSpec(memory_space=pltpu.VMEM)
    smem = pl.BlockSpec(memory_space=pltpu.SMEM)
    hbm = pl.BlockSpec(memory_space=pltpu.HBM)
    anywhere = pl.BlockSpec(memory_space=pl.ANY)
    strip = jax.ShapeDtypeStruct((3, 2, TILES, 8, LANES), F32)
    half = jax.ShapeDtypeStruct((2, size, LANES), F32)
    both = jax.ShapeDtypeStruct((2, 2, size, LANES), F32)
    ext = pltpu.VMEM((3, 2, 3 * TILES, 8, LANES), F32)
    return pl.pallas_call(
        functools.partial(gradient_kernel, first),
        out_shape=(strip, strip, strip, both, strip, half, half, jax.ShapeDtypeStruct((8, LANES), F32)),
        in_specs=[smem, hbm, hbm, hbm] + [anywhere] * 3 + [hbm] + [anywhere] * 2,
        out_specs=(hbm,) * 5 + (vmem,) * 3,
        scratch_shapes=[
            pltpu.VMEM(patterns.shape, F32),
            pltpu.VMEM(tables[0].shape, jnp.bfloat16),
            pltpu.VMEM(tables[1].shape, jnp.bfloat16),
            pltpu.VMEM(both.shape, F32),
            pltpu.VMEM(both.shape, F32),
            ext,
            ext,
            pltpu.SemaphoreType.DMA((9,)),
            pltpu.SemaphoreType.DMA((3,)),
            pltpu.SemaphoreType.DMA((2,)),
            pltpu.SemaphoreType.DMA((slots // GROUP,)),
            pltpu.SemaphoreType.DMA((4,)),
            pltpu.SemaphoreType.DMA((9,)),
        ],
        compiler_params=pltpu.CompilerParams(vmem_limit_bytes=VMEM_BYTES),
    )(live_slots, patterns, *tables, *strips, *probes)


def exchange(value, axes):
    return lax.all_to_all(value, axes, 0, 0, tiled=True)


def core_swap(value):
    return lax.ppermute(value, "core", [(0, 1), (1, 0)])


def sum_steps(keep, send):
    plane = lax.axis_size(PLANE)
    depth = lax.axis_size("z")

    def over_plane():
        half = keep + core_swap(send)
        return exchange(half.reshape(plane, -1, LANES), PLANE).sum(0)

    def over_depth(share):
        return exchange(jnp.broadcast_to(share, (depth,) + share.shape), "z").sum(0)

    def gathered(share):
        mine = exchange(jnp.broadcast_to(share, (plane,) + share.shape), PLANE).reshape(keep.shape)
        return mine, core_swap(mine)

    return over_plane, over_depth, gathered


def side_sum(own, side0, side2, at_end):
    return own + side0 + jnp.where(at_end, 0.0, side2)


def row_reach():
    index = lax.axis_index(ROW)
    odd = lax.rem(index, 2) == 1
    first = lax.rem(index, 2) == lax.rem(index // 2, 2)
    lower, upper = index >= 2, index <= lax.axis_size(ROW) - 3
    return first, jnp.where(odd, lower, upper), jnp.where(odd, upper, lower)


def row_transfers(sums):
    first = row_reach()[0]
    return (
        paired(sums[:2], ROW, 0),
        paired(sums[1:], ROW, 2),
        paired_far(jnp.where(first, sums[0], sums[2]), ROW, 0),
        paired_far(jnp.where(first, sums[2], sums[0]), ROW, 1),
    )


def updated_strip(strip, sums, arrived, peak, at_end):
    near0, near2, far_a, far_b = arrived
    first, reach0, reach2 = row_reach()
    far0, far2 = jnp.where(first, far_a, far_b), jnp.where(first, far_b, far_a)
    grad = jnp.stack(
        [
            sums[0] + near0[1] + jnp.where(reach0, far0, 0.0),
            side_sum(sums[1], near0[0], near2[1], at_end),
            sums[2] + near2[0] + jnp.where(reach2, far2, 0.0),
        ]
    )
    return strip - grad / peak


def last_probe_kernel(probe_ref, mine_ref, other_ref, out_ref):
    first = lax.axis_index("core") == 0
    mine, other = mine_ref[...], other_ref[...]
    total = jnp.stack([jnp.where(first, mine, other), jnp.where(first, other, mine)])
    new = updated_probe(probe_ref[...], total)
    for part in range(2):
        for v in range(2):
            out_ref[part, :, v * LANES : (v + 1) * LANES] = new[part, v]


def last_probe(probe, mine, other):
    vmem = pl.BlockSpec(memory_space=pltpu.VMEM)
    size = probe.shape[2]
    return pl.pallas_call(
        last_probe_kernel,
        out_shape=jax.ShapeDtypeStruct((2, size, 2 * LANES), F32),
        in_specs=[vmem] * 3,
        out_specs=vmem,
        compiler_params=pltpu.CompilerParams(vmem_limit_bytes=8 * 1024 * 1024),
    )(probe, mine, other)


def body(object_field, probe_field, intensity, scan_offsets, pattern_counts):
    size = probe_field.shape[1]
    slots = intensity.shape[2]
    patterns = intensity.reshape(slots, size, size)
    live_slots = jnp.concatenate(
        [scan_offsets.reshape(slots, 2).T, jnp.broadcast_to(pattern_counts, (1, slots))], axis=0
    )
    tables = dft_tables(size)
    row_end, col_end = place_of(ROW)[2], place_of(COL)[2]

    own = object_field.reshape(2, TILES, 8, LANES)
    strip = jnp.stack([paired(own, COL, 0), own, paired(own, COL, 2)])
    strips = (strip, paired(strip, ROW, 0), paired(strip, ROW, 2))
    out0, mid, out2, probe, strip, keep, send, peak = gradients(
        True, live_slots, patterns, tables, strips, probe_field, probe_field, probe_field
    )
    over_plane, over_depth, gathered = sum_steps(keep, send)
    sums = side_sum(mid, paired(out0, COL, 0), paired(out2, COL, 2), col_end)
    share, sums = lax.optimization_barrier((over_plane(), sums))
    strip = updated_strip(strip, sums, row_transfers(sums), peak, row_end)
    share, strip = lax.optimization_barrier((over_depth(share), strip))
    strips = (strip, paired(strip, COL, 0), paired(strip, COL, 2))
    totals = gathered(share)

    out0, mid, out2, probe, strip, keep, send, peak = gradients(
        False, live_slots, patterns, tables, strips, probe, *totals
    )
    over_plane, over_depth, gathered = sum_steps(keep, send)
    sums = side_sum(mid, paired(out0, ROW, 0), paired(out2, ROW, 2), row_end)
    share, sums = lax.optimization_barrier((over_plane(), sums))
    grad = side_sum(sums[1], paired(sums[0], COL, 0), paired(sums[2], COL, 2), col_end)
    new_object = (strip[1] - grad / peak).reshape(object_field.shape)
    share, new_object = lax.optimization_barrier((over_depth(share), new_object))
    return (new_object, last_probe(probe, *gathered(share)))


def solution(mesh):
    split = Mesh(mesh.devices.reshape(4, 2, 8, 4), ("y", "core", "z", "x"))
    in_specs = (
        P(None, ROW, COL),
        P(),
        P(ROW, COL, None, None, None),
        P(ROW, COL, None, None),
        P(ROW, COL),
    )
    out_specs = (P(None, ROW, COL), P())
    return jax.shard_map(body, mesh=split, in_specs=in_specs, out_specs=out_specs, check_vma=False)
```

time: 167 us -> 156 us (0.934)
  Pallas kernels: 44.6 us -> 17.4 us
  starting transfers between devices: 54.1 us -> 65.8 us
  waiting for transfers between devices: 40 us -> 50.4 us
  local copies, waits for them, and re-layouts: 8.03 us -> 3.61 us
  blocking collectives: 16.6 us -> 12.9 us
  other arithmetic: 0.93 us -> 3.42 us
    pallas_call x9 -> x1, Pallas kernels: 17.7 us -> 1.21 us  [last_probe(): pl.pallas_call(last_probe_kernel, out_shape=jax.ShapeDtypeStruct((2, size...]
    ppermute x0 -> x4, starting transfers between devices: none -> 14.6 us  [core_swap(): return lax.ppermute(value, 'core', [(0, 1), (1, 0)])]
    all_to_all x5, waiting for transfers between devices: 16 us -> 30 us  [exchange(): return lax.all_to_all(value, axes, 0, 0, tiled=True)]
    pallas_call x2, Pallas kernels: 26.9 us -> 16.2 us  [gradients(): pl.pallas_call(functools.partial(gradient_kernel, first), out_shape=(stri...]
    ppermute x14, waiting for transfers between devices: 23.3 us -> 14.3 us  [paired(): return lax.ppermute(value, axes, pairs)]
    unnamed x40 -> x4, local copies, waits for them, and re-layouts: 8.03 us -> 0.79 us
    all_to_all x5, starting transfers between devices: 26.2 us -> 19.3 us  [exchange(): return lax.all_to_all(value, axes, 0, 0, tiled=True)]
    ppermute x14, starting transfers between devices: 24.1 us -> 30.4 us  [paired(): return lax.ppermute(value, axes, pairs)]
  transfers between devices with their start and end apart: 21 -> 25, of which waited for: 9 -> 17; matrix products, arithmetic and copies ran while one was open for 0% -> 3% of each run, Pallas kernels for 8% -> 0%
where the time goes in v3:
time: 156 us; the launch traced here: 155 us
  starting transfers between devices  65.8 us (42%)
  waiting for transfers between devices  50.4 us (32%)
  Pallas kernels  17.4 us (11%)
  blocking collectives  12.9 us (8%)
  local copies, waits for them, and re-layouts  3.61 us (2%)
  other arithmetic  3.42 us (2%)
    ppermute x14, starting transfers between devices, paired(): return lax.ppermute(value, axes, pairs)  30.4 us
    all_to_all x5, waiting for transfers between devices, exchange(): return lax.all_to_all(value, axes, 0, 0, tiled=True)  30 us
    all_to_all x5, starting transfers between devices, exchange(): return lax.all_to_all(value, axes, 0, 0, tiled=True)  19.3 us
    pallas_call x2, Pallas kernels, gradients(): pl.pallas_call(functools.partial(gradient_kernel, first), out_shape=(stri...  16.2 us
    ppermute x4, starting transfers between devices, core_swap(): return lax.ppermute(value, 'core', [(0, 1), (1, 0)])  14.6 us
    ppermute x14, waiting for transfers between devices, paired(): return lax.ppermute(value, axes, pairs)  14.3 us
    all_to_all x1, blocking collectives, exchange(): return lax.all_to_all(value, axes, 0, 0, tiled=True)  12.9 us
    ppermute x4, waiting for transfers between devices, core_swap(): return lax.ppermute(value, 'core', [(0, 1), (1, 0)])  5.01 us
  transfers between devices with their start and end apart: 25, of which 17 were waited for; matrix products, arithmetic and copies ran while one was open for 3% of the time, Pallas kernels for 0%

profile of v3, /device:TPU:1, one launch (start us, length us, event | category | flops | bytes accessed | tf_op | source)
XLA Modules:
  0.0 155.0 jit_solution(13272873565331116680)
XLA Ops:
  0.6 8.7 %collective-permute-start.1 = (f32[2,16,8,128]{3,2,1,0:T(8,128)}, f32[2,16,8,128]{3,2,1,0:T(8,128)S(1)}, u32[]{:S(2)}, u32[]{:S(2)}) collective-permute-start(f32[2,16,8,128]{3,2,1,0:T(8,128)} %bitcast.58), channel_id=1, source_target_pairs={{0,31},{1,2},{2,1},{3,4},{4,3},{5,6},{6,5},{7,8},{8,7},{9,10},{10,... | collective-permute-start | bytes 393224 | tf_op jit(solution)/shard_map/ppermute | solution.py:42
  9.3 3.4 %collective-permute-done.1 = f32[2,16,8,128]{3,2,1,0:T(8,128)S(1)} collective-permute-done((f32[2,16,8,128]{3,2,1,0:T(8,128)}, f32[2,16,8,128]{3,2,1,0:T(8,128)S(1)}, u32[]{:S(2)}, u32[]{:S(2)}) %collective-permute-start.1) | collective-permute-done | bytes 131104 | tf_op jit(solution)/shard_map/ppermute | solution.py:42
  14.5 3.1 %collective-permute-start.3 = (f32[3,2,16,8,128]{4,3,2,1,0:T(8,128)S(1)}, f32[3,2,16,8,128]{4,3,2,1,0:T(8,128)S(1)}, u32[]{:S(2)}, u32[]{:S(2)}) collective-permute-start(f32[3,2,16,8,128]{4,3,2,1,0:T(8,128)S(1)} %pad_maximum_fusion.own_ref), channel_id=1, source_target_pairs={{0,224},{32,64},{64,32},{96,128},{128,96},{160,192},{192,160},{224... | collective-permute-start | bytes 1179656 | tf_op jit(solution)/shard_map/ppermute | solution.py:42
  19.1 4.3 %collective-permute-done.3.side2_ref = f32[3,2,16,8,128]{4,3,2,1,0:T(8,128)S(1)} collective-permute-done((f32[3,2,16,8,128]{4,3,2,1,0:T(8,128)S(1)}, f32[3,2,16,8,128]{4,3,2,1,0:T(8,128)S(1)}, u32[]{:S(2)}, u32[]{:S(2)}) %collective-permute-start.3) | collective-permute-done | bytes 393248 | tf_op jit(solution)/shard_map/ppermute | solution.py:42
  23.4 8.1 %shard_map.86 = (f32[3,2,16,8,128]{4,3,2,1,0:T(8,128)S(1)}, f32[3,2,16,8,128]{4,3,2,1,0:T(8,128)S(1)}, f32[3,2,16,8,128]{4,3,2,1,0:T(8,128)S(1)}, f32[2,2,256,12...) custom-call(s32[3,8]{1,0:T(4,128)S(1)} %concatenate.3.slots_ref, ...), custom_call_target="tpu_custom_call" | custom-call | tf_op jit(solution)/shard_map/pallas_call | solution.py:262
  32.3 4.3 %collective-permute-start.5 = (f32[3,2,16,8,128]{4,3,2,1,0:T(8,128)S(1)}, f32[3,2,16,8,128]{4,3,2,1,0:T(8,128)S(1)}, u32[]{:S(2)}, u32[]{:S(2)}) collective-permute-start(f32[3,2,16,8,128]{4,3,2,1,0:T(8,128)S(1)} %get-tuple-element.29), channel_id=1, source_target_pairs={{0,1},{1,0},{2,3},{3,2},{4,5},{5,4},{6,7},{7,6},{8,9},{9,8},{10,11... | collective-permute-start | bytes 1179656 | tf_op jit(solution)/shard_map/ppermute | solution.py:42
  36.6 3.3 %collective-permute-start.6 = (f32[3,2,16,8,128]{4,3,2,1,0:T(8,128)S(1)}, f32[3,2,16,8,128]{4,3,2,1,0:T(8,128)S(1)}, u32[]{:S(2)}, u32[]{:S(2)}) collective-permute-start(f32[3,2,16,8,128]{4,3,2,1,0:T(8,128)S(1)} %get-tuple-element.30), channel_id=1, source_target_pairs={{0,31},{1,2},{2,1},{3,4},{4,3},{5,6},{6,5},{7,8},{8,7},{9,10},{10,... | collective-permute-start | bytes 1179656 | tf_op jit(solution)/shard_map/ppermute | solution.py:42
  39.9 1.8 %collective-permute-start.4 = (f32[2,256,128]{2,1,0:T(8,128)S(1)}, f32[2,256,128]{2,1,0:T(8,128)S(1)}, u32[]{:S(2)}, u32[]{:S(2)}) collective-permute-start(f32[2,256,128]{2,1,0:T(8,128)S(1)} %get-tuple-element.27), channel_id=1, source_target_pairs={{0,32},{32,0},{1,33},{33,1},{2,34},{34,2},{3,35},{35,3},{4,36},{36... | collective-permute-start | bytes 786440 | tf_op jit(solution)/shard_map/ppermute | solution.py:291
  43.6 3.5 %all-to-all-start = ((f32[16,32,128]{2,1,0:T(8,128)}), f32[16,32,128]{2,1,0:T(8,128)S(1)}, u32[]{:S(2)}, u32[]{:S(2)}) async-start(f32[16,32,128]{2,1,0:T(8,128)} %bitcast.8), calls=%async_computation | async-start | bytes 524288 | tf_op jit(solution)/shard_map/all_to_all | solution.py:287
  47.1 1.6 %collective-permute-done.6 = f32[3,2,16,8,128]{4,3,2,1,0:T(8,128)S(1)} collective-permute-done((f32[3,2,16,8,128]{4,3,2,1,0:T(8,128)S(1)}, f32[3,2,16,8,128]{4,3,2,1,0:T(8,128)S(1)}, u32[]{:S(2)}, u32[]{:S(2)}) %collective-permute-start.6) | collective-permute-done | bytes 393248 | tf_op jit(solution)/shard_map/ppermute | solution.py:42
  48.8 6.7 %all-to-all-done = f32[16,32,128]{2,1,0:T(8,128)S(1)} async-done(((f32[16,32,128]{2,1,0:T(8,128)}), f32[16,32,128]{2,1,0:T(8,128)S(1)}, u32[]{:S(2)}, u32[]{:S(2)}) %all-to-all-start) | async-done | bytes 262176 | tf_op jit(solution)/shard_map/all_to_all | solution.py:287
  55.6 1.3 collective-permute-start.7
  57.5 3.4 %all-to-all-start.1 = ((f32[8,32,128]{2,1,0:T(8,128)}), f32[8,32,128]{2,1,0:T(8,128)S(1)}, u32[]{:S(2)}, u32[]{:S(2)}) async-start(f32[8,32,128]{2,1,0:T(8,128)} %broadcast_in_dim.36), calls=%async_computation.1 | async-start | bytes 262144 | tf_op jit(solution)/shard_map/all_to_all | solution.py:287
  60.9 2.0 %collective-permute-done.10 = f32[2,2,16,8,128]{4,3,2,1,0:T(8,128)S(1)} collective-permute-done((f32[2,2,16,8,128]{4,3,2,1,0:T(8,128)S(1)}, f32[2,2,16,8,128]{4,3,2,1,0:T(8,128)S(1)}, u32[]{:S(2)}, u32[]{:S(2)}) %collective-permute-start.10) | collective-permute-done | bytes 262176 | tf_op jit(solution)/shard_map/ppermute | solution.py:42
  63.0 1.6 %collective-permute-start.9 = (f32[2,16,8,128]{3,2,1,0:T(8,128)S(1)}, f32[2,16,8,128]{3,2,1,0:T(8,128)S(1)}, u32[]{:S(2)}, u32[]{:S(2)}) collective-permute-start(f32[2,16,8,128]{3,2,1,0:T(8,128)S(1)} %get-tuple-element.55), channel_id=1, source_target_pairs={{0,192},{32,224},{64,128},{96,160},{128,64},{160,96},{192,0},{224,... | collective-permute-start | bytes 393224 | tf_op jit(solution)/shard_map/ppermute | solution.py:48
  64.6 4.2 %all-to-all-done.1 = f32[8,32,128]{2,1,0:T(8,128)S(1)} async-done(((f32[8,32,128]{2,1,0:T(8,128)}), f32[8,32,128]{2,1,0:T(8,128)S(1)}, u32[]{:S(2)}, u32[]{:S(2)}) %all-to-all-start.1) | async-done | bytes 131104 | tf_op jit(solution)/shard_map/all_to_all | solution.py:287
  70.8 4.7 %all-to-all-start.2 = ((f32[16,32,128]{2,1,0:T(8,128)}), f32[16,32,128]{2,1,0:T(8,128)S(1)}, u32[]{:S(2)}, u32[]{:S(2)}) async-start(f32[16,32,128]{2,1,0:T(8,128)} %broadcast_in_dim.39), calls=%async_computation.2 | async-start | bytes 524288 | tf_op jit(solution)/shard_map/all_to_all | solution.py:287
  75.5 2.8 %collective-permute-start.12 = (f32[3,2,16,8,128]{4,3,2,1,0:T(8,128)S(1)}, f32[3,2,16,8,128]{4,3,2,1,0:T(8,128)S(1)}, u32[]{:S(2)}, u32[]{:S(2)}) collective-permute-start(f32[3,2,16,8,128]{4,3,2,1,0:T(8,128)S(1)} %fusion.own_ref), channel_id=1, source_target_pairs={{0,31},{1,2},{2,1},{3,4},{4,3},{5,6},{6,5},{7,8},{8,7},{9,10},{10,... | collective-permute-start | bytes 1179656 | tf_op jit(solution)/shard_map/ppermute | solution.py:42
  78.3 5.3 %all-to-all-done.2 = f32[16,32,128]{2,1,0:T(8,128)S(1)} async-done(((f32[16,32,128]{2,1,0:T(8,128)}), f32[16,32,128]{2,1,0:T(8,128)S(1)}, u32[]{:S(2)}, u32[]{:S(2)}) %all-to-all-start.2) | async-done | bytes 262176 | tf_op jit(solution)/shard_map/all_to_all | solution.py:287
  83.6 8.3 %collective-permute-start.13 = (f32[2,256,128]{2,1,0:T(8,128)S(1)}, f32[2,256,128]{2,1,0:T(8,128)S(1)}, u32[]{:S(2)}, u32[]{:S(2)}) collective-permute-start(f32[2,256,128]{2,1,0:T(8,128)S(1)} %bitcast.52), channel_id=1, source_target_pairs={{0,32},{32,0},{1,33},{33,1},{2,34},{34,2},{3,35},{35,3},{4,36},{36... | collective-permute-start | bytes 786440 | tf_op jit(solution)/shard_map/ppermute | solution.py:291
  93.0 8.1 %shard_map.87 = (f32[3,2,16,8,128]{4,3,2,1,0:T(8,128)S(1)}, f32[3,2,16,8,128]{4,3,2,1,0:T(8,128)S(1)}, f32[3,2,16,8,128]{4,3,2,1,0:T(8,128)S(1)}, f32[2,2,256,12...) custom-call(s32[3,8]{1,0:T(4,128)S(1)} %concatenate.3.slots_ref, ...), custom_call_target="tpu_custom_call" | custom-call | tf_op jit(solution)/shard_map/pallas_call | solution.py:262
  101.1 4.7 %collective-permute-start.15 = (f32[3,2,16,8,128]{4,3,2,1,0:T(8,128)S(1)}, f32[3,2,16,8,128]{4,3,2,1,0:T(8,128)S(1)}, u32[]{:S(2)}, u32[]{:S(2)}) collective-permute-start(f32[3,2,16,8,128]{4,3,2,1,0:T(8,128)S(1)} %get-tuple-element.41), channel_id=1, source_target_pairs={{0,32},{32,0},{64,96},{96,64},{128,160},{160,128},{192,224},{224,1... | collective-permute-start | bytes 1179656 | tf_op jit(solution)/shard_map/ppermute | solution.py:42
  105.8 1.3 collective-permute-start.16
  107.1 1.5 collective-permute-done.14
  109.4 3.5 %all-to-all-start.3 = ((f32[16,32,128]{2,1,0:T(8,128)}), f32[16,32,128]{2,1,0:T(8,128)S(1)}, u32[]{:S(2)}, u32[]{:S(2)}) async-start(f32[16,32,128]{2,1,0:T(8,128)} %bitcast.16), calls=%async_computation.3 | async-start | bytes 524288 | tf_op jit(solution)/shard_map/all_to_all | solution.py:287
  113.4 8.1 %all-to-all-done.3 = f32[16,32,128]{2,1,0:T(8,128)S(1)} async-done(((f32[16,32,128]{2,1,0:T(8,128)}), f32[16,32,128]{2,1,0:T(8,128)S(1)}, u32[]{:S(2)}, u32[]{:S(2)}) %all-to-all-start.3) | async-done | bytes 262176 | tf_op jit(solution)/shard_map/all_to_all | solution.py:287
  123.0 4.1 %all-to-all-start.4 = ((f32[8,32,128]{2,1,0:T(8,128)}), f32[8,32,128]{2,1,0:T(8,128)S(1)}, u32[]{:S(2)}, u32[]{:S(2)}) async-start(f32[8,32,128]{2,1,0:T(8,128)} %broadcast_in_dim.40), calls=%async_computation.4 | async-start | bytes 262144 | tf_op jit(solution)/shard_map/all_to_all | solution.py:287
  127.1 1.6 %collective-permute-done.18 = f32[2,16,8,128]{3,2,1,0:T(8,128)S(1)} collective-permute-done((f32[2,16,8,128]{3,2,1,0:T(8,128)S(1)}, f32[2,16,8,128]{3,2,1,0:T(8,128)S(1)}, u32[]{:S(2)}, u32[]{:S(2)}) %collective-permute-start.18) | collective-permute-done | bytes 131104 | tf_op jit(solution)/shard_map/ppermute | solution.py:42
  129.4 5.7 %all-to-all-done.4 = f32[8,32,128]{2,1,0:T(8,128)S(1)} async-done(((f32[8,32,128]{2,1,0:T(8,128)}), f32[8,32,128]{2,1,0:T(8,128)S(1)}, u32[]{:S(2)}, u32[]{:S(2)}) %all-to-all-start.4) | async-done | bytes 131104 | tf_op jit(solution)/shard_map/all_to_all | solution.py:287
  135.2 12.9 %all_to_all.30 = f32[16,32,128]{2,1,0:T(8,128)S(1)} all-to-all(f32[16,32,128]{2,1,0:T(8,128)S(1)} %broadcast_in_dim.41), channel_id=1, replica_groups=mesh['y'=4,'core'=2,'z'=8,'x'=4] {'y','x'}, dimensions={0} | all-to-all | bytes 524288 | tf_op jit(solution)/shard_map/all_to_all | solution.py:287
  148.1 4.5 %collective-permute-start.19 = (f32[2,256,128]{2,1,0:T(8,128)S(1)}, f32[2,256,128]{2,1,0:T(8,128)S(1)}, u32[]{:S(2)}, u32[]{:S(2)}) collective-permute-start(f32[2,256,128]{2,1,0:T(8,128)S(1)} %bitcast.54), channel_id=1, source_target_pairs={{0,32},{32,0},{1,33},{33,1},{2,34},{34,2},{3,35},{35,3},{4,36},{36... | collective-permute-start | bytes 786440 | tf_op jit(solution)/shard_map/ppermute | solution.py:291
  153.8 1.2 shard_map.88
  (46 shorter events, 13.8 us)
Async XLA Ops:
  0.6 12.1 %collective-permute-start.1 = (f32[2,16,8,128]{3,2,1,0:T(8,128)}, f32[2,16,8,128]{3,2,1,0:T(8,128)S(1)}, u32[]{:S(2)}, u32[]{:S(2)}) collective-permute-start(f32[2,16,8,128]{3,2,1,0:T(8,128)} %bitcast.58), channel_id=1, source_target_pairs={{0,31},{1,2},{2,1},{3,4},{4,3},{5,6},{6,5},{7,8},{8,7},{9,10},{10,... | collective-permute-start | bytes 393224 | tf_op jit(solution)/shard_map/ppermute | solution.py:42
  9.3 4.3 %collective-permute-start = (f32[2,16,8,128]{3,2,1,0:T(8,128)}, f32[2,16,8,128]{3,2,1,0:T(8,128)S(1)}, u32[]{:S(2)}, u32[]{:S(2)}) collective-permute-start(f32[2,16,8,128]{3,2,1,0:T(8,128)} %bitcast.59), channel_id=1, source_target_pairs={{0,1},{1,0},{2,3},{3,2},{4,5},{5,4},{6,7},{7,6},{8,9},{9,8},{10,11... | collective-permute-start | bytes 393224 | tf_op jit(solution)/shard_map/ppermute | solution.py:42
  14.5 8.9 %collective-permute-start.3 = (f32[3,2,16,8,128]{4,3,2,1,0:T(8,128)S(1)}, f32[3,2,16,8,128]{4,3,2,1,0:T(8,128)S(1)}, u32[]{:S(2)}, u32[]{:S(2)}) collective-permute-start(f32[3,2,16,8,128]{4,3,2,1,0:T(8,128)S(1)} %pad_maximum_fusion.own_ref), channel_id=1, source_target_pairs={{0,224},{32,64},{64,32},{96,128},{128,96},{160,192},{192,160},{224... | collective-permute-start | bytes 1179656 | tf_op jit(solution)/shard_map/ppermute | solution.py:42
  17.7 5.8 %collective-permute-start.2 = (f32[3,2,16,8,128]{4,3,2,1,0:T(8,128)S(1)}, f32[3,2,16,8,128]{4,3,2,1,0:T(8,128)S(1)}, u32[]{:S(2)}, u32[]{:S(2)}) collective-permute-start(f32[3,2,16,8,128]{4,3,2,1,0:T(8,128)S(1)} %pad_maximum_fusion.own_ref), channel_id=1, source_target_pairs={{0,32},{32,0},{64,96},{96,64},{128,160},{160,128},{192,224},{224,1... | collective-permute-start | bytes 1179656 | tf_op jit(solution)/shard_map/ppermute | solution.py:42
  31.5 0.8 copy-start
  32.3 14.8 %collective-permute-start.5 = (f32[3,2,16,8,128]{4,3,2,1,0:T(8,128)S(1)}, f32[3,2,16,8,128]{4,3,2,1,0:T(8,128)S(1)}, u32[]{:S(2)}, u32[]{:S(2)}) collective-permute-start(f32[3,2,16,8,128]{4,3,2,1,0:T(8,128)S(1)} %get-tuple-element.29), channel_id=1, source_target_pairs={{0,1},{1,0},{2,3},{3,2},{4,5},{5,4},{6,7},{7,6},{8,9},{9,8},{10,11... | collective-permute-start | bytes 1179656 | tf_op jit(solution)/shard_map/ppermute | solution.py:42
  36.6 12.2 %collective-permute-start.6 = (f32[3,2,16,8,128]{4,3,2,1,0:T(8,128)S(1)}, f32[3,2,16,8,128]{4,3,2,1,0:T(8,128)S(1)}, u32[]{:S(2)}, u32[]{:S(2)}) collective-permute-start(f32[3,2,16,8,128]{4,3,2,1,0:T(8,128)S(1)} %get-tuple-element.30), channel_id=1, source_target_pairs={{0,31},{1,2},{2,1},{3,4},{4,3},{5,6},{6,5},{7,8},{8,7},{9,10},{10,... | collective-permute-start | bytes 1179656 | tf_op jit(solution)/shard_map/ppermute | solution.py:42
  39.9 2.9 %collective-permute-start.4 = (f32[2,256,128]{2,1,0:T(8,128)S(1)}, f32[2,256,128]{2,1,0:T(8,128)S(1)}, u32[]{:S(2)}, u32[]{:S(2)}) collective-permute-start(f32[2,256,128]{2,1,0:T(8,128)S(1)} %get-tuple-element.27), channel_id=1, source_target_pairs={{0,32},{32,0},{1,33},{33,1},{2,34},{34,2},{3,35},{35,3},{4,36},{36... | collective-permute-start | bytes 786440 | tf_op jit(solution)/shard_map/ppermute | solution.py:291
  43.6 11.9 %all-to-all-start = ((f32[16,32,128]{2,1,0:T(8,128)}), f32[16,32,128]{2,1,0:T(8,128)S(1)}, u32[]{:S(2)}, u32[]{:S(2)}) async-start(f32[16,32,128]{2,1,0:T(8,128)} %bitcast.8), calls=%async_computation | async-start | bytes 524288 | tf_op jit(solution)/shard_map/all_to_all | solution.py:287
  55.6 5.3 %collective-permute-start.7 = (f32[2,2,16,8,128]{4,3,2,1,0:T(8,128)S(1)}, f32[2,2,16,8,128]{4,3,2,1,0:T(8,128)S(1)}, u32[]{:S(2)}, u32[]{:S(2)}) collective-permute-start(f32[2,2,16,8,128]{4,3,2,1,0:T(8,128)S(1)} %get-tuple-element.57), channel_id=1, source_target_pairs={{0,32},{32,0},{64,96},{96,64},{128,160},{160,128},{192,224},{224,1... | collective-permute-start | bytes 786440 | tf_op jit(solution)/shard_map/ppermute | solution.py:42
  56.9 6.1 %collective-permute-start.10 = (f32[2,2,16,8,128]{4,3,2,1,0:T(8,128)S(1)}, f32[2,2,16,8,128]{4,3,2,1,0:T(8,128)S(1)}, u32[]{:S(2)}, u32[]{:S(2)}) collective-permute-start(f32[2,2,16,8,128]{4,3,2,1,0:T(8,128)S(1)} %get-tuple-element.58), channel_id=1, source_target_pairs={{0,224},{32,64},{64,32},{96,128},{128,96},{160,192},{192,160},{224... | collective-permute-start | bytes 786440 | tf_op jit(solution)/shard_map/ppermute | solution.py:42
  57.5 11.2 %all-to-all-start.1 = ((f32[8,32,128]{2,1,0:T(8,128)}), f32[8,32,128]{2,1,0:T(8,128)S(1)}, u32[]{:S(2)}, u32[]{:S(2)}) async-start(f32[8,32,128]{2,1,0:T(8,128)} %broadcast_in_dim.36), calls=%async_computation.1 | async-start | bytes 262144 | tf_op jit(solution)/shard_map/all_to_all | solution.py:287
  63.0 5.8 %collective-permute-start.9 = (f32[2,16,8,128]{3,2,1,0:T(8,128)S(1)}, f32[2,16,8,128]{3,2,1,0:T(8,128)S(1)}, u32[]{:S(2)}, u32[]{:S(2)}) collective-permute-start(f32[2,16,8,128]{3,2,1,0:T(8,128)S(1)} %get-tuple-element.55), channel_id=1, source_target_pairs={{0,192},{32,224},{64,128},{96,160},{128,64},{160,96},{192,0},{224,... | collective-permute-start | bytes 393224 | tf_op jit(solution)/shard_map/ppermute | solution.py:48
  64.5 5.4 %collective-permute-start.8 = (f32[2,16,8,128]{3,2,1,0:T(8,128)S(1)}, f32[2,16,8,128]{3,2,1,0:T(8,128)S(1)}, u32[]{:S(2)}, u32[]{:S(2)}) collective-permute-start(f32[2,16,8,128]{3,2,1,0:T(8,128)S(1)} %get-tuple-element.56), channel_id=1, source_target_pairs={{0,64},{32,96},{64,0},{96,32},{128,192},{160,224},{192,128},{224,1... | collective-permute-start | bytes 393224 | tf_op jit(solution)/shard_map/ppermute | solution.py:48
  70.8 12.8 %all-to-all-start.2 = ((f32[16,32,128]{2,1,0:T(8,128)}), f32[16,32,128]{2,1,0:T(8,128)S(1)}, u32[]{:S(2)}, u32[]{:S(2)}) async-start(f32[16,32,128]{2,1,0:T(8,128)} %broadcast_in_dim.39), calls=%async_computation.2 | async-start | bytes 524288 | tf_op jit(solution)/shard_map/all_to_all | solution.py:287
  75.5 16.4 %collective-permute-start.12 = (f32[3,2,16,8,128]{4,3,2,1,0:T(8,128)S(1)}, f32[3,2,16,8,128]{4,3,2,1,0:T(8,128)S(1)}, u32[]{:S(2)}, u32[]{:S(2)}) collective-permute-start(f32[3,2,16,8,128]{4,3,2,1,0:T(8,128)S(1)} %fusion.own_ref), channel_id=1, source_target_pairs={{0,31},{1,2},{2,1},{3,4},{4,3},{5,6},{6,5},{7,8},{8,7},{9,10},{10,... | collective-permute-start | bytes 1179656 | tf_op jit(solution)/shard_map/ppermute | solution.py:42
  78.3 13.6 %collective-permute-start.11 = (f32[3,2,16,8,128]{4,3,2,1,0:T(8,128)S(1)}, f32[3,2,16,8,128]{4,3,2,1,0:T(8,128)S(1)}, u32[]{:S(2)}, u32[]{:S(2)}) collective-permute-start(f32[3,2,16,8,128]{4,3,2,1,0:T(8,128)S(1)} %fusion.own_ref), channel_id=1, source_target_pairs={{0,1},{1,0},{2,3},{3,2},{4,5},{5,4},{6,7},{7,6},{8,9},{9,8},{10,11... | collective-permute-start | bytes 1179656 | tf_op jit(solution)/shard_map/ppermute | solution.py:42
  83.6 9.5 %collective-permute-start.13 = (f32[2,256,128]{2,1,0:T(8,128)S(1)}, f32[2,256,128]{2,1,0:T(8,128)S(1)}, u32[]{:S(2)}, u32[]{:S(2)}) collective-permute-start(f32[2,256,128]{2,1,0:T(8,128)S(1)} %bitcast.52), channel_id=1, source_target_pairs={{0,32},{32,0},{1,33},{33,1},{2,34},{34,2},{3,35},{35,3},{4,36},{36... | collective-permute-start | bytes 786440 | tf_op jit(solution)/shard_map/ppermute | solution.py:291
  101.1 11.8 %collective-permute-start.15 = (f32[3,2,16,8,128]{4,3,2,1,0:T(8,128)S(1)}, f32[3,2,16,8,128]{4,3,2,1,0:T(8,128)S(1)}, u32[]{:S(2)}, u32[]{:S(2)}) collective-permute-start(f32[3,2,16,8,128]{4,3,2,1,0:T(8,128)S(1)} %get-tuple-element.41), channel_id=1, source_target_pairs={{0,32},{32,0},{64,96},{96,64},{128,160},{160,128},{192,224},{224,1... | collective-permute-start | bytes 1179656 | tf_op jit(solution)/shard_map/ppermute | solution.py:42
  105.8 7.5 %collective-permute-start.16 = (f32[3,2,16,8,128]{4,3,2,1,0:T(8,128)S(1)}, f32[3,2,16,8,128]{4,3,2,1,0:T(8,128)S(1)}, u32[]{:S(2)}, u32[]{:S(2)}) collective-permute-start(f32[3,2,16,8,128]{4,3,2,1,0:T(8,128)S(1)} %get-tuple-element.42), channel_id=1, source_target_pairs={{0,224},{32,64},{64,32},{96,128},{128,96},{160,192},{192,160},{224... | collective-permute-start | bytes 1179656 | tf_op jit(solution)/shard_map/ppermute | solution.py:42
  107.1 1.5 collective-permute-start.14
  109.4 12.0 %all-to-all-start.3 = ((f32[16,32,128]{2,1,0:T(8,128)}), f32[16,32,128]{2,1,0:T(8,128)S(1)}, u32[]{:S(2)}, u32[]{:S(2)}) async-start(f32[16,32,128]{2,1,0:T(8,128)} %bitcast.16), calls=%async_computation.3 | async-start | bytes 524288 | tf_op jit(solution)/shard_map/all_to_all | solution.py:287
  113.3 40.5 %copy-start.1 = (f32[2,2,256,128]{3,2,1,0:T(8,128)S(1)}, f32[2,2,256,128]{3,2,1,0:T(8,128)}, u32[]{:S(2)}) copy-start(f32[2,2,256,128]{3,2,1,0:T(8,128)} %get-tuple-element.48.probe_ref) | copy-start | bytes 1572868
  121.5 7.2 %collective-permute-start.18 = (f32[2,16,8,128]{3,2,1,0:T(8,128)S(1)}, f32[2,16,8,128]{3,2,1,0:T(8,128)S(1)}, u32[]{:S(2)}, u32[]{:S(2)}) collective-permute-start(f32[2,16,8,128]{3,2,1,0:T(8,128)S(1)} %get-tuple-element.52), channel_id=1, source_target_pairs={{0,31},{1,2},{2,1},{3,4},{4,3},{5,6},{6,5},{7,8},{8,7},{9,10},{10,... | collective-permute-start | bytes 393224 | tf_op jit(solution)/shard_map/ppermute | solution.py:42
  122.3 6.4 %collective-permute-start.17 = (f32[2,16,8,128]{3,2,1,0:T(8,128)S(1)}, f32[2,16,8,128]{3,2,1,0:T(8,128)S(1)}, u32[]{:S(2)}, u32[]{:S(2)}) collective-permute-start(f32[2,16,8,128]{3,2,1,0:T(8,128)S(1)} %get-tuple-element.53), channel_id=1, source_target_pairs={{0,1},{1,0},{2,3},{3,2},{4,5},{5,4},{6,7},{7,6},{8,9},{9,8},{10,11... | collective-permute-start | bytes 393224 | tf_op jit(solution)/shard_map/ppermute | solution.py:42
  123.0 12.2 %all-to-all-start.4 = ((f32[8,32,128]{2,1,0:T(8,128)}), f32[8,32,128]{2,1,0:T(8,128)S(1)}, u32[]{:S(2)}, u32[]{:S(2)}) async-start(f32[8,32,128]{2,1,0:T(8,128)} %broadcast_in_dim.40), calls=%async_computation.4 | async-start | bytes 262144 | tf_op jit(solution)/shard_map/all_to_all | solution.py:287
  148.1 5.7 %collective-permute-start.19 = (f32[2,256,128]{2,1,0:T(8,128)S(1)}, f32[2,256,128]{2,1,0:T(8,128)S(1)}, u32[]{:S(2)}, u32[]{:S(2)}) collective-permute-start(f32[2,256,128]{2,1,0:T(8,128)S(1)} %bitcast.54), channel_id=1, source_target_pairs={{0,32},{32,0},{1,33},{33,1},{2,34},{34,2},{3,35},{35,3},{4,36},{36... | collective-permute-start | bytes 786440 | tf_op jit(solution)/shard_map/ppermute | solution.py:291

commit v4 on v3

--- a/solution.py
+++ b/solution.py
@@ -15,7 +15,7 @@
 TILES = 16
 GROUP = 4
 F32 = jnp.float32
-VMEM_BYTES = 50 * 1024 * 1024
+VMEM_BYTES = 101 * 512 * 1024
 
 
 def dft_tables(length):
@@ -52,7 +52,7 @@
     return jnp.dot(a, b, preferred_element_type=F32)
 
 
-def transform(reals, imags, left, right):
+def transform_pair(reals, imags, left, right):
     size = reals[0].shape[0]
     columns = [jnp.concatenate(pair, axis=0).astype(jnp.bfloat16) for pair in zip(reals, imags)]
     mid = dot(left, jnp.concatenate(columns, axis=1)).astype(jnp.bfloat16)
@@ -61,10 +61,14 @@
         for i in range(len(reals))
     ]
     out = dot(jnp.concatenate(rows, axis=0), right)
-    return (
-        [out[i * size : (i + 1) * size, :size] for i in range(len(reals))],
-        [out[i * size : (i + 1) * size, size:] for i in range(len(reals))],
-    )
+    return [(out[i * size : (i + 1) * size, :size], out[i * size : (i + 1) * size, size:]) for i in range(len(reals))]
+
+
+def transform(reals, imags, left, right):
+    out = []
+    for i in range(0, len(reals), 2):
+        out += transform_pair(reals[i : i + 2], imags[i : i + 2], left, right)
+    return [pair[0] for pair in out], [pair[1] for pair in out]
 
 
 def updated_probe(probe, total):
@@ -88,14 +92,12 @@
 
     def window(part, at):
         tile, sub, col = at
-        pieces = [
-            pltpu.roll(ext[v, part, pl.ds(tile, tiles + 1)], lax.rem(LANES - col, LANES), 2) for v in range(3)
-        ]
+        pieces = [ext[v, part, pl.ds(tile, tiles + 1)] for v in range(3)]
         halves = []
         for v in range(2):
-            x = jnp.where(lane_id < LANES - col, pieces[v], pieces[v + 1])
-            x = pltpu.roll(x, lax.rem(8 - sub, 8), 1)
-            halves.append(jnp.where(sub_id < 8 - sub, x[:tiles], x[1:]).reshape(size, LANES))
+            x = pltpu.roll(jnp.where(lane_id >= col, pieces[v], pieces[v + 1]), lax.rem(LANES - col, LANES), 2)
+            x = pltpu.roll(jnp.where(sub_id >= sub, x[:tiles], x[1:]), lax.rem(8 - sub, 8), 1)
+            halves.append(x.reshape(size, LANES))
         return jnp.concatenate(halves, axis=1)
 
     def add_object(part, value, at):
@@ -149,77 +151,61 @@
         add_object(1, probe_real * back_imag[i] - probe_imag * back_real[i], at[i])
 
 
-def gradient_kernel(
-    first,
-    slots_ref, pattern_ref, left_ref, right_ref, own_ref, side0_ref, side2_ref, start_ref, mine_ref, other_ref,
-    out0_ref, own_out_ref, out2_ref, probe_ref, rows_ref, keep, send, peak_ref,
-    pattern, left, right, probe, total, ext, gobj,
-    strip_sems, probe_sems, table_sems, pattern_sems, rows_sems, out_sems,
-):
+def gradient_kernel(first, *refs):
+    if first:
+        slots_ref, pattern_ref, left_ref, right_ref, start_ref, own_ref, side0_ref, side2_ref = refs[:8]
+        col0_ref, col1_ref, col2_ref, keep, send, peak_ref, rows_ref = refs[8:15]
+    else:
+        slots_ref, pattern_ref, left_ref, right_ref, start_ref, own_ref, side0_ref, side2_ref = refs[:8]
+        mine_ref, other_ref = refs[8:10]
+        col0_ref, col1_ref, col2_ref, keep, send, peak_ref, probe_ref = refs[10:17]
+    pattern, left, right, probe, ext, gobj, probe_sems, table_sems, pattern_sems = refs[-9:]
     row, row_places, row_end = place_of(ROW)
     col, col_places, col_end = place_of(COL)
-    core = lax.axis_index("core")
     count = slots_ref[2, 0]
     groups = pattern.shape[0] // GROUP
-
-    def block(ref, row_order, col_order):
-        return ref.at[col_places[col_order], :, pl.ds(row_places[row_order] * TILES, TILES)]
 
     def pattern_copy(group):
         slots = pl.ds(group * GROUP, GROUP)
         return pltpu.make_async_copy(pattern_ref.at[slots], pattern.at[slots], pattern_sems.at[group])
 
-    if first:
-        probe_copies = [
-            pltpu.make_async_copy(start_ref.at[:, :, pl.ds(v * LANES, LANES)], probe.at[:, v], probe_sems.at[v])
-            for v in range(2)
-        ]
-    else:
-        probe_copies = [
-            pltpu.make_async_copy(mine_ref, total.at[core], probe_sems.at[0]),
-            pltpu.make_async_copy(other_ref, total.at[1 - core], probe_sems.at[1]),
-            pltpu.make_async_copy(start_ref, probe, probe_sems.at[2]),
-        ]
-    strip_copies = [
-        pltpu.make_async_copy(
-            ref.at[j], block(ext, i, j) if first else block(ext, j, i), strip_sems.at[i * 3 + j]
-        )
-        for i, ref in ((1, own_ref), (0, side0_ref), (2, side2_ref))
-        for j in range(3)
+    probe_copies = [
+        pltpu.make_async_copy(start_ref.at[:, :, pl.ds(v * LANES, LANES)], probe.at[:, v], probe_sems.at[v])
+        for v in range(2)
     ]
     table_copies = [
         pltpu.make_async_copy(left_ref, left, table_sems.at[0]),
         pltpu.make_async_copy(right_ref, right, table_sems.at[1]),
     ]
-    for copy in probe_copies + strip_copies + table_copies:
+    for copy in probe_copies + table_copies:
         copy.start()
     for group in range(groups):
         pattern_copy(group).start()
+
+    strips = ((1, own_ref, False), (0, side0_ref, False), (2, side2_ref, row_end if first else col_end))
+    for i, ref, outside in strips:
+        if first:
+            for j in range(3):
+                bad = outside | col_end if j == 2 else outside
+                value = ref[j] if bad is False else jnp.where(bad, 0.0, ref[j])
+                ext[col_places[j], :, pl.ds(row_places[i] * TILES, TILES)] = value
+        else:
+            ext[col_places[i]] = ref[...] if outside is False else jnp.where(outside, 0.0, ref[...])
+    if first:
+        rows_ref[...] = ext[1]
     gobj[...] = jnp.zeros_like(gobj)
     keep[...] = jnp.zeros_like(keep)
     send[...] = jnp.zeros_like(send)
     for copy in probe_copies:
         copy.wait()
     if not first:
-        probe[...] = updated_probe(probe[...], total[...])
+        real = lax.axis_index("core") == 0
+        mine, other = mine_ref[...], other_ref[...]
+        total = jnp.stack([jnp.where(real, mine, other), jnp.where(real, other, mine)])
+        probe[...] = updated_probe(probe[...], total)
+        probe_ref[...] = probe[...]
     power = probe[0] * probe[0] + probe[1] * probe[1]
     peak_ref[...] = jnp.broadcast_to(jnp.max(power, keepdims=True).reshape(1, 1) + 1e-06, peak_ref.shape)
-    for copy in strip_copies:
-        copy.wait()
-
-    @pl.when(col_end)
-    def _():
-        ext[col_places[2]] = jnp.zeros(ext.shape[1:], F32)
-
-    @pl.when(row_end)
-    def _():
-        ext[:, :, pl.ds(row_places[2] * TILES, TILES)] = jnp.zeros(ext.shape[:2] + (TILES, 8, LANES), F32)
-
-    side_copies = [pltpu.make_async_copy(probe, probe_ref, rows_sems.at[3])] + [
-        pltpu.make_async_copy(block(ext, i, 1), rows_ref.at[i], rows_sems.at[i]) for i in range(3)
-    ]
-    for copy in side_copies:
-        copy.start()
     for copy in table_copies:
         copy.wait()
 
@@ -231,56 +217,42 @@
 
     live_groups = (count + GROUP - 1) // GROUP
     lax.fori_loop(0, live_groups, visit, 0)
-
-    out_copies = [
-        pltpu.make_async_copy(block(gobj, j, i) if first else block(gobj, i, j), ref.at[j], out_sems.at[i * 3 + j])
-        for i, ref in ((0, out0_ref), (2, out2_ref), (1, own_out_ref))
-        for j in range(3)
-    ]
-    for copy in out_copies:
-        copy.start()
+    for j, ref in enumerate((col0_ref, col1_ref, col2_ref)):
+        ref[...] = gobj[col_places[j]]
     for group in range(1, groups):
 
         @pl.when(group >= live_groups)
         def _():
             pattern_copy(group).wait()
 
-    for copy in side_copies + out_copies:
-        copy.wait()
-
-
-def gradients(first, live_slots, patterns, tables, strips, *probes):
+
+def gradients(first, live_slots, patterns, tables, probe, *vmem_args):
     slots, size = patterns.shape[:2]
     vmem = pl.BlockSpec(memory_space=pltpu.VMEM)
     smem = pl.BlockSpec(memory_space=pltpu.SMEM)
     hbm = pl.BlockSpec(memory_space=pltpu.HBM)
-    anywhere = pl.BlockSpec(memory_space=pl.ANY)
-    strip = jax.ShapeDtypeStruct((3, 2, TILES, 8, LANES), F32)
+    strip = jax.ShapeDtypeStruct((2, 3 * TILES, 8, LANES), F32)
     half = jax.ShapeDtypeStruct((2, size, LANES), F32)
     both = jax.ShapeDtypeStruct((2, 2, size, LANES), F32)
     ext = pltpu.VMEM((3, 2, 3 * TILES, 8, LANES), F32)
     return pl.pallas_call(
         functools.partial(gradient_kernel, first),
-        out_shape=(strip, strip, strip, both, strip, half, half, jax.ShapeDtypeStruct((8, LANES), F32)),
-        in_specs=[smem, hbm, hbm, hbm] + [anywhere] * 3 + [hbm] + [anywhere] * 2,
-        out_specs=(hbm,) * 5 + (vmem,) * 3,
+        out_shape=(strip,) * 3 + (half, half, jax.ShapeDtypeStruct((8, LANES), F32), strip if first else both),
+        in_specs=[smem] + [hbm] * 4 + [vmem] * len(vmem_args),
+        out_specs=(vmem,) * 7,
         scratch_shapes=[
             pltpu.VMEM(patterns.shape, F32),
             pltpu.VMEM(tables[0].shape, jnp.bfloat16),
             pltpu.VMEM(tables[1].shape, jnp.bfloat16),
             pltpu.VMEM(both.shape, F32),
-            pltpu.VMEM(both.shape, F32),
             ext,
             ext,
-            pltpu.SemaphoreType.DMA((9,)),
-            pltpu.SemaphoreType.DMA((3,)),
+            pltpu.SemaphoreType.DMA((2,)),
             pltpu.SemaphoreType.DMA((2,)),
             pltpu.SemaphoreType.DMA((slots // GROUP,)),
-            pltpu.SemaphoreType.DMA((4,)),
-            pltpu.SemaphoreType.DMA((9,)),
         ],
         compiler_params=pltpu.CompilerParams(vmem_limit_bytes=VMEM_BYTES),
-    )(live_slots, patterns, *tables, *strips, *probes)
+    )(live_slots, patterns, *tables, probe, *vmem_args)
 
 
 def exchange(value, axes):
@@ -313,36 +285,31 @@
     return own + side0 + jnp.where(at_end, 0.0, side2)
 
 
-def row_reach():
-    index = lax.axis_index(ROW)
+def updated_strip(strip, sums, peak):
+    index, places, at_end = place_of(ROW)
+    last = lax.axis_size(ROW) - 1
     odd = lax.rem(index, 2) == 1
-    first = lax.rem(index, 2) == lax.rem(index // 2, 2)
-    lower, upper = index >= 2, index <= lax.axis_size(ROW) - 3
-    return first, jnp.where(odd, lower, upper), jnp.where(odd, upper, lower)
-
-
-def row_transfers(sums):
-    first = row_reach()[0]
-    return (
-        paired(sums[:2], ROW, 0),
-        paired(sums[1:], ROW, 2),
-        paired_far(jnp.where(first, sums[0], sums[2]), ROW, 0),
-        paired_far(jnp.where(first, sums[2], sums[0]), ROW, 1),
-    )
-
-
-def updated_strip(strip, sums, arrived, peak, at_end):
-    near0, near2, far_a, far_b = arrived
-    first, reach0, reach2 = row_reach()
-    far0, far2 = jnp.where(first, far_a, far_b), jnp.where(first, far_b, far_a)
-    grad = jnp.stack(
+    down_first = lax.rem(index // 2, 2) == 0
+    upper, lower = sums[:, : 2 * TILES], sums[:, TILES:]
+    near0 = paired(jnp.where(odd, upper, lower), ROW, 0)
+    near2 = paired(jnp.where(odd, lower, upper), ROW, 2)
+    above, below = sums[:, :TILES], sums[:, 2 * TILES :]
+    far_a = paired_far(jnp.where(down_first, below, above), ROW, 0)
+    far_b = paired_far(jnp.where(down_first, above, below), ROW, 1)
+    near2 = jnp.where(at_end, 0.0, near2)
+    far_b = jnp.where((index < 2) | (index > last - 2), 0.0, far_b)
+    from_upper, from_lower = jnp.where(odd, near0, near2), jnp.where(odd, near2, near0)
+    grad_above = above + from_upper[:, :TILES] + jnp.where(down_first, far_b, far_a)
+    grad = sums[:, TILES : 2 * TILES] + from_upper[:, TILES:] + from_lower[:, :TILES]
+    grad_below = below + from_lower[:, TILES:] + jnp.where(down_first, far_a, far_b)
+    return jnp.concatenate(
         [
-            sums[0] + near0[1] + jnp.where(reach0, far0, 0.0),
-            side_sum(sums[1], near0[0], near2[1], at_end),
-            sums[2] + near2[0] + jnp.where(reach2, far2, 0.0),
-        ]
-    )
-    return strip - grad / peak
+            jnp.where(index == 0, 0.0, strip[:, :TILES] - grad_above / peak),
+            strip[:, TILES : 2 * TILES] - grad / peak,
+            jnp.where(index == last, 0.0, strip[:, 2 * TILES :] - grad_below / peak),
+        ],
+        axis=1,
+    )
 
 
 def last_probe_kernel(probe_ref, mine_ref, other_ref, out_ref):
@@ -380,25 +347,26 @@
     own = object_field.reshape(2, TILES, 8, LANES)
     strip = jnp.stack([paired(own, COL, 0), own, paired(own, COL, 2)])
     strips = (strip, paired(strip, ROW, 0), paired(strip, ROW, 2))
-    out0, mid, out2, probe, strip, keep, send, peak = gradients(
-        True, live_slots, patterns, tables, strips, probe_field, probe_field, probe_field
-    )
+    col0, col1, col2, keep, send, peak, strip = gradients(True, live_slots, patterns, tables, probe_field, *strips)
     over_plane, over_depth, gathered = sum_steps(keep, send)
-    sums = side_sum(mid, paired(out0, COL, 0), paired(out2, COL, 2), col_end)
+    sums = side_sum(col1, paired(col0, COL, 0), paired(col2, COL, 2), col_end)
     share, sums = lax.optimization_barrier((over_plane(), sums))
-    strip = updated_strip(strip, sums, row_transfers(sums), peak, row_end)
+    strip = updated_strip(strip, sums, peak)
     share, strip = lax.optimization_barrier((over_depth(share), strip))
     strips = (strip, paired(strip, COL, 0), paired(strip, COL, 2))
     totals = gathered(share)
 
-    out0, mid, out2, probe, strip, keep, send, peak = gradients(
-        False, live_slots, patterns, tables, strips, probe, *totals
+    col0, col1, col2, keep, send, peak, probe = gradients(
+        False, live_slots, patterns, tables, probe_field, *strips, *totals
     )
     over_plane, over_depth, gathered = sum_steps(keep, send)
-    sums = side_sum(mid, paired(out0, ROW, 0), paired(out2, ROW, 2), row_end)
+    sums = side_sum(col1, paired(col0, COL, 0), paired(col2, COL, 2), col_end)
     share, sums = lax.optimization_barrier((over_plane(), sums))
-    grad = side_sum(sums[1], paired(sums[0], COL, 0), paired(sums[2], COL, 2), col_end)
-    new_object = (strip[1] - grad / peak).reshape(object_field.shape)
+    odd = lax.rem(lax.axis_index(ROW), 2) == 1
+    above, grad, below = (sums[:, i * TILES : (i + 1) * TILES] for i in range(3))
+    arrived = (paired(jnp.where(odd, above, below), ROW, 0), paired(jnp.where(odd, below, above), ROW, 2))
+    grad = side_sum(grad, *arrived, row_end)
+    new_object = (strip[:, TILES : 2 * TILES] - grad / peak).reshape(object_field.shape)
     share, new_object = lax.optimization_barrier((over_depth(share), new_object))
     return (new_object, last_probe(probe, *gathered(share)))
 

time: 156 us -> 152 us (0.974)
  starting transfers between devices: 65.8 us -> 57.8 us
  Pallas kernels: 17.4 us -> 22.5 us
  waiting for transfers between devices: 50.4 us -> 48.8 us
    ppermute x14, starting transfers between devices: 30.4 us -> 20.3 us  [paired(): return lax.ppermute(value, axes, pairs)]
    pallas_call x2, Pallas kernels: 16.2 us -> 21.3 us  [gradients(): pl.pallas_call(functools.partial(gradient_kernel, first), out_shape=(stri...]
    all_to_all x5, waiting for transfers between devices: 30 us -> 27.2 us  [exchange(): return lax.all_to_all(value, axes, 0, 0, tiled=True)]
    ppermute x14, waiting for transfers between devices: 14.3 us -> 16.8 us  [paired(): return lax.ppermute(value, axes, pairs)]
  transfers between devices with their start and end apart: 25 -> 25, of which waited for: 17 -> 15; matrix products, arithmetic and copies ran while one was open for 3% -> 3% of each run, Pallas kernels for 0% -> 0%
where the time goes in v4:
time: 152 us; the launch traced here: 151 us
  starting transfers between devices  57.8 us (38%)
  waiting for transfers between devices  48.8 us (32%)
  Pallas kernels  22.5 us (15%)
  blocking collectives  13.7 us (9%)
  other arithmetic  3.54 us (2%)
  local copies, waits for them, and re-layouts  2.76 us (2%)
    all_to_all x5, waiting for transfers between devices, exchange(): return lax.all_to_all(value, axes, 0, 0, tiled=True)  27.2 us
    pallas_call x2, Pallas kernels, gradients(): pl.pallas_call(functools.partial(gradient_kernel, first), out_shape=(stri...  21.3 us
    all_to_all x5, starting transfers between devices, exchange(): return lax.all_to_all(value, axes, 0, 0, tiled=True)  20.3 us
    ppermute x14, starting transfers between devices, paired(): return lax.ppermute(value, axes, pairs)  20.3 us
    ppermute x14, waiting for transfers between devices, paired(): return lax.ppermute(value, axes, pairs)  16.8 us
    ppermute x4, starting transfers between devices, core_swap(): return lax.ppermute(value, 'core', [(0, 1), (1, 0)])  14.7 us
    all_to_all x1, blocking collectives, exchange(): return lax.all_to_all(value, axes, 0, 0, tiled=True)  13.7 us
    ppermute x4, waiting for transfers between devices, core_swap(): return lax.ppermute(value, 'core', [(0, 1), (1, 0)])  4.74 us
  transfers between devices with their start and end apart: 25, of which 15 were waited for; matrix products, arithmetic and copies ran while one was open for 3% of the time, Pallas kernels for 0%

profile of v4, /device:TPU:1, one launch (start us, length us, event | category | flops | bytes accessed | tf_op | source)
XLA Modules:
  0.0 150.6 jit_solution(11687686065503772153)
XLA Ops:
  0.6 8.7 %collective-permute-start.1 = (f32[2,16,8,128]{3,2,1,0:T(8,128)}, f32[2,16,8,128]{3,2,1,0:T(8,128)S(1)}, u32[]{:S(2)}, u32[]{:S(2)}) collective-permute-start(f32[2,16,8,128]{3,2,1,0:T(8,128)} %bitcast.22), channel_id=1, source_target_pairs={{0,31},{1,2},{2,1},{3,4},{4,3},{5,6},{6,5},{7,8},{8,7},{9,10},{10,... | collective-permute-start | bytes 393224 | tf_op jit(solution)/shard_map/ppermute | solution.py:42
  9.3 3.4 %collective-permute-done.1 = f32[2,16,8,128]{3,2,1,0:T(8,128)S(1)} collective-permute-done((f32[2,16,8,128]{3,2,1,0:T(8,128)}, f32[2,16,8,128]{3,2,1,0:T(8,128)S(1)}, u32[]{:S(2)}, u32[]{:S(2)}) %collective-permute-start.1) | collective-permute-done | bytes 131104 | tf_op jit(solution)/shard_map/ppermute | solution.py:42
  13.6 0.9 pad_maximum_fusion.refs_5_
  14.5 3.1 %collective-permute-start.3 = (f32[3,2,16,8,128]{4,3,2,1,0:T(8,128)S(1)}, f32[3,2,16,8,128]{4,3,2,1,0:T(8,128)S(1)}, u32[]{:S(2)}, u32[]{:S(2)}) collective-permute-start(f32[3,2,16,8,128]{4,3,2,1,0:T(8,128)S(1)} %pad_maximum_fusion.refs_5_), channel_id=1, source_target_pairs={{0,224},{32,64},{64,32},{96,128},{128,96},{160,192},{192,160},{224... | collective-permute-start | bytes 1179656 | tf_op jit(solution)/shard_map/ppermute | solution.py:42
  19.1 4.3 %collective-permute-done.3.refs_7_ = f32[3,2,16,8,128]{4,3,2,1,0:T(8,128)S(1)} collective-permute-done((f32[3,2,16,8,128]{4,3,2,1,0:T(8,128)S(1)}, f32[3,2,16,8,128]{4,3,2,1,0:T(8,128)S(1)}, u32[]{:S(2)}, u32[]{:S(2)}) %collective-permute-start.3) | collective-permute-done | bytes 393248 | tf_op jit(solution)/shard_map/ppermute | solution.py:42
  23.4 10.3 %shard_map.86 = (f32[2,48,8,128]{3,2,1,0:T(8,128)S(1)}, f32[2,48,8,128]{3,2,1,0:T(8,128)S(1)}, f32[2,48,8,128]{3,2,1,0:T(8,128)S(1)}, f32[2,256,128]{2,1,0:T(8,1...) custom-call(s32[3,8]{1,0:T(4,128)S(1)} %concatenate.6.refs_0_, ...), custom_call_target="tpu_custom_call" | custom-call | tf_op jit(solution)/shard_map/pallas_call | solution.py:238
  33.8 3.2 %collective-permute-start.6 = (f32[2,48,8,128]{3,2,1,0:T(8,128)S(1)}, f32[2,48,8,128]{3,2,1,0:T(8,128)S(1)}, u32[]{:S(2)}, u32[]{:S(2)}) collective-permute-start(f32[2,48,8,128]{3,2,1,0:T(8,128)S(1)} %get-tuple-element.28), channel_id=1, source_target_pairs={{0,31},{1,2},{2,1},{3,4},{4,3},{5,6},{6,5},{7,8},{8,7},{9,10},{10,... | collective-permute-start | bytes 1179656 | tf_op jit(solution)/shard_map/ppermute | solution.py:42
  37.0 1.8 %collective-permute-start.4 = (f32[2,256,128]{2,1,0:T(8,128)S(1)}, f32[2,256,128]{2,1,0:T(8,128)S(1)}, u32[]{:S(2)}, u32[]{:S(2)}) collective-permute-start(f32[2,256,128]{2,1,0:T(8,128)S(1)} %get-tuple-element.25), channel_id=1, source_target_pairs={{0,32},{32,0},{1,33},{33,1},{2,34},{34,2},{3,35},{35,3},{4,36},{36... | collective-permute-start | bytes 786440 | tf_op jit(solution)/shard_map/ppermute | solution.py:263
  38.9 1.2 collective-permute-done.4
  40.8 3.5 %all-to-all-start = ((f32[16,32,128]{2,1,0:T(8,128)}), f32[16,32,128]{2,1,0:T(8,128)S(1)}, u32[]{:S(2)}, u32[]{:S(2)}) async-start(f32[16,32,128]{2,1,0:T(8,128)} %bitcast.8), calls=%async_computation | async-start | bytes 524288 | tf_op jit(solution)/shard_map/all_to_all | solution.py:259
  44.3 2.1 %collective-permute-done.6 = f32[2,48,8,128]{3,2,1,0:T(8,128)S(1)} collective-permute-done((f32[2,48,8,128]{3,2,1,0:T(8,128)S(1)}, f32[2,48,8,128]{3,2,1,0:T(8,128)S(1)}, u32[]{:S(2)}, u32[]{:S(2)}) %collective-permute-start.6) | collective-permute-done | bytes 393248 | tf_op jit(solution)/shard_map/ppermute | solution.py:42
  46.5 6.2 %all-to-all-done = f32[16,32,128]{2,1,0:T(8,128)S(1)} async-done(((f32[16,32,128]{2,1,0:T(8,128)}), f32[16,32,128]{2,1,0:T(8,128)S(1)}, u32[]{:S(2)}, u32[]{:S(2)}) %all-to-all-start) | async-done | bytes 262176 | tf_op jit(solution)/shard_map/all_to_all | solution.py:259
  54.8 3.5 %all-to-all-start.1 = ((f32[8,32,128]{2,1,0:T(8,128)}), f32[8,32,128]{2,1,0:T(8,128)S(1)}, u32[]{:S(2)}, u32[]{:S(2)}) async-start(f32[8,32,128]{2,1,0:T(8,128)} %broadcast_in_dim.39), calls=%async_computation.1 | async-start | bytes 262144 | tf_op jit(solution)/shard_map/all_to_all | solution.py:259
  58.3 2.5 %collective-permute-start.9 = (f32[2,16,8,128]{3,2,1,0:T(8,128)S(1)}, f32[2,16,8,128]{3,2,1,0:T(8,128)S(1)}, u32[]{:S(2)}, u32[]{:S(2)}) collective-permute-start(f32[2,16,8,128]{3,2,1,0:T(8,128)S(1)} %get-tuple-element.53), channel_id=1, source_target_pairs={{0,192},{32,224},{64,128},{96,160},{128,64},{160,96},{192,0},{224,... | collective-permute-start | bytes 393224 | tf_op jit(solution)/shard_map/ppermute | solution.py:48
  60.8 6.0 %all-to-all-done.1 = f32[8,32,128]{2,1,0:T(8,128)S(1)} async-done(((f32[8,32,128]{2,1,0:T(8,128)}), f32[8,32,128]{2,1,0:T(8,128)S(1)}, u32[]{:S(2)}, u32[]{:S(2)}) %all-to-all-start.1) | async-done | bytes 131104 | tf_op jit(solution)/shard_map/all_to_all | solution.py:259
  67.8 3.6 %all-to-all-start.2 = ((f32[16,32,128]{2,1,0:T(8,128)}), f32[16,32,128]{2,1,0:T(8,128)S(1)}, u32[]{:S(2)}, u32[]{:S(2)}) async-start(f32[16,32,128]{2,1,0:T(8,128)} %broadcast_in_dim.42), calls=%async_computation.2 | async-start | bytes 524288 | tf_op jit(solution)/shard_map/all_to_all | solution.py:259
  71.4 2.7 %collective-permute-start.12 = (f32[2,48,8,128]{3,2,1,0:T(8,128)S(1)}, f32[2,48,8,128]{3,2,1,0:T(8,128)S(1)}, u32[]{:S(2)}, u32[]{:S(2)}) collective-permute-start(f32[2,48,8,128]{3,2,1,0:T(8,128)S(1)} %pad_maximum_fusion.1.refs_5_), channel_id=1, source_target_pairs={{0,31},{1,2},{2,1},{3,4},{4,3},{5,6},{6,5},{7,8},{8,7},{9,10},{10,... | collective-permute-start | bytes 1179656 | tf_op jit(solution)/shard_map/ppermute | solution.py:42
  74.1 4.9 %all-to-all-done.2 = f32[16,32,128]{2,1,0:T(8,128)S(1)} async-done(((f32[16,32,128]{2,1,0:T(8,128)}), f32[16,32,128]{2,1,0:T(8,128)S(1)}, u32[]{:S(2)}, u32[]{:S(2)}) %all-to-all-start.2) | async-done | bytes 262176 | tf_op jit(solution)/shard_map/all_to_all | solution.py:259
  79.0 11.0 %collective-permute-start.13 = (f32[2,256,128]{2,1,0:T(8,128)S(1)}, f32[2,256,128]{2,1,0:T(8,128)S(1)}, u32[]{:S(2)}, u32[]{:S(2)}) collective-permute-start(f32[2,256,128]{2,1,0:T(8,128)S(1)} %bitcast.16), channel_id=1, source_target_pairs={{0,32},{32,0},{1,33},{33,1},{2,34},{34,2},{3,35},{35,3},{4,36},{36... | collective-permute-start | bytes 786440 | tf_op jit(solution)/shard_map/ppermute | solution.py:263
  89.9 1.2 collective-permute-done.13.refs_9_
  91.1 11.1 %shard_map.87 = (f32[2,48,8,128]{3,2,1,0:T(8,128)S(1)}, f32[2,48,8,128]{3,2,1,0:T(8,128)S(1)}, f32[2,48,8,128]{3,2,1,0:T(8,128)S(1)}, f32[2,256,128]{2,1,0:T(8,1...) custom-call(s32[3,8]{1,0:T(4,128)S(1)} %concatenate.6.refs_0_, ...), custom_call_target="tpu_custom_call" | custom-call | tf_op jit(solution)/shard_map/pallas_call | solution.py:238
  102.7 1.3 collective-permute-done.14
  104.7 5.7 %all-to-all-start.3 = ((f32[16,32,128]{2,1,0:T(8,128)}), f32[16,32,128]{2,1,0:T(8,128)S(1)}, u32[]{:S(2)}, u32[]{:S(2)}) async-start(f32[16,32,128]{2,1,0:T(8,128)} %bitcast.10), calls=%async_computation.3 | async-start | bytes 524288 | tf_op jit(solution)/shard_map/all_to_all | solution.py:259
  110.4 2.2 %collective-permute-done.15 = f32[2,48,8,128]{3,2,1,0:T(8,128)S(1)} collective-permute-done((f32[2,48,8,128]{3,2,1,0:T(8,128)S(1)}, f32[2,48,8,128]{3,2,1,0:T(8,128)S(1)}, u32[]{:S(2)}, u32[]{:S(2)}) %collective-permute-start.15) | collective-permute-done | bytes 393248 | tf_op jit(solution)/shard_map/ppermute | solution.py:42
  112.7 3.9 %collective-permute-done.16 = f32[2,48,8,128]{3,2,1,0:T(8,128)S(1)} collective-permute-done((f32[2,48,8,128]{3,2,1,0:T(8,128)S(1)}, f32[2,48,8,128]{3,2,1,0:T(8,128)S(1)}, u32[]{:S(2)}, u32[]{:S(2)}) %collective-permute-start.16) | collective-permute-done | bytes 393248 | tf_op jit(solution)/shard_map/ppermute | solution.py:42
  116.6 2.9 %all-to-all-done.3 = f32[16,32,128]{2,1,0:T(8,128)S(1)} async-done(((f32[16,32,128]{2,1,0:T(8,128)}), f32[16,32,128]{2,1,0:T(8,128)S(1)}, u32[]{:S(2)}, u32[]{:S(2)}) %all-to-all-start.3) | async-done | bytes 262176 | tf_op jit(solution)/shard_map/all_to_all | solution.py:259
  121.0 4.0 %all-to-all-start.4 = ((f32[8,32,128]{2,1,0:T(8,128)}), f32[8,32,128]{2,1,0:T(8,128)S(1)}, u32[]{:S(2)}, u32[]{:S(2)}) async-start(f32[8,32,128]{2,1,0:T(8,128)} %broadcast_in_dim.43), calls=%async_computation.4 | async-start | bytes 262144 | tf_op jit(solution)/shard_map/all_to_all | solution.py:259
  125.7 7.2 %all-to-all-done.4 = f32[8,32,128]{2,1,0:T(8,128)S(1)} async-done(((f32[8,32,128]{2,1,0:T(8,128)}), f32[8,32,128]{2,1,0:T(8,128)S(1)}, u32[]{:S(2)}, u32[]{:S(2)}) %all-to-all-start.4) | async-done | bytes 131104 | tf_op jit(solution)/shard_map/all_to_all | solution.py:259
  133.0 13.7 %all_to_all.30 = f32[16,32,128]{2,1,0:T(8,128)S(1)} all-to-all(f32[16,32,128]{2,1,0:T(8,128)S(1)} %broadcast_in_dim.44), channel_id=1, replica_groups=mesh['y'=4,'core'=2,'z'=8,'x'=4] {'y','x'}, dimensions={0} | all-to-all | bytes 524288 | tf_op jit(solution)/shard_map/all_to_all | solution.py:259
  146.7 1.5 %collective-permute-start.19 = (f32[2,256,128]{2,1,0:T(8,128)S(1)}, f32[2,256,128]{2,1,0:T(8,128)S(1)}, u32[]{:S(2)}, u32[]{:S(2)}) collective-permute-start(f32[2,256,128]{2,1,0:T(8,128)S(1)} %bitcast.18), channel_id=1, source_target_pairs={{0,32},{32,0},{1,33},{33,1},{2,34},{34,2},{3,35},{35,3},{4,36},{36... | collective-permute-start | bytes 786440 | tf_op jit(solution)/shard_map/ppermute | solution.py:263
  148.2 1.2 collective-permute-done.19.other_ref
  149.4 1.2 shard_map.88
  (45 shorter events, 9.1 us)
Async XLA Ops:
  0.6 12.1 %collective-permute-start.1 = (f32[2,16,8,128]{3,2,1,0:T(8,128)}, f32[2,16,8,128]{3,2,1,0:T(8,128)S(1)}, u32[]{:S(2)}, u32[]{:S(2)}) collective-permute-start(f32[2,16,8,128]{3,2,1,0:T(8,128)} %bitcast.22), channel_id=1, source_target_pairs={{0,31},{1,2},{2,1},{3,4},{4,3},{5,6},{6,5},{7,8},{8,7},{9,10},{10,... | collective-permute-start | bytes 393224 | tf_op jit(solution)/shard_map/ppermute | solution.py:42
  9.3 4.3 %collective-permute-start = (f32[2,16,8,128]{3,2,1,0:T(8,128)}, f32[2,16,8,128]{3,2,1,0:T(8,128)S(1)}, u32[]{:S(2)}, u32[]{:S(2)}) collective-permute-start(f32[2,16,8,128]{3,2,1,0:T(8,128)} %bitcast.23), channel_id=1, source_target_pairs={{0,1},{1,0},{2,3},{3,2},{4,5},{5,4},{6,7},{7,6},{8,9},{9,8},{10,11... | collective-permute-start | bytes 393224 | tf_op jit(solution)/shard_map/ppermute | solution.py:42
  14.5 8.9 %collective-permute-start.3 = (f32[3,2,16,8,128]{4,3,2,1,0:T(8,128)S(1)}, f32[3,2,16,8,128]{4,3,2,1,0:T(8,128)S(1)}, u32[]{:S(2)}, u32[]{:S(2)}) collective-permute-start(f32[3,2,16,8,128]{4,3,2,1,0:T(8,128)S(1)} %pad_maximum_fusion.refs_5_), channel_id=1, source_target_pairs={{0,224},{32,64},{64,32},{96,128},{128,96},{160,192},{192,160},{224... | collective-permute-start | bytes 1179656 | tf_op jit(solution)/shard_map/ppermute | solution.py:42
  17.7 5.8 %collective-permute-start.2 = (f32[3,2,16,8,128]{4,3,2,1,0:T(8,128)S(1)}, f32[3,2,16,8,128]{4,3,2,1,0:T(8,128)S(1)}, u32[]{:S(2)}, u32[]{:S(2)}) collective-permute-start(f32[3,2,16,8,128]{4,3,2,1,0:T(8,128)S(1)} %pad_maximum_fusion.refs_5_), channel_id=1, source_target_pairs={{0,32},{32,0},{64,96},{96,64},{128,160},{160,128},{192,224},{224,1... | collective-permute-start | bytes 1179656 | tf_op jit(solution)/shard_map/ppermute | solution.py:42
  33.7 10.6 %collective-permute-start.5 = (f32[2,48,8,128]{3,2,1,0:T(8,128)S(1)}, f32[2,48,8,128]{3,2,1,0:T(8,128)S(1)}, u32[]{:S(2)}, u32[]{:S(2)}) collective-permute-start(f32[2,48,8,128]{3,2,1,0:T(8,128)S(1)} %get-tuple-element.27), channel_id=1, source_target_pairs={{0,1},{1,0},{2,3},{3,2},{4,5},{5,4},{6,7},{7,6},{8,9},{9,8},{10,11... | collective-permute-start | bytes 1179656 | tf_op jit(solution)/shard_map/ppermute | solution.py:42
  33.8 12.6 %collective-permute-start.6 = (f32[2,48,8,128]{3,2,1,0:T(8,128)S(1)}, f32[2,48,8,128]{3,2,1,0:T(8,128)S(1)}, u32[]{:S(2)}, u32[]{:S(2)}) collective-permute-start(f32[2,48,8,128]{3,2,1,0:T(8,128)S(1)} %get-tuple-element.28), channel_id=1, source_target_pairs={{0,31},{1,2},{2,1},{3,4},{4,3},{5,6},{6,5},{7,8},{8,7},{9,10},{10,... | collective-permute-start | bytes 1179656 | tf_op jit(solution)/shard_map/ppermute | solution.py:42
  37.0 3.0 %collective-permute-start.4 = (f32[2,256,128]{2,1,0:T(8,128)S(1)}, f32[2,256,128]{2,1,0:T(8,128)S(1)}, u32[]{:S(2)}, u32[]{:S(2)}) collective-permute-start(f32[2,256,128]{2,1,0:T(8,128)S(1)} %get-tuple-element.25), channel_id=1, source_target_pairs={{0,32},{32,0},{1,33},{33,1},{2,34},{34,2},{3,35},{35,3},{4,36},{36... | collective-permute-start | bytes 786440 | tf_op jit(solution)/shard_map/ppermute | solution.py:263
  40.8 11.9 %all-to-all-start = ((f32[16,32,128]{2,1,0:T(8,128)}), f32[16,32,128]{2,1,0:T(8,128)S(1)}, u32[]{:S(2)}, u32[]{:S(2)}) async-start(f32[16,32,128]{2,1,0:T(8,128)} %bitcast.8), calls=%async_computation | async-start | bytes 524288 | tf_op jit(solution)/shard_map/all_to_all | solution.py:259
  52.8 14.1 %collective-permute-start.8 = (f32[2,32,8,128]{3,2,1,0:T(8,128)S(1)}, f32[2,32,8,128]{3,2,1,0:T(8,128)S(1)}, u32[]{:S(2)}, u32[]{:S(2)}) collective-permute-start(f32[2,32,8,128]{3,2,1,0:T(8,128)S(1)} %get-tuple-element.55), channel_id=1, source_target_pairs={{0,224},{32,64},{64,32},{96,128},{128,96},{160,192},{192,160},{224... | collective-permute-start | bytes 786440 | tf_op jit(solution)/shard_map/ppermute | solution.py:42
  53.6 13.2 %collective-permute-start.7 = (f32[2,32,8,128]{3,2,1,0:T(8,128)S(1)}, f32[2,32,8,128]{3,2,1,0:T(8,128)S(1)}, u32[]{:S(2)}, u32[]{:S(2)}) collective-permute-start(f32[2,32,8,128]{3,2,1,0:T(8,128)S(1)} %get-tuple-element.56), channel_id=1, source_target_pairs={{0,32},{32,0},{64,96},{96,64},{128,160},{160,128},{192,224},{224,1... | collective-permute-start | bytes 786440 | tf_op jit(solution)/shard_map/ppermute | solution.py:42
  54.8 12.0 %all-to-all-start.1 = ((f32[8,32,128]{2,1,0:T(8,128)}), f32[8,32,128]{2,1,0:T(8,128)S(1)}, u32[]{:S(2)}, u32[]{:S(2)}) async-start(f32[8,32,128]{2,1,0:T(8,128)} %broadcast_in_dim.39), calls=%async_computation.1 | async-start | bytes 262144 | tf_op jit(solution)/shard_map/all_to_all | solution.py:259
  58.3 8.6 %collective-permute-start.9 = (f32[2,16,8,128]{3,2,1,0:T(8,128)S(1)}, f32[2,16,8,128]{3,2,1,0:T(8,128)S(1)}, u32[]{:S(2)}, u32[]{:S(2)}) collective-permute-start(f32[2,16,8,128]{3,2,1,0:T(8,128)S(1)} %get-tuple-element.53), channel_id=1, source_target_pairs={{0,192},{32,224},{64,128},{96,160},{128,64},{160,96},{192,0},{224,... | collective-permute-start | bytes 393224 | tf_op jit(solution)/shard_map/ppermute | solution.py:48
  60.8 6.1 %collective-permute-start.10 = (f32[2,16,8,128]{3,2,1,0:T(8,128)S(1)}, f32[2,16,8,128]{3,2,1,0:T(8,128)S(1)}, u32[]{:S(2)}, u32[]{:S(2)}) collective-permute-start(f32[2,16,8,128]{3,2,1,0:T(8,128)S(1)} %get-tuple-element.54), channel_id=1, source_target_pairs={{0,64},{32,96},{64,0},{96,32},{128,192},{160,224},{192,128},{224,1... | collective-permute-start | bytes 393224 | tf_op jit(solution)/shard_map/ppermute | solution.py:48
  67.8 11.2 %all-to-all-start.2 = ((f32[16,32,128]{2,1,0:T(8,128)}), f32[16,32,128]{2,1,0:T(8,128)S(1)}, u32[]{:S(2)}, u32[]{:S(2)}) async-start(f32[16,32,128]{2,1,0:T(8,128)} %broadcast_in_dim.42), calls=%async_computation.2 | async-start | bytes 524288 | tf_op jit(solution)/shard_map/all_to_all | solution.py:259
  71.4 18.5 %collective-permute-start.12 = (f32[2,48,8,128]{3,2,1,0:T(8,128)S(1)}, f32[2,48,8,128]{3,2,1,0:T(8,128)S(1)}, u32[]{:S(2)}, u32[]{:S(2)}) collective-permute-start(f32[2,48,8,128]{3,2,1,0:T(8,128)S(1)} %pad_maximum_fusion.1.refs_5_), channel_id=1, source_target_pairs={{0,31},{1,2},{2,1},{3,4},{4,3},{5,6},{6,5},{7,8},{8,7},{9,10},{10,... | collective-permute-start | bytes 1179656 | tf_op jit(solution)/shard_map/ppermute | solution.py:42
  74.1 15.8 %collective-permute-start.11 = (f32[2,48,8,128]{3,2,1,0:T(8,128)S(1)}, f32[2,48,8,128]{3,2,1,0:T(8,128)S(1)}, u32[]{:S(2)}, u32[]{:S(2)}) collective-permute-start(f32[2,48,8,128]{3,2,1,0:T(8,128)S(1)} %pad_maximum_fusion.1.refs_5_), channel_id=1, source_target_pairs={{0,1},{1,0},{2,3},{3,2},{4,5},{5,4},{6,7},{7,6},{8,9},{9,8},{10,11... | collective-permute-start | bytes 1179656 | tf_op jit(solution)/shard_map/ppermute | solution.py:42
  79.0 12.1 %collective-permute-start.13 = (f32[2,256,128]{2,1,0:T(8,128)S(1)}, f32[2,256,128]{2,1,0:T(8,128)S(1)}, u32[]{:S(2)}, u32[]{:S(2)}) collective-permute-start(f32[2,256,128]{2,1,0:T(8,128)S(1)} %bitcast.16), channel_id=1, source_target_pairs={{0,32},{32,0},{1,33},{33,1},{2,34},{34,2},{3,35},{35,3},{4,36},{36... | collective-permute-start | bytes 786440 | tf_op jit(solution)/shard_map/ppermute | solution.py:263
  102.2 10.5 %collective-permute-start.15 = (f32[2,48,8,128]{3,2,1,0:T(8,128)S(1)}, f32[2,48,8,128]{3,2,1,0:T(8,128)S(1)}, u32[]{:S(2)}, u32[]{:S(2)}) collective-permute-start(f32[2,48,8,128]{3,2,1,0:T(8,128)S(1)} %get-tuple-element.38), channel_id=1, source_target_pairs={{0,1},{1,0},{2,3},{3,2},{4,5},{5,4},{6,7},{7,6},{8,9},{9,8},{10,11... | collective-permute-start | bytes 1179656 | tf_op jit(solution)/shard_map/ppermute | solution.py:42
  102.3 14.3 %collective-permute-start.16 = (f32[2,48,8,128]{3,2,1,0:T(8,128)S(1)}, f32[2,48,8,128]{3,2,1,0:T(8,128)S(1)}, u32[]{:S(2)}, u32[]{:S(2)}) collective-permute-start(f32[2,48,8,128]{3,2,1,0:T(8,128)S(1)} %get-tuple-element.39), channel_id=1, source_target_pairs={{0,31},{1,2},{2,1},{3,4},{4,3},{5,6},{6,5},{7,8},{8,7},{9,10},{10,... | collective-permute-start | bytes 1179656 | tf_op jit(solution)/shard_map/ppermute | solution.py:42
  102.4 1.6 %collective-permute-start.14 = (f32[2,256,128]{2,1,0:T(8,128)S(1)}, f32[2,256,128]{2,1,0:T(8,128)S(1)}, u32[]{:S(2)}, u32[]{:S(2)}) collective-permute-start(f32[2,256,128]{2,1,0:T(8,128)S(1)} %get-tuple-element.36), channel_id=1, source_target_pairs={{0,32},{32,0},{1,33},{33,1},{2,34},{34,2},{3,35},{35,3},{4,36},{36... | collective-permute-start | bytes 786440 | tf_op jit(solution)/shard_map/ppermute | solution.py:263
  104.7 14.8 %all-to-all-start.3 = ((f32[16,32,128]{2,1,0:T(8,128)}), f32[16,32,128]{2,1,0:T(8,128)S(1)}, u32[]{:S(2)}, u32[]{:S(2)}) async-start(f32[16,32,128]{2,1,0:T(8,128)} %bitcast.10), calls=%async_computation.3 | async-start | bytes 524288 | tf_op jit(solution)/shard_map/all_to_all | solution.py:259
  116.6 32.8 %copy-start = (f32[2,2,256,128]{3,2,1,0:T(8,128)S(1)}, f32[2,2,256,128]{3,2,1,0:T(8,128)}, u32[]{:S(2)}) copy-start(f32[2,2,256,128]{3,2,1,0:T(8,128)} %get-tuple-element.44.probe_ref) | copy-start | bytes 1572868
  119.6 5.4 %collective-permute-start.17 = (f32[2,16,8,128]{3,2,1,0:T(8,128)S(1)}, f32[2,16,8,128]{3,2,1,0:T(8,128)S(1)}, u32[]{:S(2)}, u32[]{:S(2)}) collective-permute-start(f32[2,16,8,128]{3,2,1,0:T(8,128)S(1)} %get-tuple-element.51), channel_id=1, source_target_pairs={{0,32},{32,0},{64,96},{96,64},{128,160},{160,128},{192,224},{224,1... | collective-permute-start | bytes 393224 | tf_op jit(solution)/shard_map/ppermute | solution.py:42
  120.2 4.8 %collective-permute-start.18 = (f32[2,16,8,128]{3,2,1,0:T(8,128)S(1)}, f32[2,16,8,128]{3,2,1,0:T(8,128)S(1)}, u32[]{:S(2)}, u32[]{:S(2)}) collective-permute-start(f32[2,16,8,128]{3,2,1,0:T(8,128)S(1)} %get-tuple-element.52), channel_id=1, source_target_pairs={{0,224},{32,64},{64,32},{96,128},{128,96},{160,192},{192,160},{224... | collective-permute-start | bytes 393224 | tf_op jit(solution)/shard_map/ppermute | solution.py:42
  121.0 11.9 %all-to-all-start.4 = ((f32[8,32,128]{2,1,0:T(8,128)}), f32[8,32,128]{2,1,0:T(8,128)S(1)}, u32[]{:S(2)}, u32[]{:S(2)}) async-start(f32[8,32,128]{2,1,0:T(8,128)} %broadcast_in_dim.43), calls=%async_computation.4 | async-start | bytes 262144 | tf_op jit(solution)/shard_map/all_to_all | solution.py:259
  146.7 2.7 %collective-permute-start.19 = (f32[2,256,128]{2,1,0:T(8,128)S(1)}, f32[2,256,128]{2,1,0:T(8,128)S(1)}, u32[]{:S(2)}, u32[]{:S(2)}) collective-permute-start(f32[2,256,128]{2,1,0:T(8,128)S(1)} %bitcast.18), channel_id=1, source_target_pairs={{0,32},{32,0},{1,33},{33,1},{2,34},{34,2},{3,35},{35,3},{4,36},{36... | collective-permute-start | bytes 786440 | tf_op jit(solution)/shard_map/ppermute | solution.py:263

commit v5 on v4

--- a/solution.py
+++ b/solution.py
@@ -10,7 +10,7 @@
 
 ROW = ("y", "core")
 COL = ("z", "x")
-PLANE = ("y", "x")
+CHIPS = ("y", "z", "x")
 LANES = 128
 TILES = 16
 GROUP = 4
@@ -263,45 +263,48 @@
     return lax.ppermute(value, "core", [(0, 1), (1, 0)])
 
 
-def sum_steps(keep, send):
-    plane = lax.axis_size(PLANE)
-    depth = lax.axis_size("z")
-
-    def over_plane():
-        half = keep + core_swap(send)
-        return exchange(half.reshape(plane, -1, LANES), PLANE).sum(0)
-
-    def over_depth(share):
-        return exchange(jnp.broadcast_to(share, (depth,) + share.shape), "z").sum(0)
-
-    def gathered(share):
-        mine = exchange(jnp.broadcast_to(share, (plane,) + share.shape), PLANE).reshape(keep.shape)
-        return mine, core_swap(mine)
-
-    return over_plane, over_depth, gathered
+def shares(keep, send):
+    half = keep + core_swap(send)
+    return exchange(half.reshape(lax.axis_size(CHIPS), -1, LANES), CHIPS).sum(0)
+
+
+def gathered(share, shape):
+    chips = lax.axis_size(CHIPS)
+    mine = exchange(jnp.broadcast_to(share, (chips,) + share.shape), CHIPS).reshape(shape)
+    return mine, core_swap(mine)
 
 
 def side_sum(own, side0, side2, at_end):
     return own + side0 + jnp.where(at_end, 0.0, side2)
 
 
-def updated_strip(strip, sums, peak):
+def row_payloads(sums):
+    index = lax.axis_index(ROW)
+    odd = lax.rem(index, 2) == 1
+    down_first = lax.rem(index // 2, 2) == 0
+    upper, lower = sums[:, : 2 * TILES], sums[:, TILES:]
+    above, below = sums[:, :TILES], sums[:, 2 * TILES :]
+    return (
+        jnp.where(odd, upper, lower),
+        jnp.where(odd, lower, upper),
+        jnp.where(down_first, below, above),
+        jnp.where(down_first, above, below),
+    )
+
+
+def updated_strip(strip, sums, payloads, peak):
     index, places, at_end = place_of(ROW)
     last = lax.axis_size(ROW) - 1
     odd = lax.rem(index, 2) == 1
     down_first = lax.rem(index // 2, 2) == 0
-    upper, lower = sums[:, : 2 * TILES], sums[:, TILES:]
-    near0 = paired(jnp.where(odd, upper, lower), ROW, 0)
-    near2 = paired(jnp.where(odd, lower, upper), ROW, 2)
-    above, below = sums[:, :TILES], sums[:, 2 * TILES :]
-    far_a = paired_far(jnp.where(down_first, below, above), ROW, 0)
-    far_b = paired_far(jnp.where(down_first, above, below), ROW, 1)
-    near2 = jnp.where(at_end, 0.0, near2)
-    far_b = jnp.where((index < 2) | (index > last - 2), 0.0, far_b)
+    near0 = paired(payloads[0], ROW, 0)
+    near2 = jnp.where(at_end, 0.0, paired(payloads[1], ROW, 2))
+    far_a = paired_far(payloads[2], ROW, 0)
+    far_b = jnp.where((index < 2) | (index > last - 2), 0.0, paired_far(payloads[3], ROW, 1))
     from_upper, from_lower = jnp.where(odd, near0, near2), jnp.where(odd, near2, near0)
-    grad_above = above + from_upper[:, :TILES] + jnp.where(down_first, far_b, far_a)
+    grad_above = sums[:, :TILES] + from_upper[:, :TILES] + jnp.where(down_first, far_b, far_a)
     grad = sums[:, TILES : 2 * TILES] + from_upper[:, TILES:] + from_lower[:, :TILES]
-    grad_below = below + from_lower[:, TILES:] + jnp.where(down_first, far_a, far_b)
+    grad_below = sums[:, 2 * TILES :] + from_lower[:, TILES:] + jnp.where(down_first, far_a, far_b)
     return jnp.concatenate(
         [
             jnp.where(index == 0, 0.0, strip[:, :TILES] - grad_above / peak),
@@ -310,6 +313,10 @@
         ],
         axis=1,
     )
+
+
+def after(value, *others):
+    return lax.optimization_barrier((value, others))[0]
 
 
 def last_probe_kernel(probe_ref, mine_ref, other_ref, out_ref):
@@ -348,27 +355,23 @@
     strip = jnp.stack([paired(own, COL, 0), own, paired(own, COL, 2)])
     strips = (strip, paired(strip, ROW, 0), paired(strip, ROW, 2))
     col0, col1, col2, keep, send, peak, strip = gradients(True, live_slots, patterns, tables, probe_field, *strips)
-    over_plane, over_depth, gathered = sum_steps(keep, send)
     sums = side_sum(col1, paired(col0, COL, 0), paired(col2, COL, 2), col_end)
-    share, sums = lax.optimization_barrier((over_plane(), sums))
-    strip = updated_strip(strip, sums, peak)
-    share, strip = lax.optimization_barrier((over_depth(share), strip))
+    payloads = row_payloads(sums)
+    totals = gathered(after(shares(keep, send), *payloads), keep.shape)
+    strip = updated_strip(strip, sums, payloads, peak)
     strips = (strip, paired(strip, COL, 0), paired(strip, COL, 2))
-    totals = gathered(share)
 
     col0, col1, col2, keep, send, peak, probe = gradients(
         False, live_slots, patterns, tables, probe_field, *strips, *totals
     )
-    over_plane, over_depth, gathered = sum_steps(keep, send)
     sums = side_sum(col1, paired(col0, COL, 0), paired(col2, COL, 2), col_end)
-    share, sums = lax.optimization_barrier((over_plane(), sums))
     odd = lax.rem(lax.axis_index(ROW), 2) == 1
     above, grad, below = (sums[:, i * TILES : (i + 1) * TILES] for i in range(3))
-    arrived = (paired(jnp.where(odd, above, below), ROW, 0), paired(jnp.where(odd, below, above), ROW, 2))
-    grad = side_sum(grad, *arrived, row_end)
+    payloads = (jnp.where(odd, above, below), jnp.where(odd, below, above))
+    totals = gathered(after(shares(keep, send), *payloads), keep.shape)
+    grad = side_sum(grad, paired(payloads[0], ROW, 0), paired(payloads[1], ROW, 2), row_end)
     new_object = (strip[:, TILES : 2 * TILES] - grad / peak).reshape(object_field.shape)
-    share, new_object = lax.optimization_barrier((over_depth(share), new_object))
-    return (new_object, last_probe(probe, *gathered(share)))
+    return (new_object, last_probe(probe, *totals))
 
 
 def solution(mesh):

time: 152 us -> 153 us (level)
  starting transfers between devices: 57.8 us -> 71.7 us
  blocking collectives: 13.7 us -> 0 us
  waiting for transfers between devices: 48.8 us -> 51.2 us
    all_to_all x5 -> x4, starting transfers between devices: 20.3 us -> 35.3 us  [exchange(): return lax.all_to_all(value, axes, 0, 0, tiled=True)]
    all_to_all x1 -> x0, blocking collectives: 13.7 us -> none  [exchange(): return lax.all_to_all(value, axes, 0, 0, tiled=True)]
    all_to_all x5 -> x4, waiting for transfers between devices: 27.2 us -> 38.1 us  [exchange(): return lax.all_to_all(value, axes, 0, 0, tiled=True)]
    ppermute x14, waiting for transfers between devices: 16.8 us -> 9.95 us  [paired(): return lax.ppermute(value, axes, pairs)]
    ppermute x14, starting transfers between devices: 20.3 us -> 26.4 us  [paired(): return lax.ppermute(value, axes, pairs)]
    ppermute x4, starting transfers between devices: 14.7 us -> 8.67 us  [core_swap(): return lax.ppermute(value, 'core', [(0, 1), (1, 0)])]
    ppermute x4, waiting for transfers between devices: 4.74 us -> 3.15 us  [core_swap(): return lax.ppermute(value, 'core', [(0, 1), (1, 0)])]
  transfers between devices with their start and end apart: 25 -> 24, of which waited for: 15 -> 11; matrix products, arithmetic and copies ran while one was open for 3% -> 3% of each run, Pallas kernels for 0% -> 0%
where the time goes in v5:
time: 153 us; the launch traced here: 152 us
  starting transfers between devices  71.7 us (47%)
  waiting for transfers between devices  51.2 us (33%)
  Pallas kernels  22 us (14%)
  other arithmetic  3.81 us (2%)
  local copies, waits for them, and re-layouts  2.17 us (1%)
    all_to_all x4, waiting for transfers between devices, exchange(): return lax.all_to_all(value, axes, 0, 0, tiled=True)  38.1 us
    all_to_all x4, starting transfers between devices, exchange(): return lax.all_to_all(value, axes, 0, 0, tiled=True)  35.3 us
    ppermute x14, starting transfers between devices, paired(): return lax.ppermute(value, axes, pairs)  26.4 us
    pallas_call x2, Pallas kernels, gradients(): pl.pallas_call(functools.partial(gradient_kernel, first), out_shape=(stri...  20.8 us
    ppermute x14, waiting for transfers between devices, paired(): return lax.ppermute(value, axes, pairs)  9.95 us
    ppermute x4, starting transfers between devices, core_swap(): return lax.ppermute(value, 'core', [(0, 1), (1, 0)])  8.67 us
    ppermute x4, waiting for transfers between devices, core_swap(): return lax.ppermute(value, 'core', [(0, 1), (1, 0)])  3.15 us
  transfers between devices with their start and end apart: 24, of which 11 were waited for; matrix products, arithmetic and copies ran while one was open for 3% of the time, Pallas kernels for 0%

profile of v5, /device:TPU:1, one launch (start us, length us, event | category | flops | bytes accessed | tf_op | source)
XLA Modules:
  0.0 152.4 jit_solution(17038165172834460967)
XLA Ops:
  0.6 8.7 %collective-permute-start.1 = (f32[2,16,8,128]{3,2,1,0:T(8,128)}, f32[2,16,8,128]{3,2,1,0:T(8,128)S(1)}, u32[]{:S(2)}, u32[]{:S(2)}) collective-permute-start(f32[2,16,8,128]{3,2,1,0:T(8,128)} %bitcast.22), channel_id=1, source_target_pairs={{0,31},{1,2},{2,1},{3,4},{4,3},{5,6},{6,5},{7,8},{8,7},{9,10},{10,... | collective-permute-start | bytes 393224 | tf_op jit(solution)/shard_map/ppermute | solution.py:42
  9.3 3.4 %collective-permute-done.1 = f32[2,16,8,128]{3,2,1,0:T(8,128)S(1)} collective-permute-done((f32[2,16,8,128]{3,2,1,0:T(8,128)}, f32[2,16,8,128]{3,2,1,0:T(8,128)S(1)}, u32[]{:S(2)}, u32[]{:S(2)}) %collective-permute-start.1) | collective-permute-done | bytes 131104 | tf_op jit(solution)/shard_map/ppermute | solution.py:42
  12.7 0.8 collective-permute-done
  13.6 0.9 pad_maximum_fusion.refs_5_
  14.5 3.1 %collective-permute-start.3 = (f32[3,2,16,8,128]{4,3,2,1,0:T(8,128)S(1)}, f32[3,2,16,8,128]{4,3,2,1,0:T(8,128)S(1)}, u32[]{:S(2)}, u32[]{:S(2)}) collective-permute-start(f32[3,2,16,8,128]{4,3,2,1,0:T(8,128)S(1)} %pad_maximum_fusion.refs_5_), channel_id=1, source_target_pairs={{0,224},{32,64},{64,32},{96,128},{128,96},{160,192},{192,160},{224... | collective-permute-start | bytes 1179656 | tf_op jit(solution)/shard_map/ppermute | solution.py:42
  19.1 4.3 %collective-permute-done.3.refs_7_ = f32[3,2,16,8,128]{4,3,2,1,0:T(8,128)S(1)} collective-permute-done((f32[3,2,16,8,128]{4,3,2,1,0:T(8,128)S(1)}, f32[3,2,16,8,128]{4,3,2,1,0:T(8,128)S(1)}, u32[]{:S(2)}, u32[]{:S(2)}) %collective-permute-start.3) | collective-permute-done | bytes 393248 | tf_op jit(solution)/shard_map/ppermute | solution.py:42
  23.4 10.0 %shard_map.86 = (f32[2,48,8,128]{3,2,1,0:T(8,128)S(1)}, f32[2,48,8,128]{3,2,1,0:T(8,128)S(1)}, f32[2,48,8,128]{3,2,1,0:T(8,128)S(1)}, f32[2,256,128]{2,1,0:T(8,1...) custom-call(s32[3,8]{1,0:T(4,128)S(1)} %concatenate.6.refs_0_, ...), custom_call_target="tpu_custom_call" | custom-call | tf_op jit(solution)/shard_map/pallas_call | solution.py:238
  33.6 3.4 %collective-permute-start.5 = (f32[2,48,8,128]{3,2,1,0:T(8,128)S(1)}, f32[2,48,8,128]{3,2,1,0:T(8,128)S(1)}, u32[]{:S(2)}, u32[]{:S(2)}) collective-permute-start(f32[2,48,8,128]{3,2,1,0:T(8,128)S(1)} %get-tuple-element.21), channel_id=1, source_target_pairs={{0,31},{1,2},{2,1},{3,4},{4,3},{5,6},{6,5},{7,8},{8,7},{9,10},{10,... | collective-permute-start | bytes 1179656 | tf_op jit(solution)/shard_map/ppermute | solution.py:42
  37.0 1.5 %collective-permute-done.12 = f32[2,256,128]{2,1,0:T(8,128)S(1)} collective-permute-done((f32[2,256,128]{2,1,0:T(8,128)S(1)}, f32[2,256,128]{2,1,0:T(8,128)S(1)}, u32[]{:S(2)}, u32[]{:S(2)}) %collective-permute-start.12) | collective-permute-done | bytes 262176 | tf_op jit(solution)/shard_map/ppermute | solution.py:263
  38.5 0.7 add.64
  39.3 8.5 %all-to-all-start = ((f32[128,4,128]{2,1,0:T(4,128)}), f32[128,4,128]{2,1,0:T(4,128)S(1)}, u32[]{:S(2)}, u32[]{:S(2)}) async-start(f32[128,4,128]{2,1,0:T(4,128)} %bitcast.8), calls=%async_computation | async-start | bytes 524288 | tf_op jit(solution)/shard_map/all_to_all | solution.py:259
  47.9 1.6 %collective-permute-start.7 = (f32[2,32,8,128]{3,2,1,0:T(8,128)S(1)}, f32[2,32,8,128]{3,2,1,0:T(8,128)S(1)}, u32[]{:S(2)}, u32[]{:S(2)}) collective-permute-start(f32[2,32,8,128]{3,2,1,0:T(8,128)S(1)} %get-tuple-element.43), channel_id=1, source_target_pairs={{0,224},{32,64},{64,32},{96,128},{128,96},{160,192},{192,160},{224... | collective-permute-start | bytes 786440 | tf_op jit(solution)/shard_map/ppermute | solution.py:42
  49.5 1.2 collective-permute-start.6
  52.2 8.6 %all-to-all-done = f32[128,4,128]{2,1,0:T(4,128)S(1)} async-done(((f32[128,4,128]{2,1,0:T(4,128)}), f32[128,4,128]{2,1,0:T(4,128)S(1)}, u32[]{:S(2)}, u32[]{:S(2)}) %all-to-all-start) | async-done | bytes 262176 | tf_op jit(solution)/shard_map/all_to_all | solution.py:259
  60.9 0.7 broadcast_in_dim.35
  61.6 7.0 %all-to-all-start.1 = ((f32[128,4,128]{2,1,0:T(4,128)}), f32[128,4,128]{2,1,0:T(4,128)S(1)}, u32[]{:S(2)}, u32[]{:S(2)}) async-start(f32[128,4,128]{2,1,0:T(4,128)} %broadcast_in_dim.35), calls=%async_computation.1 | async-start | bytes 524288 | tf_op jit(solution)/shard_map/all_to_all | solution.py:259
  68.8 4.1 %collective-permute-start.11 = (f32[2,48,8,128]{3,2,1,0:T(8,128)S(1)}, f32[2,48,8,128]{3,2,1,0:T(8,128)S(1)}, u32[]{:S(2)}, u32[]{:S(2)}) collective-permute-start(f32[2,48,8,128]{3,2,1,0:T(8,128)S(1)} %pad_maximum_fusion.1.refs_5_), channel_id=1, source_target_pairs={{0,31},{1,2},{2,1},{3,4},{4,3},{5,6},{6,5},{7,8},{8,7},{9,10},{10,... | collective-permute-start | bytes 1179656 | tf_op jit(solution)/shard_map/ppermute | solution.py:42
  72.9 7.6 %all-to-all-done.1 = f32[128,4,128]{2,1,0:T(4,128)S(1)} async-done(((f32[128,4,128]{2,1,0:T(4,128)}), f32[128,4,128]{2,1,0:T(4,128)S(1)}, u32[]{:S(2)}, u32[]{:S(2)}) %all-to-all-start.1) | async-done | bytes 262176 | tf_op jit(solution)/shard_map/all_to_all | solution.py:259
  80.5 4.1 %collective-permute-start.13 = (f32[2,256,128]{2,1,0:T(8,128)S(1)}, f32[2,256,128]{2,1,0:T(8,128)S(1)}, u32[]{:S(2)}, u32[]{:S(2)}) collective-permute-start(f32[2,256,128]{2,1,0:T(8,128)S(1)} %bitcast.16), channel_id=1, source_target_pairs={{0,32},{32,0},{1,33},{33,1},{2,34},{34,2},{3,35},{35,3},{4,36},{36... | collective-permute-start | bytes 786440 | tf_op jit(solution)/shard_map/ppermute | solution.py:263
  84.7 1.3 collective-permute-done.11.refs_7_
  86.0 10.8 %shard_map.87 = (f32[2,48,8,128]{3,2,1,0:T(8,128)S(1)}, f32[2,48,8,128]{3,2,1,0:T(8,128)S(1)}, f32[2,48,8,128]{3,2,1,0:T(8,128)S(1)}, f32[2,256,128]{2,1,0:T(8,1...) custom-call(s32[3,8]{1,0:T(4,128)S(1)} %concatenate.6.refs_0_, ...), custom_call_target="tpu_custom_call" | custom-call | tf_op jit(solution)/shard_map/pallas_call | solution.py:238
  96.8 0.9 collective-permute-start.14
  98.0 0.9 collective-permute-start.18
  98.9 1.2 collective-permute-done.18
  100.8 12.7 %all-to-all-start.2 = ((f32[128,4,128]{2,1,0:T(4,128)}), f32[128,4,128]{2,1,0:T(4,128)S(1)}, u32[]{:S(2)}, u32[]{:S(2)}) async-start(f32[128,4,128]{2,1,0:T(4,128)} %bitcast.11), calls=%async_computation.2 | async-start | bytes 524288 | tf_op jit(solution)/shard_map/all_to_all | solution.py:259
  113.6 12.8 %all-to-all-done.2 = f32[128,4,128]{2,1,0:T(4,128)S(1)} async-done(((f32[128,4,128]{2,1,0:T(4,128)}), f32[128,4,128]{2,1,0:T(4,128)S(1)}, u32[]{:S(2)}, u32[]{:S(2)}) %all-to-all-start.2) | async-done | bytes 262176 | tf_op jit(solution)/shard_map/all_to_all | solution.py:259
  126.5 0.7 broadcast_in_dim.36
  127.3 7.2 %all-to-all-start.3 = ((f32[128,4,128]{2,1,0:T(4,128)}), f32[128,4,128]{2,1,0:T(4,128)S(1)}, u32[]{:S(2)}, u32[]{:S(2)}) async-start(f32[128,4,128]{2,1,0:T(4,128)} %broadcast_in_dim.36), calls=%async_computation.3 | async-start | bytes 524288 | tf_op jit(solution)/shard_map/all_to_all | solution.py:259
  134.5 2.8 %collective-permute-start.17 = (f32[2,16,8,128]{3,2,1,0:T(8,128)S(1)}, f32[2,16,8,128]{3,2,1,0:T(8,128)S(1)}, u32[]{:S(2)}, u32[]{:S(2)}) collective-permute-start(f32[2,16,8,128]{3,2,1,0:T(8,128)S(1)} %get-tuple-element.39), channel_id=1, source_target_pairs={{0,224},{32,64},{64,32},{96,128},{128,96},{160,192},{192,160},{224... | collective-permute-start | bytes 393224 | tf_op jit(solution)/shard_map/ppermute | solution.py:42
  137.3 9.1 %all-to-all-done.3 = f32[128,4,128]{2,1,0:T(4,128)S(1)} async-done(((f32[128,4,128]{2,1,0:T(4,128)}), f32[128,4,128]{2,1,0:T(4,128)S(1)}, u32[]{:S(2)}, u32[]{:S(2)}) %all-to-all-start.3) | async-done | bytes 262176 | tf_op jit(solution)/shard_map/all_to_all | solution.py:259
  146.4 3.7 %collective-permute-start.19 = (f32[2,256,128]{2,1,0:T(8,128)S(1)}, f32[2,256,128]{2,1,0:T(8,128)S(1)}, u32[]{:S(2)}, u32[]{:S(2)}) collective-permute-start(f32[2,256,128]{2,1,0:T(8,128)S(1)} %bitcast.18), channel_id=1, source_target_pairs={{0,32},{32,0},{1,33},{33,1},{2,34},{34,2},{3,35},{35,3},{4,36},{36... | collective-permute-start | bytes 786440 | tf_op jit(solution)/shard_map/ppermute | solution.py:263
  151.2 1.2 shard_map.88
  (38 shorter events, 5.3 us)
Async XLA Ops:
  0.6 12.1 %collective-permute-start.1 = (f32[2,16,8,128]{3,2,1,0:T(8,128)}, f32[2,16,8,128]{3,2,1,0:T(8,128)S(1)}, u32[]{:S(2)}, u32[]{:S(2)}) collective-permute-start(f32[2,16,8,128]{3,2,1,0:T(8,128)} %bitcast.22), channel_id=1, source_target_pairs={{0,31},{1,2},{2,1},{3,4},{4,3},{5,6},{6,5},{7,8},{8,7},{9,10},{10,... | collective-permute-start | bytes 393224 | tf_op jit(solution)/shard_map/ppermute | solution.py:42
  9.3 4.3 %collective-permute-start = (f32[2,16,8,128]{3,2,1,0:T(8,128)}, f32[2,16,8,128]{3,2,1,0:T(8,128)S(1)}, u32[]{:S(2)}, u32[]{:S(2)}) collective-permute-start(f32[2,16,8,128]{3,2,1,0:T(8,128)} %bitcast.23), channel_id=1, source_target_pairs={{0,1},{1,0},{2,3},{3,2},{4,5},{5,4},{6,7},{7,6},{8,9},{9,8},{10,11... | collective-permute-start | bytes 393224 | tf_op jit(solution)/shard_map/ppermute | solution.py:42
  14.5 8.9 %collective-permute-start.3 = (f32[3,2,16,8,128]{4,3,2,1,0:T(8,128)S(1)}, f32[3,2,16,8,128]{4,3,2,1,0:T(8,128)S(1)}, u32[]{:S(2)}, u32[]{:S(2)}) collective-permute-start(f32[3,2,16,8,128]{4,3,2,1,0:T(8,128)S(1)} %pad_maximum_fusion.refs_5_), channel_id=1, source_target_pairs={{0,224},{32,64},{64,32},{96,128},{128,96},{160,192},{192,160},{224... | collective-permute-start | bytes 1179656 | tf_op jit(solution)/shard_map/ppermute | solution.py:42
  17.7 5.8 %collective-permute-start.2 = (f32[3,2,16,8,128]{4,3,2,1,0:T(8,128)S(1)}, f32[3,2,16,8,128]{4,3,2,1,0:T(8,128)S(1)}, u32[]{:S(2)}, u32[]{:S(2)}) collective-permute-start(f32[3,2,16,8,128]{4,3,2,1,0:T(8,128)S(1)} %pad_maximum_fusion.refs_5_), channel_id=1, source_target_pairs={{0,32},{32,0},{64,96},{96,64},{128,160},{160,128},{192,224},{224,1... | collective-permute-start | bytes 1179656 | tf_op jit(solution)/shard_map/ppermute | solution.py:42
  33.4 14.4 %collective-permute-start.4 = (f32[2,48,8,128]{3,2,1,0:T(8,128)S(1)}, f32[2,48,8,128]{3,2,1,0:T(8,128)S(1)}, u32[]{:S(2)}, u32[]{:S(2)}) collective-permute-start(f32[2,48,8,128]{3,2,1,0:T(8,128)S(1)} %get-tuple-element.20), channel_id=1, source_target_pairs={{0,1},{1,0},{2,3},{3,2},{4,5},{5,4},{6,7},{7,6},{8,9},{9,8},{10,11... | collective-permute-start | bytes 1179656 | tf_op jit(solution)/shard_map/ppermute | solution.py:42
  33.6 14.2 %collective-permute-start.5 = (f32[2,48,8,128]{3,2,1,0:T(8,128)S(1)}, f32[2,48,8,128]{3,2,1,0:T(8,128)S(1)}, u32[]{:S(2)}, u32[]{:S(2)}) collective-permute-start(f32[2,48,8,128]{3,2,1,0:T(8,128)S(1)} %get-tuple-element.21), channel_id=1, source_target_pairs={{0,31},{1,2},{2,1},{3,4},{4,3},{5,6},{6,5},{7,8},{8,7},{9,10},{10,... | collective-permute-start | bytes 1179656 | tf_op jit(solution)/shard_map/ppermute | solution.py:42
  37.0 1.5 %collective-permute-start.12 = (f32[2,256,128]{2,1,0:T(8,128)S(1)}, f32[2,256,128]{2,1,0:T(8,128)S(1)}, u32[]{:S(2)}, u32[]{:S(2)}) collective-permute-start(f32[2,256,128]{2,1,0:T(8,128)S(1)} %get-tuple-element.24), channel_id=1, source_target_pairs={{0,32},{32,0},{1,33},{33,1},{2,34},{34,2},{3,35},{35,3},{4,36},{36... | collective-permute-start | bytes 786440 | tf_op jit(solution)/shard_map/ppermute | solution.py:263
  39.3 21.5 %all-to-all-start = ((f32[128,4,128]{2,1,0:T(4,128)}), f32[128,4,128]{2,1,0:T(4,128)S(1)}, u32[]{:S(2)}, u32[]{:S(2)}) async-start(f32[128,4,128]{2,1,0:T(4,128)} %bitcast.8), calls=%async_computation | async-start | bytes 524288 | tf_op jit(solution)/shard_map/all_to_all | solution.py:259
  47.9 20.6 %collective-permute-start.7 = (f32[2,32,8,128]{3,2,1,0:T(8,128)S(1)}, f32[2,32,8,128]{3,2,1,0:T(8,128)S(1)}, u32[]{:S(2)}, u32[]{:S(2)}) collective-permute-start(f32[2,32,8,128]{3,2,1,0:T(8,128)S(1)} %get-tuple-element.43), channel_id=1, source_target_pairs={{0,224},{32,64},{64,32},{96,128},{128,96},{160,192},{192,160},{224... | collective-permute-start | bytes 786440 | tf_op jit(solution)/shard_map/ppermute | solution.py:42
  49.5 19.1 %collective-permute-start.6 = (f32[2,32,8,128]{3,2,1,0:T(8,128)S(1)}, f32[2,32,8,128]{3,2,1,0:T(8,128)S(1)}, u32[]{:S(2)}, u32[]{:S(2)}) collective-permute-start(f32[2,32,8,128]{3,2,1,0:T(8,128)S(1)} %get-tuple-element.44), channel_id=1, source_target_pairs={{0,32},{32,0},{64,96},{96,64},{128,160},{160,128},{192,224},{224,1... | collective-permute-start | bytes 786440 | tf_op jit(solution)/shard_map/ppermute | solution.py:42
  50.8 17.9 %collective-permute-start.8 = (f32[2,16,8,128]{3,2,1,0:T(8,128)S(1)}, f32[2,16,8,128]{3,2,1,0:T(8,128)S(1)}, u32[]{:S(2)}, u32[]{:S(2)}) collective-permute-start(f32[2,16,8,128]{3,2,1,0:T(8,128)S(1)} %get-tuple-element.41), channel_id=1, source_target_pairs={{0,192},{32,224},{64,128},{96,160},{128,64},{160,96},{192,0},{224,... | collective-permute-start | bytes 393224 | tf_op jit(solution)/shard_map/ppermute | solution.py:48
  51.5 17.2 %collective-permute-start.9 = (f32[2,16,8,128]{3,2,1,0:T(8,128)S(1)}, f32[2,16,8,128]{3,2,1,0:T(8,128)S(1)}, u32[]{:S(2)}, u32[]{:S(2)}) collective-permute-start(f32[2,16,8,128]{3,2,1,0:T(8,128)S(1)} %get-tuple-element.42), channel_id=1, source_target_pairs={{0,64},{32,96},{64,0},{96,32},{128,192},{160,224},{192,128},{224,1... | collective-permute-start | bytes 393224 | tf_op jit(solution)/shard_map/ppermute | solution.py:48
  61.6 18.9 %all-to-all-start.1 = ((f32[128,4,128]{2,1,0:T(4,128)}), f32[128,4,128]{2,1,0:T(4,128)S(1)}, u32[]{:S(2)}, u32[]{:S(2)}) async-start(f32[128,4,128]{2,1,0:T(4,128)} %broadcast_in_dim.35), calls=%async_computation.1 | async-start | bytes 524288 | tf_op jit(solution)/shard_map/all_to_all | solution.py:259
  68.8 17.1 %collective-permute-start.11 = (f32[2,48,8,128]{3,2,1,0:T(8,128)S(1)}, f32[2,48,8,128]{3,2,1,0:T(8,128)S(1)}, u32[]{:S(2)}, u32[]{:S(2)}) collective-permute-start(f32[2,48,8,128]{3,2,1,0:T(8,128)S(1)} %pad_maximum_fusion.1.refs_5_), channel_id=1, source_target_pairs={{0,31},{1,2},{2,1},{3,4},{4,3},{5,6},{6,5},{7,8},{8,7},{9,10},{10,... | collective-permute-start | bytes 1179656 | tf_op jit(solution)/shard_map/ppermute | solution.py:42
  72.9 13.1 %collective-permute-start.10 = (f32[2,48,8,128]{3,2,1,0:T(8,128)S(1)}, f32[2,48,8,128]{3,2,1,0:T(8,128)S(1)}, u32[]{:S(2)}, u32[]{:S(2)}) collective-permute-start(f32[2,48,8,128]{3,2,1,0:T(8,128)S(1)} %pad_maximum_fusion.1.refs_5_), channel_id=1, source_target_pairs={{0,1},{1,0},{2,3},{3,2},{4,5},{5,4},{6,7},{7,6},{8,9},{9,8},{10,11... | collective-permute-start | bytes 1179656 | tf_op jit(solution)/shard_map/ppermute | solution.py:42
  80.5 5.4 %collective-permute-start.13 = (f32[2,256,128]{2,1,0:T(8,128)S(1)}, f32[2,256,128]{2,1,0:T(8,128)S(1)}, u32[]{:S(2)}, u32[]{:S(2)}) collective-permute-start(f32[2,256,128]{2,1,0:T(8,128)S(1)} %bitcast.16), channel_id=1, source_target_pairs={{0,32},{32,0},{1,33},{33,1},{2,34},{34,2},{3,35},{35,3},{4,36},{36... | collective-permute-start | bytes 786440 | tf_op jit(solution)/shard_map/ppermute | solution.py:263
  96.8 16.6 %collective-permute-start.14 = (f32[2,48,8,128]{3,2,1,0:T(8,128)S(1)}, f32[2,48,8,128]{3,2,1,0:T(8,128)S(1)}, u32[]{:S(2)}, u32[]{:S(2)}) collective-permute-start(f32[2,48,8,128]{3,2,1,0:T(8,128)S(1)} %get-tuple-element.27), channel_id=1, source_target_pairs={{0,1},{1,0},{2,3},{3,2},{4,5},{5,4},{6,7},{7,6},{8,9},{9,8},{10,11... | collective-permute-start | bytes 1179656 | tf_op jit(solution)/shard_map/ppermute | solution.py:42
  97.7 15.8 %collective-permute-start.15 = (f32[2,48,8,128]{3,2,1,0:T(8,128)S(1)}, f32[2,48,8,128]{3,2,1,0:T(8,128)S(1)}, u32[]{:S(2)}, u32[]{:S(2)}) collective-permute-start(f32[2,48,8,128]{3,2,1,0:T(8,128)S(1)} %get-tuple-element.28), channel_id=1, source_target_pairs={{0,31},{1,2},{2,1},{3,4},{4,3},{5,6},{6,5},{7,8},{8,7},{9,10},{10,... | collective-permute-start | bytes 1179656 | tf_op jit(solution)/shard_map/ppermute | solution.py:42
  98.0 2.0 %collective-permute-start.18 = (f32[2,256,128]{2,1,0:T(8,128)S(1)}, f32[2,256,128]{2,1,0:T(8,128)S(1)}, u32[]{:S(2)}, u32[]{:S(2)}) collective-permute-start(f32[2,256,128]{2,1,0:T(8,128)S(1)} %get-tuple-element.32), channel_id=1, source_target_pairs={{0,32},{32,0},{1,33},{33,1},{2,34},{34,2},{3,35},{35,3},{4,36},{36... | collective-permute-start | bytes 786440 | tf_op jit(solution)/shard_map/ppermute | solution.py:263
  100.8 50.5 %copy-start = (f32[2,2,256,128]{3,2,1,0:T(8,128)S(1)}, f32[2,2,256,128]{3,2,1,0:T(8,128)}, u32[]{:S(2)}) copy-start(f32[2,2,256,128]{3,2,1,0:T(8,128)} %get-tuple-element.30.probe_ref) | copy-start | bytes 1572868
  100.8 25.6 %all-to-all-start.2 = ((f32[128,4,128]{2,1,0:T(4,128)}), f32[128,4,128]{2,1,0:T(4,128)S(1)}, u32[]{:S(2)}, u32[]{:S(2)}) async-start(f32[128,4,128]{2,1,0:T(4,128)} %bitcast.11), calls=%async_computation.2 | async-start | bytes 524288 | tf_op jit(solution)/shard_map/all_to_all | solution.py:259
  127.3 19.1 %all-to-all-start.3 = ((f32[128,4,128]{2,1,0:T(4,128)}), f32[128,4,128]{2,1,0:T(4,128)S(1)}, u32[]{:S(2)}, u32[]{:S(2)}) async-start(f32[128,4,128]{2,1,0:T(4,128)} %broadcast_in_dim.36), calls=%async_computation.3 | async-start | bytes 524288 | tf_op jit(solution)/shard_map/all_to_all | solution.py:259
  134.5 15.6 %collective-permute-start.17 = (f32[2,16,8,128]{3,2,1,0:T(8,128)S(1)}, f32[2,16,8,128]{3,2,1,0:T(8,128)S(1)}, u32[]{:S(2)}, u32[]{:S(2)}) collective-permute-start(f32[2,16,8,128]{3,2,1,0:T(8,128)S(1)} %get-tuple-element.39), channel_id=1, source_target_pairs={{0,224},{32,64},{64,32},{96,128},{128,96},{160,192},{192,160},{224... | collective-permute-start | bytes 393224 | tf_op jit(solution)/shard_map/ppermute | solution.py:42
  137.2 12.8 %collective-permute-start.16 = (f32[2,16,8,128]{3,2,1,0:T(8,128)S(1)}, f32[2,16,8,128]{3,2,1,0:T(8,128)S(1)}, u32[]{:S(2)}, u32[]{:S(2)}) collective-permute-start(f32[2,16,8,128]{3,2,1,0:T(8,128)S(1)} %get-tuple-element.40), channel_id=1, source_target_pairs={{0,32},{32,0},{64,96},{96,64},{128,160},{160,128},{192,224},{224,1... | collective-permute-start | bytes 393224 | tf_op jit(solution)/shard_map/ppermute | solution.py:42
  146.4 4.8 %collective-permute-start.19 = (f32[2,256,128]{2,1,0:T(8,128)S(1)}, f32[2,256,128]{2,1,0:T(8,128)S(1)}, u32[]{:S(2)}, u32[]{:S(2)}) collective-permute-start(f32[2,256,128]{2,1,0:T(8,128)S(1)} %bitcast.18), channel_id=1, source_target_pairs={{0,32},{32,0},{1,33},{33,1},{2,34},{34,2},{3,35},{35,3},{4,36},{36... | collective-permute-start | bytes 786440 | tf_op jit(solution)/shard_map/ppermute | solution.py:263

commit v6 on v5

--- a/solution.py
+++ b/solution.py
@@ -10,12 +10,12 @@
 
 ROW = ("y", "core")
 COL = ("z", "x")
-CHIPS = ("y", "z", "x")
+PLANE = ("y", "x")
 LANES = 128
 TILES = 16
 GROUP = 4
 F32 = jnp.float32
-VMEM_BYTES = 101 * 512 * 1024
+VMEM_BYTES = 102 * 512 * 1024
 
 
 def dft_tables(length):
@@ -152,16 +152,14 @@
 
 
 def gradient_kernel(first, *refs):
+    slots_ref, pattern_ref, left_ref, right_ref, start_ref, own_ref, side0_ref, side2_ref = refs[:8]
     if first:
-        slots_ref, pattern_ref, left_ref, right_ref, start_ref, own_ref, side0_ref, side2_ref = refs[:8]
-        col0_ref, col1_ref, col2_ref, keep, send, peak_ref, rows_ref = refs[8:15]
+        row0_ref, row1_ref, row2_ref, keep, send, peak_ref = refs[8:14]
     else:
-        slots_ref, pattern_ref, left_ref, right_ref, start_ref, own_ref, side0_ref, side2_ref = refs[:8]
         mine_ref, other_ref = refs[8:10]
-        col0_ref, col1_ref, col2_ref, keep, send, peak_ref, probe_ref = refs[10:17]
+        row0_ref, row1_ref, row2_ref, keep, send, peak_ref, probe_ref = refs[10:17]
     pattern, left, right, probe, ext, gobj, probe_sems, table_sems, pattern_sems = refs[-9:]
     row, row_places, row_end = place_of(ROW)
-    col, col_places, col_end = place_of(COL)
     count = slots_ref[2, 0]
     groups = pattern.shape[0] // GROUP
 
@@ -182,17 +180,9 @@
     for group in range(groups):
         pattern_copy(group).start()
 
-    strips = ((1, own_ref, False), (0, side0_ref, False), (2, side2_ref, row_end if first else col_end))
-    for i, ref, outside in strips:
-        if first:
-            for j in range(3):
-                bad = outside | col_end if j == 2 else outside
-                value = ref[j] if bad is False else jnp.where(bad, 0.0, ref[j])
-                ext[col_places[j], :, pl.ds(row_places[i] * TILES, TILES)] = value
-        else:
-            ext[col_places[i]] = ref[...] if outside is False else jnp.where(outside, 0.0, ref[...])
-    if first:
-        rows_ref[...] = ext[1]
+    for i, ref in ((1, own_ref), (0, side0_ref), (2, side2_ref)):
+        value = jnp.where(row_end, 0.0, ref[...]) if i == 2 else ref[...]
+        ext[:, :, pl.ds(row_places[i] * TILES, TILES)] = value
     gobj[...] = jnp.zeros_like(gobj)
     keep[...] = jnp.zeros_like(keep)
     send[...] = jnp.zeros_like(send)
@@ -217,8 +207,8 @@
 
     live_groups = (count + GROUP - 1) // GROUP
     lax.fori_loop(0, live_groups, visit, 0)
-    for j, ref in enumerate((col0_ref, col1_ref, col2_ref)):
-        ref[...] = gobj[col_places[j]]
+    for i, ref in enumerate((row0_ref, row1_ref, row2_ref)):
+        ref[...] = gobj[:, :, pl.ds(row_places[i] * TILES, TILES)]
     for group in range(1, groups):
 
         @pl.when(group >= live_groups)
@@ -231,15 +221,15 @@
     vmem = pl.BlockSpec(memory_space=pltpu.VMEM)
     smem = pl.BlockSpec(memory_space=pltpu.SMEM)
     hbm = pl.BlockSpec(memory_space=pltpu.HBM)
-    strip = jax.ShapeDtypeStruct((2, 3 * TILES, 8, LANES), F32)
+    strip = jax.ShapeDtypeStruct((3, 2, TILES, 8, LANES), F32)
     half = jax.ShapeDtypeStruct((2, size, LANES), F32)
     both = jax.ShapeDtypeStruct((2, 2, size, LANES), F32)
     ext = pltpu.VMEM((3, 2, 3 * TILES, 8, LANES), F32)
     return pl.pallas_call(
         functools.partial(gradient_kernel, first),
-        out_shape=(strip,) * 3 + (half, half, jax.ShapeDtypeStruct((8, LANES), F32), strip if first else both),
+        out_shape=(strip,) * 3 + (half, half, jax.ShapeDtypeStruct((8, LANES), F32)) + (() if first else (both,)),
         in_specs=[smem] + [hbm] * 4 + [vmem] * len(vmem_args),
-        out_specs=(vmem,) * 7,
+        out_specs=(vmem,) * (6 if first else 7),
         scratch_shapes=[
             pltpu.VMEM(patterns.shape, F32),
             pltpu.VMEM(tables[0].shape, jnp.bfloat16),
@@ -263,55 +253,59 @@
     return lax.ppermute(value, "core", [(0, 1), (1, 0)])
 
 
-def shares(keep, send):
+def plane_shares(keep, send):
     half = keep + core_swap(send)
-    return exchange(half.reshape(lax.axis_size(CHIPS), -1, LANES), CHIPS).sum(0)
+    return exchange(half.reshape(lax.axis_size(PLANE), -1, LANES), PLANE).sum(0)
+
+
+def depth_sum(share):
+    return exchange(jnp.broadcast_to(share, (lax.axis_size("z"),) + share.shape), "z").sum(0)
 
 
 def gathered(share, shape):
-    chips = lax.axis_size(CHIPS)
-    mine = exchange(jnp.broadcast_to(share, (chips,) + share.shape), CHIPS).reshape(shape)
-    return mine, core_swap(mine)
+    plane = lax.axis_size(PLANE)
+    return exchange(jnp.broadcast_to(share, (plane,) + share.shape), PLANE).reshape(shape)
 
 
 def side_sum(own, side0, side2, at_end):
     return own + side0 + jnp.where(at_end, 0.0, side2)
 
 
-def row_payloads(sums):
-    index = lax.axis_index(ROW)
+def column_payloads(sums):
+    index = lax.axis_index(COL)
     odd = lax.rem(index, 2) == 1
-    down_first = lax.rem(index // 2, 2) == 0
-    upper, lower = sums[:, : 2 * TILES], sums[:, TILES:]
-    above, below = sums[:, :TILES], sums[:, 2 * TILES :]
+    right_first = lax.rem(index // 2, 2) == 0
     return (
-        jnp.where(odd, upper, lower),
-        jnp.where(odd, lower, upper),
-        jnp.where(down_first, below, above),
-        jnp.where(down_first, above, below),
-    )
-
-
-def updated_strip(strip, sums, payloads, peak):
-    index, places, at_end = place_of(ROW)
-    last = lax.axis_size(ROW) - 1
+        jnp.where(odd, sums[:2], sums[1:]),
+        jnp.where(odd, sums[1:], sums[:2]),
+        jnp.where(right_first, sums[2], sums[0]),
+        jnp.where(right_first, sums[0], sums[2]),
+    )
+
+
+def column_transfers(payloads):
+    near0, near2, far_a, far_b = payloads
+    return paired(near0, COL, 0), paired(near2, COL, 2), paired_far(far_a, COL, 0), paired_far(far_b, COL, 1)
+
+
+def updated_strip(strip, sums, arrived, peak):
+    index, places, at_end = place_of(COL)
+    last = lax.axis_size(COL) - 1
     odd = lax.rem(index, 2) == 1
-    down_first = lax.rem(index // 2, 2) == 0
-    near0 = paired(payloads[0], ROW, 0)
-    near2 = jnp.where(at_end, 0.0, paired(payloads[1], ROW, 2))
-    far_a = paired_far(payloads[2], ROW, 0)
-    far_b = jnp.where((index < 2) | (index > last - 2), 0.0, paired_far(payloads[3], ROW, 1))
-    from_upper, from_lower = jnp.where(odd, near0, near2), jnp.where(odd, near2, near0)
-    grad_above = sums[:, :TILES] + from_upper[:, :TILES] + jnp.where(down_first, far_b, far_a)
-    grad = sums[:, TILES : 2 * TILES] + from_upper[:, TILES:] + from_lower[:, :TILES]
-    grad_below = sums[:, 2 * TILES :] + from_lower[:, TILES:] + jnp.where(down_first, far_a, far_b)
-    return jnp.concatenate(
+    right_first = lax.rem(index // 2, 2) == 0
+    near0, near2, far_a, far_b = arrived
+    near2 = jnp.where(at_end, 0.0, near2)
+    far_b = jnp.where((index < 2) | (index > last - 2), 0.0, far_b)
+    from_left, from_right = jnp.where(odd, near0, near2), jnp.where(odd, near2, near0)
+    grad_left = sums[0] + from_left[0] + jnp.where(right_first, far_b, far_a)
+    grad = sums[1] + from_left[1] + from_right[0]
+    grad_right = sums[2] + from_right[1] + jnp.where(right_first, far_a, far_b)
+    return jnp.stack(
         [
-            jnp.where(index == 0, 0.0, strip[:, :TILES] - grad_above / peak),
-            strip[:, TILES : 2 * TILES] - grad / peak,
-            jnp.where(index == last, 0.0, strip[:, 2 * TILES :] - grad_below / peak),
-        ],
-        axis=1,
+            jnp.where(index == 0, 0.0, strip[0] - grad_left / peak),
+            strip[1] - grad / peak,
+            jnp.where(index == last, 0.0, strip[2] - grad_right / peak),
+        ]
     )
 
 
@@ -350,28 +344,35 @@
     )
     tables = dft_tables(size)
     row_end, col_end = place_of(ROW)[2], place_of(COL)[2]
+    odd = lax.rem(lax.axis_index(COL), 2) == 1
 
     own = object_field.reshape(2, TILES, 8, LANES)
-    strip = jnp.stack([paired(own, COL, 0), own, paired(own, COL, 2)])
+    side0, side2 = paired(own, COL, 0), jnp.where(col_end, 0.0, paired(own, COL, 2))
+    strip = jnp.stack([jnp.where(odd, side0, side2), own, jnp.where(odd, side2, side0)])
     strips = (strip, paired(strip, ROW, 0), paired(strip, ROW, 2))
-    col0, col1, col2, keep, send, peak, strip = gradients(True, live_slots, patterns, tables, probe_field, *strips)
-    sums = side_sum(col1, paired(col0, COL, 0), paired(col2, COL, 2), col_end)
-    payloads = row_payloads(sums)
-    totals = gathered(after(shares(keep, send), *payloads), keep.shape)
-    strip = updated_strip(strip, sums, payloads, peak)
-    strips = (strip, paired(strip, COL, 0), paired(strip, COL, 2))
-
-    col0, col1, col2, keep, send, peak, probe = gradients(
+    row0, row1, row2, keep, send, peak = gradients(True, live_slots, patterns, tables, probe_field, *strips)
+    arrived = (paired(row0, ROW, 0), paired(row2, ROW, 2))
+    share, arrived = lax.optimization_barrier((plane_shares(keep, send), arrived))
+    sums = side_sum(row1, *arrived, row_end)
+    payloads = column_payloads(sums)
+    arrived = column_transfers(payloads)
+    share, arrived = lax.optimization_barrier((depth_sum(after(share, *payloads)), arrived))
+    strip = updated_strip(strip, sums, arrived, peak)
+    sides = (paired(strip, ROW, 0), paired(strip, ROW, 2))
+    mine, sides = lax.optimization_barrier((gathered(after(share, strip), keep.shape), sides))
+    totals = (mine, core_swap(mine))
+
+    strips = (strip,) + sides
+    row0, row1, row2, keep, send, peak, probe = gradients(
         False, live_slots, patterns, tables, probe_field, *strips, *totals
     )
-    sums = side_sum(col1, paired(col0, COL, 0), paired(col2, COL, 2), col_end)
-    odd = lax.rem(lax.axis_index(ROW), 2) == 1
-    above, grad, below = (sums[:, i * TILES : (i + 1) * TILES] for i in range(3))
-    payloads = (jnp.where(odd, above, below), jnp.where(odd, below, above))
-    totals = gathered(after(shares(keep, send), *payloads), keep.shape)
-    grad = side_sum(grad, paired(payloads[0], ROW, 0), paired(payloads[1], ROW, 2), row_end)
-    new_object = (strip[:, TILES : 2 * TILES] - grad / peak).reshape(object_field.shape)
-    return (new_object, last_probe(probe, *totals))
+    sums = side_sum(row1, paired(row0, ROW, 0), paired(row2, ROW, 2), row_end)
+    payloads = (jnp.where(odd, sums[0], sums[2]), jnp.where(odd, sums[2], sums[0]))
+    share = after(plane_shares(keep, send), *payloads)
+    grad = side_sum(sums[1], paired(payloads[0], COL, 0), paired(payloads[1], COL, 2), col_end)
+    new_object = (strip[1] - grad / peak).reshape(object_field.shape)
+    mine = gathered(after(depth_sum(share), new_object), keep.shape)
+    return (new_object, last_probe(probe, mine, core_swap(mine)))
 
 
 def solution(mesh):

time: 153 us -> 146 us (0.954)
  blocking collectives: 0 us -> 22.8 us
  starting transfers between devices: 71.7 us -> 51.8 us
  waiting for transfers between devices: 51.2 us -> 40.2 us
    all_to_all x0 -> x2, blocking collectives: none -> 22.8 us  [exchange(): return lax.all_to_all(value, axes, 0, 0, tiled=True)]
    all_to_all x4, starting transfers between devices: 35.3 us -> 17.1 us  [exchange(): return lax.all_to_all(value, axes, 0, 0, tiled=True)]
    all_to_all x4, waiting for transfers between devices: 38.1 us -> 21.8 us  [exchange(): return lax.all_to_all(value, axes, 0, 0, tiled=True)]
    ppermute x14, starting transfers between devices: 26.4 us -> 21.1 us  [paired(): return lax.ppermute(value, axes, pairs)]
    ppermute x2, waiting for transfers between devices: 0.01 us -> 4.32 us  [paired_far(): return lax.ppermute(value, axes, pairs)]
    ppermute x2, starting transfers between devices: 1.38 us -> 5.38 us  [paired_far(): return lax.ppermute(value, axes, pairs)]
  transfers between devices with their start and end apart: 24 -> 24, of which waited for: 11 -> 14; matrix products, arithmetic and copies ran while one was open for 3% -> 3% of each run, Pallas kernels for 0% -> 0%
where the time goes in v6:
time: 146 us; the launch traced here: 145 us
  starting transfers between devices  51.8 us (35%)
  waiting for transfers between devices  40.2 us (28%)
  blocking collectives  22.8 us (16%)
  Pallas kernels  22.7 us (16%)
  other arithmetic  3.64 us (2%)
  local copies, waits for them, and re-layouts  2.06 us (1%)
  between operations  1.51 us (1%)
    all_to_all x2, blocking collectives, exchange(): return lax.all_to_all(value, axes, 0, 0, tiled=True)  22.8 us
    all_to_all x4, waiting for transfers between devices, exchange(): return lax.all_to_all(value, axes, 0, 0, tiled=True)  21.8 us
    pallas_call x2, Pallas kernels, gradients(): pl.pallas_call(functools.partial(gradient_kernel, first), out_shape=(stri...  21.5 us
    ppermute x14, starting transfers between devices, paired(): return lax.ppermute(value, axes, pairs)  21.1 us
    all_to_all x4, starting transfers between devices, exchange(): return lax.all_to_all(value, axes, 0, 0, tiled=True)  17.1 us
    ppermute x14, waiting for transfers between devices, paired(): return lax.ppermute(value, axes, pairs)  9.47 us
    ppermute x4, starting transfers between devices, core_swap(): return lax.ppermute(value, 'core', [(0, 1), (1, 0)])  8.15 us
    ppermute x2, starting transfers between devices, paired_far(): return lax.ppermute(value, axes, pairs)  5.38 us
  transfers between devices with their start and end apart: 24, of which 14 were waited for; matrix products, arithmetic and copies ran while one was open for 3% of the time, Pallas kernels for 0%

profile of v6, /device:TPU:1, one launch (start us, length us, event | category | flops | bytes accessed | tf_op | source)
XLA Modules:
  0.0 144.6 jit_solution(12070057003467559560)
XLA Ops:
  0.6 8.7 %collective-permute-start.1 = (f32[2,16,8,128]{3,2,1,0:T(8,128)}, f32[2,16,8,128]{3,2,1,0:T(8,128)S(1)}, u32[]{:S(2)}, u32[]{:S(2)}) collective-permute-start(f32[2,16,8,128]{3,2,1,0:T(8,128)} %bitcast.80), channel_id=1, source_target_pairs={{0,31},{1,2},{2,1},{3,4},{4,3},{5,6},{6,5},{7,8},{8,7},{9,10},{10,... | collective-permute-start | bytes 393224 | tf_op jit(solution)/shard_map/ppermute | solution.py:42
  9.3 3.4 %collective-permute-done.1 = f32[2,16,8,128]{3,2,1,0:T(8,128)S(1)} collective-permute-done((f32[2,16,8,128]{3,2,1,0:T(8,128)}, f32[2,16,8,128]{3,2,1,0:T(8,128)S(1)}, u32[]{:S(2)}, u32[]{:S(2)}) %collective-permute-start.1) | collective-permute-done | bytes 131104 | tf_op jit(solution)/shard_map/ppermute | solution.py:42
  13.6 0.9 pad_maximum_fusion.refs_5_
  14.5 3.1 %collective-permute-start.3 = (f32[3,2,16,8,128]{4,3,2,1,0:T(8,128)S(1)}, f32[3,2,16,8,128]{4,3,2,1,0:T(8,128)S(1)}, u32[]{:S(2)}, u32[]{:S(2)}) collective-permute-start(f32[3,2,16,8,128]{4,3,2,1,0:T(8,128)S(1)} %pad_maximum_fusion.refs_5_), channel_id=1, source_target_pairs={{0,224},{32,64},{64,32},{96,128},{128,96},{160,192},{192,160},{224... | collective-permute-start | bytes 1179656 | tf_op jit(solution)/shard_map/ppermute | solution.py:42
  19.1 4.3 %collective-permute-done.3.refs_7_ = f32[3,2,16,8,128]{4,3,2,1,0:T(8,128)S(1)} collective-permute-done((f32[3,2,16,8,128]{4,3,2,1,0:T(8,128)S(1)}, f32[3,2,16,8,128]{4,3,2,1,0:T(8,128)S(1)}, u32[]{:S(2)}, u32[]{:S(2)}) %collective-permute-start.3) | collective-permute-done | bytes 393248 | tf_op jit(solution)/shard_map/ppermute | solution.py:42
  23.4 10.1 %shard_map.86 = (f32[3,2,16,8,128]{4,3,2,1,0:T(8,128)S(1)}, f32[3,2,16,8,128]{4,3,2,1,0:T(8,128)S(1)}, f32[3,2,16,8,128]{4,3,2,1,0:T(8,128)S(1)}, f32[2,256,128]...) custom-call(s32[3,8]{1,0:T(4,128)S(1)} %concatenate.3.refs_0_, f32[8,256,256]{2,1,0:T(8,128)} %bitcast.78, ...), custom_call_target="tpu_custom_call" | custom-call | tf_op jit(solution)/shard_map/pallas_call | solution.py:228
  33.6 1.5 %collective-permute-start.4 = (f32[2,256,128]{2,1,0:T(8,128)S(1)}, f32[2,256,128]{2,1,0:T(8,128)S(1)}, u32[]{:S(2)}, u32[]{:S(2)}) collective-permute-start(f32[2,256,128]{2,1,0:T(8,128)S(1)} %get-tuple-element.32), channel_id=1, source_target_pairs={{0,32},{32,0},{1,33},{33,1},{2,34},{34,2},{3,35},{35,3},{4,36},{36... | collective-permute-start | bytes 786440 | tf_op jit(solution)/shard_map/ppermute | solution.py:253
  35.2 1.1 collective-permute-done.4
  37.0 3.5 %all-to-all-start = ((f32[16,32,128]{2,1,0:T(8,128)}), f32[16,32,128]{2,1,0:T(8,128)S(1)}, u32[]{:S(2)}, u32[]{:S(2)}) async-start(f32[16,32,128]{2,1,0:T(8,128)} %bitcast.8), calls=%async_computation | async-start | bytes 524288 | tf_op jit(solution)/shard_map/all_to_all | solution.py:249
  40.6 7.8 %all-to-all-done = f32[16,32,128]{2,1,0:T(8,128)S(1)} async-done(((f32[16,32,128]{2,1,0:T(8,128)}), f32[16,32,128]{2,1,0:T(8,128)S(1)}, u32[]{:S(2)}, u32[]{:S(2)}) %all-to-all-start) | async-done | bytes 262176 | tf_op jit(solution)/shard_map/all_to_all | solution.py:249
  48.6 3.0 %collective-permute-start.8 = (f32[2,2,16,8,128]{4,3,2,1,0:T(8,128)S(1)}, f32[2,2,16,8,128]{4,3,2,1,0:T(8,128)S(1)}, u32[]{:S(2)}, u32[]{:S(2)}) collective-permute-start(f32[2,2,16,8,128]{4,3,2,1,0:T(8,128)S(1)} %get-tuple-element.66), channel_id=1, source_target_pairs={{0,31},{1,2},{2,1},{3,4},{4,3},{5,6},{6,5},{7,8},{8,7},{9,10},{10,... | collective-permute-start | bytes 786440 | tf_op jit(solution)/shard_map/ppermute | solution.py:42
  52.3 3.4 %all-to-all-start.1 = ((f32[8,32,128]{2,1,0:T(8,128)}), f32[8,32,128]{2,1,0:T(8,128)S(1)}, u32[]{:S(2)}, u32[]{:S(2)}) async-start(f32[8,32,128]{2,1,0:T(8,128)} %broadcast_in_dim.41), calls=%async_computation.1 | async-start | bytes 262144 | tf_op jit(solution)/shard_map/all_to_all | solution.py:249
  55.7 5.4 %collective-permute-start.10 = (f32[2,16,8,128]{3,2,1,0:T(8,128)S(1)}, f32[2,16,8,128]{3,2,1,0:T(8,128)S(1)}, u32[]{:S(2)}, u32[]{:S(2)}) collective-permute-start(f32[2,16,8,128]{3,2,1,0:T(8,128)S(1)} %get-tuple-element.64), channel_id=1, source_target_pairs={{0,30},{1,31},{2,4},{3,5},{4,2},{5,3},{6,8},{7,9},{8,6},{9,7},{10,... | collective-permute-start | bytes 393224 | tf_op jit(solution)/shard_map/ppermute | solution.py:48
  61.0 2.6 %all-to-all-done.1 = f32[8,32,128]{2,1,0:T(8,128)S(1)} async-done(((f32[8,32,128]{2,1,0:T(8,128)}), f32[8,32,128]{2,1,0:T(8,128)S(1)}, u32[]{:S(2)}, u32[]{:S(2)}) %all-to-all-start.1) | async-done | bytes 131104 | tf_op jit(solution)/shard_map/all_to_all | solution.py:249
  63.6 1.2 collective-permute-done.10
  64.8 3.1 %collective-permute-done.9 = f32[2,16,8,128]{3,2,1,0:T(8,128)S(1)} collective-permute-done((f32[2,16,8,128]{3,2,1,0:T(8,128)S(1)}, f32[2,16,8,128]{3,2,1,0:T(8,128)S(1)}, u32[]{:S(2)}, u32[]{:S(2)}) %collective-permute-start.9) | collective-permute-done | bytes 131104 | tf_op jit(solution)/shard_map/ppermute | solution.py:48
  68.2 2.0 %collective-permute-start.12 = (f32[3,2,16,8,128]{4,3,2,1,0:T(8,128)S(1)}, f32[3,2,16,8,128]{4,3,2,1,0:T(8,128)S(1)}, u32[]{:S(2)}, u32[]{:S(2)}) collective-permute-start(f32[3,2,16,8,128]{4,3,2,1,0:T(8,128)S(1)} %pad_maximum_fusion.1.refs_5_), channel_id=1, source_target_pairs={{0,224},{32,64},{64,32},{96,128},{128,96},{160,192},{192,160},{224... | collective-permute-start | bytes 1179656 | tf_op jit(solution)/shard_map/ppermute | solution.py:42
  70.6 11.8 %all_to_all.30 = f32[16,32,128]{2,1,0:T(8,128)S(1)} all-to-all(f32[16,32,128]{2,1,0:T(8,128)S(1)} %broadcast_in_dim.43), channel_id=1, replica_groups=mesh['y'=4,'core'=2,'z'=8,'x'=4] {'y','x'}, dimensions={0} | all-to-all | bytes 524288 | tf_op jit(solution)/shard_map/all_to_all | solution.py:249
  82.5 1.8 %collective-permute-start.13 = (f32[2,256,128]{2,1,0:T(8,128)S(1)}, f32[2,256,128]{2,1,0:T(8,128)S(1)}, u32[]{:S(2)}, u32[]{:S(2)}) collective-permute-start(f32[2,256,128]{2,1,0:T(8,128)S(1)} %bitcast.74), channel_id=1, source_target_pairs={{0,32},{32,0},{1,33},{33,1},{2,34},{34,2},{3,35},{35,3},{4,36},{36... | collective-permute-start | bytes 786440 | tf_op jit(solution)/shard_map/ppermute | solution.py:253
  84.2 1.2 collective-permute-done.13.refs_9_
  85.4 11.4 %shard_map.87 = (f32[3,2,16,8,128]{4,3,2,1,0:T(8,128)S(1)}, f32[3,2,16,8,128]{4,3,2,1,0:T(8,128)S(1)}, f32[3,2,16,8,128]{4,3,2,1,0:T(8,128)S(1)}, f32[2,256,128]...) custom-call(s32[3,8]{1,0:T(4,128)S(1)} %concatenate.3.refs_0_, ...), custom_call_target="tpu_custom_call" | custom-call | tf_op jit(solution)/shard_map/pallas_call | solution.py:228
  97.2 0.9 collective-permute-start.18
  98.1 1.2 collective-permute-done.18
  100.0 3.8 %all-to-all-start.3 = ((f32[16,32,128]{2,1,0:T(8,128)}), f32[16,32,128]{2,1,0:T(8,128)S(1)}, u32[]{:S(2)}, u32[]{:S(2)}) async-start(f32[16,32,128]{2,1,0:T(8,128)} %bitcast.21), calls=%async_computation.3 | async-start | bytes 524288 | tf_op jit(solution)/shard_map/all_to_all | solution.py:249
  104.8 3.3 %collective-permute-start.17 = (f32[2,16,8,128]{3,2,1,0:T(8,128)S(1)}, f32[2,16,8,128]{3,2,1,0:T(8,128)S(1)}, u32[]{:S(2)}, u32[]{:S(2)}) collective-permute-start(f32[2,16,8,128]{3,2,1,0:T(8,128)S(1)} %get-tuple-element.62), channel_id=1, source_target_pairs={{0,31},{1,2},{2,1},{3,4},{4,3},{5,6},{6,5},{7,8},{8,7},{9,10},{10,... | collective-permute-start | bytes 393224 | tf_op jit(solution)/shard_map/ppermute | solution.py:42
  108.0 4.1 %all-to-all-done.3 = f32[16,32,128]{2,1,0:T(8,128)S(1)} async-done(((f32[16,32,128]{2,1,0:T(8,128)}), f32[16,32,128]{2,1,0:T(8,128)S(1)}, u32[]{:S(2)}, u32[]{:S(2)}) %all-to-all-start.3) | async-done | bytes 262176 | tf_op jit(solution)/shard_map/all_to_all | solution.py:249
  112.9 6.5 %all-to-all-start.4 = ((f32[8,32,128]{2,1,0:T(8,128)}), f32[8,32,128]{2,1,0:T(8,128)S(1)}, u32[]{:S(2)}, u32[]{:S(2)}) async-start(f32[8,32,128]{2,1,0:T(8,128)} %broadcast_in_dim.44), calls=%async_computation.4 | async-start | bytes 262144 | tf_op jit(solution)/shard_map/all_to_all | solution.py:249
  120.0 7.3 %all-to-all-done.4 = f32[8,32,128]{2,1,0:T(8,128)S(1)} async-done(((f32[8,32,128]{2,1,0:T(8,128)}), f32[8,32,128]{2,1,0:T(8,128)S(1)}, u32[]{:S(2)}, u32[]{:S(2)}) %all-to-all-start.4) | async-done | bytes 131104 | tf_op jit(solution)/shard_map/all_to_all | solution.py:249
  127.4 10.9 %all_to_all.31 = f32[16,32,128]{2,1,0:T(8,128)S(1)} all-to-all(f32[16,32,128]{2,1,0:T(8,128)S(1)} %broadcast_in_dim.45), channel_id=1, replica_groups=mesh['y'=4,'core'=2,'z'=8,'x'=4] {'y','x'}, dimensions={0} | all-to-all | bytes 524288 | tf_op jit(solution)/shard_map/all_to_all | solution.py:249
  138.3 3.9 %collective-permute-start.19 = (f32[2,256,128]{2,1,0:T(8,128)S(1)}, f32[2,256,128]{2,1,0:T(8,128)S(1)}, u32[]{:S(2)}, u32[]{:S(2)}) collective-permute-start(f32[2,256,128]{2,1,0:T(8,128)S(1)} %bitcast.76), channel_id=1, source_target_pairs={{0,32},{32,0},{1,33},{33,1},{2,34},{34,2},{3,35},{35,3},{4,36},{36... | collective-permute-start | bytes 786440 | tf_op jit(solution)/shard_map/ppermute | solution.py:253
  142.3 1.2 collective-permute-done.19.other_ref
  143.4 1.2 shard_map.88
  (50 shorter events, 7.5 us)
Async XLA Ops:
  0.6 12.1 %collective-permute-start.1 = (f32[2,16,8,128]{3,2,1,0:T(8,128)}, f32[2,16,8,128]{3,2,1,0:T(8,128)S(1)}, u32[]{:S(2)}, u32[]{:S(2)}) collective-permute-start(f32[2,16,8,128]{3,2,1,0:T(8,128)} %bitcast.80), channel_id=1, source_target_pairs={{0,31},{1,2},{2,1},{3,4},{4,3},{5,6},{6,5},{7,8},{8,7},{9,10},{10,... | collective-permute-start | bytes 393224 | tf_op jit(solution)/shard_map/ppermute | solution.py:42
  9.3 4.3 %collective-permute-start = (f32[2,16,8,128]{3,2,1,0:T(8,128)}, f32[2,16,8,128]{3,2,1,0:T(8,128)S(1)}, u32[]{:S(2)}, u32[]{:S(2)}) collective-permute-start(f32[2,16,8,128]{3,2,1,0:T(8,128)} %bitcast.81), channel_id=1, source_target_pairs={{0,1},{1,0},{2,3},{3,2},{4,5},{5,4},{6,7},{7,6},{8,9},{9,8},{10,11... | collective-permute-start | bytes 393224 | tf_op jit(solution)/shard_map/ppermute | solution.py:42
  14.5 8.9 %collective-permute-start.3 = (f32[3,2,16,8,128]{4,3,2,1,0:T(8,128)S(1)}, f32[3,2,16,8,128]{4,3,2,1,0:T(8,128)S(1)}, u32[]{:S(2)}, u32[]{:S(2)}) collective-permute-start(f32[3,2,16,8,128]{4,3,2,1,0:T(8,128)S(1)} %pad_maximum_fusion.refs_5_), channel_id=1, source_target_pairs={{0,224},{32,64},{64,32},{96,128},{128,96},{160,192},{192,160},{224... | collective-permute-start | bytes 1179656 | tf_op jit(solution)/shard_map/ppermute | solution.py:42
  17.7 5.8 %collective-permute-start.2 = (f32[3,2,16,8,128]{4,3,2,1,0:T(8,128)S(1)}, f32[3,2,16,8,128]{4,3,2,1,0:T(8,128)S(1)}, u32[]{:S(2)}, u32[]{:S(2)}) collective-permute-start(f32[3,2,16,8,128]{4,3,2,1,0:T(8,128)S(1)} %pad_maximum_fusion.refs_5_), channel_id=1, source_target_pairs={{0,32},{32,0},{64,96},{96,64},{128,160},{160,128},{192,224},{224,1... | collective-permute-start | bytes 1179656 | tf_op jit(solution)/shard_map/ppermute | solution.py:42
  33.6 2.7 %collective-permute-start.4 = (f32[2,256,128]{2,1,0:T(8,128)S(1)}, f32[2,256,128]{2,1,0:T(8,128)S(1)}, u32[]{:S(2)}, u32[]{:S(2)}) collective-permute-start(f32[2,256,128]{2,1,0:T(8,128)S(1)} %get-tuple-element.32), channel_id=1, source_target_pairs={{0,32},{32,0},{1,33},{33,1},{2,34},{34,2},{3,35},{35,3},{4,36},{36... | collective-permute-start | bytes 786440 | tf_op jit(solution)/shard_map/ppermute | solution.py:253
  35.1 13.4 %collective-permute-start.5 = (f32[3,2,16,8,128]{4,3,2,1,0:T(8,128)S(1)}, f32[3,2,16,8,128]{4,3,2,1,0:T(8,128)S(1)}, u32[]{:S(2)}, u32[]{:S(2)}) collective-permute-start(f32[3,2,16,8,128]{4,3,2,1,0:T(8,128)S(1)} %get-tuple-element.33), channel_id=1, source_target_pairs={{0,32},{32,0},{64,96},{96,64},{128,160},{160,128},{192,224},{224,1... | collective-permute-start | bytes 1179656 | tf_op jit(solution)/shard_map/ppermute | solution.py:42
  35.2 13.3 %collective-permute-start.6 = (f32[3,2,16,8,128]{4,3,2,1,0:T(8,128)S(1)}, f32[3,2,16,8,128]{4,3,2,1,0:T(8,128)S(1)}, u32[]{:S(2)}, u32[]{:S(2)}) collective-permute-start(f32[3,2,16,8,128]{4,3,2,1,0:T(8,128)S(1)} %get-tuple-element.34), channel_id=1, source_target_pairs={{0,224},{32,64},{64,32},{96,128},{128,96},{160,192},{192,160},{224... | collective-permute-start | bytes 1179656 | tf_op jit(solution)/shard_map/ppermute | solution.py:42
  37.0 11.4 %all-to-all-start = ((f32[16,32,128]{2,1,0:T(8,128)}), f32[16,32,128]{2,1,0:T(8,128)S(1)}, u32[]{:S(2)}, u32[]{:S(2)}) async-start(f32[16,32,128]{2,1,0:T(8,128)} %bitcast.8), calls=%async_computation | async-start | bytes 524288 | tf_op jit(solution)/shard_map/all_to_all | solution.py:249
  48.5 19.5 %copy-start.1 = (f32[2,128,128]{2,1,0:T(8,128)S(1)}, f32[2,128,128]{2,1,0:T(8,128)}, u32[]{:S(2)}) copy-start(f32[2,128,128]{2,1,0:T(8,128)} %param.7) | copy-start | bytes 393220
  48.6 19.3 %collective-permute-start.8 = (f32[2,2,16,8,128]{4,3,2,1,0:T(8,128)S(1)}, f32[2,2,16,8,128]{4,3,2,1,0:T(8,128)S(1)}, u32[]{:S(2)}, u32[]{:S(2)}) collective-permute-start(f32[2,2,16,8,128]{4,3,2,1,0:T(8,128)S(1)} %get-tuple-element.66), channel_id=1, source_target_pairs={{0,31},{1,2},{2,1},{3,4},{4,3},{5,6},{6,5},{7,8},{8,7},{9,10},{10,... | collective-permute-start | bytes 786440 | tf_op jit(solution)/shard_map/ppermute | solution.py:42
  51.6 16.4 %collective-permute-start.7 = (f32[2,2,16,8,128]{4,3,2,1,0:T(8,128)S(1)}, f32[2,2,16,8,128]{4,3,2,1,0:T(8,128)S(1)}, u32[]{:S(2)}, u32[]{:S(2)}) collective-permute-start(f32[2,2,16,8,128]{4,3,2,1,0:T(8,128)S(1)} %get-tuple-element.67), channel_id=1, source_target_pairs={{0,1},{1,0},{2,3},{3,2},{4,5},{5,4},{6,7},{7,6},{8,9},{9,8},{10,11... | collective-permute-start | bytes 786440 | tf_op jit(solution)/shard_map/ppermute | solution.py:42
  52.3 11.3 %all-to-all-start.1 = ((f32[8,32,128]{2,1,0:T(8,128)}), f32[8,32,128]{2,1,0:T(8,128)S(1)}, u32[]{:S(2)}, u32[]{:S(2)}) async-start(f32[8,32,128]{2,1,0:T(8,128)} %broadcast_in_dim.41), calls=%async_computation.1 | async-start | bytes 262144 | tf_op jit(solution)/shard_map/all_to_all | solution.py:249
  55.7 9.2 %collective-permute-start.10 = (f32[2,16,8,128]{3,2,1,0:T(8,128)S(1)}, f32[2,16,8,128]{3,2,1,0:T(8,128)S(1)}, u32[]{:S(2)}, u32[]{:S(2)}) collective-permute-start(f32[2,16,8,128]{3,2,1,0:T(8,128)S(1)} %get-tuple-element.64), channel_id=1, source_target_pairs={{0,30},{1,31},{2,4},{3,5},{4,2},{5,3},{6,8},{7,9},{8,6},{9,7},{10,... | collective-permute-start | bytes 393224 | tf_op jit(solution)/shard_map/ppermute | solution.py:48
  61.0 6.9 %collective-permute-start.9 = (f32[2,16,8,128]{3,2,1,0:T(8,128)S(1)}, f32[2,16,8,128]{3,2,1,0:T(8,128)S(1)}, u32[]{:S(2)}, u32[]{:S(2)}) collective-permute-start(f32[2,16,8,128]{3,2,1,0:T(8,128)S(1)} %get-tuple-element.65), channel_id=1, source_target_pairs={{0,2},{1,3},{2,0},{3,1},{4,6},{5,7},{6,4},{7,5},{8,10},{9,11},{10,... | collective-permute-start | bytes 393224 | tf_op jit(solution)/shard_map/ppermute | solution.py:48
  68.2 14.3 %collective-permute-start.12 = (f32[3,2,16,8,128]{4,3,2,1,0:T(8,128)S(1)}, f32[3,2,16,8,128]{4,3,2,1,0:T(8,128)S(1)}, u32[]{:S(2)}, u32[]{:S(2)}) collective-permute-start(f32[3,2,16,8,128]{4,3,2,1,0:T(8,128)S(1)} %pad_maximum_fusion.1.refs_5_), channel_id=1, source_target_pairs={{0,224},{32,64},{64,32},{96,128},{128,96},{160,192},{192,160},{224... | collective-permute-start | bytes 1179656 | tf_op jit(solution)/shard_map/ppermute | solution.py:42
  70.2 12.3 %collective-permute-start.11 = (f32[3,2,16,8,128]{4,3,2,1,0:T(8,128)S(1)}, f32[3,2,16,8,128]{4,3,2,1,0:T(8,128)S(1)}, u32[]{:S(2)}, u32[]{:S(2)}) collective-permute-start(f32[3,2,16,8,128]{4,3,2,1,0:T(8,128)S(1)} %pad_maximum_fusion.1.refs_5_), channel_id=1, source_target_pairs={{0,32},{32,0},{64,96},{96,64},{128,160},{160,128},{192,224},{224,1... | collective-permute-start | bytes 1179656 | tf_op jit(solution)/shard_map/ppermute | solution.py:42
  82.5 2.9 %copy-start.2 = (f32[3,2,16,8,128]{4,3,2,1,0:T(8,128)}, f32[3,2,16,8,128]{4,3,2,1,0:T(8,128)S(1)}, u32[]{:S(2)}) copy-start(f32[3,2,16,8,128]{4,3,2,1,0:T(8,128)S(1)} %collective-permute-done.12.refs_7_) | copy-start | bytes 1179652
  82.5 2.9 %collective-permute-start.13 = (f32[2,256,128]{2,1,0:T(8,128)S(1)}, f32[2,256,128]{2,1,0:T(8,128)S(1)}, u32[]{:S(2)}, u32[]{:S(2)}) collective-permute-start(f32[2,256,128]{2,1,0:T(8,128)S(1)} %bitcast.74), channel_id=1, source_target_pairs={{0,32},{32,0},{1,33},{33,1},{2,34},{34,2},{3,35},{35,3},{4,36},{36... | collective-permute-start | bytes 786440 | tf_op jit(solution)/shard_map/ppermute | solution.py:253
  96.8 7.0 %collective-permute-start.14 = (f32[3,2,16,8,128]{4,3,2,1,0:T(8,128)S(1)}, f32[3,2,16,8,128]{4,3,2,1,0:T(8,128)S(1)}, u32[]{:S(2)}, u32[]{:S(2)}) collective-permute-start(f32[3,2,16,8,128]{4,3,2,1,0:T(8,128)S(1)} %get-tuple-element.50), channel_id=1, source_target_pairs={{0,32},{32,0},{64,96},{96,64},{128,160},{160,128},{192,224},{224,1... | collective-permute-start | bytes 1179656 | tf_op jit(solution)/shard_map/ppermute | solution.py:42
  97.2 7.5 %collective-permute-start.15 = (f32[3,2,16,8,128]{4,3,2,1,0:T(8,128)S(1)}, f32[3,2,16,8,128]{4,3,2,1,0:T(8,128)S(1)}, u32[]{:S(2)}, u32[]{:S(2)}) collective-permute-start(f32[3,2,16,8,128]{4,3,2,1,0:T(8,128)S(1)} %get-tuple-element.51), channel_id=1, source_target_pairs={{0,224},{32,64},{64,32},{96,128},{128,96},{160,192},{192,160},{224... | collective-permute-start | bytes 1179656 | tf_op jit(solution)/shard_map/ppermute | solution.py:42
  97.2 2.1 %collective-permute-start.18 = (f32[2,256,128]{2,1,0:T(8,128)S(1)}, f32[2,256,128]{2,1,0:T(8,128)S(1)}, u32[]{:S(2)}, u32[]{:S(2)}) collective-permute-start(f32[2,256,128]{2,1,0:T(8,128)S(1)} %get-tuple-element.55), channel_id=1, source_target_pairs={{0,32},{32,0},{1,33},{33,1},{2,34},{34,2},{3,35},{35,3},{4,36},{36... | collective-permute-start | bytes 786440 | tf_op jit(solution)/shard_map/ppermute | solution.py:253
  100.0 12.2 %all-to-all-start.3 = ((f32[16,32,128]{2,1,0:T(8,128)}), f32[16,32,128]{2,1,0:T(8,128)S(1)}, u32[]{:S(2)}, u32[]{:S(2)}) async-start(f32[16,32,128]{2,1,0:T(8,128)} %bitcast.21), calls=%async_computation.3 | async-start | bytes 524288 | tf_op jit(solution)/shard_map/all_to_all | solution.py:249
  104.7 38.8 %copy-start = (f32[2,2,256,128]{3,2,1,0:T(8,128)S(1)}, f32[2,2,256,128]{3,2,1,0:T(8,128)}, u32[]{:S(2)}) copy-start(f32[2,2,256,128]{3,2,1,0:T(8,128)} %get-tuple-element.53.probe_ref) | copy-start | bytes 1572868
  104.8 14.5 %collective-permute-start.17 = (f32[2,16,8,128]{3,2,1,0:T(8,128)S(1)}, f32[2,16,8,128]{3,2,1,0:T(8,128)S(1)}, u32[]{:S(2)}, u32[]{:S(2)}) collective-permute-start(f32[2,16,8,128]{3,2,1,0:T(8,128)S(1)} %get-tuple-element.62), channel_id=1, source_target_pairs={{0,31},{1,2},{2,1},{3,4},{4,3},{5,6},{6,5},{7,8},{8,7},{9,10},{10,... | collective-permute-start | bytes 393224 | tf_op jit(solution)/shard_map/ppermute | solution.py:42
  108.0 11.3 %collective-permute-start.16 = (f32[2,16,8,128]{3,2,1,0:T(8,128)S(1)}, f32[2,16,8,128]{3,2,1,0:T(8,128)S(1)}, u32[]{:S(2)}, u32[]{:S(2)}) collective-permute-start(f32[2,16,8,128]{3,2,1,0:T(8,128)S(1)} %get-tuple-element.63), channel_id=1, source_target_pairs={{0,1},{1,0},{2,3},{3,2},{4,5},{5,4},{6,7},{7,6},{8,9},{9,8},{10,11... | collective-permute-start | bytes 393224 | tf_op jit(solution)/shard_map/ppermute | solution.py:42
  112.9 14.5 %all-to-all-start.4 = ((f32[8,32,128]{2,1,0:T(8,128)}), f32[8,32,128]{2,1,0:T(8,128)S(1)}, u32[]{:S(2)}, u32[]{:S(2)}) async-start(f32[8,32,128]{2,1,0:T(8,128)} %broadcast_in_dim.44), calls=%async_computation.4 | async-start | bytes 262144 | tf_op jit(solution)/shard_map/all_to_all | solution.py:249
  138.3 5.1 %collective-permute-start.19 = (f32[2,256,128]{2,1,0:T(8,128)S(1)}, f32[2,256,128]{2,1,0:T(8,128)S(1)}, u32[]{:S(2)}, u32[]{:S(2)}) collective-permute-start(f32[2,256,128]{2,1,0:T(8,128)S(1)} %bitcast.76), channel_id=1, source_target_pairs={{0,32},{32,0},{1,33},{33,1},{2,34},{34,2},{3,35},{35,3},{4,36},{36... | collective-permute-start | bytes 786440 | tf_op jit(solution)/shard_map/ppermute | solution.py:253

commit v7 on v6

--- a/solution.py
+++ b/solution.py
@@ -50,25 +50,6 @@
 
 def dot(a, b):
     return jnp.dot(a, b, preferred_element_type=F32)
-
-
-def transform_pair(reals, imags, left, right):
-    size = reals[0].shape[0]
-    columns = [jnp.concatenate(pair, axis=0).astype(jnp.bfloat16) for pair in zip(reals, imags)]
-    mid = dot(left, jnp.concatenate(columns, axis=1)).astype(jnp.bfloat16)
-    rows = [
-        jnp.concatenate([mid[:size, i * size : (i + 1) * size], mid[size:, i * size : (i + 1) * size]], axis=1)
-        for i in range(len(reals))
-    ]
-    out = dot(jnp.concatenate(rows, axis=0), right)
-    return [(out[i * size : (i + 1) * size, :size], out[i * size : (i + 1) * size, size:]) for i in range(len(reals))]
-
-
-def transform(reals, imags, left, right):
-    out = []
-    for i in range(0, len(reals), 2):
-        out += transform_pair(reals[i : i + 2], imags[i : i + 2], left, right)
-    return [pair[0] for pair in out], [pair[1] for pair in out]
 
 
 def updated_probe(probe, total):
@@ -123,32 +104,66 @@
             keep[v] += jnp.where(first, real[:, lanes], imag[:, lanes])
             send[v] += jnp.where(first, imag[:, lanes], real[:, lanes])
 
-    at = [corner(slot) for slot in slots]
-    win_real = [window(0, a) for a in at]
-    win_imag = [window(1, a) for a in at]
     probe_real = jnp.concatenate([probe[0, 0], probe[0, 1]], axis=1)
     probe_imag = jnp.concatenate([probe[1, 0], probe[1, 1]], axis=1)
-    far_real, far_imag = transform(
-        [probe_real * a - probe_imag * b for a, b in zip(win_real, win_imag)],
-        [probe_real * b + probe_imag * a for a, b in zip(win_real, win_imag)],
-        left[...],
-        right[...],
-    )
+    lanes2 = range(2)
+
+    def windows(pair):
+        at = [corner(slot) for slot in pair]
+        return at, [window(0, a) for a in at], [window(1, a) for a in at]
+
+    def exits(state):
+        at, reals, imags = state
+        return [
+            jnp.concatenate([probe_real * a - probe_imag * b, probe_real * b + probe_imag * a], axis=0).astype(jnp.bfloat16)
+            for a, b in zip(reals, imags)
+        ]
+
+    def left_side(columns, table):
+        mid = dot(table[...], jnp.concatenate(columns, axis=1)).astype(jnp.bfloat16)
+        return jnp.concatenate(
+            [
+                jnp.concatenate([mid[:size, i * size : (i + 1) * size], mid[size:, i * size : (i + 1) * size]], axis=1)
+                for i in lanes2
+            ],
+            axis=0,
+        )
+
+    def right_side(rows, table):
+        out = dot(rows, table[...])
+        return [(out[i * size : (i + 1) * size, :size], out[i * size : (i + 1) * size, size:]) for i in lanes2]
+
+    def misfits(far, pair):
+        out = []
+        for (a, b), slot in zip(far, pair):
+            m = jnp.where(slot < count, a * a + b * b - pattern[slot], 0.0)
+            out.append(jnp.concatenate([m * a, m * b], axis=0).astype(jnp.bfloat16))
+        return out
+
+    def add(state, back):
+        both = list(zip(state[1], state[2], back))
+        add_probe(sum(a * c + b * d for a, b, (c, d) in both), sum(a * d - b * c for a, b, (c, d) in both))
+        for a, (c, d) in zip(state[0], back):
+            add_object(0, probe_real * c + probe_imag * d, a)
+            add_object(1, probe_real * d - probe_imag * c, a)
+
+    pairs = slots[:2], slots[2:]
+    state_a = windows(pairs[0])
+    mid_a = left_side(exits(state_a), left)
+    state_b = windows(pairs[1])
+    exit_b = exits(state_b)
+    far_a = right_side(mid_a, right)
+    mid_b = left_side(exit_b, left)
     pattern_copy(group).wait()
-    misfit = [
-        jnp.where(slot < count, a * a + b * b - pattern[slot], 0.0) for a, b, slot in zip(far_real, far_imag, slots)
-    ]
-    back_real, back_imag = transform(
-        [m * a for m, a in zip(misfit, far_real)],
-        [m * b for m, b in zip(misfit, far_imag)],
-        right[...],
-        left[...],
-    )
-    both = list(zip(win_real, win_imag, back_real, back_imag))
-    add_probe(sum(a * c + b * d for a, b, c, d in both), sum(a * d - b * c for a, b, c, d in both))
-    for i in range(GROUP):
-        add_object(0, probe_real * back_real[i] + probe_imag * back_imag[i], at[i])
-        add_object(1, probe_real * back_imag[i] - probe_imag * back_real[i], at[i])
+    misfit_a = misfits(far_a, pairs[0])
+    far_b = right_side(mid_b, right)
+    mid_a = left_side(misfit_a, right)
+    misfit_b = misfits(far_b, pairs[1])
+    back_a = right_side(mid_a, left)
+    mid_b = left_side(misfit_b, right)
+    add(state_a, back_a)
+    back_b = right_side(mid_b, left)
+    add(state_b, back_b)
 
 
 def gradient_kernel(first, *refs):
@@ -177,8 +192,6 @@
     ]
     for copy in probe_copies + table_copies:
         copy.start()
-    for group in range(groups):
-        pattern_copy(group).start()
 
     for i, ref in ((1, own_ref), (0, side0_ref), (2, side2_ref)):
         value = jnp.where(row_end, 0.0, ref[...]) if i == 2 else ref[...]
@@ -198,6 +211,8 @@
     peak_ref[...] = jnp.broadcast_to(jnp.max(power, keepdims=True).reshape(1, 1) + 1e-06, peak_ref.shape)
     for copy in table_copies:
         copy.wait()
+    for group in range(groups):
+        pattern_copy(group).start()
 
     def visit(group, carry):
         pattern_group(
@@ -255,15 +270,17 @@
 
 def plane_shares(keep, send):
     half = keep + core_swap(send)
-    return exchange(half.reshape(lax.axis_size(PLANE), -1, LANES), PLANE).sum(0)
-
-
-def depth_sum(share):
-    return exchange(jnp.broadcast_to(share, (lax.axis_size("z"),) + share.shape), "z").sum(0)
-
-
-def gathered(share, shape):
+    return exchange(half.reshape(lax.axis_size(PLANE), -1, LANES), PLANE)
+
+
+def depth_shares(shares):
+    share = shares.sum(0)
+    return exchange(jnp.broadcast_to(share, (lax.axis_size("z"),) + share.shape), "z")
+
+
+def gathered(shares, shape):
     plane = lax.axis_size(PLANE)
+    share = shares.sum(0)
     return exchange(jnp.broadcast_to(share, (plane,) + share.shape), PLANE).reshape(shape)
 
 
@@ -352,14 +369,14 @@
     strips = (strip, paired(strip, ROW, 0), paired(strip, ROW, 2))
     row0, row1, row2, keep, send, peak = gradients(True, live_slots, patterns, tables, probe_field, *strips)
     arrived = (paired(row0, ROW, 0), paired(row2, ROW, 2))
-    share, arrived = lax.optimization_barrier((plane_shares(keep, send), arrived))
+    shares, arrived = lax.optimization_barrier((plane_shares(keep, send), arrived))
     sums = side_sum(row1, *arrived, row_end)
     payloads = column_payloads(sums)
     arrived = column_transfers(payloads)
-    share, arrived = lax.optimization_barrier((depth_sum(after(share, *payloads)), arrived))
+    shares, arrived = lax.optimization_barrier((depth_shares(after(shares, *payloads)), arrived))
     strip = updated_strip(strip, sums, arrived, peak)
     sides = (paired(strip, ROW, 0), paired(strip, ROW, 2))
-    mine, sides = lax.optimization_barrier((gathered(after(share, strip), keep.shape), sides))
+    mine, sides = lax.optimization_barrier((gathered(after(shares, strip), keep.shape), sides))
     totals = (mine, core_swap(mine))
 
     strips = (strip,) + sides
@@ -368,10 +385,10 @@
     )
     sums = side_sum(row1, paired(row0, ROW, 0), paired(row2, ROW, 2), row_end)
     payloads = (jnp.where(odd, sums[0], sums[2]), jnp.where(odd, sums[2], sums[0]))
-    share = after(plane_shares(keep, send), *payloads)
+    shares = after(plane_shares(keep, send), *payloads)
     grad = side_sum(sums[1], paired(payloads[0], COL, 0), paired(payloads[1], COL, 2), col_end)
     new_object = (strip[1] - grad / peak).reshape(object_field.shape)
-    mine = gathered(after(depth_sum(share), new_object), keep.shape)
+    mine = gathered(after(depth_shares(shares), new_object), keep.shape)
     return (new_object, last_probe(probe, mine, core_swap(mine)))
 
 

time: 146 us -> 145 us (level)
    all_to_all x4, waiting for transfers between devices: 21.8 us -> 16.2 us  [exchange(): return lax.all_to_all(value, axes, 0, 0, tiled=True)]
    ppermute x2, waiting for transfers between devices: 4.32 us -> 6.89 us  [paired_far(): return lax.ppermute(value, axes, pairs)]
    ppermute x14, waiting for transfers between devices: 9.47 us -> 11.6 us  [paired(): return lax.ppermute(value, axes, pairs)]
  transfers between devices with their start and end apart: 24 -> 24, of which waited for: 14 -> 14; matrix products, arithmetic and copies ran while one was open for 3% -> 4% of each run, Pallas kernels for 0% -> 0%
where the time goes in v7:
time: 145 us; the launch traced here: 144 us
  starting transfers between devices  51.4 us (35%)
  waiting for transfers between devices  38.9 us (27%)
  blocking collectives  23.5 us (16%)
  Pallas kernels  22 us (15%)
  other arithmetic  4.71 us (3%)
  local copies, waits for them, and re-layouts  2.06 us (1%)
  between operations  1.51 us (1%)
    all_to_all x2, blocking collectives, exchange(): return lax.all_to_all(value, axes, 0, 0, tiled=True)  23.5 us
    ppermute x14, starting transfers between devices, paired(): return lax.ppermute(value, axes, pairs)  21.2 us
    pallas_call x2, Pallas kernels, gradients(): pl.pallas_call(functools.partial(gradient_kernel, first), out_shape=(stri...  20.8 us
    all_to_all x4, waiting for transfers between devices, exchange(): return lax.all_to_all(value, axes, 0, 0, tiled=True)  16.2 us
    all_to_all x4, starting transfers between devices, exchange(): return lax.all_to_all(value, axes, 0, 0, tiled=True)  15.9 us
    ppermute x14, waiting for transfers between devices, paired(): return lax.ppermute(value, axes, pairs)  11.6 us
    ppermute x4, starting transfers between devices, core_swap(): return lax.ppermute(value, 'core', [(0, 1), (1, 0)])  8.71 us
    ppermute x2, waiting for transfers between devices, paired_far(): return lax.ppermute(value, axes, pairs)  6.89 us
  transfers between devices with their start and end apart: 24, of which 14 were waited for; matrix products, arithmetic and copies ran while one was open for 4% of the time, Pallas kernels for 0%

profile of v7, /device:TPU:1, one launch (start us, length us, event | category | flops | bytes accessed | tf_op | source)
XLA Modules:
  0.0 144.1 jit_solution(17250030603214228009)
XLA Ops:
  0.6 8.7 %collective-permute-start.1 = (f32[2,16,8,128]{3,2,1,0:T(8,128)}, f32[2,16,8,128]{3,2,1,0:T(8,128)S(1)}, u32[]{:S(2)}, u32[]{:S(2)}) collective-permute-start(f32[2,16,8,128]{3,2,1,0:T(8,128)} %bitcast.80), channel_id=1, source_target_pairs={{0,31},{1,2},{2,1},{3,4},{4,3},{5,6},{6,5},{7,8},{8,7},{9,10},{10,... | collective-permute-start | bytes 393224 | tf_op jit(solution)/shard_map/ppermute | solution.py:42
  9.3 3.4 %collective-permute-done.1 = f32[2,16,8,128]{3,2,1,0:T(8,128)S(1)} collective-permute-done((f32[2,16,8,128]{3,2,1,0:T(8,128)}, f32[2,16,8,128]{3,2,1,0:T(8,128)S(1)}, u32[]{:S(2)}, u32[]{:S(2)}) %collective-permute-start.1) | collective-permute-done | bytes 131104 | tf_op jit(solution)/shard_map/ppermute | solution.py:42
  13.6 0.9 pad_maximum_fusion.refs_5_
  14.5 3.1 %collective-permute-start.3 = (f32[3,2,16,8,128]{4,3,2,1,0:T(8,128)S(1)}, f32[3,2,16,8,128]{4,3,2,1,0:T(8,128)S(1)}, u32[]{:S(2)}, u32[]{:S(2)}) collective-permute-start(f32[3,2,16,8,128]{4,3,2,1,0:T(8,128)S(1)} %pad_maximum_fusion.refs_5_), channel_id=1, source_target_pairs={{0,224},{32,64},{64,32},{96,128},{128,96},{160,192},{192,160},{224... | collective-permute-start | bytes 1179656 | tf_op jit(solution)/shard_map/ppermute | solution.py:42
  19.1 4.3 %collective-permute-done.3.refs_7_ = f32[3,2,16,8,128]{4,3,2,1,0:T(8,128)S(1)} collective-permute-done((f32[3,2,16,8,128]{4,3,2,1,0:T(8,128)S(1)}, f32[3,2,16,8,128]{4,3,2,1,0:T(8,128)S(1)}, u32[]{:S(2)}, u32[]{:S(2)}) %collective-permute-start.3) | collective-permute-done | bytes 393248 | tf_op jit(solution)/shard_map/ppermute | solution.py:42
  23.4 9.6 %shard_map.86 = (f32[3,2,16,8,128]{4,3,2,1,0:T(8,128)S(1)}, f32[3,2,16,8,128]{4,3,2,1,0:T(8,128)S(1)}, f32[3,2,16,8,128]{4,3,2,1,0:T(8,128)S(1)}, f32[2,256,128]...) custom-call(s32[3,8]{1,0:T(4,128)S(1)} %concatenate.3.refs_0_, f32[8,256,256]{2,1,0:T(8,128)} %bitcast.78, ...), custom_call_target="tpu_custom_call" | custom-call | tf_op jit(solution)/shard_map/pallas_call | solution.py:243
  33.1 1.6 %collective-permute-start.4 = (f32[2,256,128]{2,1,0:T(8,128)S(1)}, f32[2,256,128]{2,1,0:T(8,128)S(1)}, u32[]{:S(2)}, u32[]{:S(2)}) collective-permute-start(f32[2,256,128]{2,1,0:T(8,128)S(1)} %get-tuple-element.32), channel_id=1, source_target_pairs={{0,32},{32,0},{1,33},{33,1},{2,34},{34,2},{3,35},{35,3},{4,36},{36... | collective-permute-start | bytes 786440 | tf_op jit(solution)/shard_map/ppermute | solution.py:268
  36.6 3.5 %all-to-all-start = ((f32[16,32,128]{2,1,0:T(8,128)}), f32[16,32,128]{2,1,0:T(8,128)S(1)}, u32[]{:S(2)}, u32[]{:S(2)}) async-start(f32[16,32,128]{2,1,0:T(8,128)} %bitcast.8), calls=%async_computation | async-start | bytes 524288 | tf_op jit(solution)/shard_map/all_to_all | solution.py:264
  40.1 2.1 %collective-permute-done.6 = f32[3,2,16,8,128]{4,3,2,1,0:T(8,128)S(1)} collective-permute-done((f32[3,2,16,8,128]{4,3,2,1,0:T(8,128)S(1)}, f32[3,2,16,8,128]{4,3,2,1,0:T(8,128)S(1)}, u32[]{:S(2)}, u32[]{:S(2)}) %collective-permute-start.6) | collective-permute-done | bytes 393248 | tf_op jit(solution)/shard_map/ppermute | solution.py:42
  42.3 5.7 %all-to-all-done = f32[16,32,128]{2,1,0:T(8,128)S(1)} async-done(((f32[16,32,128]{2,1,0:T(8,128)}), f32[16,32,128]{2,1,0:T(8,128)S(1)}, u32[]{:S(2)}, u32[]{:S(2)}) %all-to-all-start) | async-done | bytes 262176 | tf_op jit(solution)/shard_map/all_to_all | solution.py:264
  48.1 3.0 %collective-permute-start.8 = (f32[2,2,16,8,128]{4,3,2,1,0:T(8,128)S(1)}, f32[2,2,16,8,128]{4,3,2,1,0:T(8,128)S(1)}, u32[]{:S(2)}, u32[]{:S(2)}) collective-permute-start(f32[2,2,16,8,128]{4,3,2,1,0:T(8,128)S(1)} %get-tuple-element.66), channel_id=1, source_target_pairs={{0,31},{1,2},{2,1},{3,4},{4,3},{5,6},{6,5},{7,8},{8,7},{9,10},{10,... | collective-permute-start | bytes 786440 | tf_op jit(solution)/shard_map/ppermute | solution.py:42
  51.8 3.4 %all-to-all-start.1 = ((f32[8,32,128]{2,1,0:T(8,128)}), f32[8,32,128]{2,1,0:T(8,128)S(1)}, u32[]{:S(2)}, u32[]{:S(2)}) async-start(f32[8,32,128]{2,1,0:T(8,128)} %broadcast_in_dim.41), calls=%async_computation.1 | async-start | bytes 262144 | tf_op jit(solution)/shard_map/all_to_all | solution.py:264
  55.2 5.5 %collective-permute-start.10 = (f32[2,16,8,128]{3,2,1,0:T(8,128)S(1)}, f32[2,16,8,128]{3,2,1,0:T(8,128)S(1)}, u32[]{:S(2)}, u32[]{:S(2)}) collective-permute-start(f32[2,16,8,128]{3,2,1,0:T(8,128)S(1)} %get-tuple-element.64), channel_id=1, source_target_pairs={{0,30},{1,31},{2,4},{3,5},{4,2},{5,3},{6,8},{7,9},{8,6},{9,7},{10,... | collective-permute-start | bytes 393224 | tf_op jit(solution)/shard_map/ppermute | solution.py:48
  60.7 3.8 %collective-permute-done.10 = f32[2,16,8,128]{3,2,1,0:T(8,128)S(1)} collective-permute-done((f32[2,16,8,128]{3,2,1,0:T(8,128)S(1)}, f32[2,16,8,128]{3,2,1,0:T(8,128)S(1)}, u32[]{:S(2)}, u32[]{:S(2)}) %collective-permute-start.10) | collective-permute-done | bytes 131104 | tf_op jit(solution)/shard_map/ppermute | solution.py:48
  64.5 3.1 %collective-permute-done.9 = f32[2,16,8,128]{3,2,1,0:T(8,128)S(1)} collective-permute-done((f32[2,16,8,128]{3,2,1,0:T(8,128)S(1)}, f32[2,16,8,128]{3,2,1,0:T(8,128)S(1)}, u32[]{:S(2)}, u32[]{:S(2)}) %collective-permute-start.9) | collective-permute-done | bytes 131104 | tf_op jit(solution)/shard_map/ppermute | solution.py:48
  67.8 2.0 %collective-permute-start.12 = (f32[3,2,16,8,128]{4,3,2,1,0:T(8,128)S(1)}, f32[3,2,16,8,128]{4,3,2,1,0:T(8,128)S(1)}, u32[]{:S(2)}, u32[]{:S(2)}) collective-permute-start(f32[3,2,16,8,128]{4,3,2,1,0:T(8,128)S(1)} %pad_maximum_fusion.1.refs_5_), channel_id=1, source_target_pairs={{0,224},{32,64},{64,32},{96,128},{128,96},{160,192},{192,160},{224... | collective-permute-start | bytes 1179656 | tf_op jit(solution)/shard_map/ppermute | solution.py:42
  70.3 11.8 %all_to_all.30 = f32[16,32,128]{2,1,0:T(8,128)S(1)} all-to-all(f32[16,32,128]{2,1,0:T(8,128)S(1)} %broadcast_in_dim.43), channel_id=1, replica_groups=mesh['y'=4,'core'=2,'z'=8,'x'=4] {'y','x'}, dimensions={0} | all-to-all | bytes 524288 | tf_op jit(solution)/shard_map/all_to_all | solution.py:264
  82.1 1.8 %collective-permute-start.13 = (f32[2,256,128]{2,1,0:T(8,128)S(1)}, f32[2,256,128]{2,1,0:T(8,128)S(1)}, u32[]{:S(2)}, u32[]{:S(2)}) collective-permute-start(f32[2,256,128]{2,1,0:T(8,128)S(1)} %bitcast.74), channel_id=1, source_target_pairs={{0,32},{32,0},{1,33},{33,1},{2,34},{34,2},{3,35},{35,3},{4,36},{36... | collective-permute-start | bytes 786440 | tf_op jit(solution)/shard_map/ppermute | solution.py:268
  83.9 1.2 collective-permute-done.13.refs_9_
  85.1 11.2 %shard_map.87 = (f32[3,2,16,8,128]{4,3,2,1,0:T(8,128)S(1)}, f32[3,2,16,8,128]{4,3,2,1,0:T(8,128)S(1)}, f32[3,2,16,8,128]{4,3,2,1,0:T(8,128)S(1)}, f32[2,256,128]...) custom-call(s32[3,8]{1,0:T(4,128)S(1)} %concatenate.3.refs_0_, ...), custom_call_target="tpu_custom_call" | custom-call | tf_op jit(solution)/shard_map/pallas_call | solution.py:243
  96.7 1.0 collective-permute-start.18
  97.7 1.2 collective-permute-done.18
  99.6 3.8 %all-to-all-start.3 = ((f32[16,32,128]{2,1,0:T(8,128)}), f32[16,32,128]{2,1,0:T(8,128)S(1)}, u32[]{:S(2)}, u32[]{:S(2)}) async-start(f32[16,32,128]{2,1,0:T(8,128)} %bitcast.21), calls=%async_computation.3 | async-start | bytes 524288 | tf_op jit(solution)/shard_map/all_to_all | solution.py:264
  104.3 1.1 select_add_fusion
  105.5 3.0 %collective-permute-start.17 = (f32[2,16,8,128]{3,2,1,0:T(8,128)S(1)}, f32[2,16,8,128]{3,2,1,0:T(8,128)S(1)}, u32[]{:S(2)}, u32[]{:S(2)}) collective-permute-start(f32[2,16,8,128]{3,2,1,0:T(8,128)S(1)} %get-tuple-element.62), channel_id=1, source_target_pairs={{0,31},{1,2},{2,1},{3,4},{4,3},{5,6},{6,5},{7,8},{8,7},{9,10},{10,... | collective-permute-start | bytes 393224 | tf_op jit(solution)/shard_map/ppermute | solution.py:42
  108.5 3.3 %all-to-all-done.3 = f32[16,32,128]{2,1,0:T(8,128)S(1)} async-done(((f32[16,32,128]{2,1,0:T(8,128)}), f32[16,32,128]{2,1,0:T(8,128)S(1)}, u32[]{:S(2)}, u32[]{:S(2)}) %all-to-all-start.3) | async-done | bytes 262176 | tf_op jit(solution)/shard_map/all_to_all | solution.py:264
  112.5 5.2 %all-to-all-start.4 = ((f32[8,32,128]{2,1,0:T(8,128)}), f32[8,32,128]{2,1,0:T(8,128)S(1)}, u32[]{:S(2)}, u32[]{:S(2)}) async-start(f32[8,32,128]{2,1,0:T(8,128)} %broadcast_in_dim.44), calls=%async_computation.4 | async-start | bytes 262144 | tf_op jit(solution)/shard_map/all_to_all | solution.py:264
  118.4 7.2 %all-to-all-done.4 = f32[8,32,128]{2,1,0:T(8,128)S(1)} async-done(((f32[8,32,128]{2,1,0:T(8,128)}), f32[8,32,128]{2,1,0:T(8,128)S(1)}, u32[]{:S(2)}, u32[]{:S(2)}) %all-to-all-start.4) | async-done | bytes 131104 | tf_op jit(solution)/shard_map/all_to_all | solution.py:264
  125.6 11.7 %all_to_all.31 = f32[16,32,128]{2,1,0:T(8,128)S(1)} all-to-all(f32[16,32,128]{2,1,0:T(8,128)S(1)} %broadcast_in_dim.45), channel_id=1, replica_groups=mesh['y'=4,'core'=2,'z'=8,'x'=4] {'y','x'}, dimensions={0} | all-to-all | bytes 524288 | tf_op jit(solution)/shard_map/all_to_all | solution.py:264
  137.3 4.4 %collective-permute-start.19 = (f32[2,256,128]{2,1,0:T(8,128)S(1)}, f32[2,256,128]{2,1,0:T(8,128)S(1)}, u32[]{:S(2)}, u32[]{:S(2)}) collective-permute-start(f32[2,256,128]{2,1,0:T(8,128)S(1)} %bitcast.76), channel_id=1, source_target_pairs={{0,32},{32,0},{1,33},{33,1},{2,34},{34,2},{3,35},{35,3},{4,36},{36... | collective-permute-start | bytes 786440 | tf_op jit(solution)/shard_map/ppermute | solution.py:268
  141.7 1.2 collective-permute-done.19.other_ref
  142.9 1.2 shard_map.88
  (50 shorter events, 8.6 us)
Async XLA Ops:
  0.6 12.1 %collective-permute-start.1 = (f32[2,16,8,128]{3,2,1,0:T(8,128)}, f32[2,16,8,128]{3,2,1,0:T(8,128)S(1)}, u32[]{:S(2)}, u32[]{:S(2)}) collective-permute-start(f32[2,16,8,128]{3,2,1,0:T(8,128)} %bitcast.80), channel_id=1, source_target_pairs={{0,31},{1,2},{2,1},{3,4},{4,3},{5,6},{6,5},{7,8},{8,7},{9,10},{10,... | collective-permute-start | bytes 393224 | tf_op jit(solution)/shard_map/ppermute | solution.py:42
  9.3 4.3 %collective-permute-start = (f32[2,16,8,128]{3,2,1,0:T(8,128)}, f32[2,16,8,128]{3,2,1,0:T(8,128)S(1)}, u32[]{:S(2)}, u32[]{:S(2)}) collective-permute-start(f32[2,16,8,128]{3,2,1,0:T(8,128)} %bitcast.81), channel_id=1, source_target_pairs={{0,1},{1,0},{2,3},{3,2},{4,5},{5,4},{6,7},{7,6},{8,9},{9,8},{10,11... | collective-permute-start | bytes 393224 | tf_op jit(solution)/shard_map/ppermute | solution.py:42
  14.5 8.9 %collective-permute-start.3 = (f32[3,2,16,8,128]{4,3,2,1,0:T(8,128)S(1)}, f32[3,2,16,8,128]{4,3,2,1,0:T(8,128)S(1)}, u32[]{:S(2)}, u32[]{:S(2)}) collective-permute-start(f32[3,2,16,8,128]{4,3,2,1,0:T(8,128)S(1)} %pad_maximum_fusion.refs_5_), channel_id=1, source_target_pairs={{0,224},{32,64},{64,32},{96,128},{128,96},{160,192},{192,160},{224... | collective-permute-start | bytes 1179656 | tf_op jit(solution)/shard_map/ppermute | solution.py:42
  17.7 5.8 %collective-permute-start.2 = (f32[3,2,16,8,128]{4,3,2,1,0:T(8,128)S(1)}, f32[3,2,16,8,128]{4,3,2,1,0:T(8,128)S(1)}, u32[]{:S(2)}, u32[]{:S(2)}) collective-permute-start(f32[3,2,16,8,128]{4,3,2,1,0:T(8,128)S(1)} %pad_maximum_fusion.refs_5_), channel_id=1, source_target_pairs={{0,32},{32,0},{64,96},{96,64},{128,160},{160,128},{192,224},{224,1... | collective-permute-start | bytes 1179656 | tf_op jit(solution)/shard_map/ppermute | solution.py:42
  33.1 2.7 %collective-permute-start.4 = (f32[2,256,128]{2,1,0:T(8,128)S(1)}, f32[2,256,128]{2,1,0:T(8,128)S(1)}, u32[]{:S(2)}, u32[]{:S(2)}) collective-permute-start(f32[2,256,128]{2,1,0:T(8,128)S(1)} %get-tuple-element.32), channel_id=1, source_target_pairs={{0,32},{32,0},{1,33},{33,1},{2,34},{34,2},{3,35},{35,3},{4,36},{36... | collective-permute-start | bytes 786440 | tf_op jit(solution)/shard_map/ppermute | solution.py:268
  34.7 5.5 %collective-permute-start.5 = (f32[3,2,16,8,128]{4,3,2,1,0:T(8,128)S(1)}, f32[3,2,16,8,128]{4,3,2,1,0:T(8,128)S(1)}, u32[]{:S(2)}, u32[]{:S(2)}) collective-permute-start(f32[3,2,16,8,128]{4,3,2,1,0:T(8,128)S(1)} %get-tuple-element.33), channel_id=1, source_target_pairs={{0,32},{32,0},{64,96},{96,64},{128,160},{160,128},{192,224},{224,1... | collective-permute-start | bytes 1179656 | tf_op jit(solution)/shard_map/ppermute | solution.py:42
  34.8 7.5 %collective-permute-start.6 = (f32[3,2,16,8,128]{4,3,2,1,0:T(8,128)S(1)}, f32[3,2,16,8,128]{4,3,2,1,0:T(8,128)S(1)}, u32[]{:S(2)}, u32[]{:S(2)}) collective-permute-start(f32[3,2,16,8,128]{4,3,2,1,0:T(8,128)S(1)} %get-tuple-element.34), channel_id=1, source_target_pairs={{0,224},{32,64},{64,32},{96,128},{128,96},{160,192},{192,160},{224... | collective-permute-start | bytes 1179656 | tf_op jit(solution)/shard_map/ppermute | solution.py:42
  36.6 11.4 %all-to-all-start = ((f32[16,32,128]{2,1,0:T(8,128)}), f32[16,32,128]{2,1,0:T(8,128)S(1)}, u32[]{:S(2)}, u32[]{:S(2)}) async-start(f32[16,32,128]{2,1,0:T(8,128)} %bitcast.8), calls=%async_computation | async-start | bytes 524288 | tf_op jit(solution)/shard_map/all_to_all | solution.py:264
  48.0 19.7 %copy-start.1 = (f32[2,128,128]{2,1,0:T(8,128)S(1)}, f32[2,128,128]{2,1,0:T(8,128)}, u32[]{:S(2)}) copy-start(f32[2,128,128]{2,1,0:T(8,128)} %param.7) | copy-start | bytes 393220
  48.1 19.5 %collective-permute-start.8 = (f32[2,2,16,8,128]{4,3,2,1,0:T(8,128)S(1)}, f32[2,2,16,8,128]{4,3,2,1,0:T(8,128)S(1)}, u32[]{:S(2)}, u32[]{:S(2)}) collective-permute-start(f32[2,2,16,8,128]{4,3,2,1,0:T(8,128)S(1)} %get-tuple-element.66), channel_id=1, source_target_pairs={{0,31},{1,2},{2,1},{3,4},{4,3},{5,6},{6,5},{7,8},{8,7},{9,10},{10,... | collective-permute-start | bytes 786440 | tf_op jit(solution)/shard_map/ppermute | solution.py:42
  51.1 16.5 %collective-permute-start.7 = (f32[2,2,16,8,128]{4,3,2,1,0:T(8,128)S(1)}, f32[2,2,16,8,128]{4,3,2,1,0:T(8,128)S(1)}, u32[]{:S(2)}, u32[]{:S(2)}) collective-permute-start(f32[2,2,16,8,128]{4,3,2,1,0:T(8,128)S(1)} %get-tuple-element.67), channel_id=1, source_target_pairs={{0,1},{1,0},{2,3},{3,2},{4,5},{5,4},{6,7},{7,6},{8,9},{9,8},{10,11... | collective-permute-start | bytes 786440 | tf_op jit(solution)/shard_map/ppermute | solution.py:42
  51.8 15.8 %all-to-all-start.1 = ((f32[8,32,128]{2,1,0:T(8,128)}), f32[8,32,128]{2,1,0:T(8,128)S(1)}, u32[]{:S(2)}, u32[]{:S(2)}) async-start(f32[8,32,128]{2,1,0:T(8,128)} %broadcast_in_dim.41), calls=%async_computation.1 | async-start | bytes 262144 | tf_op jit(solution)/shard_map/all_to_all | solution.py:264
  55.2 9.3 %collective-permute-start.10 = (f32[2,16,8,128]{3,2,1,0:T(8,128)S(1)}, f32[2,16,8,128]{3,2,1,0:T(8,128)S(1)}, u32[]{:S(2)}, u32[]{:S(2)}) collective-permute-start(f32[2,16,8,128]{3,2,1,0:T(8,128)S(1)} %get-tuple-element.64), channel_id=1, source_target_pairs={{0,30},{1,31},{2,4},{3,5},{4,2},{5,3},{6,8},{7,9},{8,6},{9,7},{10,... | collective-permute-start | bytes 393224 | tf_op jit(solution)/shard_map/ppermute | solution.py:48
  60.7 6.9 %collective-permute-start.9 = (f32[2,16,8,128]{3,2,1,0:T(8,128)S(1)}, f32[2,16,8,128]{3,2,1,0:T(8,128)S(1)}, u32[]{:S(2)}, u32[]{:S(2)}) collective-permute-start(f32[2,16,8,128]{3,2,1,0:T(8,128)S(1)} %get-tuple-element.65), channel_id=1, source_target_pairs={{0,2},{1,3},{2,0},{3,1},{4,6},{5,7},{6,4},{7,5},{8,10},{9,11},{10,... | collective-permute-start | bytes 393224 | tf_op jit(solution)/shard_map/ppermute | solution.py:48
  67.8 14.3 %collective-permute-start.12 = (f32[3,2,16,8,128]{4,3,2,1,0:T(8,128)S(1)}, f32[3,2,16,8,128]{4,3,2,1,0:T(8,128)S(1)}, u32[]{:S(2)}, u32[]{:S(2)}) collective-permute-start(f32[3,2,16,8,128]{4,3,2,1,0:T(8,128)S(1)} %pad_maximum_fusion.1.refs_5_), channel_id=1, source_target_pairs={{0,224},{32,64},{64,32},{96,128},{128,96},{160,192},{192,160},{224... | collective-permute-start | bytes 1179656 | tf_op jit(solution)/shard_map/ppermute | solution.py:42
  69.8 12.3 %collective-permute-start.11 = (f32[3,2,16,8,128]{4,3,2,1,0:T(8,128)S(1)}, f32[3,2,16,8,128]{4,3,2,1,0:T(8,128)S(1)}, u32[]{:S(2)}, u32[]{:S(2)}) collective-permute-start(f32[3,2,16,8,128]{4,3,2,1,0:T(8,128)S(1)} %pad_maximum_fusion.1.refs_5_), channel_id=1, source_target_pairs={{0,32},{32,0},{64,96},{96,64},{128,160},{160,128},{192,224},{224,1... | collective-permute-start | bytes 1179656 | tf_op jit(solution)/shard_map/ppermute | solution.py:42
  82.1 2.9 %copy-start.2 = (f32[3,2,16,8,128]{4,3,2,1,0:T(8,128)}, f32[3,2,16,8,128]{4,3,2,1,0:T(8,128)S(1)}, u32[]{:S(2)}) copy-start(f32[3,2,16,8,128]{4,3,2,1,0:T(8,128)S(1)} %collective-permute-done.12.refs_7_) | copy-start | bytes 1179652
  82.1 2.9 %collective-permute-start.13 = (f32[2,256,128]{2,1,0:T(8,128)S(1)}, f32[2,256,128]{2,1,0:T(8,128)S(1)}, u32[]{:S(2)}, u32[]{:S(2)}) collective-permute-start(f32[2,256,128]{2,1,0:T(8,128)S(1)} %bitcast.74), channel_id=1, source_target_pairs={{0,32},{32,0},{1,33},{33,1},{2,34},{34,2},{3,35},{35,3},{4,36},{36... | collective-permute-start | bytes 786440 | tf_op jit(solution)/shard_map/ppermute | solution.py:268
  96.2 7.2 %collective-permute-start.14 = (f32[3,2,16,8,128]{4,3,2,1,0:T(8,128)S(1)}, f32[3,2,16,8,128]{4,3,2,1,0:T(8,128)S(1)}, u32[]{:S(2)}, u32[]{:S(2)}) collective-permute-start(f32[3,2,16,8,128]{4,3,2,1,0:T(8,128)S(1)} %get-tuple-element.50), channel_id=1, source_target_pairs={{0,32},{32,0},{64,96},{96,64},{128,160},{160,128},{192,224},{224,1... | collective-permute-start | bytes 1179656 | tf_op jit(solution)/shard_map/ppermute | solution.py:42
  96.7 7.6 %collective-permute-start.15 = (f32[3,2,16,8,128]{4,3,2,1,0:T(8,128)S(1)}, f32[3,2,16,8,128]{4,3,2,1,0:T(8,128)}, u32[]{:S(2)}, u32[]{:S(2)}) collective-permute-start(f32[3,2,16,8,128]{4,3,2,1,0:T(8,128)S(1)} %get-tuple-element.51), channel_id=1, source_target_pairs={{0,224},{32,64},{64,32},{96,128},{128,96},{160,192},{192,160},{224... | collective-permute-start | bytes 1179656 | tf_op jit(solution)/shard_map/ppermute | solution.py:42
  96.7 2.1 %collective-permute-start.18 = (f32[2,256,128]{2,1,0:T(8,128)S(1)}, f32[2,256,128]{2,1,0:T(8,128)S(1)}, u32[]{:S(2)}, u32[]{:S(2)}) collective-permute-start(f32[2,256,128]{2,1,0:T(8,128)S(1)} %get-tuple-element.55), channel_id=1, source_target_pairs={{0,32},{32,0},{1,33},{33,1},{2,34},{34,2},{3,35},{35,3},{4,36},{36... | collective-permute-start | bytes 786440 | tf_op jit(solution)/shard_map/ppermute | solution.py:268
  99.6 12.2 %all-to-all-start.3 = ((f32[16,32,128]{2,1,0:T(8,128)}), f32[16,32,128]{2,1,0:T(8,128)S(1)}, u32[]{:S(2)}, u32[]{:S(2)}) async-start(f32[16,32,128]{2,1,0:T(8,128)} %bitcast.21), calls=%async_computation.3 | async-start | bytes 524288 | tf_op jit(solution)/shard_map/all_to_all | solution.py:264
  104.3 38.6 %copy-start = (f32[2,2,256,128]{3,2,1,0:T(8,128)S(1)}, f32[2,2,256,128]{3,2,1,0:T(8,128)}, u32[]{:S(2)}) copy-start(f32[2,2,256,128]{3,2,1,0:T(8,128)} %get-tuple-element.53.probe_ref) | copy-start | bytes 1572868
  105.5 12.2 %collective-permute-start.17 = (f32[2,16,8,128]{3,2,1,0:T(8,128)S(1)}, f32[2,16,8,128]{3,2,1,0:T(8,128)S(1)}, u32[]{:S(2)}, u32[]{:S(2)}) collective-permute-start(f32[2,16,8,128]{3,2,1,0:T(8,128)S(1)} %get-tuple-element.62), channel_id=1, source_target_pairs={{0,31},{1,2},{2,1},{3,4},{4,3},{5,6},{6,5},{7,8},{8,7},{9,10},{10,... | collective-permute-start | bytes 393224 | tf_op jit(solution)/shard_map/ppermute | solution.py:42
  108.5 9.2 %collective-permute-start.16 = (f32[2,16,8,128]{3,2,1,0:T(8,128)S(1)}, f32[2,16,8,128]{3,2,1,0:T(8,128)S(1)}, u32[]{:S(2)}, u32[]{:S(2)}) collective-permute-start(f32[2,16,8,128]{3,2,1,0:T(8,128)S(1)} %get-tuple-element.63), channel_id=1, source_target_pairs={{0,1},{1,0},{2,3},{3,2},{4,5},{5,4},{6,7},{7,6},{8,9},{9,8},{10,11... | collective-permute-start | bytes 393224 | tf_op jit(solution)/shard_map/ppermute | solution.py:42
  112.5 13.1 %all-to-all-start.4 = ((f32[8,32,128]{2,1,0:T(8,128)}), f32[8,32,128]{2,1,0:T(8,128)S(1)}, u32[]{:S(2)}, u32[]{:S(2)}) async-start(f32[8,32,128]{2,1,0:T(8,128)} %broadcast_in_dim.44), calls=%async_computation.4 | async-start | bytes 262144 | tf_op jit(solution)/shard_map/all_to_all | solution.py:264
  137.3 5.6 %collective-permute-start.19 = (f32[2,256,128]{2,1,0:T(8,128)S(1)}, f32[2,256,128]{2,1,0:T(8,128)S(1)}, u32[]{:S(2)}, u32[]{:S(2)}) collective-permute-start(f32[2,256,128]{2,1,0:T(8,128)S(1)} %bitcast.76), channel_id=1, source_target_pairs={{0,32},{32,0},{1,33},{33,1},{2,34},{34,2},{3,35},{35,3},{4,36},{36... | collective-permute-start | bytes 786440 | tf_op jit(solution)/shard_map/ppermute | solution.py:268

commit v8 on v7

--- a/solution.py
+++ b/solution.py
@@ -15,7 +15,7 @@
 TILES = 16
 GROUP = 4
 F32 = jnp.float32
-VMEM_BYTES = 102 * 512 * 1024
+VMEM_BYTES = 101 * 512 * 1024
 
 
 def dft_tables(length):
@@ -169,12 +169,13 @@
 def gradient_kernel(first, *refs):
     slots_ref, pattern_ref, left_ref, right_ref, start_ref, own_ref, side0_ref, side2_ref = refs[:8]
     if first:
-        row0_ref, row1_ref, row2_ref, keep, send, peak_ref = refs[8:14]
+        out0_ref, out1_ref, out2_ref, keep, send, peak_ref, rows_ref = refs[8:15]
     else:
         mine_ref, other_ref = refs[8:10]
-        row0_ref, row1_ref, row2_ref, keep, send, peak_ref, probe_ref = refs[10:17]
+        out0_ref, out1_ref, out2_ref, keep, send, peak_ref, probe_ref = refs[10:17]
     pattern, left, right, probe, ext, gobj, probe_sems, table_sems, pattern_sems = refs[-9:]
     row, row_places, row_end = place_of(ROW)
+    col, col_places, col_end = place_of(COL)
     count = slots_ref[2, 0]
     groups = pattern.shape[0] // GROUP
 
@@ -194,8 +195,13 @@
         copy.start()
 
     for i, ref in ((1, own_ref), (0, side0_ref), (2, side2_ref)):
-        value = jnp.where(row_end, 0.0, ref[...]) if i == 2 else ref[...]
-        ext[:, :, pl.ds(row_places[i] * TILES, TILES)] = value
+        value = jnp.where(row_end if first else col_end, 0.0, ref[...]) if i == 2 else ref[...]
+        if first:
+            ext[:, :, pl.ds(row_places[i] * TILES, TILES)] = value
+        else:
+            ext[col_places[i]] = value
+    if first:
+        rows_ref[...] = ext[1]
     gobj[...] = jnp.zeros_like(gobj)
     keep[...] = jnp.zeros_like(keep)
     send[...] = jnp.zeros_like(send)
@@ -222,8 +228,8 @@
 
     live_groups = (count + GROUP - 1) // GROUP
     lax.fori_loop(0, live_groups, visit, 0)
-    for i, ref in enumerate((row0_ref, row1_ref, row2_ref)):
-        ref[...] = gobj[:, :, pl.ds(row_places[i] * TILES, TILES)]
+    for i, ref in enumerate((out0_ref, out1_ref, out2_ref)):
+        ref[...] = gobj[col_places[i]] if first else gobj[:, :, pl.ds(row_places[i] * TILES, TILES)]
     for group in range(1, groups):
 
         @pl.when(group >= live_groups)
@@ -236,15 +242,19 @@
     vmem = pl.BlockSpec(memory_space=pltpu.VMEM)
     smem = pl.BlockSpec(memory_space=pltpu.SMEM)
     hbm = pl.BlockSpec(memory_space=pltpu.HBM)
-    strip = jax.ShapeDtypeStruct((3, 2, TILES, 8, LANES), F32)
+    row_strip = jax.ShapeDtypeStruct((3, 2, TILES, 8, LANES), F32)
+    col_strip = jax.ShapeDtypeStruct((2, 3 * TILES, 8, LANES), F32)
     half = jax.ShapeDtypeStruct((2, size, LANES), F32)
     both = jax.ShapeDtypeStruct((2, 2, size, LANES), F32)
     ext = pltpu.VMEM((3, 2, 3 * TILES, 8, LANES), F32)
     return pl.pallas_call(
         functools.partial(gradient_kernel, first),
-        out_shape=(strip,) * 3 + (half, half, jax.ShapeDtypeStruct((8, LANES), F32)) + (() if first else (both,)),
+        out_shape=(
+            (col_strip if first else row_strip,) * 3
+            + (half, half, jax.ShapeDtypeStruct((8, LANES), F32), col_strip if first else both)
+        ),
         in_specs=[smem] + [hbm] * 4 + [vmem] * len(vmem_args),
-        out_specs=(vmem,) * (6 if first else 7),
+        out_specs=(vmem,) * 7,
         scratch_shapes=[
             pltpu.VMEM(patterns.shape, F32),
             pltpu.VMEM(tables[0].shape, jnp.bfloat16),
@@ -288,41 +298,44 @@
     return own + side0 + jnp.where(at_end, 0.0, side2)
 
 
-def column_payloads(sums):
-    index = lax.axis_index(COL)
+def row_payloads(sums):
+    index = lax.axis_index(ROW)
     odd = lax.rem(index, 2) == 1
-    right_first = lax.rem(index // 2, 2) == 0
+    down_first = lax.rem(index // 2, 2) == 0
+    upper, lower = sums[:, : 2 * TILES], sums[:, TILES:]
+    above, below = sums[:, :TILES], sums[:, 2 * TILES :]
     return (
-        jnp.where(odd, sums[:2], sums[1:]),
-        jnp.where(odd, sums[1:], sums[:2]),
-        jnp.where(right_first, sums[2], sums[0]),
-        jnp.where(right_first, sums[0], sums[2]),
+        jnp.where(odd, upper, lower),
+        jnp.where(odd, lower, upper),
+        jnp.where(down_first, below, above),
+        jnp.where(down_first, above, below),
     )
 
 
-def column_transfers(payloads):
+def row_transfers(payloads):
     near0, near2, far_a, far_b = payloads
-    return paired(near0, COL, 0), paired(near2, COL, 2), paired_far(far_a, COL, 0), paired_far(far_b, COL, 1)
+    return paired(near0, ROW, 0), paired(near2, ROW, 2), paired_far(far_a, ROW, 0), paired_far(far_b, ROW, 1)
 
 
 def updated_strip(strip, sums, arrived, peak):
-    index, places, at_end = place_of(COL)
-    last = lax.axis_size(COL) - 1
+    index, places, at_end = place_of(ROW)
+    last = lax.axis_size(ROW) - 1
     odd = lax.rem(index, 2) == 1
-    right_first = lax.rem(index // 2, 2) == 0
+    down_first = lax.rem(index // 2, 2) == 0
     near0, near2, far_a, far_b = arrived
     near2 = jnp.where(at_end, 0.0, near2)
     far_b = jnp.where((index < 2) | (index > last - 2), 0.0, far_b)
-    from_left, from_right = jnp.where(odd, near0, near2), jnp.where(odd, near2, near0)
-    grad_left = sums[0] + from_left[0] + jnp.where(right_first, far_b, far_a)
-    grad = sums[1] + from_left[1] + from_right[0]
-    grad_right = sums[2] + from_right[1] + jnp.where(right_first, far_a, far_b)
-    return jnp.stack(
+    from_upper, from_lower = jnp.where(odd, near0, near2), jnp.where(odd, near2, near0)
+    grad_above = sums[:, :TILES] + from_upper[:, :TILES] + jnp.where(down_first, far_b, far_a)
+    grad = sums[:, TILES : 2 * TILES] + from_upper[:, TILES:] + from_lower[:, :TILES]
+    grad_below = sums[:, 2 * TILES :] + from_lower[:, TILES:] + jnp.where(down_first, far_a, far_b)
+    return jnp.concatenate(
         [
-            jnp.where(index == 0, 0.0, strip[0] - grad_left / peak),
-            strip[1] - grad / peak,
-            jnp.where(index == last, 0.0, strip[2] - grad_right / peak),
-        ]
+            jnp.where(index == 0, 0.0, strip[:, :TILES] - grad_above / peak),
+            strip[:, TILES : 2 * TILES] - grad / peak,
+            jnp.where(index == last, 0.0, strip[:, 2 * TILES :] - grad_below / peak),
+        ],
+        axis=1,
     )
 
 
@@ -367,15 +380,15 @@
     side0, side2 = paired(own, COL, 0), jnp.where(col_end, 0.0, paired(own, COL, 2))
     strip = jnp.stack([jnp.where(odd, side0, side2), own, jnp.where(odd, side2, side0)])
     strips = (strip, paired(strip, ROW, 0), paired(strip, ROW, 2))
-    row0, row1, row2, keep, send, peak = gradients(True, live_slots, patterns, tables, probe_field, *strips)
-    arrived = (paired(row0, ROW, 0), paired(row2, ROW, 2))
+    col0, col1, col2, keep, send, peak, strip = gradients(True, live_slots, patterns, tables, probe_field, *strips)
+    arrived = (paired(col0, COL, 0), paired(col2, COL, 2))
     shares, arrived = lax.optimization_barrier((plane_shares(keep, send), arrived))
-    sums = side_sum(row1, *arrived, row_end)
-    payloads = column_payloads(sums)
-    arrived = column_transfers(payloads)
+    sums = side_sum(col1, *arrived, col_end)
+    payloads = row_payloads(sums)
+    arrived = row_transfers(payloads)
     shares, arrived = lax.optimization_barrier((depth_shares(after(shares, *payloads)), arrived))
     strip = updated_strip(strip, sums, arrived, peak)
-    sides = (paired(strip, ROW, 0), paired(strip, ROW, 2))
+    sides = (paired(strip, COL, 0), paired(strip, COL, 2))
     mine, sides = lax.optimization_barrier((gathered(after(shares, strip), keep.shape), sides))
     totals = (mine, core_swap(mine))
 
@@ -387,7 +400,7 @@
     payloads = (jnp.where(odd, sums[0], sums[2]), jnp.where(odd, sums[2], sums[0]))
     shares = after(plane_shares(keep, send), *payloads)
     grad = side_sum(sums[1], paired(payloads[0], COL, 0), paired(payloads[1], COL, 2), col_end)
-    new_object = (strip[1] - grad / peak).reshape(object_field.shape)
+    new_object = (strip[:, TILES : 2 * TILES] - grad / peak).reshape(object_field.shape)
     mine = gathered(after(depth_shares(shares), new_object), keep.shape)
     return (new_object, last_probe(probe, mine, core_swap(mine)))
 

time: 145 us -> 145 us (level)
  Pallas kernels: 22 us -> 13.9 us
  starting transfers between devices: 51.4 us -> 55.3 us
  waiting for transfers between devices: 38.9 us -> 42.2 us
  blocking collectives: 23.5 us -> 26.7 us
    pallas_call x2, Pallas kernels: 20.8 us -> 12.7 us  [gradients(): pl.pallas_call(functools.partial(gradient_kernel, first), out_shape=(col_...]
    ppermute x14, starting transfers between devices: 21.2 us -> 26.1 us  [paired(): return lax.ppermute(value, axes, pairs)]
    ppermute x4, starting transfers between devices: 8.71 us -> 13.3 us  [core_swap(): return lax.ppermute(value, 'core', [(0, 1), (1, 0)])]
    ppermute x2, starting transfers between devices: 5.52 us -> 1.26 us  [paired_far(): return lax.ppermute(value, axes, pairs)]
    ppermute x14, waiting for transfers between devices: 11.6 us -> 15.8 us  [paired(): return lax.ppermute(value, axes, pairs)]
    all_to_all x2, blocking collectives: 23.5 us -> 26.7 us  [exchange(): return lax.all_to_all(value, axes, 0, 0, tiled=True)]
    ppermute x2, waiting for transfers between devices: 6.89 us -> 4.84 us  [paired_far(): return lax.ppermute(value, axes, pairs)]
    all_to_all x4, waiting for transfers between devices: 16.2 us -> 18 us  [exchange(): return lax.all_to_all(value, axes, 0, 0, tiled=True)]
  transfers between devices with their start and end apart: 24 -> 24, of which waited for: 14 -> 13; matrix products, arithmetic and copies ran while one was open for 4% -> 3% of each run, Pallas kernels for 0% -> 0%
where the time goes in v8:
time: 145 us
  starting transfers between devices  55.3 us (38%)
  waiting for transfers between devices  42.2 us (29%)
  blocking collectives  26.7 us (18%)
  Pallas kernels  13.9 us (10%)
  other arithmetic  3.59 us (2%)
  local copies, waits for them, and re-layouts  2.05 us (1%)
  between operations  1.47 us (1%)
    all_to_all x2, blocking collectives, exchange(): return lax.all_to_all(value, axes, 0, 0, tiled=True)  26.7 us
    ppermute x14, starting transfers between devices, paired(): return lax.ppermute(value, axes, pairs)  26.1 us
    all_to_all x4, waiting for transfers between devices, exchange(): return lax.all_to_all(value, axes, 0, 0, tiled=True)  18 us
    ppermute x14, waiting for transfers between devices, paired(): return lax.ppermute(value, axes, pairs)  15.8 us
    all_to_all x4, starting transfers between devices, exchange(): return lax.all_to_all(value, axes, 0, 0, tiled=True)  14.6 us
    ppermute x4, starting transfers between devices, core_swap(): return lax.ppermute(value, 'core', [(0, 1), (1, 0)])  13.3 us
    pallas_call x2, Pallas kernels, gradients(): pl.pallas_call(functools.partial(gradient_kernel, first), out_shape=(col_...  12.7 us
    ppermute x2, waiting for transfers between devices, paired_far(): return lax.ppermute(value, axes, pairs)  4.84 us
  transfers between devices with their start and end apart: 24, of which 13 were waited for; matrix products, arithmetic and copies ran while one was open for 3% of the time, Pallas kernels for 0%

profile of v8, /device:TPU:1, one launch (start us, length us, event | category | flops | bytes accessed | tf_op | source)
XLA Modules:
  0.0 145.1 jit_solution(2142279440655575184)
XLA Ops:
  0.6 8.7 %collective-permute-start.1 = (f32[2,16,8,128]{3,2,1,0:T(8,128)}, f32[2,16,8,128]{3,2,1,0:T(8,128)S(1)}, u32[]{:S(2)}, u32[]{:S(2)}) collective-permute-start(f32[2,16,8,128]{3,2,1,0:T(8,128)} %bitcast.40), channel_id=1, source_target_pairs={{0,31},{1,2},{2,1},{3,4},{4,3},{5,6},{6,5},{7,8},{8,7},{9,10},{10,... | collective-permute-start | bytes 393224 | tf_op jit(solution)/shard_map/ppermute | solution.py:42
  9.3 3.4 %collective-permute-done.1 = f32[2,16,8,128]{3,2,1,0:T(8,128)S(1)} collective-permute-done((f32[2,16,8,128]{3,2,1,0:T(8,128)}, f32[2,16,8,128]{3,2,1,0:T(8,128)S(1)}, u32[]{:S(2)}, u32[]{:S(2)}) %collective-permute-start.1) | collective-permute-done | bytes 131104 | tf_op jit(solution)/shard_map/ppermute | solution.py:42
  14.5 3.1 %collective-permute-start.3 = (f32[3,2,16,8,128]{4,3,2,1,0:T(8,128)S(1)}, f32[3,2,16,8,128]{4,3,2,1,0:T(8,128)S(1)}, u32[]{:S(2)}, u32[]{:S(2)}) collective-permute-start(f32[3,2,16,8,128]{4,3,2,1,0:T(8,128)S(1)} %pad_maximum_fusion.refs_5_), channel_id=1, source_target_pairs={{0,224},{32,64},{64,32},{96,128},{128,96},{160,192},{192,160},{224... | collective-permute-start | bytes 1179656 | tf_op jit(solution)/shard_map/ppermute | solution.py:42
  19.1 4.3 %collective-permute-done.3.refs_7_ = f32[3,2,16,8,128]{4,3,2,1,0:T(8,128)S(1)} collective-permute-done((f32[3,2,16,8,128]{4,3,2,1,0:T(8,128)S(1)}, f32[3,2,16,8,128]{4,3,2,1,0:T(8,128)S(1)}, u32[]{:S(2)}, u32[]{:S(2)}) %collective-permute-start.3) | collective-permute-done | bytes 393248 | tf_op jit(solution)/shard_map/ppermute | solution.py:42
  23.4 5.8 %shard_map.86 = (f32[2,48,8,128]{3,2,1,0:T(8,128)S(1)}, f32[2,48,8,128]{3,2,1,0:T(8,128)S(1)}, f32[2,48,8,128]{3,2,1,0:T(8,128)S(1)}, f32[2,256,128]{2,1,0:T(8,1...) custom-call(s32[3,8]{1,0:T(4,128)S(1)} %concatenate.6.refs_0_, ...), custom_call_target="tpu_custom_call" | custom-call | tf_op jit(solution)/shard_map/pallas_call | solution.py:250
  29.2 5.4 %collective-permute-start.4 = (f32[2,256,128]{2,1,0:T(8,128)S(1)}, f32[2,256,128]{2,1,0:T(8,128)S(1)}, u32[]{:S(2)}, u32[]{:S(2)}) collective-permute-start(f32[2,256,128]{2,1,0:T(8,128)S(1)} %get-tuple-element.34), channel_id=1, source_target_pairs={{0,32},{32,0},{1,33},{33,1},{2,34},{34,2},{3,35},{35,3},{4,36},{36... | collective-permute-start | bytes 786440 | tf_op jit(solution)/shard_map/ppermute | solution.py:278
  34.8 3.2 %collective-permute-start.6 = (f32[2,48,8,128]{3,2,1,0:T(8,128)S(1)}, f32[2,48,8,128]{3,2,1,0:T(8,128)S(1)}, u32[]{:S(2)}, u32[]{:S(2)}) collective-permute-start(f32[2,48,8,128]{3,2,1,0:T(8,128)S(1)} %get-tuple-element.36), channel_id=1, source_target_pairs={{0,31},{1,2},{2,1},{3,4},{4,3},{5,6},{6,5},{7,8},{8,7},{9,10},{10,... | collective-permute-start | bytes 1179656 | tf_op jit(solution)/shard_map/ppermute | solution.py:42
  38.7 3.5 %all-to-all-start = ((f32[16,32,128]{2,1,0:T(8,128)}), f32[16,32,128]{2,1,0:T(8,128)S(1)}, u32[]{:S(2)}, u32[]{:S(2)}) async-start(f32[16,32,128]{2,1,0:T(8,128)} %bitcast.8), calls=%async_computation | async-start | bytes 524288 | tf_op jit(solution)/shard_map/all_to_all | solution.py:274
  42.2 3.0 %collective-permute-done.5 = f32[2,48,8,128]{3,2,1,0:T(8,128)S(1)} collective-permute-done((f32[2,48,8,128]{3,2,1,0:T(8,128)S(1)}, f32[2,48,8,128]{3,2,1,0:T(8,128)S(1)}, u32[]{:S(2)}, u32[]{:S(2)}) %collective-permute-start.5) | collective-permute-done | bytes 393248 | tf_op jit(solution)/shard_map/ppermute | solution.py:42
  45.3 4.2 %collective-permute-done.6 = f32[2,48,8,128]{3,2,1,0:T(8,128)S(1)} collective-permute-done((f32[2,48,8,128]{3,2,1,0:T(8,128)S(1)}, f32[2,48,8,128]{3,2,1,0:T(8,128)S(1)}, u32[]{:S(2)}, u32[]{:S(2)}) %collective-permute-start.6) | collective-permute-done | bytes 393248 | tf_op jit(solution)/shard_map/ppermute | solution.py:42
  49.4 3.1 %all-to-all-done = f32[16,32,128]{2,1,0:T(8,128)S(1)} async-done(((f32[16,32,128]{2,1,0:T(8,128)}), f32[16,32,128]{2,1,0:T(8,128)S(1)}, u32[]{:S(2)}, u32[]{:S(2)}) %all-to-all-start) | async-done | bytes 262176 | tf_op jit(solution)/shard_map/all_to_all | solution.py:274
  52.6 1.0 collective-permute-start.8
  55.3 3.5 %all-to-all-start.1 = ((f32[8,32,128]{2,1,0:T(8,128)}), f32[8,32,128]{2,1,0:T(8,128)S(1)}, u32[]{:S(2)}, u32[]{:S(2)}) async-start(f32[8,32,128]{2,1,0:T(8,128)} %broadcast_in_dim.44), calls=%async_computation.1 | async-start | bytes 262144 | tf_op jit(solution)/shard_map/all_to_all | solution.py:274
  58.8 1.3 collective-permute-start.10
  60.0 4.8 %collective-permute-done.10 = f32[2,16,8,128]{3,2,1,0:T(8,128)S(1)} collective-permute-done((f32[2,16,8,128]{3,2,1,0:T(8,128)S(1)}, f32[2,16,8,128]{3,2,1,0:T(8,128)S(1)}, u32[]{:S(2)}, u32[]{:S(2)}) %collective-permute-start.10) | collective-permute-done | bytes 131104 | tf_op jit(solution)/shard_map/ppermute | solution.py:48
  64.9 2.4 %all-to-all-done.1 = f32[8,32,128]{2,1,0:T(8,128)S(1)} async-done(((f32[8,32,128]{2,1,0:T(8,128)}), f32[8,32,128]{2,1,0:T(8,128)S(1)}, u32[]{:S(2)}, u32[]{:S(2)}) %all-to-all-start.1) | async-done | bytes 131104 | tf_op jit(solution)/shard_map/all_to_all | solution.py:274
  67.5 1.3 collective-permute-start.12
  68.8 15.9 %all_to_all.30 = f32[16,32,128]{2,1,0:T(8,128)S(1)} all-to-all(f32[16,32,128]{2,1,0:T(8,128)S(1)} %broadcast_in_dim.46), channel_id=1, replica_groups=mesh['y'=4,'core'=2,'z'=8,'x'=4] {'y','x'}, dimensions={0} | all-to-all | bytes 524288 | tf_op jit(solution)/shard_map/all_to_all | solution.py:274
  85.2 1.2 collective-permute-done.13.refs_9_
  86.4 6.9 %shard_map.87 = (f32[3,2,16,8,128]{4,3,2,1,0:T(8,128)S(1)}, f32[3,2,16,8,128]{4,3,2,1,0:T(8,128)S(1)}, f32[3,2,16,8,128]{4,3,2,1,0:T(8,128)S(1)}, f32[2,256,128]...) custom-call(s32[3,8]{1,0:T(4,128)S(1)} %concatenate.6.refs_0_, ...), custom_call_target="tpu_custom_call" | custom-call | tf_op jit(solution)/shard_map/pallas_call | solution.py:250
  93.3 4.3 %collective-permute-start.14 = (f32[3,2,16,8,128]{4,3,2,1,0:T(8,128)S(1)}, f32[3,2,16,8,128]{4,3,2,1,0:T(8,128)S(1)}, u32[]{:S(2)}, u32[]{:S(2)}) collective-permute-start(f32[3,2,16,8,128]{4,3,2,1,0:T(8,128)S(1)} %get-tuple-element.52), channel_id=1, source_target_pairs={{0,32},{32,0},{64,96},{96,64},{128,160},{160,128},{192,224},{224,1... | collective-permute-start | bytes 1179656 | tf_op jit(solution)/shard_map/ppermute | solution.py:42
  97.9 2.2 %collective-permute-start.18 = (f32[2,256,128]{2,1,0:T(8,128)S(1)}, f32[2,256,128]{2,1,0:T(8,128)S(1)}, u32[]{:S(2)}, u32[]{:S(2)}) collective-permute-start(f32[2,256,128]{2,1,0:T(8,128)S(1)} %get-tuple-element.57), channel_id=1, source_target_pairs={{0,32},{32,0},{1,33},{33,1},{2,34},{34,2},{3,35},{35,3},{4,36},{36... | collective-permute-start | bytes 786440 | tf_op jit(solution)/shard_map/ppermute | solution.py:278
  100.1 1.2 collective-permute-done.18
  102.0 3.5 %all-to-all-start.3 = ((f32[16,32,128]{2,1,0:T(8,128)}), f32[16,32,128]{2,1,0:T(8,128)S(1)}, u32[]{:S(2)}, u32[]{:S(2)}) async-start(f32[16,32,128]{2,1,0:T(8,128)} %bitcast.14), calls=%async_computation.3 | async-start | bytes 524288 | tf_op jit(solution)/shard_map/all_to_all | solution.py:274
  105.7 3.0 %collective-permute-start.17 = (f32[2,16,8,128]{3,2,1,0:T(8,128)S(1)}, f32[2,16,8,128]{3,2,1,0:T(8,128)S(1)}, u32[]{:S(2)}, u32[]{:S(2)}) collective-permute-start(f32[2,16,8,128]{3,2,1,0:T(8,128)S(1)} %get-tuple-element.65), channel_id=1, source_target_pairs={{0,31},{1,2},{2,1},{3,4},{4,3},{5,6},{6,5},{7,8},{8,7},{9,10},{10,... | collective-permute-start | bytes 393224 | tf_op jit(solution)/shard_map/ppermute | solution.py:42
  108.7 5.2 %all-to-all-done.3 = f32[16,32,128]{2,1,0:T(8,128)S(1)} async-done(((f32[16,32,128]{2,1,0:T(8,128)}), f32[16,32,128]{2,1,0:T(8,128)S(1)}, u32[]{:S(2)}, u32[]{:S(2)}) %all-to-all-start.3) | async-done | bytes 262176 | tf_op jit(solution)/shard_map/all_to_all | solution.py:274
  114.6 4.1 %all-to-all-start.4 = ((f32[8,32,128]{2,1,0:T(8,128)}), f32[8,32,128]{2,1,0:T(8,128)S(1)}, u32[]{:S(2)}, u32[]{:S(2)}) async-start(f32[8,32,128]{2,1,0:T(8,128)} %broadcast_in_dim.48), calls=%async_computation.4 | async-start | bytes 262144 | tf_op jit(solution)/shard_map/all_to_all | solution.py:274
  119.4 7.3 %all-to-all-done.4 = f32[8,32,128]{2,1,0:T(8,128)S(1)} async-done(((f32[8,32,128]{2,1,0:T(8,128)}), f32[8,32,128]{2,1,0:T(8,128)S(1)}, u32[]{:S(2)}, u32[]{:S(2)}) %all-to-all-start.4) | async-done | bytes 131104 | tf_op jit(solution)/shard_map/all_to_all | solution.py:274
  126.8 10.8 %all_to_all.31 = f32[16,32,128]{2,1,0:T(8,128)S(1)} all-to-all(f32[16,32,128]{2,1,0:T(8,128)S(1)} %broadcast_in_dim.49), channel_id=1, replica_groups=mesh['y'=4,'core'=2,'z'=8,'x'=4] {'y','x'}, dimensions={0} | all-to-all | bytes 524288 | tf_op jit(solution)/shard_map/all_to_all | solution.py:274
  137.5 5.2 %collective-permute-start.19 = (f32[2,256,128]{2,1,0:T(8,128)S(1)}, f32[2,256,128]{2,1,0:T(8,128)S(1)}, u32[]{:S(2)}, u32[]{:S(2)}) collective-permute-start(f32[2,256,128]{2,1,0:T(8,128)S(1)} %bitcast.36), channel_id=1, source_target_pairs={{0,32},{32,0},{1,33},{33,1},{2,34},{34,2},{3,35},{35,3},{4,36},{36... | collective-permute-start | bytes 786440 | tf_op jit(solution)/shard_map/ppermute | solution.py:278
  142.8 1.2 collective-permute-done.19.other_ref
  143.9 1.2 shard_map.88
  (45 shorter events, 8.5 us)
Async XLA Ops:
  0.6 12.1 %collective-permute-start.1 = (f32[2,16,8,128]{3,2,1,0:T(8,128)}, f32[2,16,8,128]{3,2,1,0:T(8,128)S(1)}, u32[]{:S(2)}, u32[]{:S(2)}) collective-permute-start(f32[2,16,8,128]{3,2,1,0:T(8,128)} %bitcast.40), channel_id=1, source_target_pairs={{0,31},{1,2},{2,1},{3,4},{4,3},{5,6},{6,5},{7,8},{8,7},{9,10},{10,... | collective-permute-start | bytes 393224 | tf_op jit(solution)/shard_map/ppermute | solution.py:42
  9.3 4.3 %collective-permute-start = (f32[2,16,8,128]{3,2,1,0:T(8,128)}, f32[2,16,8,128]{3,2,1,0:T(8,128)S(1)}, u32[]{:S(2)}, u32[]{:S(2)}) collective-permute-start(f32[2,16,8,128]{3,2,1,0:T(8,128)} %bitcast.41), channel_id=1, source_target_pairs={{0,1},{1,0},{2,3},{3,2},{4,5},{5,4},{6,7},{7,6},{8,9},{9,8},{10,11... | collective-permute-start | bytes 393224 | tf_op jit(solution)/shard_map/ppermute | solution.py:42
  14.5 8.9 %collective-permute-start.3 = (f32[3,2,16,8,128]{4,3,2,1,0:T(8,128)S(1)}, f32[3,2,16,8,128]{4,3,2,1,0:T(8,128)S(1)}, u32[]{:S(2)}, u32[]{:S(2)}) collective-permute-start(f32[3,2,16,8,128]{4,3,2,1,0:T(8,128)S(1)} %pad_maximum_fusion.refs_5_), channel_id=1, source_target_pairs={{0,224},{32,64},{64,32},{96,128},{128,96},{160,192},{192,160},{224... | collective-permute-start | bytes 1179656 | tf_op jit(solution)/shard_map/ppermute | solution.py:42
  17.7 5.8 %collective-permute-start.2 = (f32[3,2,16,8,128]{4,3,2,1,0:T(8,128)S(1)}, f32[3,2,16,8,128]{4,3,2,1,0:T(8,128)S(1)}, u32[]{:S(2)}, u32[]{:S(2)}) collective-permute-start(f32[3,2,16,8,128]{4,3,2,1,0:T(8,128)S(1)} %pad_maximum_fusion.refs_5_), channel_id=1, source_target_pairs={{0,32},{32,0},{64,96},{96,64},{128,160},{160,128},{192,224},{224,1... | collective-permute-start | bytes 1179656 | tf_op jit(solution)/shard_map/ppermute | solution.py:42
  29.2 8.7 %collective-permute-start.4 = (f32[2,256,128]{2,1,0:T(8,128)S(1)}, f32[2,256,128]{2,1,0:T(8,128)S(1)}, u32[]{:S(2)}, u32[]{:S(2)}) collective-permute-start(f32[2,256,128]{2,1,0:T(8,128)S(1)} %get-tuple-element.34), channel_id=1, source_target_pairs={{0,32},{32,0},{1,33},{33,1},{2,34},{34,2},{3,35},{35,3},{4,36},{36... | collective-permute-start | bytes 786440 | tf_op jit(solution)/shard_map/ppermute | solution.py:278
  34.6 10.7 %collective-permute-start.5 = (f32[2,48,8,128]{3,2,1,0:T(8,128)S(1)}, f32[2,48,8,128]{3,2,1,0:T(8,128)S(1)}, u32[]{:S(2)}, u32[]{:S(2)}) collective-permute-start(f32[2,48,8,128]{3,2,1,0:T(8,128)S(1)} %get-tuple-element.35), channel_id=1, source_target_pairs={{0,1},{1,0},{2,3},{3,2},{4,5},{5,4},{6,7},{7,6},{8,9},{9,8},{10,11... | collective-permute-start | bytes 1179656 | tf_op jit(solution)/shard_map/ppermute | solution.py:42
  34.8 14.7 %collective-permute-start.6 = (f32[2,48,8,128]{3,2,1,0:T(8,128)S(1)}, f32[2,48,8,128]{3,2,1,0:T(8,128)S(1)}, u32[]{:S(2)}, u32[]{:S(2)}) collective-permute-start(f32[2,48,8,128]{3,2,1,0:T(8,128)S(1)} %get-tuple-element.36), channel_id=1, source_target_pairs={{0,31},{1,2},{2,1},{3,4},{4,3},{5,6},{6,5},{7,8},{8,7},{9,10},{10,... | collective-permute-start | bytes 1179656 | tf_op jit(solution)/shard_map/ppermute | solution.py:42
  38.7 13.8 %all-to-all-start = ((f32[16,32,128]{2,1,0:T(8,128)}), f32[16,32,128]{2,1,0:T(8,128)S(1)}, u32[]{:S(2)}, u32[]{:S(2)}) async-start(f32[16,32,128]{2,1,0:T(8,128)} %bitcast.8), calls=%async_computation | async-start | bytes 524288 | tf_op jit(solution)/shard_map/all_to_all | solution.py:274
  52.6 14.7 %collective-permute-start.8 = (f32[2,32,8,128]{3,2,1,0:T(8,128)S(1)}, f32[2,32,8,128]{3,2,1,0:T(8,128)S(1)}, u32[]{:S(2)}, u32[]{:S(2)}) collective-permute-start(f32[2,32,8,128]{3,2,1,0:T(8,128)S(1)} %get-tuple-element.69), channel_id=1, source_target_pairs={{0,224},{32,64},{64,32},{96,128},{128,96},{160,192},{192,160},{224... | collective-permute-start | bytes 786440 | tf_op jit(solution)/shard_map/ppermute | solution.py:42
  53.6 13.6 %collective-permute-start.7 = (f32[2,32,8,128]{3,2,1,0:T(8,128)S(1)}, f32[2,32,8,128]{3,2,1,0:T(8,128)S(1)}, u32[]{:S(2)}, u32[]{:S(2)}) collective-permute-start(f32[2,32,8,128]{3,2,1,0:T(8,128)S(1)} %get-tuple-element.70), channel_id=1, source_target_pairs={{0,32},{32,0},{64,96},{96,64},{128,160},{160,128},{192,224},{224,1... | collective-permute-start | bytes 786440 | tf_op jit(solution)/shard_map/ppermute | solution.py:42
  55.3 12.0 %all-to-all-start.1 = ((f32[8,32,128]{2,1,0:T(8,128)}), f32[8,32,128]{2,1,0:T(8,128)S(1)}, u32[]{:S(2)}, u32[]{:S(2)}) async-start(f32[8,32,128]{2,1,0:T(8,128)} %broadcast_in_dim.44), calls=%async_computation.1 | async-start | bytes 262144 | tf_op jit(solution)/shard_map/all_to_all | solution.py:274
  58.8 6.1 %collective-permute-start.10 = (f32[2,16,8,128]{3,2,1,0:T(8,128)S(1)}, f32[2,16,8,128]{3,2,1,0:T(8,128)S(1)}, u32[]{:S(2)}, u32[]{:S(2)}) collective-permute-start(f32[2,16,8,128]{3,2,1,0:T(8,128)S(1)} %get-tuple-element.67), channel_id=1, source_target_pairs={{0,192},{32,224},{64,128},{96,160},{128,64},{160,96},{192,0},{224,... | collective-permute-start | bytes 393224 | tf_op jit(solution)/shard_map/ppermute | solution.py:48
  60.0 4.8 %collective-permute-start.9 = (f32[2,16,8,128]{3,2,1,0:T(8,128)S(1)}, f32[2,16,8,128]{3,2,1,0:T(8,128)S(1)}, u32[]{:S(2)}, u32[]{:S(2)}) collective-permute-start(f32[2,16,8,128]{3,2,1,0:T(8,128)S(1)} %get-tuple-element.68), channel_id=1, source_target_pairs={{0,64},{32,96},{64,0},{96,32},{128,192},{160,224},{192,128},{224,1... | collective-permute-start | bytes 393224 | tf_op jit(solution)/shard_map/ppermute | solution.py:48
  67.5 17.3 %collective-permute-start.12 = (f32[2,48,8,128]{3,2,1,0:T(8,128)S(1)}, f32[2,48,8,128]{3,2,1,0:T(8,128)S(1)}, u32[]{:S(2)}, u32[]{:S(2)}) collective-permute-start(f32[2,48,8,128]{3,2,1,0:T(8,128)S(1)} %pad_maximum_fusion.1.refs_5_), channel_id=1, source_target_pairs={{0,31},{1,2},{2,1},{3,4},{4,3},{5,6},{6,5},{7,8},{8,7},{9,10},{10,... | collective-permute-start | bytes 1179656 | tf_op jit(solution)/shard_map/ppermute | solution.py:42
  68.8 16.0 %collective-permute-start.11 = (f32[2,48,8,128]{3,2,1,0:T(8,128)S(1)}, f32[2,48,8,128]{3,2,1,0:T(8,128)S(1)}, u32[]{:S(2)}, u32[]{:S(2)}) collective-permute-start(f32[2,48,8,128]{3,2,1,0:T(8,128)S(1)} %pad_maximum_fusion.1.refs_5_), channel_id=1, source_target_pairs={{0,1},{1,0},{2,3},{3,2},{4,5},{5,4},{6,7},{7,6},{8,9},{9,8},{10,11... | collective-permute-start | bytes 1179656 | tf_op jit(solution)/shard_map/ppermute | solution.py:42
  84.7 1.7 %collective-permute-start.13 = (f32[2,256,128]{2,1,0:T(8,128)S(1)}, f32[2,256,128]{2,1,0:T(8,128)S(1)}, u32[]{:S(2)}, u32[]{:S(2)}) collective-permute-start(f32[2,256,128]{2,1,0:T(8,128)S(1)} %bitcast.34), channel_id=1, source_target_pairs={{0,32},{32,0},{1,33},{33,1},{2,34},{34,2},{3,35},{35,3},{4,36},{36... | collective-permute-start | bytes 786440 | tf_op jit(solution)/shard_map/ppermute | solution.py:278
  93.3 12.2 %collective-permute-start.14 = (f32[3,2,16,8,128]{4,3,2,1,0:T(8,128)S(1)}, f32[3,2,16,8,128]{4,3,2,1,0:T(8,128)S(1)}, u32[]{:S(2)}, u32[]{:S(2)}) collective-permute-start(f32[3,2,16,8,128]{4,3,2,1,0:T(8,128)S(1)} %get-tuple-element.52), channel_id=1, source_target_pairs={{0,32},{32,0},{64,96},{96,64},{128,160},{160,128},{192,224},{224,1... | collective-permute-start | bytes 1179656 | tf_op jit(solution)/shard_map/ppermute | solution.py:42
  97.6 8.0 %collective-permute-start.15 = (f32[3,2,16,8,128]{4,3,2,1,0:T(8,128)S(1)}, f32[3,2,16,8,128]{4,3,2,1,0:T(8,128)S(1)}, u32[]{:S(2)}, u32[]{:S(2)}) collective-permute-start(f32[3,2,16,8,128]{4,3,2,1,0:T(8,128)S(1)} %get-tuple-element.53), channel_id=1, source_target_pairs={{0,224},{32,64},{64,32},{96,128},{128,96},{160,192},{192,160},{224... | collective-permute-start | bytes 1179656 | tf_op jit(solution)/shard_map/ppermute | solution.py:42
  97.9 3.4 %collective-permute-start.18 = (f32[2,256,128]{2,1,0:T(8,128)S(1)}, f32[2,256,128]{2,1,0:T(8,128)S(1)}, u32[]{:S(2)}, u32[]{:S(2)}) collective-permute-start(f32[2,256,128]{2,1,0:T(8,128)S(1)} %get-tuple-element.57), channel_id=1, source_target_pairs={{0,32},{32,0},{1,33},{33,1},{2,34},{34,2},{3,35},{35,3},{4,36},{36... | collective-permute-start | bytes 786440 | tf_op jit(solution)/shard_map/ppermute | solution.py:278
  102.0 11.9 %all-to-all-start.3 = ((f32[16,32,128]{2,1,0:T(8,128)}), f32[16,32,128]{2,1,0:T(8,128)S(1)}, u32[]{:S(2)}, u32[]{:S(2)}) async-start(f32[16,32,128]{2,1,0:T(8,128)} %bitcast.14), calls=%async_computation.3 | async-start | bytes 524288 | tf_op jit(solution)/shard_map/all_to_all | solution.py:274
  105.5 38.4 %copy-start = (f32[2,2,256,128]{3,2,1,0:T(8,128)S(1)}, f32[2,2,256,128]{3,2,1,0:T(8,128)}, u32[]{:S(2)}) copy-start(f32[2,2,256,128]{3,2,1,0:T(8,128)} %get-tuple-element.55.probe_ref) | copy-start | bytes 1572868
  105.7 13.0 %collective-permute-start.17 = (f32[2,16,8,128]{3,2,1,0:T(8,128)S(1)}, f32[2,16,8,128]{3,2,1,0:T(8,128)S(1)}, u32[]{:S(2)}, u32[]{:S(2)}) collective-permute-start(f32[2,16,8,128]{3,2,1,0:T(8,128)S(1)} %get-tuple-element.65), channel_id=1, source_target_pairs={{0,31},{1,2},{2,1},{3,4},{4,3},{5,6},{6,5},{7,8},{8,7},{9,10},{10,... | collective-permute-start | bytes 393224 | tf_op jit(solution)/shard_map/ppermute | solution.py:42
  108.7 10.0 %collective-permute-start.16 = (f32[2,16,8,128]{3,2,1,0:T(8,128)S(1)}, f32[2,16,8,128]{3,2,1,0:T(8,128)S(1)}, u32[]{:S(2)}, u32[]{:S(2)}) collective-permute-start(f32[2,16,8,128]{3,2,1,0:T(8,128)S(1)} %get-tuple-element.66), channel_id=1, source_target_pairs={{0,1},{1,0},{2,3},{3,2},{4,5},{5,4},{6,7},{7,6},{8,9},{9,8},{10,11... | collective-permute-start | bytes 393224 | tf_op jit(solution)/shard_map/ppermute | solution.py:42
  114.6 12.1 %all-to-all-start.4 = ((f32[8,32,128]{2,1,0:T(8,128)}), f32[8,32,128]{2,1,0:T(8,128)S(1)}, u32[]{:S(2)}, u32[]{:S(2)}) async-start(f32[8,32,128]{2,1,0:T(8,128)} %broadcast_in_dim.48), calls=%async_computation.4 | async-start | bytes 262144 | tf_op jit(solution)/shard_map/all_to_all | solution.py:274
  137.5 6.4 %collective-permute-start.19 = (f32[2,256,128]{2,1,0:T(8,128)S(1)}, f32[2,256,128]{2,1,0:T(8,128)S(1)}, u32[]{:S(2)}, u32[]{:S(2)}) collective-permute-start(f32[2,256,128]{2,1,0:T(8,128)S(1)} %bitcast.36), channel_id=1, source_target_pairs={{0,32},{32,0},{1,33},{33,1},{2,34},{34,2},{3,35},{35,3},{4,36},{36... | collective-permute-start | bytes 786440 | tf_op jit(solution)/shard_map/ppermute | solution.py:278

commit v9 on v7

--- a/solution.py
+++ b/solution.py
@@ -54,7 +54,7 @@
 
 def updated_probe(probe, total):
     mean = jnp.sum(total * total, keepdims=True) / total.size
-    return probe - 0.3 * total / jnp.sqrt(mean + 1e-06)
+    return probe - total * (0.3 / jnp.sqrt(mean + 1e-06))
 
 
 def pattern_group(group, count, slots_ref, pattern, pattern_copy, left, right, probe, ext, gobj, keep, send):
@@ -206,7 +206,8 @@
         mine, other = mine_ref[...], other_ref[...]
         total = jnp.stack([jnp.where(real, mine, other), jnp.where(real, other, mine)])
         probe[...] = updated_probe(probe[...], total)
-        probe_ref[...] = probe[...]
+        probe_out = pltpu.make_async_copy(probe, probe_ref, probe_sems.at[2])
+        probe_out.start()
     power = probe[0] * probe[0] + probe[1] * probe[1]
     peak_ref[...] = jnp.broadcast_to(jnp.max(power, keepdims=True).reshape(1, 1) + 1e-06, peak_ref.shape)
     for copy in table_copies:
@@ -229,6 +230,9 @@
         @pl.when(group >= live_groups)
         def _():
             pattern_copy(group).wait()
+
+    if not first:
+        probe_out.wait()
 
 
 def gradients(first, live_slots, patterns, tables, probe, *vmem_args):
@@ -244,7 +248,7 @@
         functools.partial(gradient_kernel, first),
         out_shape=(strip,) * 3 + (half, half, jax.ShapeDtypeStruct((8, LANES), F32)) + (() if first else (both,)),
         in_specs=[smem] + [hbm] * 4 + [vmem] * len(vmem_args),
-        out_specs=(vmem,) * (6 if first else 7),
+        out_specs=(vmem,) * 6 + (() if first else (hbm,)),
         scratch_shapes=[
             pltpu.VMEM(patterns.shape, F32),
             pltpu.VMEM(tables[0].shape, jnp.bfloat16),
@@ -252,7 +256,7 @@
             pltpu.VMEM(both.shape, F32),
             ext,
             ext,
-            pltpu.SemaphoreType.DMA((2,)),
+            pltpu.SemaphoreType.DMA((3,)),
             pltpu.SemaphoreType.DMA((2,)),
             pltpu.SemaphoreType.DMA((slots // GROUP,)),
         ],
@@ -268,8 +272,7 @@
     return lax.ppermute(value, "core", [(0, 1), (1, 0)])
 
 
-def plane_shares(keep, send):
-    half = keep + core_swap(send)
+def plane_shares(half):
     return exchange(half.reshape(lax.axis_size(PLANE), -1, LANES), PLANE)
 
 
@@ -368,15 +371,17 @@
     strip = jnp.stack([jnp.where(odd, side0, side2), own, jnp.where(odd, side2, side0)])
     strips = (strip, paired(strip, ROW, 0), paired(strip, ROW, 2))
     row0, row1, row2, keep, send, peak = gradients(True, live_slots, patterns, tables, probe_field, *strips)
-    arrived = (paired(row0, ROW, 0), paired(row2, ROW, 2))
-    shares, arrived = lax.optimization_barrier((plane_shares(keep, send), arrived))
-    sums = side_sum(row1, *arrived, row_end)
+    half = keep + core_swap(send)
+    row0, row2 = after((row0, row2), half)
+    sums = side_sum(row1, paired(row0, ROW, 0), paired(row2, ROW, 2), row_end)
     payloads = column_payloads(sums)
+    shares = after(plane_shares(half), *payloads)
     arrived = column_transfers(payloads)
-    shares, arrived = lax.optimization_barrier((depth_shares(after(shares, *payloads)), arrived))
+    shares, arrived = lax.optimization_barrier((depth_shares(shares), arrived))
     strip = updated_strip(strip, sums, arrived, peak)
+    shares = after(shares, strip)
     sides = (paired(strip, ROW, 0), paired(strip, ROW, 2))
-    mine, sides = lax.optimization_barrier((gathered(after(shares, strip), keep.shape), sides))
+    mine, sides = lax.optimization_barrier((gathered(shares, keep.shape), sides))
     totals = (mine, core_swap(mine))
 
     strips = (strip,) + sides
@@ -385,7 +390,7 @@
     )
     sums = side_sum(row1, paired(row0, ROW, 0), paired(row2, ROW, 2), row_end)
     payloads = (jnp.where(odd, sums[0], sums[2]), jnp.where(odd, sums[2], sums[0]))
-    shares = after(plane_shares(keep, send), *payloads)
+    shares = after(plane_shares(keep + core_swap(send)), *payloads)
     grad = side_sum(sums[1], paired(payloads[0], COL, 0), paired(payloads[1], COL, 2), col_end)
     new_object = (strip[1] - grad / peak).reshape(object_field.shape)
     mine = gathered(after(depth_shares(shares), new_object), keep.shape)

time: 145 us -> 147 us (1.014)
  starting transfers between devices: 51.4 us -> 59.9 us
  waiting for transfers between devices: 38.9 us -> 33.4 us
    all_to_all x4, starting transfers between devices: 15.9 us -> 23.7 us  [exchange(): return lax.all_to_all(value, axes, 0, 0, tiled=True)]
    all_to_all x4, waiting for transfers between devices: 16.2 us -> 11.7 us  [exchange(): return lax.all_to_all(value, axes, 0, 0, tiled=True)]
    ppermute x2, waiting for transfers between devices: 6.89 us -> 3.76 us  [paired_far(): return lax.ppermute(value, axes, pairs)]
    ppermute x14, starting transfers between devices: 21.2 us -> 23.4 us  [paired(): return lax.ppermute(value, axes, pairs)]
    ppermute x14, waiting for transfers between devices: 11.6 us -> 13.3 us  [paired(): return lax.ppermute(value, axes, pairs)]
  transfers between devices with their start and end apart: 24 -> 24, of which waited for: 14 -> 14; matrix products, arithmetic and copies ran while one was open for 4% -> 3% of each run, Pallas kernels for 0% -> 0%
where the time goes in v9:
time: 147 us; the launch traced here: 146 us
  starting transfers between devices  59.9 us (41%)
  waiting for transfers between devices  33.4 us (23%)
  blocking collectives  23.6 us (16%)
  Pallas kernels  21.2 us (14%)
  other arithmetic  4.7 us (3%)
  local copies, waits for them, and re-layouts  2.06 us (1%)
    all_to_all x4, starting transfers between devices, exchange(): return lax.all_to_all(value, axes, 0, 0, tiled=True)  23.7 us
    all_to_all x2, blocking collectives, exchange(): return lax.all_to_all(value, axes, 0, 0, tiled=True)  23.6 us
    ppermute x14, starting transfers between devices, paired(): return lax.ppermute(value, axes, pairs)  23.4 us
    pallas_call x2, Pallas kernels, gradients(): pl.pallas_call(functools.partial(gradient_kernel, first), out_shape=(stri...  20.1 us
    ppermute x14, waiting for transfers between devices, paired(): return lax.ppermute(value, axes, pairs)  13.3 us
    all_to_all x4, waiting for transfers between devices, exchange(): return lax.all_to_all(value, axes, 0, 0, tiled=True)  11.7 us
    ppermute x4, starting transfers between devices, core_swap(): return lax.ppermute(value, 'core', [(0, 1), (1, 0)])  8.62 us
    ppermute x4, waiting for transfers between devices, core_swap(): return lax.ppermute(value, 'core', [(0, 1), (1, 0)])  4.65 us
  transfers between devices with their start and end apart: 24, of which 14 were waited for; matrix products, arithmetic and copies ran while one was open for 3% of the time, Pallas kernels for 0%

profile of v9, /device:TPU:1, one launch (start us, length us, event | category | flops | bytes accessed | tf_op | source)
XLA Modules:
  0.0 146.4 jit_solution(8340666990169268960)
XLA Ops:
  0.6 8.7 %collective-permute-start.1 = (f32[2,16,8,128]{3,2,1,0:T(8,128)}, f32[2,16,8,128]{3,2,1,0:T(8,128)S(1)}, u32[]{:S(2)}, u32[]{:S(2)}) collective-permute-start(f32[2,16,8,128]{3,2,1,0:T(8,128)} %bitcast.80), channel_id=1, source_target_pairs={{0,31},{1,2},{2,1},{3,4},{4,3},{5,6},{6,5},{7,8},{8,7},{9,10},{10,... | collective-permute-start | bytes 393224 | tf_op jit(solution)/shard_map/ppermute | solution.py:42
  9.3 3.4 %collective-permute-done.1 = f32[2,16,8,128]{3,2,1,0:T(8,128)S(1)} collective-permute-done((f32[2,16,8,128]{3,2,1,0:T(8,128)}, f32[2,16,8,128]{3,2,1,0:T(8,128)S(1)}, u32[]{:S(2)}, u32[]{:S(2)}) %collective-permute-start.1) | collective-permute-done | bytes 131104 | tf_op jit(solution)/shard_map/ppermute | solution.py:42
  13.6 0.9 pad_maximum_fusion.refs_5_
  14.5 3.1 %collective-permute-start.3 = (f32[3,2,16,8,128]{4,3,2,1,0:T(8,128)S(1)}, f32[3,2,16,8,128]{4,3,2,1,0:T(8,128)S(1)}, u32[]{:S(2)}, u32[]{:S(2)}) collective-permute-start(f32[3,2,16,8,128]{4,3,2,1,0:T(8,128)S(1)} %pad_maximum_fusion.refs_5_), channel_id=1, source_target_pairs={{0,224},{32,64},{64,32},{96,128},{128,96},{160,192},{192,160},{224... | collective-permute-start | bytes 1179656 | tf_op jit(solution)/shard_map/ppermute | solution.py:42
  19.1 4.3 %collective-permute-done.3.refs_7_ = f32[3,2,16,8,128]{4,3,2,1,0:T(8,128)S(1)} collective-permute-done((f32[3,2,16,8,128]{4,3,2,1,0:T(8,128)S(1)}, f32[3,2,16,8,128]{4,3,2,1,0:T(8,128)S(1)}, u32[]{:S(2)}, u32[]{:S(2)}) %collective-permute-start.3) | collective-permute-done | bytes 393248 | tf_op jit(solution)/shard_map/ppermute | solution.py:42
  23.4 9.7 %shard_map.86 = (f32[3,2,16,8,128]{4,3,2,1,0:T(8,128)S(1)}, f32[3,2,16,8,128]{4,3,2,1,0:T(8,128)S(1)}, f32[3,2,16,8,128]{4,3,2,1,0:T(8,128)S(1)}, f32[2,256,128]...) custom-call(s32[3,8]{1,0:T(4,128)S(1)} %concatenate.3.refs_0_, f32[8,256,256]{2,1,0:T(8,128)} %bitcast.78, ...), custom_call_target="tpu_custom_call" | custom-call | tf_op jit(solution)/shard_map/pallas_call | solution.py:247
  33.1 1.5 %collective-permute-start.4 = (f32[2,256,128]{2,1,0:T(8,128)S(1)}, f32[2,256,128]{2,1,0:T(8,128)S(1)}, u32[]{:S(2)}, u32[]{:S(2)}) collective-permute-start(f32[2,256,128]{2,1,0:T(8,128)S(1)} %get-tuple-element.33), channel_id=1, source_target_pairs={{0,32},{32,0},{1,33},{33,1},{2,34},{34,2},{3,35},{35,3},{4,36},{36... | collective-permute-start | bytes 786440 | tf_op jit(solution)/shard_map/ppermute | solution.py:272
  34.6 1.2 collective-permute-done.4
  37.0 4.0 %all-to-all-start = ((f32[16,32,128]{2,1,0:T(8,128)}), f32[16,32,128]{2,1,0:T(8,128)S(1)}, u32[]{:S(2)}, u32[]{:S(2)}) async-start(f32[16,32,128]{2,1,0:T(8,128)} %bitcast.8), calls=%async_computation | async-start | bytes 524288 | tf_op jit(solution)/shard_map/all_to_all | solution.py:268
  41.0 3.7 %collective-permute-done.6 = f32[3,2,16,8,128]{4,3,2,1,0:T(8,128)S(1)} collective-permute-done((f32[3,2,16,8,128]{4,3,2,1,0:T(8,128)S(1)}, f32[3,2,16,8,128]{4,3,2,1,0:T(8,128)S(1)}, u32[]{:S(2)}, u32[]{:S(2)}) %collective-permute-start.6) | collective-permute-done | bytes 393248 | tf_op jit(solution)/shard_map/ppermute | solution.py:42
  44.9 3.0 %collective-permute-start.8 = (f32[2,2,16,8,128]{4,3,2,1,0:T(8,128)S(1)}, f32[2,2,16,8,128]{4,3,2,1,0:T(8,128)S(1)}, u32[]{:S(2)}, u32[]{:S(2)}) collective-permute-start(f32[2,2,16,8,128]{4,3,2,1,0:T(8,128)S(1)} %get-tuple-element.64), channel_id=1, source_target_pairs={{0,31},{1,2},{2,1},{3,4},{4,3},{5,6},{6,5},{7,8},{8,7},{9,10},{10,... | collective-permute-start | bytes 786440 | tf_op jit(solution)/shard_map/ppermute | solution.py:42
  49.4 9.3 %all-to-all-start.1 = ((f32[8,32,128]{2,1,0:T(8,128)}), f32[8,32,128]{2,1,0:T(8,128)S(1)}, u32[]{:S(2)}, u32[]{:S(2)}) async-start(f32[8,32,128]{2,1,0:T(8,128)} %broadcast_in_dim.41), calls=%async_computation.1 | async-start | bytes 262144 | tf_op jit(solution)/shard_map/all_to_all | solution.py:268
  58.7 4.1 %collective-permute-start.9 = (f32[2,16,8,128]{3,2,1,0:T(8,128)S(1)}, f32[2,16,8,128]{3,2,1,0:T(8,128)S(1)}, u32[]{:S(2)}, u32[]{:S(2)}) collective-permute-start(f32[2,16,8,128]{3,2,1,0:T(8,128)S(1)} %get-tuple-element.63), channel_id=1, source_target_pairs={{0,2},{1,3},{2,0},{3,1},{4,6},{5,7},{6,4},{7,5},{8,10},{9,11},{10,... | collective-permute-start | bytes 393224 | tf_op jit(solution)/shard_map/ppermute | solution.py:48
  62.9 3.5 %collective-permute-done.10 = f32[2,16,8,128]{3,2,1,0:T(8,128)S(1)} collective-permute-done((f32[2,16,8,128]{3,2,1,0:T(8,128)S(1)}, f32[2,16,8,128]{3,2,1,0:T(8,128)S(1)}, u32[]{:S(2)}, u32[]{:S(2)}) %collective-permute-start.10) | collective-permute-done | bytes 131104 | tf_op jit(solution)/shard_map/ppermute | solution.py:48
  66.9 4.9 %collective-permute-start.12 = (f32[3,2,16,8,128]{4,3,2,1,0:T(8,128)S(1)}, f32[3,2,16,8,128]{4,3,2,1,0:T(8,128)S(1)}, u32[]{:S(2)}, u32[]{:S(2)}) collective-permute-start(f32[3,2,16,8,128]{4,3,2,1,0:T(8,128)S(1)} %pad_maximum_fusion.1.refs_5_), channel_id=1, source_target_pairs={{0,224},{32,64},{64,32},{96,128},{128,96},{160,192},{192,160},{224... | collective-permute-start | bytes 1179656 | tf_op jit(solution)/shard_map/ppermute | solution.py:42
  71.9 12.5 %all_to_all.30 = f32[16,32,128]{2,1,0:T(8,128)S(1)} all-to-all(f32[16,32,128]{2,1,0:T(8,128)S(1)} %broadcast_in_dim.43), channel_id=1, replica_groups=mesh['y'=4,'core'=2,'z'=8,'x'=4] {'y','x'}, dimensions={0} | all-to-all | bytes 524288 | tf_op jit(solution)/shard_map/all_to_all | solution.py:268
  84.4 1.8 %collective-permute-start.13 = (f32[2,256,128]{2,1,0:T(8,128)S(1)}, f32[2,256,128]{2,1,0:T(8,128)S(1)}, u32[]{:S(2)}, u32[]{:S(2)}) collective-permute-start(f32[2,256,128]{2,1,0:T(8,128)S(1)} %bitcast.74), channel_id=1, source_target_pairs={{0,32},{32,0},{1,33},{33,1},{2,34},{34,2},{3,35},{35,3},{4,36},{36... | collective-permute-start | bytes 786440 | tf_op jit(solution)/shard_map/ppermute | solution.py:272
  86.2 1.2 collective-permute-done.13.refs_9_
  87.4 10.4 %shard_map.87 = (f32[3,2,16,8,128]{4,3,2,1,0:T(8,128)S(1)}, f32[3,2,16,8,128]{4,3,2,1,0:T(8,128)S(1)}, f32[3,2,16,8,128]{4,3,2,1,0:T(8,128)S(1)}, f32[2,256,128]...) custom-call(s32[3,8]{1,0:T(4,128)S(1)} %concatenate.3.refs_0_, ...), custom_call_target="tpu_custom_call" | custom-call | tf_op jit(solution)/shard_map/pallas_call | solution.py:247
  98.1 1.0 collective-permute-start.18
  99.1 1.2 collective-permute-done.18
  101.0 3.8 %all-to-all-start.3 = ((f32[16,32,128]{2,1,0:T(8,128)}), f32[16,32,128]{2,1,0:T(8,128)S(1)}, u32[]{:S(2)}, u32[]{:S(2)}) async-start(f32[16,32,128]{2,1,0:T(8,128)} %bitcast.21), calls=%async_computation.3 | async-start | bytes 524288 | tf_op jit(solution)/shard_map/all_to_all | solution.py:268
  104.8 1.0 collective-permute-done.15
  105.7 1.1 select_add_fusion
  106.9 2.7 %collective-permute-start.17 = (f32[2,16,8,128]{3,2,1,0:T(8,128)S(1)}, f32[2,16,8,128]{3,2,1,0:T(8,128)S(1)}, u32[]{:S(2)}, u32[]{:S(2)}) collective-permute-start(f32[2,16,8,128]{3,2,1,0:T(8,128)S(1)} %get-tuple-element.60), channel_id=1, source_target_pairs={{0,31},{1,2},{2,1},{3,4},{4,3},{5,6},{6,5},{7,8},{8,7},{9,10},{10,... | collective-permute-start | bytes 393224 | tf_op jit(solution)/shard_map/ppermute | solution.py:42
  109.6 3.5 %all-to-all-done.3 = f32[16,32,128]{2,1,0:T(8,128)S(1)} async-done(((f32[16,32,128]{2,1,0:T(8,128)}), f32[16,32,128]{2,1,0:T(8,128)S(1)}, u32[]{:S(2)}, u32[]{:S(2)}) %all-to-all-start.3) | async-done | bytes 262176 | tf_op jit(solution)/shard_map/all_to_all | solution.py:268
  113.8 6.7 %all-to-all-start.4 = ((f32[8,32,128]{2,1,0:T(8,128)}), f32[8,32,128]{2,1,0:T(8,128)S(1)}, u32[]{:S(2)}, u32[]{:S(2)}) async-start(f32[8,32,128]{2,1,0:T(8,128)} %broadcast_in_dim.44), calls=%async_computation.4 | async-start | bytes 262144 | tf_op jit(solution)/shard_map/all_to_all | solution.py:268
  121.2 7.3 %all-to-all-done.4 = f32[8,32,128]{2,1,0:T(8,128)S(1)} async-done(((f32[8,32,128]{2,1,0:T(8,128)}), f32[8,32,128]{2,1,0:T(8,128)S(1)}, u32[]{:S(2)}, u32[]{:S(2)}) %all-to-all-start.4) | async-done | bytes 131104 | tf_op jit(solution)/shard_map/all_to_all | solution.py:268
  128.6 11.0 %all_to_all.31 = f32[16,32,128]{2,1,0:T(8,128)S(1)} all-to-all(f32[16,32,128]{2,1,0:T(8,128)S(1)} %broadcast_in_dim.45), channel_id=1, replica_groups=mesh['y'=4,'core'=2,'z'=8,'x'=4] {'y','x'}, dimensions={0} | all-to-all | bytes 524288 | tf_op jit(solution)/shard_map/all_to_all | solution.py:268
  139.6 4.4 %collective-permute-start.19 = (f32[2,256,128]{2,1,0:T(8,128)S(1)}, f32[2,256,128]{2,1,0:T(8,128)S(1)}, u32[]{:S(2)}, u32[]{:S(2)}) collective-permute-start(f32[2,256,128]{2,1,0:T(8,128)S(1)} %bitcast.76), channel_id=1, source_target_pairs={{0,32},{32,0},{1,33},{33,1},{2,34},{34,2},{3,35},{35,3},{4,36},{36... | collective-permute-start | bytes 786440 | tf_op jit(solution)/shard_map/ppermute | solution.py:272
  144.0 1.2 collective-permute-done.19.other_ref
  145.2 1.2 shard_map.88
  (50 shorter events, 7.7 us)
Async XLA Ops:
  0.6 12.1 %collective-permute-start.1 = (f32[2,16,8,128]{3,2,1,0:T(8,128)}, f32[2,16,8,128]{3,2,1,0:T(8,128)S(1)}, u32[]{:S(2)}, u32[]{:S(2)}) collective-permute-start(f32[2,16,8,128]{3,2,1,0:T(8,128)} %bitcast.80), channel_id=1, source_target_pairs={{0,31},{1,2},{2,1},{3,4},{4,3},{5,6},{6,5},{7,8},{8,7},{9,10},{10,... | collective-permute-start | bytes 393224 | tf_op jit(solution)/shard_map/ppermute | solution.py:42
  9.3 4.3 %collective-permute-start = (f32[2,16,8,128]{3,2,1,0:T(8,128)}, f32[2,16,8,128]{3,2,1,0:T(8,128)S(1)}, u32[]{:S(2)}, u32[]{:S(2)}) collective-permute-start(f32[2,16,8,128]{3,2,1,0:T(8,128)} %bitcast.81), channel_id=1, source_target_pairs={{0,1},{1,0},{2,3},{3,2},{4,5},{5,4},{6,7},{7,6},{8,9},{9,8},{10,11... | collective-permute-start | bytes 393224 | tf_op jit(solution)/shard_map/ppermute | solution.py:42
  14.5 8.9 %collective-permute-start.3 = (f32[3,2,16,8,128]{4,3,2,1,0:T(8,128)S(1)}, f32[3,2,16,8,128]{4,3,2,1,0:T(8,128)S(1)}, u32[]{:S(2)}, u32[]{:S(2)}) collective-permute-start(f32[3,2,16,8,128]{4,3,2,1,0:T(8,128)S(1)} %pad_maximum_fusion.refs_5_), channel_id=1, source_target_pairs={{0,224},{32,64},{64,32},{96,128},{128,96},{160,192},{192,160},{224... | collective-permute-start | bytes 1179656 | tf_op jit(solution)/shard_map/ppermute | solution.py:42
  17.7 5.8 %collective-permute-start.2 = (f32[3,2,16,8,128]{4,3,2,1,0:T(8,128)S(1)}, f32[3,2,16,8,128]{4,3,2,1,0:T(8,128)S(1)}, u32[]{:S(2)}, u32[]{:S(2)}) collective-permute-start(f32[3,2,16,8,128]{4,3,2,1,0:T(8,128)S(1)} %pad_maximum_fusion.refs_5_), channel_id=1, source_target_pairs={{0,32},{32,0},{64,96},{96,64},{128,160},{160,128},{192,224},{224,1... | collective-permute-start | bytes 1179656 | tf_op jit(solution)/shard_map/ppermute | solution.py:42
  33.1 2.7 %collective-permute-start.4 = (f32[2,256,128]{2,1,0:T(8,128)S(1)}, f32[2,256,128]{2,1,0:T(8,128)S(1)}, u32[]{:S(2)}, u32[]{:S(2)}) collective-permute-start(f32[2,256,128]{2,1,0:T(8,128)S(1)} %get-tuple-element.33), channel_id=1, source_target_pairs={{0,32},{32,0},{1,33},{33,1},{2,34},{34,2},{3,35},{35,3},{4,36},{36... | collective-permute-start | bytes 786440 | tf_op jit(solution)/shard_map/ppermute | solution.py:272
  36.5 4.5 %collective-permute-start.5 = (f32[3,2,16,8,128]{4,3,2,1,0:T(8,128)S(1)}, f32[3,2,16,8,128]{4,3,2,1,0:T(8,128)S(1)}, u32[]{:S(2)}, u32[]{:S(2)}) collective-permute-start(f32[3,2,16,8,128]{4,3,2,1,0:T(8,128)S(1)} %get-tuple-element.34), channel_id=1, source_target_pairs={{0,32},{32,0},{64,96},{96,64},{128,160},{160,128},{192,224},{224,1... | collective-permute-start | bytes 1179656 | tf_op jit(solution)/shard_map/ppermute | solution.py:42
  36.9 7.8 %collective-permute-start.6 = (f32[3,2,16,8,128]{4,3,2,1,0:T(8,128)S(1)}, f32[3,2,16,8,128]{4,3,2,1,0:T(8,128)S(1)}, u32[]{:S(2)}, u32[]{:S(2)}) collective-permute-start(f32[3,2,16,8,128]{4,3,2,1,0:T(8,128)S(1)} %get-tuple-element.35), channel_id=1, source_target_pairs={{0,224},{32,64},{64,32},{96,128},{128,96},{160,192},{192,160},{224... | collective-permute-start | bytes 1179656 | tf_op jit(solution)/shard_map/ppermute | solution.py:42
  37.0 11.7 %all-to-all-start = ((f32[16,32,128]{2,1,0:T(8,128)}), f32[16,32,128]{2,1,0:T(8,128)S(1)}, u32[]{:S(2)}, u32[]{:S(2)}) async-start(f32[16,32,128]{2,1,0:T(8,128)} %bitcast.8), calls=%async_computation | async-start | bytes 524288 | tf_op jit(solution)/shard_map/all_to_all | solution.py:268
  44.7 22.0 %copy-start.1 = (f32[2,128,128]{2,1,0:T(8,128)S(1)}, f32[2,128,128]{2,1,0:T(8,128)}, u32[]{:S(2)}) copy-start(f32[2,128,128]{2,1,0:T(8,128)} %param.7) | copy-start | bytes 393220
  44.9 21.8 %collective-permute-start.8 = (f32[2,2,16,8,128]{4,3,2,1,0:T(8,128)S(1)}, f32[2,2,16,8,128]{4,3,2,1,0:T(8,128)S(1)}, u32[]{:S(2)}, u32[]{:S(2)}) collective-permute-start(f32[2,2,16,8,128]{4,3,2,1,0:T(8,128)S(1)} %get-tuple-element.64), channel_id=1, source_target_pairs={{0,31},{1,2},{2,1},{3,4},{4,3},{5,6},{6,5},{7,8},{8,7},{9,10},{10,... | collective-permute-start | bytes 786440 | tf_op jit(solution)/shard_map/ppermute | solution.py:42
  47.9 18.8 %collective-permute-start.7 = (f32[2,2,16,8,128]{4,3,2,1,0:T(8,128)S(1)}, f32[2,2,16,8,128]{4,3,2,1,0:T(8,128)S(1)}, u32[]{:S(2)}, u32[]{:S(2)}) collective-permute-start(f32[2,2,16,8,128]{4,3,2,1,0:T(8,128)S(1)} %get-tuple-element.65), channel_id=1, source_target_pairs={{0,1},{1,0},{2,3},{3,2},{4,5},{5,4},{6,7},{7,6},{8,9},{9,8},{10,11... | collective-permute-start | bytes 786440 | tf_op jit(solution)/shard_map/ppermute | solution.py:42
  49.4 17.2 %all-to-all-start.1 = ((f32[8,32,128]{2,1,0:T(8,128)}), f32[8,32,128]{2,1,0:T(8,128)S(1)}, u32[]{:S(2)}, u32[]{:S(2)}) async-start(f32[8,32,128]{2,1,0:T(8,128)} %broadcast_in_dim.41), calls=%async_computation.1 | async-start | bytes 262144 | tf_op jit(solution)/shard_map/all_to_all | solution.py:268
  58.7 7.6 %collective-permute-start.10 = (f32[2,16,8,128]{3,2,1,0:T(8,128)S(1)}, f32[2,16,8,128]{3,2,1,0:T(8,128)S(1)}, u32[]{:S(2)}, u32[]{:S(2)}) collective-permute-start(f32[2,16,8,128]{3,2,1,0:T(8,128)S(1)} %get-tuple-element.62), channel_id=1, source_target_pairs={{0,30},{1,31},{2,4},{3,5},{4,2},{5,3},{6,8},{7,9},{8,6},{9,7},{10,... | collective-permute-start | bytes 393224 | tf_op jit(solution)/shard_map/ppermute | solution.py:48
  58.7 7.9 %collective-permute-start.9 = (f32[2,16,8,128]{3,2,1,0:T(8,128)S(1)}, f32[2,16,8,128]{3,2,1,0:T(8,128)S(1)}, u32[]{:S(2)}, u32[]{:S(2)}) collective-permute-start(f32[2,16,8,128]{3,2,1,0:T(8,128)S(1)} %get-tuple-element.63), channel_id=1, source_target_pairs={{0,2},{1,3},{2,0},{3,1},{4,6},{5,7},{6,4},{7,5},{8,10},{9,11},{10,... | collective-permute-start | bytes 393224 | tf_op jit(solution)/shard_map/ppermute | solution.py:48
  66.9 17.5 %collective-permute-start.12 = (f32[3,2,16,8,128]{4,3,2,1,0:T(8,128)S(1)}, f32[3,2,16,8,128]{4,3,2,1,0:T(8,128)S(1)}, u32[]{:S(2)}, u32[]{:S(2)}) collective-permute-start(f32[3,2,16,8,128]{4,3,2,1,0:T(8,128)S(1)} %pad_maximum_fusion.1.refs_5_), channel_id=1, source_target_pairs={{0,224},{32,64},{64,32},{96,128},{128,96},{160,192},{192,160},{224... | collective-permute-start | bytes 1179656 | tf_op jit(solution)/shard_map/ppermute | solution.py:42
  71.8 12.6 %collective-permute-start.11 = (f32[3,2,16,8,128]{4,3,2,1,0:T(8,128)S(1)}, f32[3,2,16,8,128]{4,3,2,1,0:T(8,128)S(1)}, u32[]{:S(2)}, u32[]{:S(2)}) collective-permute-start(f32[3,2,16,8,128]{4,3,2,1,0:T(8,128)S(1)} %pad_maximum_fusion.1.refs_5_), channel_id=1, source_target_pairs={{0,32},{32,0},{64,96},{96,64},{128,160},{160,128},{192,224},{224,1... | collective-permute-start | bytes 1179656 | tf_op jit(solution)/shard_map/ppermute | solution.py:42
  84.4 2.9 %copy-start.2 = (f32[3,2,16,8,128]{4,3,2,1,0:T(8,128)}, f32[3,2,16,8,128]{4,3,2,1,0:T(8,128)S(1)}, u32[]{:S(2)}) copy-start(f32[3,2,16,8,128]{4,3,2,1,0:T(8,128)S(1)} %collective-permute-done.12.refs_7_) | copy-start | bytes 1179652
  84.4 2.9 %collective-permute-start.13 = (f32[2,256,128]{2,1,0:T(8,128)S(1)}, f32[2,256,128]{2,1,0:T(8,128)S(1)}, u32[]{:S(2)}, u32[]{:S(2)}) collective-permute-start(f32[2,256,128]{2,1,0:T(8,128)S(1)} %bitcast.74), channel_id=1, source_target_pairs={{0,32},{32,0},{1,33},{33,1},{2,34},{34,2},{3,35},{35,3},{4,36},{36... | collective-permute-start | bytes 786440 | tf_op jit(solution)/shard_map/ppermute | solution.py:272
  97.7 7.0 %collective-permute-start.14 = (f32[3,2,16,8,128]{4,3,2,1,0:T(8,128)S(1)}, f32[3,2,16,8,128]{4,3,2,1,0:T(8,128)S(1)}, u32[]{:S(2)}, u32[]{:S(2)}) collective-permute-start(f32[3,2,16,8,128]{4,3,2,1,0:T(8,128)S(1)} %get-tuple-element.48), channel_id=1, source_target_pairs={{0,32},{32,0},{64,96},{96,64},{128,160},{160,128},{192,224},{224,1... | collective-permute-start | bytes 1179656 | tf_op jit(solution)/shard_map/ppermute | solution.py:42
  98.1 7.6 %collective-permute-start.15 = (f32[3,2,16,8,128]{4,3,2,1,0:T(8,128)S(1)}, f32[3,2,16,8,128]{4,3,2,1,0:T(8,128)}, u32[]{:S(2)}, u32[]{:S(2)}) collective-permute-start(f32[3,2,16,8,128]{4,3,2,1,0:T(8,128)S(1)} %get-tuple-element.49), channel_id=1, source_target_pairs={{0,224},{32,64},{64,32},{96,128},{128,96},{160,192},{192,160},{224... | collective-permute-start | bytes 1179656 | tf_op jit(solution)/shard_map/ppermute | solution.py:42
  98.1 2.1 %collective-permute-start.18 = (f32[2,256,128]{2,1,0:T(8,128)S(1)}, f32[2,256,128]{2,1,0:T(8,128)S(1)}, u32[]{:S(2)}, u32[]{:S(2)}) collective-permute-start(f32[2,256,128]{2,1,0:T(8,128)S(1)} %get-tuple-element.53), channel_id=1, source_target_pairs={{0,32},{32,0},{1,33},{33,1},{2,34},{34,2},{3,35},{35,3},{4,36},{36... | collective-permute-start | bytes 786440 | tf_op jit(solution)/shard_map/ppermute | solution.py:272
  101.0 12.1 %all-to-all-start.3 = ((f32[16,32,128]{2,1,0:T(8,128)}), f32[16,32,128]{2,1,0:T(8,128)S(1)}, u32[]{:S(2)}, u32[]{:S(2)}) async-start(f32[16,32,128]{2,1,0:T(8,128)} %bitcast.21), calls=%async_computation.3 | async-start | bytes 524288 | tf_op jit(solution)/shard_map/all_to_all | solution.py:268
  105.7 39.4 %copy-start = (f32[2,2,256,128]{3,2,1,0:T(8,128)S(1)}, f32[2,2,256,128]{3,2,1,0:T(8,128)}, u32[]{:S(2)}) copy-start(f32[2,2,256,128]{3,2,1,0:T(8,128)} %get-tuple-element.51.probe_ref) | copy-start | bytes 1572868
  106.9 13.6 %collective-permute-start.17 = (f32[2,16,8,128]{3,2,1,0:T(8,128)S(1)}, f32[2,16,8,128]{3,2,1,0:T(8,128)S(1)}, u32[]{:S(2)}, u32[]{:S(2)}) collective-permute-start(f32[2,16,8,128]{3,2,1,0:T(8,128)S(1)} %get-tuple-element.60), channel_id=1, source_target_pairs={{0,31},{1,2},{2,1},{3,4},{4,3},{5,6},{6,5},{7,8},{8,7},{9,10},{10,... | collective-permute-start | bytes 393224 | tf_op jit(solution)/shard_map/ppermute | solution.py:42
  109.6 10.9 %collective-permute-start.16 = (f32[2,16,8,128]{3,2,1,0:T(8,128)S(1)}, f32[2,16,8,128]{3,2,1,0:T(8,128)S(1)}, u32[]{:S(2)}, u32[]{:S(2)}) collective-permute-start(f32[2,16,8,128]{3,2,1,0:T(8,128)S(1)} %get-tuple-element.61), channel_id=1, source_target_pairs={{0,1},{1,0},{2,3},{3,2},{4,5},{5,4},{6,7},{7,6},{8,9},{9,8},{10,11... | collective-permute-start | bytes 393224 | tf_op jit(solution)/shard_map/ppermute | solution.py:42
  113.8 14.7 %all-to-all-start.4 = ((f32[8,32,128]{2,1,0:T(8,128)}), f32[8,32,128]{2,1,0:T(8,128)S(1)}, u32[]{:S(2)}, u32[]{:S(2)}) async-start(f32[8,32,128]{2,1,0:T(8,128)} %broadcast_in_dim.44), calls=%async_computation.4 | async-start | bytes 262144 | tf_op jit(solution)/shard_map/all_to_all | solution.py:268
  139.6 5.5 %collective-permute-start.19 = (f32[2,256,128]{2,1,0:T(8,128)S(1)}, f32[2,256,128]{2,1,0:T(8,128)S(1)}, u32[]{:S(2)}, u32[]{:S(2)}) collective-permute-start(f32[2,256,128]{2,1,0:T(8,128)S(1)} %bitcast.76), channel_id=1, source_target_pairs={{0,32},{32,0},{1,33},{33,1},{2,34},{34,2},{3,35},{35,3},{4,36},{36... | collective-permute-start | bytes 786440 | tf_op jit(solution)/shard_map/ppermute | solution.py:272

commit v10 on v9

--- a/solution.py
+++ b/solution.py
@@ -39,12 +39,6 @@
 def paired(value, axes, side):
     count = lax.axis_size(axes)
     pairs = [(i, (i + (1 if (i + side // 2) % 2 == 0 else -1)) % count) for i in range(count)]
-    return lax.ppermute(value, axes, pairs)
-
-
-def paired_far(value, axes, phase):
-    count = lax.axis_size(axes)
-    pairs = [(i, (i + (2 if (i // 2 + phase) % 2 == 0 else -2)) % count) for i in range(count)]
     return lax.ppermute(value, axes, pairs)
 
 
@@ -291,42 +285,16 @@
     return own + side0 + jnp.where(at_end, 0.0, side2)
 
 
-def column_payloads(sums):
-    index = lax.axis_index(COL)
-    odd = lax.rem(index, 2) == 1
-    right_first = lax.rem(index // 2, 2) == 0
-    return (
-        jnp.where(odd, sums[:2], sums[1:]),
-        jnp.where(odd, sums[1:], sums[:2]),
-        jnp.where(right_first, sums[2], sums[0]),
-        jnp.where(right_first, sums[0], sums[2]),
-    )
-
-
-def column_transfers(payloads):
-    near0, near2, far_a, far_b = payloads
-    return paired(near0, COL, 0), paired(near2, COL, 2), paired_far(far_a, COL, 0), paired_far(far_b, COL, 1)
-
-
-def updated_strip(strip, sums, arrived, peak):
-    index, places, at_end = place_of(COL)
-    last = lax.axis_size(COL) - 1
-    odd = lax.rem(index, 2) == 1
-    right_first = lax.rem(index // 2, 2) == 0
-    near0, near2, far_a, far_b = arrived
-    near2 = jnp.where(at_end, 0.0, near2)
-    far_b = jnp.where((index < 2) | (index > last - 2), 0.0, far_b)
-    from_left, from_right = jnp.where(odd, near0, near2), jnp.where(odd, near2, near0)
-    grad_left = sums[0] + from_left[0] + jnp.where(right_first, far_b, far_a)
-    grad = sums[1] + from_left[1] + from_right[0]
-    grad_right = sums[2] + from_right[1] + jnp.where(right_first, far_a, far_b)
-    return jnp.stack(
-        [
-            jnp.where(index == 0, 0.0, strip[0] - grad_left / peak),
-            strip[1] - grad / peak,
-            jnp.where(index == last, 0.0, strip[2] - grad_right / peak),
-        ]
-    )
+def to_sides(blocks):
+    odd = lax.rem(lax.axis_index(COL), 2) == 1
+    return jnp.where(odd, blocks[0], blocks[2]), jnp.where(odd, blocks[2], blocks[0])
+
+
+def strip_around(own):
+    odd = lax.rem(lax.axis_index(COL), 2) == 1
+    side0 = paired(own, COL, 0)
+    side2 = jnp.where(place_of(COL)[2], 0.0, paired(own, COL, 2))
+    return jnp.stack([jnp.where(odd, side0, side2), own, jnp.where(odd, side2, side0)])
 
 
 def after(value, *others):
@@ -364,35 +332,32 @@
     )
     tables = dft_tables(size)
     row_end, col_end = place_of(ROW)[2], place_of(COL)[2]
-    odd = lax.rem(lax.axis_index(COL), 2) == 1
 
     own = object_field.reshape(2, TILES, 8, LANES)
-    side0, side2 = paired(own, COL, 0), jnp.where(col_end, 0.0, paired(own, COL, 2))
-    strip = jnp.stack([jnp.where(odd, side0, side2), own, jnp.where(odd, side2, side0)])
+    strip = strip_around(own)
     strips = (strip, paired(strip, ROW, 0), paired(strip, ROW, 2))
     row0, row1, row2, keep, send, peak = gradients(True, live_slots, patterns, tables, probe_field, *strips)
     half = keep + core_swap(send)
     row0, row2 = after((row0, row2), half)
     sums = side_sum(row1, paired(row0, ROW, 0), paired(row2, ROW, 2), row_end)
-    payloads = column_payloads(sums)
+    payloads = to_sides(sums)
     shares = after(plane_shares(half), *payloads)
-    arrived = column_transfers(payloads)
-    shares, arrived = lax.optimization_barrier((depth_shares(shares), arrived))
-    strip = updated_strip(strip, sums, arrived, peak)
-    shares = after(shares, strip)
-    sides = (paired(strip, ROW, 0), paired(strip, ROW, 2))
-    mine, sides = lax.optimization_barrier((gathered(shares, keep.shape), sides))
+    grad = side_sum(sums[1], paired(payloads[0], COL, 0), paired(payloads[1], COL, 2), col_end)
+    own = own - grad / peak
+    shares = after(depth_shares(shares), own)
+    strip = strip_around(own)
+    strips = (strip, paired(strip, ROW, 0), paired(strip, ROW, 2))
+    mine = gathered(shares, keep.shape)
     totals = (mine, core_swap(mine))
 
-    strips = (strip,) + sides
     row0, row1, row2, keep, send, peak, probe = gradients(
         False, live_slots, patterns, tables, probe_field, *strips, *totals
     )
     sums = side_sum(row1, paired(row0, ROW, 0), paired(row2, ROW, 2), row_end)
-    payloads = (jnp.where(odd, sums[0], sums[2]), jnp.where(odd, sums[2], sums[0]))
+    payloads = to_sides(sums)
     shares = after(plane_shares(keep + core_swap(send)), *payloads)
     grad = side_sum(sums[1], paired(payloads[0], COL, 0), paired(payloads[1], COL, 2), col_end)
-    new_object = (strip[1] - grad / peak).reshape(object_field.shape)
+    new_object = (own - grad / peak).reshape(object_field.shape)
     mine = gathered(after(depth_shares(shares), new_object), keep.shape)
     return (new_object, last_probe(probe, mine, core_swap(mine)))
 

time: 147 us -> 141 us (0.959)
  blocking collectives: 23.6 us -> 10.9 us
  waiting for transfers between devices: 33.4 us -> 43.1 us
  Pallas kernels: 21.2 us -> 13.5 us
  starting transfers between devices: 59.9 us -> 64.9 us
    all_to_all x4 -> x5, waiting for transfers between devices: 11.7 us -> 25.9 us  [exchange(): return lax.all_to_all(value, axes, 0, 0, tiled=True)]
    all_to_all x2 -> x1, blocking collectives: 23.6 us -> 10.9 us  [exchange(): return lax.all_to_all(value, axes, 0, 0, tiled=True)]
    pallas_call x2, Pallas kernels: 20.1 us -> 12.3 us  [gradients(): pl.pallas_call(functools.partial(gradient_kernel, first), out_shape=(stri...]
    ppermute x4, starting transfers between devices: 8.62 us -> 13.3 us  [core_swap(): return lax.ppermute(value, 'core', [(0, 1), (1, 0)])]
    ppermute x14 -> x16, starting transfers between devices: 23.4 us -> 27.6 us  [paired(): return lax.ppermute(value, axes, pairs)]
    ppermute x2 -> x0, starting transfers between devices: 4.14 us -> none  [paired_far(): return lax.ppermute(value, axes, pairs)]
    ppermute x2 -> x0, waiting for transfers between devices: 3.76 us -> none  [paired_far(): return lax.ppermute(value, axes, pairs)]
    ppermute x14 -> x16, waiting for transfers between devices: 13.3 us -> 12.9 us  [paired(): return lax.ppermute(value, axes, pairs)]
  transfers between devices with their start and end apart: 24 -> 25, of which waited for: 14 -> 14; matrix products, arithmetic and copies ran while one was open for 3% -> 3% of each run, Pallas kernels for 0% -> 0%
where the time goes in v10:
time: 141 us; the launch traced here: 140 us
  starting transfers between devices  64.9 us (46%)
  waiting for transfers between devices  43.1 us (31%)
  Pallas kernels  13.5 us (10%)
  blocking collectives  10.9 us (8%)
  other arithmetic  3.46 us (2%)
  local copies, waits for them, and re-layouts  2.83 us (2%)
  between operations  1.5 us (1%)
    ppermute x16, starting transfers between devices, paired(): return lax.ppermute(value, axes, pairs)  27.6 us
    all_to_all x5, waiting for transfers between devices, exchange(): return lax.all_to_all(value, axes, 0, 0, tiled=True)  25.9 us
    all_to_all x5, starting transfers between devices, exchange(): return lax.all_to_all(value, axes, 0, 0, tiled=True)  24 us
    ppermute x4, starting transfers between devices, core_swap(): return lax.ppermute(value, 'core', [(0, 1), (1, 0)])  13.3 us
    ppermute x16, waiting for transfers between devices, paired(): return lax.ppermute(value, axes, pairs)  12.9 us
    pallas_call x2, Pallas kernels, gradients(): pl.pallas_call(functools.partial(gradient_kernel, first), out_shape=(stri...  12.3 us
    all_to_all x1, blocking collectives, exchange(): return lax.all_to_all(value, axes, 0, 0, tiled=True)  10.9 us
    ppermute x4, waiting for transfers between devices, core_swap(): return lax.ppermute(value, 'core', [(0, 1), (1, 0)])  4.33 us
  transfers between devices with their start and end apart: 25, of which 14 were waited for; matrix products, arithmetic and copies ran while one was open for 3% of the time, Pallas kernels for 0%

profile of v10, /device:TPU:1, one launch (start us, length us, event | category | flops | bytes accessed | tf_op | source)
XLA Modules:
  0.0 140.1 jit_solution(15486140606899685444)
XLA Ops:
  0.6 8.7 %collective-permute-start.1 = (f32[2,16,8,128]{3,2,1,0:T(8,128)}, f32[2,16,8,128]{3,2,1,0:T(8,128)S(1)}, u32[]{:S(2)}, u32[]{:S(2)}) collective-permute-start(f32[2,16,8,128]{3,2,1,0:T(8,128)} %bitcast.61), channel_id=1, source_target_pairs={{0,31},{1,2},{2,1},{3,4},{4,3},{5,6},{6,5},{7,8},{8,7},{9,10},{10,... | collective-permute-start | bytes 393224 | tf_op jit(solution)/shard_map/ppermute | solution.py:42
  9.3 3.4 %collective-permute-done.1 = f32[2,16,8,128]{3,2,1,0:T(8,128)S(1)} collective-permute-done((f32[2,16,8,128]{3,2,1,0:T(8,128)}, f32[2,16,8,128]{3,2,1,0:T(8,128)S(1)}, u32[]{:S(2)}, u32[]{:S(2)}) %collective-permute-start.1) | collective-permute-done | bytes 131104 | tf_op jit(solution)/shard_map/ppermute | solution.py:42
  12.8 0.8 collective-permute-done
  13.6 0.9 pad_maximum_fusion.refs_5_
  14.5 3.1 %collective-permute-start.3 = (f32[3,2,16,8,128]{4,3,2,1,0:T(8,128)S(1)}, f32[3,2,16,8,128]{4,3,2,1,0:T(8,128)S(1)}, u32[]{:S(2)}, u32[]{:S(2)}) collective-permute-start(f32[3,2,16,8,128]{4,3,2,1,0:T(8,128)S(1)} %pad_maximum_fusion.refs_5_), channel_id=1, source_target_pairs={{0,224},{32,64},{64,32},{96,128},{128,96},{160,192},{192,160},{224... | collective-permute-start | bytes 1179656 | tf_op jit(solution)/shard_map/ppermute | solution.py:42
  19.1 4.3 %collective-permute-done.3.refs_7_ = f32[3,2,16,8,128]{4,3,2,1,0:T(8,128)S(1)} collective-permute-done((f32[3,2,16,8,128]{4,3,2,1,0:T(8,128)S(1)}, f32[3,2,16,8,128]{4,3,2,1,0:T(8,128)S(1)}, u32[]{:S(2)}, u32[]{:S(2)}) %collective-permute-start.3) | collective-permute-done | bytes 393248 | tf_op jit(solution)/shard_map/ppermute | solution.py:42
  23.4 5.8 %shard_map.86 = (f32[3,2,16,8,128]{4,3,2,1,0:T(8,128)S(1)}, f32[3,2,16,8,128]{4,3,2,1,0:T(8,128)S(1)}, f32[3,2,16,8,128]{4,3,2,1,0:T(8,128)S(1)}, f32[2,256,128]...) custom-call(s32[3,8]{1,0:T(4,128)S(1)} %concatenate.3.refs_0_, f32[8,256,256]{2,1,0:T(8,128)} %bitcast.58, ...), custom_call_target="tpu_custom_call" | custom-call | tf_op jit(solution)/shard_map/pallas_call | solution.py:241
  29.3 5.4 %collective-permute-start.4 = (f32[2,256,128]{2,1,0:T(8,128)S(1)}, f32[2,256,128]{2,1,0:T(8,128)S(1)}, u32[]{:S(2)}, u32[]{:S(2)}) collective-permute-start(f32[2,256,128]{2,1,0:T(8,128)S(1)} %get-tuple-element.25), channel_id=1, source_target_pairs={{0,32},{32,0},{1,33},{33,1},{2,34},{34,2},{3,35},{35,3},{4,36},{36... | collective-permute-start | bytes 786440 | tf_op jit(solution)/shard_map/ppermute | solution.py:266
  34.7 1.2 collective-permute-done.4
  35.8 0.7 add.45
  36.9 4.1 %all-to-all-start = ((f32[16,32,128]{2,1,0:T(8,128)}), f32[16,32,128]{2,1,0:T(8,128)S(1)}, u32[]{:S(2)}, u32[]{:S(2)}) async-start(f32[16,32,128]{2,1,0:T(8,128)} %bitcast.14), calls=%async_computation | async-start | bytes 524288 | tf_op jit(solution)/shard_map/all_to_all | solution.py:262
  41.0 3.8 %collective-permute-done.6 = f32[3,2,16,8,128]{4,3,2,1,0:T(8,128)S(1)} collective-permute-done((f32[3,2,16,8,128]{4,3,2,1,0:T(8,128)S(1)}, f32[3,2,16,8,128]{4,3,2,1,0:T(8,128)S(1)}, u32[]{:S(2)}, u32[]{:S(2)}) %collective-permute-start.6) | collective-permute-done | bytes 393248 | tf_op jit(solution)/shard_map/ppermute | solution.py:42
  44.9 2.0 %collective-permute-start.8 = (f32[2,16,8,128]{3,2,1,0:T(8,128)S(1)}, f32[2,16,8,128]{3,2,1,0:T(8,128)S(1)}, u32[]{:S(2)}, u32[]{:S(2)}) collective-permute-start(f32[2,16,8,128]{3,2,1,0:T(8,128)S(1)} %get-tuple-element.42), channel_id=1, source_target_pairs={{0,31},{1,2},{2,1},{3,4},{4,3},{5,6},{6,5},{7,8},{8,7},{9,10},{10,... | collective-permute-start | bytes 393224 | tf_op jit(solution)/shard_map/ppermute | solution.py:42
  46.9 2.3 %all-to-all-done = f32[16,32,128]{2,1,0:T(8,128)S(1)} async-done(((f32[16,32,128]{2,1,0:T(8,128)}), f32[16,32,128]{2,1,0:T(8,128)S(1)}, u32[]{:S(2)}, u32[]{:S(2)}) %all-to-all-start) | async-done | bytes 262176 | tf_op jit(solution)/shard_map/all_to_all | solution.py:262
  49.8 7.8 %all-to-all-start.1 = ((f32[8,32,128]{2,1,0:T(8,128)}), f32[8,32,128]{2,1,0:T(8,128)S(1)}, u32[]{:S(2)}, u32[]{:S(2)}) async-start(f32[8,32,128]{2,1,0:T(8,128)} %broadcast_in_dim.34), calls=%async_computation.1 | async-start | bytes 262144 | tf_op jit(solution)/shard_map/all_to_all | solution.py:262
  58.4 7.1 %all-to-all-done.1 = f32[8,32,128]{2,1,0:T(8,128)S(1)} async-done(((f32[8,32,128]{2,1,0:T(8,128)}), f32[8,32,128]{2,1,0:T(8,128)S(1)}, u32[]{:S(2)}, u32[]{:S(2)}) %all-to-all-start.1) | async-done | bytes 131104 | tf_op jit(solution)/shard_map/all_to_all | solution.py:262
  66.2 3.5 %all-to-all-start.2 = ((f32[16,32,128]{2,1,0:T(8,128)}), f32[16,32,128]{2,1,0:T(8,128)S(1)}, u32[]{:S(2)}, u32[]{:S(2)}) async-start(f32[16,32,128]{2,1,0:T(8,128)} %broadcast_in_dim.35), calls=%async_computation.2 | async-start | bytes 524288 | tf_op jit(solution)/shard_map/all_to_all | solution.py:262
  69.9 3.7 %collective-permute-start.12 = (f32[3,2,16,8,128]{4,3,2,1,0:T(8,128)S(1)}, f32[3,2,16,8,128]{4,3,2,1,0:T(8,128)S(1)}, u32[]{:S(2)}, u32[]{:S(2)}) collective-permute-start(f32[3,2,16,8,128]{4,3,2,1,0:T(8,128)S(1)} %pad_maximum_fusion.1.refs_5_), channel_id=1, source_target_pairs={{0,224},{32,64},{64,32},{96,128},{128,96},{160,192},{192,160},{224... | collective-permute-start | bytes 1179656 | tf_op jit(solution)/shard_map/ppermute | solution.py:42
  73.6 3.7 %all-to-all-done.2 = f32[16,32,128]{2,1,0:T(8,128)S(1)} async-done(((f32[16,32,128]{2,1,0:T(8,128)}), f32[16,32,128]{2,1,0:T(8,128)S(1)}, u32[]{:S(2)}, u32[]{:S(2)}) %all-to-all-start.2) | async-done | bytes 262176 | tf_op jit(solution)/shard_map/all_to_all | solution.py:262
  77.3 3.3 %collective-permute-start.13 = (f32[2,256,128]{2,1,0:T(8,128)S(1)}, f32[2,256,128]{2,1,0:T(8,128)S(1)}, u32[]{:S(2)}, u32[]{:S(2)}) collective-permute-start(f32[2,256,128]{2,1,0:T(8,128)S(1)} %bitcast.54), channel_id=1, source_target_pairs={{0,32},{32,0},{1,33},{33,1},{2,34},{34,2},{3,35},{35,3},{4,36},{36... | collective-permute-start | bytes 786440 | tf_op jit(solution)/shard_map/ppermute | solution.py:266
  81.9 6.5 %shard_map.87 = (f32[3,2,16,8,128]{4,3,2,1,0:T(8,128)S(1)}, f32[3,2,16,8,128]{4,3,2,1,0:T(8,128)S(1)}, f32[3,2,16,8,128]{4,3,2,1,0:T(8,128)S(1)}, f32[2,256,128]...) custom-call(s32[3,8]{1,0:T(4,128)S(1)} %concatenate.3.refs_0_, ...), custom_call_target="tpu_custom_call" | custom-call | tf_op jit(solution)/shard_map/pallas_call | solution.py:241
  88.4 5.4 %collective-permute-start.14 = (f32[3,2,16,8,128]{4,3,2,1,0:T(8,128)S(1)}, f32[3,2,16,8,128]{4,3,2,1,0:T(8,128)S(1)}, u32[]{:S(2)}, u32[]{:S(2)}) collective-permute-start(f32[3,2,16,8,128]{4,3,2,1,0:T(8,128)S(1)} %get-tuple-element.32), channel_id=1, source_target_pairs={{0,32},{32,0},{64,96},{96,64},{128,160},{160,128},{192,224},{224,1... | collective-permute-start | bytes 1179656 | tf_op jit(solution)/shard_map/ppermute | solution.py:42
  94.2 1.3 collective-permute-done.18
  96.2 5.2 %all-to-all-start.3 = ((f32[16,32,128]{2,1,0:T(8,128)}), f32[16,32,128]{2,1,0:T(8,128)S(1)}, u32[]{:S(2)}, u32[]{:S(2)}) async-start(f32[16,32,128]{2,1,0:T(8,128)} %bitcast.20), calls=%async_computation.3 | async-start | bytes 524288 | tf_op jit(solution)/shard_map/all_to_all | solution.py:262
  101.5 3.7 %collective-permute-start.17 = (f32[2,16,8,128]{3,2,1,0:T(8,128)S(1)}, f32[2,16,8,128]{3,2,1,0:T(8,128)S(1)}, u32[]{:S(2)}, u32[]{:S(2)}) collective-permute-start(f32[2,16,8,128]{3,2,1,0:T(8,128)S(1)} %get-tuple-element.40), channel_id=1, source_target_pairs={{0,31},{1,2},{2,1},{3,4},{4,3},{5,6},{6,5},{7,8},{8,7},{9,10},{10,... | collective-permute-start | bytes 393224 | tf_op jit(solution)/shard_map/ppermute | solution.py:42
  105.2 5.5 %all-to-all-done.3 = f32[16,32,128]{2,1,0:T(8,128)S(1)} async-done(((f32[16,32,128]{2,1,0:T(8,128)}), f32[16,32,128]{2,1,0:T(8,128)S(1)}, u32[]{:S(2)}, u32[]{:S(2)}) %all-to-all-start.3) | async-done | bytes 262176 | tf_op jit(solution)/shard_map/all_to_all | solution.py:262
  111.3 3.4 %all-to-all-start.4 = ((f32[8,32,128]{2,1,0:T(8,128)}), f32[8,32,128]{2,1,0:T(8,128)S(1)}, u32[]{:S(2)}, u32[]{:S(2)}) async-start(f32[8,32,128]{2,1,0:T(8,128)} %broadcast_in_dim.36), calls=%async_computation.4 | async-start | bytes 262144 | tf_op jit(solution)/shard_map/all_to_all | solution.py:262
  115.4 7.3 %all-to-all-done.4 = f32[8,32,128]{2,1,0:T(8,128)S(1)} async-done(((f32[8,32,128]{2,1,0:T(8,128)}), f32[8,32,128]{2,1,0:T(8,128)S(1)}, u32[]{:S(2)}, u32[]{:S(2)}) %all-to-all-start.4) | async-done | bytes 131104 | tf_op jit(solution)/shard_map/all_to_all | solution.py:262
  122.8 10.9 %all_to_all.30 = f32[16,32,128]{2,1,0:T(8,128)S(1)} all-to-all(f32[16,32,128]{2,1,0:T(8,128)S(1)} %broadcast_in_dim.37), channel_id=1, replica_groups=mesh['y'=4,'core'=2,'z'=8,'x'=4] {'y','x'}, dimensions={0} | all-to-all | bytes 524288 | tf_op jit(solution)/shard_map/all_to_all | solution.py:262
  133.6 4.1 %collective-permute-start.19 = (f32[2,256,128]{2,1,0:T(8,128)S(1)}, f32[2,256,128]{2,1,0:T(8,128)S(1)}, u32[]{:S(2)}, u32[]{:S(2)}) collective-permute-start(f32[2,256,128]{2,1,0:T(8,128)S(1)} %bitcast.56), channel_id=1, source_target_pairs={{0,32},{32,0},{1,33},{33,1},{2,34},{34,2},{3,35},{35,3},{4,36},{36... | collective-permute-start | bytes 786440 | tf_op jit(solution)/shard_map/ppermute | solution.py:266
  137.8 1.2 collective-permute-done.19.other_ref
  139.0 1.2 shard_map.88
  (49 shorter events, 7.3 us)
Async XLA Ops:
  0.6 12.1 %collective-permute-start.1 = (f32[2,16,8,128]{3,2,1,0:T(8,128)}, f32[2,16,8,128]{3,2,1,0:T(8,128)S(1)}, u32[]{:S(2)}, u32[]{:S(2)}) collective-permute-start(f32[2,16,8,128]{3,2,1,0:T(8,128)} %bitcast.61), channel_id=1, source_target_pairs={{0,31},{1,2},{2,1},{3,4},{4,3},{5,6},{6,5},{7,8},{8,7},{9,10},{10,... | collective-permute-start | bytes 393224 | tf_op jit(solution)/shard_map/ppermute | solution.py:42
  9.3 4.3 %collective-permute-start = (f32[2,16,8,128]{3,2,1,0:T(8,128)}, f32[2,16,8,128]{3,2,1,0:T(8,128)S(1)}, u32[]{:S(2)}, u32[]{:S(2)}) collective-permute-start(f32[2,16,8,128]{3,2,1,0:T(8,128)} %bitcast.62), channel_id=1, source_target_pairs={{0,1},{1,0},{2,3},{3,2},{4,5},{5,4},{6,7},{7,6},{8,9},{9,8},{10,11... | collective-permute-start | bytes 393224 | tf_op jit(solution)/shard_map/ppermute | solution.py:42
  14.5 8.9 %collective-permute-start.3 = (f32[3,2,16,8,128]{4,3,2,1,0:T(8,128)S(1)}, f32[3,2,16,8,128]{4,3,2,1,0:T(8,128)S(1)}, u32[]{:S(2)}, u32[]{:S(2)}) collective-permute-start(f32[3,2,16,8,128]{4,3,2,1,0:T(8,128)S(1)} %pad_maximum_fusion.refs_5_), channel_id=1, source_target_pairs={{0,224},{32,64},{64,32},{96,128},{128,96},{160,192},{192,160},{224... | collective-permute-start | bytes 1179656 | tf_op jit(solution)/shard_map/ppermute | solution.py:42
  17.7 5.8 %collective-permute-start.2 = (f32[3,2,16,8,128]{4,3,2,1,0:T(8,128)S(1)}, f32[3,2,16,8,128]{4,3,2,1,0:T(8,128)S(1)}, u32[]{:S(2)}, u32[]{:S(2)}) collective-permute-start(f32[3,2,16,8,128]{4,3,2,1,0:T(8,128)S(1)} %pad_maximum_fusion.refs_5_), channel_id=1, source_target_pairs={{0,32},{32,0},{64,96},{96,64},{128,160},{160,128},{192,224},{224,1... | collective-permute-start | bytes 1179656 | tf_op jit(solution)/shard_map/ppermute | solution.py:42
  29.3 28.4 %copy-start.1 = (f32[2,128,128]{2,1,0:T(8,128)S(1)}, f32[2,128,128]{2,1,0:T(8,128)}, u32[]{:S(2)}) copy-start(f32[2,128,128]{2,1,0:T(8,128)} %param.7) | copy-start | bytes 393220
  29.3 6.6 %collective-permute-start.4 = (f32[2,256,128]{2,1,0:T(8,128)S(1)}, f32[2,256,128]{2,1,0:T(8,128)S(1)}, u32[]{:S(2)}, u32[]{:S(2)}) collective-permute-start(f32[2,256,128]{2,1,0:T(8,128)S(1)} %get-tuple-element.25), channel_id=1, source_target_pairs={{0,32},{32,0},{1,33},{33,1},{2,34},{34,2},{3,35},{35,3},{4,36},{36... | collective-permute-start | bytes 786440 | tf_op jit(solution)/shard_map/ppermute | solution.py:266
  36.6 4.5 %collective-permute-start.5 = (f32[3,2,16,8,128]{4,3,2,1,0:T(8,128)S(1)}, f32[3,2,16,8,128]{4,3,2,1,0:T(8,128)S(1)}, u32[]{:S(2)}, u32[]{:S(2)}) collective-permute-start(f32[3,2,16,8,128]{4,3,2,1,0:T(8,128)S(1)} %get-tuple-element.26), channel_id=1, source_target_pairs={{0,32},{32,0},{64,96},{96,64},{128,160},{160,128},{192,224},{224,1... | collective-permute-start | bytes 1179656 | tf_op jit(solution)/shard_map/ppermute | solution.py:42
  36.9 7.8 %collective-permute-start.6 = (f32[3,2,16,8,128]{4,3,2,1,0:T(8,128)S(1)}, f32[3,2,16,8,128]{4,3,2,1,0:T(8,128)S(1)}, u32[]{:S(2)}, u32[]{:S(2)}) collective-permute-start(f32[3,2,16,8,128]{4,3,2,1,0:T(8,128)S(1)} %get-tuple-element.27), channel_id=1, source_target_pairs={{0,224},{32,64},{64,32},{96,128},{128,96},{160,192},{192,160},{224... | collective-permute-start | bytes 1179656 | tf_op jit(solution)/shard_map/ppermute | solution.py:42
  36.9 12.2 %all-to-all-start = ((f32[16,32,128]{2,1,0:T(8,128)}), f32[16,32,128]{2,1,0:T(8,128)S(1)}, u32[]{:S(2)}, u32[]{:S(2)}) async-start(f32[16,32,128]{2,1,0:T(8,128)} %bitcast.14), calls=%async_computation | async-start | bytes 524288 | tf_op jit(solution)/shard_map/all_to_all | solution.py:262
  44.9 12.8 %collective-permute-start.8 = (f32[2,16,8,128]{3,2,1,0:T(8,128)S(1)}, f32[2,16,8,128]{3,2,1,0:T(8,128)S(1)}, u32[]{:S(2)}, u32[]{:S(2)}) collective-permute-start(f32[2,16,8,128]{3,2,1,0:T(8,128)S(1)} %get-tuple-element.42), channel_id=1, source_target_pairs={{0,31},{1,2},{2,1},{3,4},{4,3},{5,6},{6,5},{7,8},{8,7},{9,10},{10,... | collective-permute-start | bytes 393224 | tf_op jit(solution)/shard_map/ppermute | solution.py:42
  46.9 10.8 %collective-permute-start.7 = (f32[2,16,8,128]{3,2,1,0:T(8,128)S(1)}, f32[2,16,8,128]{3,2,1,0:T(8,128)S(1)}, u32[]{:S(2)}, u32[]{:S(2)}) collective-permute-start(f32[2,16,8,128]{3,2,1,0:T(8,128)S(1)} %get-tuple-element.43), channel_id=1, source_target_pairs={{0,1},{1,0},{2,3},{3,2},{4,5},{5,4},{6,7},{7,6},{8,9},{9,8},{10,11... | collective-permute-start | bytes 393224 | tf_op jit(solution)/shard_map/ppermute | solution.py:42
  49.8 15.7 %all-to-all-start.1 = ((f32[8,32,128]{2,1,0:T(8,128)}), f32[8,32,128]{2,1,0:T(8,128)S(1)}, u32[]{:S(2)}, u32[]{:S(2)}) async-start(f32[8,32,128]{2,1,0:T(8,128)} %broadcast_in_dim.34), calls=%async_computation.1 | async-start | bytes 262144 | tf_op jit(solution)/shard_map/all_to_all | solution.py:262
  57.7 12.1 %collective-permute-start.10 = (f32[2,16,8,128]{3,2,1,0:T(8,128)S(1)}, f32[2,16,8,128]{3,2,1,0:T(8,128)S(1)}, u32[]{:S(2)}, u32[]{:S(2)}) collective-permute-start(f32[2,16,8,128]{3,2,1,0:T(8,128)S(1)} %fusion.8), channel_id=1, source_target_pairs={{0,31},{1,2},{2,1},{3,4},{4,3},{5,6},{6,5},{7,8},{8,7},{9,10},{10,... | collective-permute-start | bytes 393224 | tf_op jit(solution)/shard_map/ppermute | solution.py:42
  58.4 11.4 %collective-permute-start.9 = (f32[2,16,8,128]{3,2,1,0:T(8,128)S(1)}, f32[2,16,8,128]{3,2,1,0:T(8,128)S(1)}, u32[]{:S(2)}, u32[]{:S(2)}) collective-permute-start(f32[2,16,8,128]{3,2,1,0:T(8,128)S(1)} %fusion.8), channel_id=1, source_target_pairs={{0,1},{1,0},{2,3},{3,2},{4,5},{5,4},{6,7},{7,6},{8,9},{9,8},{10,11... | collective-permute-start | bytes 393224 | tf_op jit(solution)/shard_map/ppermute | solution.py:42
  66.2 11.1 %all-to-all-start.2 = ((f32[16,32,128]{2,1,0:T(8,128)}), f32[16,32,128]{2,1,0:T(8,128)S(1)}, u32[]{:S(2)}, u32[]{:S(2)}) async-start(f32[16,32,128]{2,1,0:T(8,128)} %broadcast_in_dim.35), calls=%async_computation.2 | async-start | bytes 524288 | tf_op jit(solution)/shard_map/all_to_all | solution.py:262
  69.9 11.3 %collective-permute-start.12 = (f32[3,2,16,8,128]{4,3,2,1,0:T(8,128)S(1)}, f32[3,2,16,8,128]{4,3,2,1,0:T(8,128)S(1)}, u32[]{:S(2)}, u32[]{:S(2)}) collective-permute-start(f32[3,2,16,8,128]{4,3,2,1,0:T(8,128)S(1)} %pad_maximum_fusion.1.refs_5_), channel_id=1, source_target_pairs={{0,224},{32,64},{64,32},{96,128},{128,96},{160,192},{192,160},{224... | collective-permute-start | bytes 1179656 | tf_op jit(solution)/shard_map/ppermute | solution.py:42
  73.6 7.6 %collective-permute-start.11 = (f32[3,2,16,8,128]{4,3,2,1,0:T(8,128)S(1)}, f32[3,2,16,8,128]{4,3,2,1,0:T(8,128)S(1)}, u32[]{:S(2)}, u32[]{:S(2)}) collective-permute-start(f32[3,2,16,8,128]{4,3,2,1,0:T(8,128)S(1)} %pad_maximum_fusion.1.refs_5_), channel_id=1, source_target_pairs={{0,32},{32,0},{64,96},{96,64},{128,160},{160,128},{192,224},{224,1... | collective-permute-start | bytes 1179656 | tf_op jit(solution)/shard_map/ppermute | solution.py:42
  77.3 4.5 %collective-permute-start.13 = (f32[2,256,128]{2,1,0:T(8,128)S(1)}, f32[2,256,128]{2,1,0:T(8,128)S(1)}, u32[]{:S(2)}, u32[]{:S(2)}) collective-permute-start(f32[2,256,128]{2,1,0:T(8,128)S(1)} %bitcast.54), channel_id=1, source_target_pairs={{0,32},{32,0},{1,33},{33,1},{2,34},{34,2},{3,35},{35,3},{4,36},{36... | collective-permute-start | bytes 786440 | tf_op jit(solution)/shard_map/ppermute | solution.py:266
  81.1 0.7 copy-start.2
  88.4 13.0 %collective-permute-start.14 = (f32[3,2,16,8,128]{4,3,2,1,0:T(8,128)S(1)}, f32[3,2,16,8,128]{4,3,2,1,0:T(8,128)S(1)}, u32[]{:S(2)}, u32[]{:S(2)}) collective-permute-start(f32[3,2,16,8,128]{4,3,2,1,0:T(8,128)S(1)} %get-tuple-element.32), channel_id=1, source_target_pairs={{0,32},{32,0},{64,96},{96,64},{128,160},{160,128},{192,224},{224,1... | collective-permute-start | bytes 1179656 | tf_op jit(solution)/shard_map/ppermute | solution.py:42
  93.8 7.6 %collective-permute-start.15 = (f32[3,2,16,8,128]{4,3,2,1,0:T(8,128)S(1)}, f32[3,2,16,8,128]{4,3,2,1,0:T(8,128)S(1)}, u32[]{:S(2)}, u32[]{:S(2)}) collective-permute-start(f32[3,2,16,8,128]{4,3,2,1,0:T(8,128)S(1)} %get-tuple-element.33), channel_id=1, source_target_pairs={{0,224},{32,64},{64,32},{96,128},{128,96},{160,192},{192,160},{224... | collective-permute-start | bytes 1179656 | tf_op jit(solution)/shard_map/ppermute | solution.py:42
  93.8 1.7 %collective-permute-start.18 = (f32[2,256,128]{2,1,0:T(8,128)S(1)}, f32[2,256,128]{2,1,0:T(8,128)S(1)}, u32[]{:S(2)}, u32[]{:S(2)}) collective-permute-start(f32[2,256,128]{2,1,0:T(8,128)S(1)} %get-tuple-element.37), channel_id=1, source_target_pairs={{0,32},{32,0},{1,33},{33,1},{2,34},{34,2},{3,35},{35,3},{4,36},{36... | collective-permute-start | bytes 786440 | tf_op jit(solution)/shard_map/ppermute | solution.py:266
  96.2 14.4 %all-to-all-start.3 = ((f32[16,32,128]{2,1,0:T(8,128)}), f32[16,32,128]{2,1,0:T(8,128)S(1)}, u32[]{:S(2)}, u32[]{:S(2)}) async-start(f32[16,32,128]{2,1,0:T(8,128)} %bitcast.20), calls=%async_computation.3 | async-start | bytes 524288 | tf_op jit(solution)/shard_map/all_to_all | solution.py:262
  101.4 37.6 %copy-start = (f32[2,2,256,128]{3,2,1,0:T(8,128)S(1)}, f32[2,2,256,128]{3,2,1,0:T(8,128)}, u32[]{:S(2)}) copy-start(f32[2,2,256,128]{3,2,1,0:T(8,128)} %get-tuple-element.35.probe_ref) | copy-start | bytes 1572868
  101.5 13.2 %collective-permute-start.17 = (f32[2,16,8,128]{3,2,1,0:T(8,128)S(1)}, f32[2,16,8,128]{3,2,1,0:T(8,128)S(1)}, u32[]{:S(2)}, u32[]{:S(2)}) collective-permute-start(f32[2,16,8,128]{3,2,1,0:T(8,128)S(1)} %get-tuple-element.40), channel_id=1, source_target_pairs={{0,31},{1,2},{2,1},{3,4},{4,3},{5,6},{6,5},{7,8},{8,7},{9,10},{10,... | collective-permute-start | bytes 393224 | tf_op jit(solution)/shard_map/ppermute | solution.py:42
  105.2 9.6 %collective-permute-start.16 = (f32[2,16,8,128]{3,2,1,0:T(8,128)S(1)}, f32[2,16,8,128]{3,2,1,0:T(8,128)S(1)}, u32[]{:S(2)}, u32[]{:S(2)}) collective-permute-start(f32[2,16,8,128]{3,2,1,0:T(8,128)S(1)} %get-tuple-element.41), channel_id=1, source_target_pairs={{0,1},{1,0},{2,3},{3,2},{4,5},{5,4},{6,7},{7,6},{8,9},{9,8},{10,11... | collective-permute-start | bytes 393224 | tf_op jit(solution)/shard_map/ppermute | solution.py:42
  111.3 11.4 %all-to-all-start.4 = ((f32[8,32,128]{2,1,0:T(8,128)}), f32[8,32,128]{2,1,0:T(8,128)S(1)}, u32[]{:S(2)}, u32[]{:S(2)}) async-start(f32[8,32,128]{2,1,0:T(8,128)} %broadcast_in_dim.36), calls=%async_computation.4 | async-start | bytes 262144 | tf_op jit(solution)/shard_map/all_to_all | solution.py:262
  133.6 5.3 %collective-permute-start.19 = (f32[2,256,128]{2,1,0:T(8,128)S(1)}, f32[2,256,128]{2,1,0:T(8,128)S(1)}, u32[]{:S(2)}, u32[]{:S(2)}) collective-permute-start(f32[2,256,128]{2,1,0:T(8,128)S(1)} %bitcast.56), channel_id=1, source_target_pairs={{0,32},{32,0},{1,33},{33,1},{2,34},{34,2},{3,35},{35,3},{4,36},{36... | collective-permute-start | bytes 786440 | tf_op jit(solution)/shard_map/ppermute | solution.py:266

commit v11 on v10

--- a/solution.py
+++ b/solution.py
@@ -353,12 +353,14 @@
     row0, row1, row2, keep, send, peak, probe = gradients(
         False, live_slots, patterns, tables, probe_field, *strips, *totals
     )
+    shares = plane_shares(keep + core_swap(send))
+    shares, (row0, row2) = lax.optimization_barrier((shares, (row0, row2)))
     sums = side_sum(row1, paired(row0, ROW, 0), paired(row2, ROW, 2), row_end)
     payloads = to_sides(sums)
-    shares = after(plane_shares(keep + core_swap(send)), *payloads)
+    shares = after(depth_shares(shares), *payloads)
     grad = side_sum(sums[1], paired(payloads[0], COL, 0), paired(payloads[1], COL, 2), col_end)
     new_object = (own - grad / peak).reshape(object_field.shape)
-    mine = gathered(after(depth_shares(shares), new_object), keep.shape)
+    mine = gathered(shares, keep.shape)
     return (new_object, last_probe(probe, mine, core_swap(mine)))
 
 

time: 141 us -> 141 us (level)
  Pallas kernels: 13.5 us -> 21.1 us
  starting transfers between devices: 64.9 us -> 57.6 us
  waiting for transfers between devices: 43.1 us -> 41.3 us
  blocking collectives: 10.9 us -> 12.6 us
    pallas_call x2, Pallas kernels: 12.3 us -> 19.9 us  [gradients(): pl.pallas_call(functools.partial(gradient_kernel, first), out_shape=(stri...]
    all_to_all x5, waiting for transfers between devices: 25.9 us -> 21.6 us  [exchange(): return lax.all_to_all(value, axes, 0, 0, tiled=True)]
    ppermute x16, starting transfers between devices: 27.6 us -> 24 us  [paired(): return lax.ppermute(value, axes, pairs)]
    ppermute x4, starting transfers between devices: 13.3 us -> 9.79 us  [core_swap(): return lax.ppermute(value, 'core', [(0, 1), (1, 0)])]
    ppermute x16, waiting for transfers between devices: 12.9 us -> 16 us  [paired(): return lax.ppermute(value, axes, pairs)]
    all_to_all x1, blocking collectives: 10.9 us -> 12.6 us  [exchange(): return lax.all_to_all(value, axes, 0, 0, tiled=True)]
  transfers between devices with their start and end apart: 25 -> 25, of which waited for: 14 -> 15; matrix products, arithmetic and copies ran while one was open for 3% -> 3% of each run, Pallas kernels for 0% -> 0%
where the time goes in v11:
time: 141 us; the launch traced here: 140 us
  starting transfers between devices  57.6 us (41%)
  waiting for transfers between devices  41.3 us (29%)
  Pallas kernels  21.1 us (15%)
  blocking collectives  12.6 us (9%)
  local copies, waits for them, and re-layouts  3.48 us (2%)
  other arithmetic  2.76 us (2%)
  between operations  1.48 us (1%)
    ppermute x16, starting transfers between devices, paired(): return lax.ppermute(value, axes, pairs)  24 us
    all_to_all x5, starting transfers between devices, exchange(): return lax.all_to_all(value, axes, 0, 0, tiled=True)  23.8 us
    all_to_all x5, waiting for transfers between devices, exchange(): return lax.all_to_all(value, axes, 0, 0, tiled=True)  21.6 us
    pallas_call x2, Pallas kernels, gradients(): pl.pallas_call(functools.partial(gradient_kernel, first), out_shape=(stri...  19.9 us
    ppermute x16, waiting for transfers between devices, paired(): return lax.ppermute(value, axes, pairs)  16 us
    all_to_all x1, blocking collectives, exchange(): return lax.all_to_all(value, axes, 0, 0, tiled=True)  12.6 us
    ppermute x4, starting transfers between devices, core_swap(): return lax.ppermute(value, 'core', [(0, 1), (1, 0)])  9.79 us
    ppermute x4, waiting for transfers between devices, core_swap(): return lax.ppermute(value, 'core', [(0, 1), (1, 0)])  3.69 us
  transfers between devices with their start and end apart: 25, of which 15 were waited for; matrix products, arithmetic and copies ran while one was open for 3% of the time, Pallas kernels for 0%

profile of v11, /device:TPU:1, one launch (start us, length us, event | category | flops | bytes accessed | tf_op | source)
XLA Modules:
  0.0 140.3 jit_solution(695684947388252381)
XLA Ops:
  0.6 8.7 %collective-permute-start.1 = (f32[2,16,8,128]{3,2,1,0:T(8,128)}, f32[2,16,8,128]{3,2,1,0:T(8,128)S(1)}, u32[]{:S(2)}, u32[]{:S(2)}) collective-permute-start(f32[2,16,8,128]{3,2,1,0:T(8,128)} %bitcast.62), channel_id=1, source_target_pairs={{0,31},{1,2},{2,1},{3,4},{4,3},{5,6},{6,5},{7,8},{8,7},{9,10},{10,... | collective-permute-start | bytes 393224 | tf_op jit(solution)/shard_map/ppermute | solution.py:42
  9.3 3.4 %collective-permute-done.1 = f32[2,16,8,128]{3,2,1,0:T(8,128)S(1)} collective-permute-done((f32[2,16,8,128]{3,2,1,0:T(8,128)}, f32[2,16,8,128]{3,2,1,0:T(8,128)S(1)}, u32[]{:S(2)}, u32[]{:S(2)}) %collective-permute-start.1) | collective-permute-done | bytes 131104 | tf_op jit(solution)/shard_map/ppermute | solution.py:42
  13.6 0.9 pad_maximum_fusion.refs_5_
  14.5 3.1 %collective-permute-start.3 = (f32[3,2,16,8,128]{4,3,2,1,0:T(8,128)S(1)}, f32[3,2,16,8,128]{4,3,2,1,0:T(8,128)S(1)}, u32[]{:S(2)}, u32[]{:S(2)}) collective-permute-start(f32[3,2,16,8,128]{4,3,2,1,0:T(8,128)S(1)} %pad_maximum_fusion.refs_5_), channel_id=1, source_target_pairs={{0,224},{32,64},{64,32},{96,128},{128,96},{160,192},{192,160},{224... | collective-permute-start | bytes 1179656 | tf_op jit(solution)/shard_map/ppermute | solution.py:42
  19.1 4.3 %collective-permute-done.3.refs_7_ = f32[3,2,16,8,128]{4,3,2,1,0:T(8,128)S(1)} collective-permute-done((f32[3,2,16,8,128]{4,3,2,1,0:T(8,128)S(1)}, f32[3,2,16,8,128]{4,3,2,1,0:T(8,128)S(1)}, u32[]{:S(2)}, u32[]{:S(2)}) %collective-permute-start.3) | collective-permute-done | bytes 393248 | tf_op jit(solution)/shard_map/ppermute | solution.py:42
  23.4 9.6 %shard_map.86 = (f32[3,2,16,8,128]{4,3,2,1,0:T(8,128)S(1)}, f32[3,2,16,8,128]{4,3,2,1,0:T(8,128)S(1)}, f32[3,2,16,8,128]{4,3,2,1,0:T(8,128)S(1)}, f32[2,256,128]...) custom-call(s32[3,8]{1,0:T(4,128)S(1)} %concatenate.3.refs_0_, f32[8,256,256]{2,1,0:T(8,128)} %bitcast.58, ...), custom_call_target="tpu_custom_call" | custom-call | tf_op jit(solution)/shard_map/pallas_call | solution.py:241
  33.1 1.5 %collective-permute-start.4 = (f32[2,256,128]{2,1,0:T(8,128)S(1)}, f32[2,256,128]{2,1,0:T(8,128)S(1)}, u32[]{:S(2)}, u32[]{:S(2)}) collective-permute-start(f32[2,256,128]{2,1,0:T(8,128)S(1)} %get-tuple-element.27), channel_id=1, source_target_pairs={{0,32},{32,0},{1,33},{33,1},{2,34},{34,2},{3,35},{35,3},{4,36},{36... | collective-permute-start | bytes 786440 | tf_op jit(solution)/shard_map/ppermute | solution.py:266
  34.6 1.2 collective-permute-done.4
  37.0 3.9 %all-to-all-start = ((f32[16,32,128]{2,1,0:T(8,128)}), f32[16,32,128]{2,1,0:T(8,128)S(1)}, u32[]{:S(2)}, u32[]{:S(2)}) async-start(f32[16,32,128]{2,1,0:T(8,128)} %bitcast.14), calls=%async_computation | async-start | bytes 524288 | tf_op jit(solution)/shard_map/all_to_all | solution.py:262
  41.0 3.8 %collective-permute-done.6 = f32[3,2,16,8,128]{4,3,2,1,0:T(8,128)S(1)} collective-permute-done((f32[3,2,16,8,128]{4,3,2,1,0:T(8,128)S(1)}, f32[3,2,16,8,128]{4,3,2,1,0:T(8,128)S(1)}, u32[]{:S(2)}, u32[]{:S(2)}) %collective-permute-start.6) | collective-permute-done | bytes 393248 | tf_op jit(solution)/shard_map/ppermute | solution.py:42
  44.8 3.1 %collective-permute-start.8 = (f32[2,16,8,128]{3,2,1,0:T(8,128)S(1)}, f32[2,16,8,128]{3,2,1,0:T(8,128)S(1)}, u32[]{:S(2)}, u32[]{:S(2)}) collective-permute-start(f32[2,16,8,128]{3,2,1,0:T(8,128)S(1)} %get-tuple-element.46), channel_id=1, source_target_pairs={{0,31},{1,2},{2,1},{3,4},{4,3},{5,6},{6,5},{7,8},{8,7},{9,10},{10,... | collective-permute-start | bytes 393224 | tf_op jit(solution)/shard_map/ppermute | solution.py:42
  47.9 1.1 all-to-all-done
  49.7 7.5 %all-to-all-start.1 = ((f32[8,32,128]{2,1,0:T(8,128)}), f32[8,32,128]{2,1,0:T(8,128)S(1)}, u32[]{:S(2)}, u32[]{:S(2)}) async-start(f32[8,32,128]{2,1,0:T(8,128)} %broadcast_in_dim.34), calls=%async_computation.1 | async-start | bytes 262144 | tf_op jit(solution)/shard_map/all_to_all | solution.py:262
  57.7 7.4 %all-to-all-done.1 = f32[8,32,128]{2,1,0:T(8,128)S(1)} async-done(((f32[8,32,128]{2,1,0:T(8,128)}), f32[8,32,128]{2,1,0:T(8,128)S(1)}, u32[]{:S(2)}, u32[]{:S(2)}) %all-to-all-start.1) | async-done | bytes 131104 | tf_op jit(solution)/shard_map/all_to_all | solution.py:262
  65.9 3.5 %all-to-all-start.2 = ((f32[16,32,128]{2,1,0:T(8,128)}), f32[16,32,128]{2,1,0:T(8,128)S(1)}, u32[]{:S(2)}, u32[]{:S(2)}) async-start(f32[16,32,128]{2,1,0:T(8,128)} %broadcast_in_dim.35), calls=%async_computation.2 | async-start | bytes 524288 | tf_op jit(solution)/shard_map/all_to_all | solution.py:262
  69.6 4.1 %collective-permute-start.12 = (f32[3,2,16,8,128]{4,3,2,1,0:T(8,128)S(1)}, f32[3,2,16,8,128]{4,3,2,1,0:T(8,128)S(1)}, u32[]{:S(2)}, u32[]{:S(2)}) collective-permute-start(f32[3,2,16,8,128]{4,3,2,1,0:T(8,128)S(1)} %pad_maximum_fusion.1.refs_5_), channel_id=1, source_target_pairs={{0,224},{32,64},{64,32},{96,128},{128,96},{160,192},{192,160},{224... | collective-permute-start | bytes 1179656 | tf_op jit(solution)/shard_map/ppermute | solution.py:42
  73.6 3.4 %all-to-all-done.2 = f32[16,32,128]{2,1,0:T(8,128)S(1)} async-done(((f32[16,32,128]{2,1,0:T(8,128)}), f32[16,32,128]{2,1,0:T(8,128)S(1)}, u32[]{:S(2)}, u32[]{:S(2)}) %all-to-all-start.2) | async-done | bytes 262176 | tf_op jit(solution)/shard_map/all_to_all | solution.py:262
  77.0 3.7 %collective-permute-start.13 = (f32[2,256,128]{2,1,0:T(8,128)S(1)}, f32[2,256,128]{2,1,0:T(8,128)S(1)}, u32[]{:S(2)}, u32[]{:S(2)}) collective-permute-start(f32[2,256,128]{2,1,0:T(8,128)S(1)} %bitcast.54), channel_id=1, source_target_pairs={{0,32},{32,0},{1,33},{33,1},{2,34},{34,2},{3,35},{35,3},{4,36},{36... | collective-permute-start | bytes 786440 | tf_op jit(solution)/shard_map/ppermute | solution.py:266
  81.8 10.3 %shard_map.87 = (f32[3,2,16,8,128]{4,3,2,1,0:T(8,128)S(1)}, f32[3,2,16,8,128]{4,3,2,1,0:T(8,128)S(1)}, f32[3,2,16,8,128]{4,3,2,1,0:T(8,128)S(1)}, f32[2,256,128]...) custom-call(s32[3,8]{1,0:T(4,128)S(1)} %concatenate.3.refs_0_, ...), custom_call_target="tpu_custom_call" | custom-call | tf_op jit(solution)/shard_map/pallas_call | solution.py:241
  92.2 1.5 %collective-permute-start.14 = (f32[2,256,128]{2,1,0:T(8,128)S(1)}, f32[2,256,128]{2,1,0:T(8,128)S(1)}, u32[]{:S(2)}, u32[]{:S(2)}) collective-permute-start(f32[2,256,128]{2,1,0:T(8,128)S(1)} %get-tuple-element.35), channel_id=1, source_target_pairs={{0,32},{32,0},{1,33},{33,1},{2,34},{34,2},{3,35},{35,3},{4,36},{36... | collective-permute-start | bytes 786440 | tf_op jit(solution)/shard_map/ppermute | solution.py:266
  93.7 1.2 collective-permute-done.14
  94.9 12.6 %all_to_all.30 = f32[16,32,128]{2,1,0:T(8,128)S(1)} all-to-all(f32[16,32,128]{2,1,0:T(8,128)S(1)} %bitcast.61), channel_id=1, replica_groups=mesh['y'=4,'core'=2,'z'=8,'x'=4] {'y','x'}, dimensions={0} | all-to-all | bytes 524288 | tf_op jit(solution)/shard_map/all_to_all | solution.py:262
  107.5 1.3 collective-permute-start.15
  109.5 3.4 %all-to-all-start.4 = ((f32[8,32,128]{2,1,0:T(8,128)}), f32[8,32,128]{2,1,0:T(8,128)S(1)}, u32[]{:S(2)}, u32[]{:S(2)}) async-start(f32[8,32,128]{2,1,0:T(8,128)} %broadcast_in_dim.36), calls=%async_computation.4 | async-start | bytes 262144 | tf_op jit(solution)/shard_map/all_to_all | solution.py:262
  112.9 3.4 %collective-permute-done.16 = f32[3,2,16,8,128]{4,3,2,1,0:T(8,128)S(1)} collective-permute-done((f32[3,2,16,8,128]{4,3,2,1,0:T(8,128)S(1)}, f32[3,2,16,8,128]{4,3,2,1,0:T(8,128)S(1)}, u32[]{:S(2)}, u32[]{:S(2)}) %collective-permute-start.16) | collective-permute-done | bytes 393248 | tf_op jit(solution)/shard_map/ppermute | solution.py:42
  116.4 4.2 %all-to-all-done.4 = f32[8,32,128]{2,1,0:T(8,128)S(1)} async-done(((f32[8,32,128]{2,1,0:T(8,128)}), f32[8,32,128]{2,1,0:T(8,128)S(1)}, u32[]{:S(2)}, u32[]{:S(2)}) %all-to-all-start.4) | async-done | bytes 131104 | tf_op jit(solution)/shard_map/all_to_all | solution.py:262
  121.3 5.5 %all-to-all-start.5 = ((f32[16,32,128]{2,1,0:T(8,128)}), f32[16,32,128]{2,1,0:T(8,128)S(1)}, u32[]{:S(2)}, u32[]{:S(2)}) async-start(f32[16,32,128]{2,1,0:T(8,128)} %broadcast_in_dim.37), calls=%async_computation.5 | async-start | bytes 524288 | tf_op jit(solution)/shard_map/all_to_all | solution.py:262
  126.9 1.2 collective-permute-start.18
  128.0 1.4 collective-permute-start.17
  129.4 5.5 %all-to-all-done.5 = f32[16,32,128]{2,1,0:T(8,128)S(1)} async-done(((f32[16,32,128]{2,1,0:T(8,128)}), f32[16,32,128]{2,1,0:T(8,128)S(1)}, u32[]{:S(2)}, u32[]{:S(2)}) %all-to-all-start.5) | async-done | bytes 262176 | tf_op jit(solution)/shard_map/all_to_all | solution.py:262
  134.9 3.1 %collective-permute-start.19 = (f32[2,256,128]{2,1,0:T(8,128)S(1)}, f32[2,256,128]{2,1,0:T(8,128)S(1)}, u32[]{:S(2)}, u32[]{:S(2)}) collective-permute-start(f32[2,256,128]{2,1,0:T(8,128)S(1)} %bitcast.56), channel_id=1, source_target_pairs={{0,32},{32,0},{1,33},{33,1},{2,34},{34,2},{3,35},{35,3},{4,36},{36... | collective-permute-start | bytes 786440 | tf_op jit(solution)/shard_map/ppermute | solution.py:266
  139.1 1.2 shard_map.88
  (49 shorter events, 9.0 us)
Async XLA Ops:
  0.6 12.1 %collective-permute-start.1 = (f32[2,16,8,128]{3,2,1,0:T(8,128)}, f32[2,16,8,128]{3,2,1,0:T(8,128)S(1)}, u32[]{:S(2)}, u32[]{:S(2)}) collective-permute-start(f32[2,16,8,128]{3,2,1,0:T(8,128)} %bitcast.62), channel_id=1, source_target_pairs={{0,31},{1,2},{2,1},{3,4},{4,3},{5,6},{6,5},{7,8},{8,7},{9,10},{10,... | collective-permute-start | bytes 393224 | tf_op jit(solution)/shard_map/ppermute | solution.py:42
  9.3 4.3 %collective-permute-start = (f32[2,16,8,128]{3,2,1,0:T(8,128)}, f32[2,16,8,128]{3,2,1,0:T(8,128)S(1)}, u32[]{:S(2)}, u32[]{:S(2)}) collective-permute-start(f32[2,16,8,128]{3,2,1,0:T(8,128)} %bitcast.63), channel_id=1, source_target_pairs={{0,1},{1,0},{2,3},{3,2},{4,5},{5,4},{6,7},{7,6},{8,9},{9,8},{10,11... | collective-permute-start | bytes 393224 | tf_op jit(solution)/shard_map/ppermute | solution.py:42
  14.5 8.9 %collective-permute-start.3 = (f32[3,2,16,8,128]{4,3,2,1,0:T(8,128)S(1)}, f32[3,2,16,8,128]{4,3,2,1,0:T(8,128)S(1)}, u32[]{:S(2)}, u32[]{:S(2)}) collective-permute-start(f32[3,2,16,8,128]{4,3,2,1,0:T(8,128)S(1)} %pad_maximum_fusion.refs_5_), channel_id=1, source_target_pairs={{0,224},{32,64},{64,32},{96,128},{128,96},{160,192},{192,160},{224... | collective-permute-start | bytes 1179656 | tf_op jit(solution)/shard_map/ppermute | solution.py:42
  17.7 5.8 %collective-permute-start.2 = (f32[3,2,16,8,128]{4,3,2,1,0:T(8,128)S(1)}, f32[3,2,16,8,128]{4,3,2,1,0:T(8,128)S(1)}, u32[]{:S(2)}, u32[]{:S(2)}) collective-permute-start(f32[3,2,16,8,128]{4,3,2,1,0:T(8,128)S(1)} %pad_maximum_fusion.refs_5_), channel_id=1, source_target_pairs={{0,32},{32,0},{64,96},{96,64},{128,160},{160,128},{192,224},{224,1... | collective-permute-start | bytes 1179656 | tf_op jit(solution)/shard_map/ppermute | solution.py:42
  33.0 24.1 %copy-start.1 = (f32[2,128,128]{2,1,0:T(8,128)S(1)}, f32[2,128,128]{2,1,0:T(8,128)}, u32[]{:S(2)}) copy-start(f32[2,128,128]{2,1,0:T(8,128)} %param.7) | copy-start | bytes 393220
  33.1 2.7 %collective-permute-start.4 = (f32[2,256,128]{2,1,0:T(8,128)S(1)}, f32[2,256,128]{2,1,0:T(8,128)S(1)}, u32[]{:S(2)}, u32[]{:S(2)}) collective-permute-start(f32[2,256,128]{2,1,0:T(8,128)S(1)} %get-tuple-element.27), channel_id=1, source_target_pairs={{0,32},{32,0},{1,33},{33,1},{2,34},{34,2},{3,35},{35,3},{4,36},{36... | collective-permute-start | bytes 786440 | tf_op jit(solution)/shard_map/ppermute | solution.py:266
  36.5 4.5 %collective-permute-start.5 = (f32[3,2,16,8,128]{4,3,2,1,0:T(8,128)S(1)}, f32[3,2,16,8,128]{4,3,2,1,0:T(8,128)S(1)}, u32[]{:S(2)}, u32[]{:S(2)}) collective-permute-start(f32[3,2,16,8,128]{4,3,2,1,0:T(8,128)S(1)} %get-tuple-element.28), channel_id=1, source_target_pairs={{0,32},{32,0},{64,96},{96,64},{128,160},{160,128},{192,224},{224,1... | collective-permute-start | bytes 1179656 | tf_op jit(solution)/shard_map/ppermute | solution.py:42
  36.9 7.8 %collective-permute-start.6 = (f32[3,2,16,8,128]{4,3,2,1,0:T(8,128)S(1)}, f32[3,2,16,8,128]{4,3,2,1,0:T(8,128)S(1)}, u32[]{:S(2)}, u32[]{:S(2)}) collective-permute-start(f32[3,2,16,8,128]{4,3,2,1,0:T(8,128)S(1)} %get-tuple-element.29), channel_id=1, source_target_pairs={{0,224},{32,64},{64,32},{96,128},{128,96},{160,192},{192,160},{224... | collective-permute-start | bytes 1179656 | tf_op jit(solution)/shard_map/ppermute | solution.py:42
  37.0 11.9 %all-to-all-start = ((f32[16,32,128]{2,1,0:T(8,128)}), f32[16,32,128]{2,1,0:T(8,128)S(1)}, u32[]{:S(2)}, u32[]{:S(2)}) async-start(f32[16,32,128]{2,1,0:T(8,128)} %bitcast.14), calls=%async_computation | async-start | bytes 524288 | tf_op jit(solution)/shard_map/all_to_all | solution.py:262
  44.8 12.3 %collective-permute-start.8 = (f32[2,16,8,128]{3,2,1,0:T(8,128)S(1)}, f32[2,16,8,128]{3,2,1,0:T(8,128)S(1)}, u32[]{:S(2)}, u32[]{:S(2)}) collective-permute-start(f32[2,16,8,128]{3,2,1,0:T(8,128)S(1)} %get-tuple-element.46), channel_id=1, source_target_pairs={{0,31},{1,2},{2,1},{3,4},{4,3},{5,6},{6,5},{7,8},{8,7},{9,10},{10,... | collective-permute-start | bytes 393224 | tf_op jit(solution)/shard_map/ppermute | solution.py:42
  47.9 9.2 %collective-permute-start.7 = (f32[2,16,8,128]{3,2,1,0:T(8,128)S(1)}, f32[2,16,8,128]{3,2,1,0:T(8,128)S(1)}, u32[]{:S(2)}, u32[]{:S(2)}) collective-permute-start(f32[2,16,8,128]{3,2,1,0:T(8,128)S(1)} %get-tuple-element.47), channel_id=1, source_target_pairs={{0,1},{1,0},{2,3},{3,2},{4,5},{5,4},{6,7},{7,6},{8,9},{9,8},{10,11... | collective-permute-start | bytes 393224 | tf_op jit(solution)/shard_map/ppermute | solution.py:42
  49.7 15.5 %all-to-all-start.1 = ((f32[8,32,128]{2,1,0:T(8,128)}), f32[8,32,128]{2,1,0:T(8,128)S(1)}, u32[]{:S(2)}, u32[]{:S(2)}) async-start(f32[8,32,128]{2,1,0:T(8,128)} %broadcast_in_dim.34), calls=%async_computation.1 | async-start | bytes 262144 | tf_op jit(solution)/shard_map/all_to_all | solution.py:262
  57.2 12.3 %collective-permute-start.10 = (f32[2,16,8,128]{3,2,1,0:T(8,128)S(1)}, f32[2,16,8,128]{3,2,1,0:T(8,128)S(1)}, u32[]{:S(2)}, u32[]{:S(2)}) collective-permute-start(f32[2,16,8,128]{3,2,1,0:T(8,128)S(1)} %fusion.8), channel_id=1, source_target_pairs={{0,31},{1,2},{2,1},{3,4},{4,3},{5,6},{6,5},{7,8},{8,7},{9,10},{10,... | collective-permute-start | bytes 393224 | tf_op jit(solution)/shard_map/ppermute | solution.py:42
  57.7 11.7 %collective-permute-start.9 = (f32[2,16,8,128]{3,2,1,0:T(8,128)S(1)}, f32[2,16,8,128]{3,2,1,0:T(8,128)S(1)}, u32[]{:S(2)}, u32[]{:S(2)}) collective-permute-start(f32[2,16,8,128]{3,2,1,0:T(8,128)S(1)} %fusion.8), channel_id=1, source_target_pairs={{0,1},{1,0},{2,3},{3,2},{4,5},{5,4},{6,7},{7,6},{8,9},{9,8},{10,11... | collective-permute-start | bytes 393224 | tf_op jit(solution)/shard_map/ppermute | solution.py:42
  65.9 11.1 %all-to-all-start.2 = ((f32[16,32,128]{2,1,0:T(8,128)}), f32[16,32,128]{2,1,0:T(8,128)S(1)}, u32[]{:S(2)}, u32[]{:S(2)}) async-start(f32[16,32,128]{2,1,0:T(8,128)} %broadcast_in_dim.35), calls=%async_computation.2 | async-start | bytes 524288 | tf_op jit(solution)/shard_map/all_to_all | solution.py:262
  69.6 11.4 %collective-permute-start.12 = (f32[3,2,16,8,128]{4,3,2,1,0:T(8,128)S(1)}, f32[3,2,16,8,128]{4,3,2,1,0:T(8,128)S(1)}, u32[]{:S(2)}, u32[]{:S(2)}) collective-permute-start(f32[3,2,16,8,128]{4,3,2,1,0:T(8,128)S(1)} %pad_maximum_fusion.1.refs_5_), channel_id=1, source_target_pairs={{0,224},{32,64},{64,32},{96,128},{128,96},{160,192},{192,160},{224... | collective-permute-start | bytes 1179656 | tf_op jit(solution)/shard_map/ppermute | solution.py:42
  73.6 7.3 %collective-permute-start.11 = (f32[3,2,16,8,128]{4,3,2,1,0:T(8,128)S(1)}, f32[3,2,16,8,128]{4,3,2,1,0:T(8,128)S(1)}, u32[]{:S(2)}, u32[]{:S(2)}) collective-permute-start(f32[3,2,16,8,128]{4,3,2,1,0:T(8,128)S(1)} %pad_maximum_fusion.1.refs_5_), channel_id=1, source_target_pairs={{0,32},{32,0},{64,96},{96,64},{128,160},{160,128},{192,224},{224,1... | collective-permute-start | bytes 1179656 | tf_op jit(solution)/shard_map/ppermute | solution.py:42
  77.0 4.8 %collective-permute-start.13 = (f32[2,256,128]{2,1,0:T(8,128)S(1)}, f32[2,256,128]{2,1,0:T(8,128)S(1)}, u32[]{:S(2)}, u32[]{:S(2)}) collective-permute-start(f32[2,256,128]{2,1,0:T(8,128)S(1)} %bitcast.54), channel_id=1, source_target_pairs={{0,32},{32,0},{1,33},{33,1},{2,34},{34,2},{3,35},{35,3},{4,36},{36... | collective-permute-start | bytes 786440 | tf_op jit(solution)/shard_map/ppermute | solution.py:266
  80.9 0.9 copy-start.2
  92.2 2.7 %collective-permute-start.14 = (f32[2,256,128]{2,1,0:T(8,128)S(1)}, f32[2,256,128]{2,1,0:T(8,128)S(1)}, u32[]{:S(2)}, u32[]{:S(2)}) collective-permute-start(f32[2,256,128]{2,1,0:T(8,128)S(1)} %get-tuple-element.35), channel_id=1, source_target_pairs={{0,32},{32,0},{1,33},{33,1},{2,34},{34,2},{3,35},{35,3},{4,36},{36... | collective-permute-start | bytes 786440 | tf_op jit(solution)/shard_map/ppermute | solution.py:266
  107.5 5.4 %collective-permute-start.15 = (f32[3,2,16,8,128]{4,3,2,1,0:T(8,128)S(1)}, f32[3,2,16,8,128]{4,3,2,1,0:T(8,128)S(1)}, u32[]{:S(2)}, u32[]{:S(2)}) collective-permute-start(f32[3,2,16,8,128]{4,3,2,1,0:T(8,128)S(1)} %get-tuple-element.38), channel_id=1, source_target_pairs={{0,32},{32,0},{64,96},{96,64},{128,160},{160,128},{192,224},{224,1... | collective-permute-start | bytes 1179656 | tf_op jit(solution)/shard_map/ppermute | solution.py:42
  108.8 7.5 %collective-permute-start.16 = (f32[3,2,16,8,128]{4,3,2,1,0:T(8,128)S(1)}, f32[3,2,16,8,128]{4,3,2,1,0:T(8,128)S(1)}, u32[]{:S(2)}, u32[]{:S(2)}) collective-permute-start(f32[3,2,16,8,128]{4,3,2,1,0:T(8,128)S(1)} %get-tuple-element.39), channel_id=1, source_target_pairs={{0,224},{32,64},{64,32},{96,128},{128,96},{160,192},{192,160},{224... | collective-permute-start | bytes 1179656 | tf_op jit(solution)/shard_map/ppermute | solution.py:42
  108.8 30.3 %copy-start = (f32[2,2,256,128]{3,2,1,0:T(8,128)S(1)}, f32[2,2,256,128]{3,2,1,0:T(8,128)}, u32[]{:S(2)}) copy-start(f32[2,2,256,128]{3,2,1,0:T(8,128)} %get-tuple-element.41.probe_ref) | copy-start | bytes 1572868
  109.5 11.1 %all-to-all-start.4 = ((f32[8,32,128]{2,1,0:T(8,128)}), f32[8,32,128]{2,1,0:T(8,128)S(1)}, u32[]{:S(2)}, u32[]{:S(2)}) async-start(f32[8,32,128]{2,1,0:T(8,128)} %broadcast_in_dim.36), calls=%async_computation.4 | async-start | bytes 262144 | tf_op jit(solution)/shard_map/all_to_all | solution.py:262
  121.3 13.6 %all-to-all-start.5 = ((f32[16,32,128]{2,1,0:T(8,128)}), f32[16,32,128]{2,1,0:T(8,128)S(1)}, u32[]{:S(2)}, u32[]{:S(2)}) async-start(f32[16,32,128]{2,1,0:T(8,128)} %broadcast_in_dim.37), calls=%async_computation.5 | async-start | bytes 524288 | tf_op jit(solution)/shard_map/all_to_all | solution.py:262
  126.9 11.1 %collective-permute-start.18 = (f32[2,16,8,128]{3,2,1,0:T(8,128)S(1)}, f32[2,16,8,128]{3,2,1,0:T(8,128)S(1)}, u32[]{:S(2)}, u32[]{:S(2)}) collective-permute-start(f32[2,16,8,128]{3,2,1,0:T(8,128)S(1)} %get-tuple-element.44), channel_id=1, source_target_pairs={{0,31},{1,2},{2,1},{3,4},{4,3},{5,6},{6,5},{7,8},{8,7},{9,10},{10,... | collective-permute-start | bytes 393224 | tf_op jit(solution)/shard_map/ppermute | solution.py:42
  128.0 10.0 %collective-permute-start.17 = (f32[2,16,8,128]{3,2,1,0:T(8,128)S(1)}, f32[2,16,8,128]{3,2,1,0:T(8,128)S(1)}, u32[]{:S(2)}, u32[]{:S(2)}) collective-permute-start(f32[2,16,8,128]{3,2,1,0:T(8,128)S(1)} %get-tuple-element.45), channel_id=1, source_target_pairs={{0,1},{1,0},{2,3},{3,2},{4,5},{5,4},{6,7},{7,6},{8,9},{9,8},{10,11... | collective-permute-start | bytes 393224 | tf_op jit(solution)/shard_map/ppermute | solution.py:42
  134.9 4.2 %collective-permute-start.19 = (f32[2,256,128]{2,1,0:T(8,128)S(1)}, f32[2,256,128]{2,1,0:T(8,128)S(1)}, u32[]{:S(2)}, u32[]{:S(2)}) collective-permute-start(f32[2,256,128]{2,1,0:T(8,128)S(1)} %bitcast.56), channel_id=1, source_target_pairs={{0,32},{32,0},{1,33},{33,1},{2,34},{34,2},{3,35},{35,3},{4,36},{36... | collective-permute-start | bytes 786440 | tf_op jit(solution)/shard_map/ppermute | solution.py:266

commit v12 on v11

--- a/solution.py
+++ b/solution.py
@@ -338,7 +338,7 @@
     strips = (strip, paired(strip, ROW, 0), paired(strip, ROW, 2))
     row0, row1, row2, keep, send, peak = gradients(True, live_slots, patterns, tables, probe_field, *strips)
     half = keep + core_swap(send)
-    row0, row2 = after((row0, row2), half)
+    row2 = after(row2, half)
     sums = side_sum(row1, paired(row0, ROW, 0), paired(row2, ROW, 2), row_end)
     payloads = to_sides(sums)
     shares = after(plane_shares(half), *payloads)

time: 141 us -> 141 us (level)
  starting transfers between devices: 57.6 us -> 65.9 us
  Pallas kernels: 21.1 us -> 13.5 us
    pallas_call x2, Pallas kernels: 19.9 us -> 12.3 us  [gradients(): pl.pallas_call(functools.partial(gradient_kernel, first), out_shape=(stri...]
    ppermute x4, starting transfers between devices: 9.79 us -> 17.1 us  [core_swap(): return lax.ppermute(value, 'core', [(0, 1), (1, 0)])]
where the time goes in v12:
time: 141 us; the launch traced here: 140 us
  starting transfers between devices  65.9 us (47%)
  waiting for transfers between devices  40.4 us (29%)
  Pallas kernels  13.5 us (10%)
  blocking collectives  12.2 us (9%)
  local copies, waits for them, and re-layouts  3.48 us (2%)
  other arithmetic  2.76 us (2%)
  between operations  1.48 us (1%)
    ppermute x16, starting transfers between devices, paired(): return lax.ppermute(value, axes, pairs)  24.4 us
    all_to_all x5, starting transfers between devices, exchange(): return lax.all_to_all(value, axes, 0, 0, tiled=True)  24.3 us
    all_to_all x5, waiting for transfers between devices, exchange(): return lax.all_to_all(value, axes, 0, 0, tiled=True)  21.2 us
    ppermute x4, starting transfers between devices, core_swap(): return lax.ppermute(value, 'core', [(0, 1), (1, 0)])  17.1 us
    ppermute x16, waiting for transfers between devices, paired(): return lax.ppermute(value, axes, pairs)  15.6 us
    pallas_call x2, Pallas kernels, gradients(): pl.pallas_call(functools.partial(gradient_kernel, first), out_shape=(stri...  12.3 us
    all_to_all x1, blocking collectives, exchange(): return lax.all_to_all(value, axes, 0, 0, tiled=True)  12.2 us
    ppermute x4, waiting for transfers between devices, core_swap(): return lax.ppermute(value, 'core', [(0, 1), (1, 0)])  3.55 us
  transfers between devices with their start and end apart: 25, of which 15 were waited for; matrix products, arithmetic and copies ran while one was open for 3% of the time, Pallas kernels for 0%

profile of v12, /device:TPU:1, one launch (start us, length us, event | category | flops | bytes accessed | tf_op | source)
XLA Modules:
  0.0 139.7 jit_solution(11050479413567786691)
XLA Ops:
  0.6 8.7 %collective-permute-start.1 = (f32[2,16,8,128]{3,2,1,0:T(8,128)}, f32[2,16,8,128]{3,2,1,0:T(8,128)S(1)}, u32[]{:S(2)}, u32[]{:S(2)}) collective-permute-start(f32[2,16,8,128]{3,2,1,0:T(8,128)} %bitcast.62), channel_id=1, source_target_pairs={{0,31},{1,2},{2,1},{3,4},{4,3},{5,6},{6,5},{7,8},{8,7},{9,10},{10,... | collective-permute-start | bytes 393224 | tf_op jit(solution)/shard_map/ppermute | solution.py:42
  9.3 3.4 %collective-permute-done.1 = f32[2,16,8,128]{3,2,1,0:T(8,128)S(1)} collective-permute-done((f32[2,16,8,128]{3,2,1,0:T(8,128)}, f32[2,16,8,128]{3,2,1,0:T(8,128)S(1)}, u32[]{:S(2)}, u32[]{:S(2)}) %collective-permute-start.1) | collective-permute-done | bytes 131104 | tf_op jit(solution)/shard_map/ppermute | solution.py:42
  13.6 0.9 pad_maximum_fusion.refs_5_
  14.5 3.1 %collective-permute-start.3 = (f32[3,2,16,8,128]{4,3,2,1,0:T(8,128)S(1)}, f32[3,2,16,8,128]{4,3,2,1,0:T(8,128)S(1)}, u32[]{:S(2)}, u32[]{:S(2)}) collective-permute-start(f32[3,2,16,8,128]{4,3,2,1,0:T(8,128)S(1)} %pad_maximum_fusion.refs_5_), channel_id=1, source_target_pairs={{0,224},{32,64},{64,32},{96,128},{128,96},{160,192},{192,160},{224... | collective-permute-start | bytes 1179656 | tf_op jit(solution)/shard_map/ppermute | solution.py:42
  19.1 4.3 %collective-permute-done.3.refs_7_ = f32[3,2,16,8,128]{4,3,2,1,0:T(8,128)S(1)} collective-permute-done((f32[3,2,16,8,128]{4,3,2,1,0:T(8,128)S(1)}, f32[3,2,16,8,128]{4,3,2,1,0:T(8,128)S(1)}, u32[]{:S(2)}, u32[]{:S(2)}) %collective-permute-start.3) | collective-permute-done | bytes 393248 | tf_op jit(solution)/shard_map/ppermute | solution.py:42
  23.4 5.8 %shard_map.86 = (f32[3,2,16,8,128]{4,3,2,1,0:T(8,128)S(1)}, f32[3,2,16,8,128]{4,3,2,1,0:T(8,128)S(1)}, f32[3,2,16,8,128]{4,3,2,1,0:T(8,128)S(1)}, f32[2,256,128]...) custom-call(s32[3,8]{1,0:T(4,128)S(1)} %concatenate.3.refs_0_, f32[8,256,256]{2,1,0:T(8,128)} %bitcast.58, ...), custom_call_target="tpu_custom_call" | custom-call | tf_op jit(solution)/shard_map/pallas_call | solution.py:241
  29.3 5.3 %collective-permute-start.5 = (f32[2,256,128]{2,1,0:T(8,128)S(1)}, f32[2,256,128]{2,1,0:T(8,128)S(1)}, u32[]{:S(2)}, u32[]{:S(2)}) collective-permute-start(f32[2,256,128]{2,1,0:T(8,128)S(1)} %get-tuple-element.26), channel_id=1, source_target_pairs={{0,32},{32,0},{1,33},{33,1},{2,34},{34,2},{3,35},{35,3},{4,36},{36... | collective-permute-start | bytes 786440 | tf_op jit(solution)/shard_map/ppermute | solution.py:266
  34.7 1.1 collective-permute-done.5
  36.9 4.0 %all-to-all-start = ((f32[16,32,128]{2,1,0:T(8,128)}), f32[16,32,128]{2,1,0:T(8,128)S(1)}, u32[]{:S(2)}, u32[]{:S(2)}) async-start(f32[16,32,128]{2,1,0:T(8,128)} %bitcast.14), calls=%async_computation | async-start | bytes 524288 | tf_op jit(solution)/shard_map/all_to_all | solution.py:262
  40.9 3.3 %collective-permute-done.6 = f32[3,2,16,8,128]{4,3,2,1,0:T(8,128)S(1)} collective-permute-done((f32[3,2,16,8,128]{4,3,2,1,0:T(8,128)S(1)}, f32[3,2,16,8,128]{4,3,2,1,0:T(8,128)S(1)}, u32[]{:S(2)}, u32[]{:S(2)}) %collective-permute-start.6) | collective-permute-done | bytes 393248 | tf_op jit(solution)/shard_map/ppermute | solution.py:42
  44.3 3.2 %collective-permute-start.8 = (f32[2,16,8,128]{3,2,1,0:T(8,128)S(1)}, f32[2,16,8,128]{3,2,1,0:T(8,128)S(1)}, u32[]{:S(2)}, u32[]{:S(2)}) collective-permute-start(f32[2,16,8,128]{3,2,1,0:T(8,128)S(1)} %get-tuple-element.44), channel_id=1, source_target_pairs={{0,31},{1,2},{2,1},{3,4},{4,3},{5,6},{6,5},{7,8},{8,7},{9,10},{10,... | collective-permute-start | bytes 393224 | tf_op jit(solution)/shard_map/ppermute | solution.py:42
  47.5 0.9 all-to-all-done
  49.1 7.9 %all-to-all-start.1 = ((f32[8,32,128]{2,1,0:T(8,128)}), f32[8,32,128]{2,1,0:T(8,128)S(1)}, u32[]{:S(2)}, u32[]{:S(2)}) async-start(f32[8,32,128]{2,1,0:T(8,128)} %broadcast_in_dim.34), calls=%async_computation.1 | async-start | bytes 262144 | tf_op jit(solution)/shard_map/all_to_all | solution.py:262
  57.9 7.1 %all-to-all-done.1 = f32[8,32,128]{2,1,0:T(8,128)S(1)} async-done(((f32[8,32,128]{2,1,0:T(8,128)}), f32[8,32,128]{2,1,0:T(8,128)S(1)}, u32[]{:S(2)}, u32[]{:S(2)}) %all-to-all-start.1) | async-done | bytes 131104 | tf_op jit(solution)/shard_map/all_to_all | solution.py:262
  65.8 3.5 %all-to-all-start.2 = ((f32[16,32,128]{2,1,0:T(8,128)}), f32[16,32,128]{2,1,0:T(8,128)S(1)}, u32[]{:S(2)}, u32[]{:S(2)}) async-start(f32[16,32,128]{2,1,0:T(8,128)} %broadcast_in_dim.35), calls=%async_computation.2 | async-start | bytes 524288 | tf_op jit(solution)/shard_map/all_to_all | solution.py:262
  69.4 3.9 %collective-permute-start.12 = (f32[3,2,16,8,128]{4,3,2,1,0:T(8,128)S(1)}, f32[3,2,16,8,128]{4,3,2,1,0:T(8,128)S(1)}, u32[]{:S(2)}, u32[]{:S(2)}) collective-permute-start(f32[3,2,16,8,128]{4,3,2,1,0:T(8,128)S(1)} %pad_maximum_fusion.1.refs_5_), channel_id=1, source_target_pairs={{0,224},{32,64},{64,32},{96,128},{128,96},{160,192},{192,160},{224... | collective-permute-start | bytes 1179656 | tf_op jit(solution)/shard_map/ppermute | solution.py:42
  73.3 3.5 %all-to-all-done.2 = f32[16,32,128]{2,1,0:T(8,128)S(1)} async-done(((f32[16,32,128]{2,1,0:T(8,128)}), f32[16,32,128]{2,1,0:T(8,128)S(1)}, u32[]{:S(2)}, u32[]{:S(2)}) %all-to-all-start.2) | async-done | bytes 262176 | tf_op jit(solution)/shard_map/all_to_all | solution.py:262
  76.8 3.5 %collective-permute-start.13 = (f32[2,256,128]{2,1,0:T(8,128)S(1)}, f32[2,256,128]{2,1,0:T(8,128)S(1)}, u32[]{:S(2)}, u32[]{:S(2)}) collective-permute-start(f32[2,256,128]{2,1,0:T(8,128)S(1)} %bitcast.54), channel_id=1, source_target_pairs={{0,32},{32,0},{1,33},{33,1},{2,34},{34,2},{3,35},{35,3},{4,36},{36... | collective-permute-start | bytes 786440 | tf_op jit(solution)/shard_map/ppermute | solution.py:266
  81.5 6.5 %shard_map.87 = (f32[3,2,16,8,128]{4,3,2,1,0:T(8,128)S(1)}, f32[3,2,16,8,128]{4,3,2,1,0:T(8,128)S(1)}, f32[3,2,16,8,128]{4,3,2,1,0:T(8,128)S(1)}, f32[2,256,128]...) custom-call(s32[3,8]{1,0:T(4,128)S(1)} %concatenate.3.refs_0_, ...), custom_call_target="tpu_custom_call" | custom-call | tf_op jit(solution)/shard_map/pallas_call | solution.py:241
  88.0 5.2 %collective-permute-start.14 = (f32[2,256,128]{2,1,0:T(8,128)S(1)}, f32[2,256,128]{2,1,0:T(8,128)S(1)}, u32[]{:S(2)}, u32[]{:S(2)}) collective-permute-start(f32[2,256,128]{2,1,0:T(8,128)S(1)} %get-tuple-element.33), channel_id=1, source_target_pairs={{0,32},{32,0},{1,33},{33,1},{2,34},{34,2},{3,35},{35,3},{4,36},{36... | collective-permute-start | bytes 786440 | tf_op jit(solution)/shard_map/ppermute | solution.py:266
  93.3 1.2 collective-permute-done.14
  94.5 12.2 %all_to_all.30 = f32[16,32,128]{2,1,0:T(8,128)S(1)} all-to-all(f32[16,32,128]{2,1,0:T(8,128)S(1)} %bitcast.61), channel_id=1, replica_groups=mesh['y'=4,'core'=2,'z'=8,'x'=4] {'y','x'}, dimensions={0} | all-to-all | bytes 524288 | tf_op jit(solution)/shard_map/all_to_all | solution.py:262
  106.7 1.5 %collective-permute-start.15 = (f32[3,2,16,8,128]{4,3,2,1,0:T(8,128)S(1)}, f32[3,2,16,8,128]{4,3,2,1,0:T(8,128)S(1)}, u32[]{:S(2)}, u32[]{:S(2)}) collective-permute-start(f32[3,2,16,8,128]{4,3,2,1,0:T(8,128)S(1)} %get-tuple-element.36), channel_id=1, source_target_pairs={{0,32},{32,0},{64,96},{96,64},{128,160},{160,128},{192,224},{224,1... | collective-permute-start | bytes 1179656 | tf_op jit(solution)/shard_map/ppermute | solution.py:42
  108.9 3.4 %all-to-all-start.4 = ((f32[8,32,128]{2,1,0:T(8,128)}), f32[8,32,128]{2,1,0:T(8,128)S(1)}, u32[]{:S(2)}, u32[]{:S(2)}) async-start(f32[8,32,128]{2,1,0:T(8,128)} %broadcast_in_dim.36), calls=%async_computation.4 | async-start | bytes 262144 | tf_op jit(solution)/shard_map/all_to_all | solution.py:262
  112.3 3.4 %collective-permute-done.16 = f32[3,2,16,8,128]{4,3,2,1,0:T(8,128)S(1)} collective-permute-done((f32[3,2,16,8,128]{4,3,2,1,0:T(8,128)S(1)}, f32[3,2,16,8,128]{4,3,2,1,0:T(8,128)S(1)}, u32[]{:S(2)}, u32[]{:S(2)}) %collective-permute-start.16) | collective-permute-done | bytes 393248 | tf_op jit(solution)/shard_map/ppermute | solution.py:42
  115.8 4.2 %all-to-all-done.4 = f32[8,32,128]{2,1,0:T(8,128)S(1)} async-done(((f32[8,32,128]{2,1,0:T(8,128)}), f32[8,32,128]{2,1,0:T(8,128)S(1)}, u32[]{:S(2)}, u32[]{:S(2)}) %all-to-all-start.4) | async-done | bytes 131104 | tf_op jit(solution)/shard_map/all_to_all | solution.py:262
  120.7 5.5 %all-to-all-start.5 = ((f32[16,32,128]{2,1,0:T(8,128)}), f32[16,32,128]{2,1,0:T(8,128)S(1)}, u32[]{:S(2)}, u32[]{:S(2)}) async-start(f32[16,32,128]{2,1,0:T(8,128)} %broadcast_in_dim.37), calls=%async_computation.5 | async-start | bytes 524288 | tf_op jit(solution)/shard_map/all_to_all | solution.py:262
  126.2 1.2 collective-permute-start.18
  127.4 1.4 collective-permute-start.17
  128.8 5.5 %all-to-all-done.5 = f32[16,32,128]{2,1,0:T(8,128)S(1)} async-done(((f32[16,32,128]{2,1,0:T(8,128)}), f32[16,32,128]{2,1,0:T(8,128)S(1)}, u32[]{:S(2)}, u32[]{:S(2)}) %all-to-all-start.5) | async-done | bytes 262176 | tf_op jit(solution)/shard_map/all_to_all | solution.py:262
  134.3 3.1 %collective-permute-start.19 = (f32[2,256,128]{2,1,0:T(8,128)S(1)}, f32[2,256,128]{2,1,0:T(8,128)S(1)}, u32[]{:S(2)}, u32[]{:S(2)}) collective-permute-start(f32[2,256,128]{2,1,0:T(8,128)S(1)} %bitcast.56), channel_id=1, source_target_pairs={{0,32},{32,0},{1,33},{33,1},{2,34},{34,2},{3,35},{35,3},{4,36},{36... | collective-permute-start | bytes 786440 | tf_op jit(solution)/shard_map/ppermute | solution.py:266
  138.5 1.2 shard_map.88
  (49 shorter events, 9.2 us)
Async XLA Ops:
  0.6 12.1 %collective-permute-start.1 = (f32[2,16,8,128]{3,2,1,0:T(8,128)}, f32[2,16,8,128]{3,2,1,0:T(8,128)S(1)}, u32[]{:S(2)}, u32[]{:S(2)}) collective-permute-start(f32[2,16,8,128]{3,2,1,0:T(8,128)} %bitcast.62), channel_id=1, source_target_pairs={{0,31},{1,2},{2,1},{3,4},{4,3},{5,6},{6,5},{7,8},{8,7},{9,10},{10,... | collective-permute-start | bytes 393224 | tf_op jit(solution)/shard_map/ppermute | solution.py:42
  9.3 4.3 %collective-permute-start = (f32[2,16,8,128]{3,2,1,0:T(8,128)}, f32[2,16,8,128]{3,2,1,0:T(8,128)S(1)}, u32[]{:S(2)}, u32[]{:S(2)}) collective-permute-start(f32[2,16,8,128]{3,2,1,0:T(8,128)} %bitcast.63), channel_id=1, source_target_pairs={{0,1},{1,0},{2,3},{3,2},{4,5},{5,4},{6,7},{7,6},{8,9},{9,8},{10,11... | collective-permute-start | bytes 393224 | tf_op jit(solution)/shard_map/ppermute | solution.py:42
  14.5 8.9 %collective-permute-start.3 = (f32[3,2,16,8,128]{4,3,2,1,0:T(8,128)S(1)}, f32[3,2,16,8,128]{4,3,2,1,0:T(8,128)S(1)}, u32[]{:S(2)}, u32[]{:S(2)}) collective-permute-start(f32[3,2,16,8,128]{4,3,2,1,0:T(8,128)S(1)} %pad_maximum_fusion.refs_5_), channel_id=1, source_target_pairs={{0,224},{32,64},{64,32},{96,128},{128,96},{160,192},{192,160},{224... | collective-permute-start | bytes 1179656 | tf_op jit(solution)/shard_map/ppermute | solution.py:42
  17.7 5.8 %collective-permute-start.2 = (f32[3,2,16,8,128]{4,3,2,1,0:T(8,128)S(1)}, f32[3,2,16,8,128]{4,3,2,1,0:T(8,128)S(1)}, u32[]{:S(2)}, u32[]{:S(2)}) collective-permute-start(f32[3,2,16,8,128]{4,3,2,1,0:T(8,128)S(1)} %pad_maximum_fusion.refs_5_), channel_id=1, source_target_pairs={{0,32},{32,0},{64,96},{96,64},{128,160},{160,128},{192,224},{224,1... | collective-permute-start | bytes 1179656 | tf_op jit(solution)/shard_map/ppermute | solution.py:42
  29.3 27.7 %copy-start.1 = (f32[2,128,128]{2,1,0:T(8,128)S(1)}, f32[2,128,128]{2,1,0:T(8,128)}, u32[]{:S(2)}) copy-start(f32[2,128,128]{2,1,0:T(8,128)} %param.7) | copy-start | bytes 393220
  29.3 6.5 %collective-permute-start.5 = (f32[2,256,128]{2,1,0:T(8,128)S(1)}, f32[2,256,128]{2,1,0:T(8,128)S(1)}, u32[]{:S(2)}, u32[]{:S(2)}) collective-permute-start(f32[2,256,128]{2,1,0:T(8,128)S(1)} %get-tuple-element.26), channel_id=1, source_target_pairs={{0,32},{32,0},{1,33},{33,1},{2,34},{34,2},{3,35},{35,3},{4,36},{36... | collective-permute-start | bytes 786440 | tf_op jit(solution)/shard_map/ppermute | solution.py:266
  34.6 6.3 %collective-permute-start.4 = (f32[3,2,16,8,128]{4,3,2,1,0:T(8,128)S(1)}, f32[3,2,16,8,128]{4,3,2,1,0:T(8,128)S(1)}, u32[]{:S(2)}, u32[]{:S(2)}) collective-permute-start(f32[3,2,16,8,128]{4,3,2,1,0:T(8,128)S(1)} %get-tuple-element.23), channel_id=1, source_target_pairs={{0,32},{32,0},{64,96},{96,64},{128,160},{160,128},{192,224},{224,1... | collective-permute-start | bytes 1179656 | tf_op jit(solution)/shard_map/ppermute | solution.py:42
  36.5 7.7 %collective-permute-start.6 = (f32[3,2,16,8,128]{4,3,2,1,0:T(8,128)S(1)}, f32[3,2,16,8,128]{4,3,2,1,0:T(8,128)S(1)}, u32[]{:S(2)}, u32[]{:S(2)}) collective-permute-start(f32[3,2,16,8,128]{4,3,2,1,0:T(8,128)S(1)} %get-tuple-element.27), channel_id=1, source_target_pairs={{0,224},{32,64},{64,32},{96,128},{128,96},{160,192},{192,160},{224... | collective-permute-start | bytes 1179656 | tf_op jit(solution)/shard_map/ppermute | solution.py:42
  36.9 11.6 %all-to-all-start = ((f32[16,32,128]{2,1,0:T(8,128)}), f32[16,32,128]{2,1,0:T(8,128)S(1)}, u32[]{:S(2)}, u32[]{:S(2)}) async-start(f32[16,32,128]{2,1,0:T(8,128)} %bitcast.14), calls=%async_computation | async-start | bytes 524288 | tf_op jit(solution)/shard_map/all_to_all | solution.py:262
  44.3 12.7 %collective-permute-start.8 = (f32[2,16,8,128]{3,2,1,0:T(8,128)S(1)}, f32[2,16,8,128]{3,2,1,0:T(8,128)S(1)}, u32[]{:S(2)}, u32[]{:S(2)}) collective-permute-start(f32[2,16,8,128]{3,2,1,0:T(8,128)S(1)} %get-tuple-element.44), channel_id=1, source_target_pairs={{0,31},{1,2},{2,1},{3,4},{4,3},{5,6},{6,5},{7,8},{8,7},{9,10},{10,... | collective-permute-start | bytes 393224 | tf_op jit(solution)/shard_map/ppermute | solution.py:42
  47.5 9.5 %collective-permute-start.7 = (f32[2,16,8,128]{3,2,1,0:T(8,128)S(1)}, f32[2,16,8,128]{3,2,1,0:T(8,128)S(1)}, u32[]{:S(2)}, u32[]{:S(2)}) collective-permute-start(f32[2,16,8,128]{3,2,1,0:T(8,128)S(1)} %get-tuple-element.45), channel_id=1, source_target_pairs={{0,1},{1,0},{2,3},{3,2},{4,5},{5,4},{6,7},{7,6},{8,9},{9,8},{10,11... | collective-permute-start | bytes 393224 | tf_op jit(solution)/shard_map/ppermute | solution.py:42
  49.1 15.9 %all-to-all-start.1 = ((f32[8,32,128]{2,1,0:T(8,128)}), f32[8,32,128]{2,1,0:T(8,128)S(1)}, u32[]{:S(2)}, u32[]{:S(2)}) async-start(f32[8,32,128]{2,1,0:T(8,128)} %broadcast_in_dim.34), calls=%async_computation.1 | async-start | bytes 262144 | tf_op jit(solution)/shard_map/all_to_all | solution.py:262
  57.1 12.3 %collective-permute-start.10 = (f32[2,16,8,128]{3,2,1,0:T(8,128)S(1)}, f32[2,16,8,128]{3,2,1,0:T(8,128)S(1)}, u32[]{:S(2)}, u32[]{:S(2)}) collective-permute-start(f32[2,16,8,128]{3,2,1,0:T(8,128)S(1)} %fusion.8), channel_id=1, source_target_pairs={{0,31},{1,2},{2,1},{3,4},{4,3},{5,6},{6,5},{7,8},{8,7},{9,10},{10,... | collective-permute-start | bytes 393224 | tf_op jit(solution)/shard_map/ppermute | solution.py:42
  57.9 11.4 %collective-permute-start.9 = (f32[2,16,8,128]{3,2,1,0:T(8,128)S(1)}, f32[2,16,8,128]{3,2,1,0:T(8,128)S(1)}, u32[]{:S(2)}, u32[]{:S(2)}) collective-permute-start(f32[2,16,8,128]{3,2,1,0:T(8,128)S(1)} %fusion.8), channel_id=1, source_target_pairs={{0,1},{1,0},{2,3},{3,2},{4,5},{5,4},{6,7},{7,6},{8,9},{9,8},{10,11... | collective-permute-start | bytes 393224 | tf_op jit(solution)/shard_map/ppermute | solution.py:42
  65.8 11.1 %all-to-all-start.2 = ((f32[16,32,128]{2,1,0:T(8,128)}), f32[16,32,128]{2,1,0:T(8,128)S(1)}, u32[]{:S(2)}, u32[]{:S(2)}) async-start(f32[16,32,128]{2,1,0:T(8,128)} %broadcast_in_dim.35), calls=%async_computation.2 | async-start | bytes 524288 | tf_op jit(solution)/shard_map/all_to_all | solution.py:262
  69.4 11.3 %collective-permute-start.12 = (f32[3,2,16,8,128]{4,3,2,1,0:T(8,128)S(1)}, f32[3,2,16,8,128]{4,3,2,1,0:T(8,128)S(1)}, u32[]{:S(2)}, u32[]{:S(2)}) collective-permute-start(f32[3,2,16,8,128]{4,3,2,1,0:T(8,128)S(1)} %pad_maximum_fusion.1.refs_5_), channel_id=1, source_target_pairs={{0,224},{32,64},{64,32},{96,128},{128,96},{160,192},{192,160},{224... | collective-permute-start | bytes 1179656 | tf_op jit(solution)/shard_map/ppermute | solution.py:42
  73.3 7.4 %collective-permute-start.11 = (f32[3,2,16,8,128]{4,3,2,1,0:T(8,128)S(1)}, f32[3,2,16,8,128]{4,3,2,1,0:T(8,128)S(1)}, u32[]{:S(2)}, u32[]{:S(2)}) collective-permute-start(f32[3,2,16,8,128]{4,3,2,1,0:T(8,128)S(1)} %pad_maximum_fusion.1.refs_5_), channel_id=1, source_target_pairs={{0,32},{32,0},{64,96},{96,64},{128,160},{160,128},{192,224},{224,1... | collective-permute-start | bytes 1179656 | tf_op jit(solution)/shard_map/ppermute | solution.py:42
  76.8 4.7 %collective-permute-start.13 = (f32[2,256,128]{2,1,0:T(8,128)S(1)}, f32[2,256,128]{2,1,0:T(8,128)S(1)}, u32[]{:S(2)}, u32[]{:S(2)}) collective-permute-start(f32[2,256,128]{2,1,0:T(8,128)S(1)} %bitcast.54), channel_id=1, source_target_pairs={{0,32},{32,0},{1,33},{33,1},{2,34},{34,2},{3,35},{35,3},{4,36},{36... | collective-permute-start | bytes 786440 | tf_op jit(solution)/shard_map/ppermute | solution.py:266
  80.6 0.9 copy-start.2
  88.0 6.4 %collective-permute-start.14 = (f32[2,256,128]{2,1,0:T(8,128)S(1)}, f32[2,256,128]{2,1,0:T(8,128)S(1)}, u32[]{:S(2)}, u32[]{:S(2)}) collective-permute-start(f32[2,256,128]{2,1,0:T(8,128)S(1)} %get-tuple-element.33), channel_id=1, source_target_pairs={{0,32},{32,0},{1,33},{33,1},{2,34},{34,2},{3,35},{35,3},{4,36},{36... | collective-permute-start | bytes 786440 | tf_op jit(solution)/shard_map/ppermute | solution.py:266
  106.7 5.6 %collective-permute-start.15 = (f32[3,2,16,8,128]{4,3,2,1,0:T(8,128)S(1)}, f32[3,2,16,8,128]{4,3,2,1,0:T(8,128)S(1)}, u32[]{:S(2)}, u32[]{:S(2)}) collective-permute-start(f32[3,2,16,8,128]{4,3,2,1,0:T(8,128)S(1)} %get-tuple-element.36), channel_id=1, source_target_pairs={{0,32},{32,0},{64,96},{96,64},{128,160},{160,128},{192,224},{224,1... | collective-permute-start | bytes 1179656 | tf_op jit(solution)/shard_map/ppermute | solution.py:42
  108.2 7.5 %collective-permute-start.16 = (f32[3,2,16,8,128]{4,3,2,1,0:T(8,128)S(1)}, f32[3,2,16,8,128]{4,3,2,1,0:T(8,128)S(1)}, u32[]{:S(2)}, u32[]{:S(2)}) collective-permute-start(f32[3,2,16,8,128]{4,3,2,1,0:T(8,128)S(1)} %get-tuple-element.37), channel_id=1, source_target_pairs={{0,224},{32,64},{64,32},{96,128},{128,96},{160,192},{192,160},{224... | collective-permute-start | bytes 1179656 | tf_op jit(solution)/shard_map/ppermute | solution.py:42
  108.2 30.3 %copy-start = (f32[2,2,256,128]{3,2,1,0:T(8,128)S(1)}, f32[2,2,256,128]{3,2,1,0:T(8,128)}, u32[]{:S(2)}) copy-start(f32[2,2,256,128]{3,2,1,0:T(8,128)} %get-tuple-element.39.probe_ref) | copy-start | bytes 1572868
  108.9 11.1 %all-to-all-start.4 = ((f32[8,32,128]{2,1,0:T(8,128)}), f32[8,32,128]{2,1,0:T(8,128)S(1)}, u32[]{:S(2)}, u32[]{:S(2)}) async-start(f32[8,32,128]{2,1,0:T(8,128)} %broadcast_in_dim.36), calls=%async_computation.4 | async-start | bytes 262144 | tf_op jit(solution)/shard_map/all_to_all | solution.py:262
  120.7 13.6 %all-to-all-start.5 = ((f32[16,32,128]{2,1,0:T(8,128)}), f32[16,32,128]{2,1,0:T(8,128)S(1)}, u32[]{:S(2)}, u32[]{:S(2)}) async-start(f32[16,32,128]{2,1,0:T(8,128)} %broadcast_in_dim.37), calls=%async_computation.5 | async-start | bytes 524288 | tf_op jit(solution)/shard_map/all_to_all | solution.py:262
  126.2 11.1 %collective-permute-start.18 = (f32[2,16,8,128]{3,2,1,0:T(8,128)S(1)}, f32[2,16,8,128]{3,2,1,0:T(8,128)S(1)}, u32[]{:S(2)}, u32[]{:S(2)}) collective-permute-start(f32[2,16,8,128]{3,2,1,0:T(8,128)S(1)} %get-tuple-element.42), channel_id=1, source_target_pairs={{0,31},{1,2},{2,1},{3,4},{4,3},{5,6},{6,5},{7,8},{8,7},{9,10},{10,... | collective-permute-start | bytes 393224 | tf_op jit(solution)/shard_map/ppermute | solution.py:42
  127.4 10.0 %collective-permute-start.17 = (f32[2,16,8,128]{3,2,1,0:T(8,128)S(1)}, f32[2,16,8,128]{3,2,1,0:T(8,128)S(1)}, u32[]{:S(2)}, u32[]{:S(2)}) collective-permute-start(f32[2,16,8,128]{3,2,1,0:T(8,128)S(1)} %get-tuple-element.43), channel_id=1, source_target_pairs={{0,1},{1,0},{2,3},{3,2},{4,5},{5,4},{6,7},{7,6},{8,9},{9,8},{10,11... | collective-permute-start | bytes 393224 | tf_op jit(solution)/shard_map/ppermute | solution.py:42
  134.3 4.2 %collective-permute-start.19 = (f32[2,256,128]{2,1,0:T(8,128)S(1)}, f32[2,256,128]{2,1,0:T(8,128)S(1)}, u32[]{:S(2)}, u32[]{:S(2)}) collective-permute-start(f32[2,256,128]{2,1,0:T(8,128)S(1)} %bitcast.56), channel_id=1, source_target_pairs={{0,32},{32,0},{1,33},{33,1},{2,34},{34,2},{3,35},{35,3},{4,36},{36... | collective-permute-start | bytes 786440 | tf_op jit(solution)/shard_map/ppermute | solution.py:266

commit v13 on v11

--- a/solution.py
+++ b/solution.py
@@ -147,11 +147,11 @@
     state_b = windows(pairs[1])
     exit_b = exits(state_b)
     far_a = right_side(mid_a, right)
+    pattern_copy(group).wait()
     mid_b = left_side(exit_b, left)
-    pattern_copy(group).wait()
     misfit_a = misfits(far_a, pairs[0])
+    mid_a = left_side(misfit_a, right)
     far_b = right_side(mid_b, right)
-    mid_a = left_side(misfit_a, right)
     misfit_b = misfits(far_b, pairs[1])
     back_a = right_side(mid_a, left)
     mid_b = left_side(misfit_b, right)

time: 141 us -> 141 us (level)
  Pallas kernels: 21.1 us -> 13.7 us
  starting transfers between devices: 57.6 us -> 62.4 us
  blocking collectives: 12.6 us -> 16.9 us
  waiting for transfers between devices: 41.3 us -> 39 us
    pallas_call x2, Pallas kernels: 19.9 us -> 12.5 us  [gradients(): pl.pallas_call(functools.partial(gradient_kernel, first), out_shape=(stri...]
    ppermute x16, starting transfers between devices: 24 us -> 29.4 us  [paired(): return lax.ppermute(value, axes, pairs)]
    all_to_all x1, blocking collectives: 12.6 us -> 16.9 us  [exchange(): return lax.all_to_all(value, axes, 0, 0, tiled=True)]
    ppermute x16, waiting for transfers between devices: 16 us -> 14.1 us  [paired(): return lax.ppermute(value, axes, pairs)]
where the time goes in v13:
time: 141 us; the launch traced here: 140 us
  starting transfers between devices  62.4 us (44%)
  waiting for transfers between devices  39 us (28%)
  blocking collectives  16.9 us (12%)
  Pallas kernels  13.7 us (10%)
  local copies, waits for them, and re-layouts  3.48 us (2%)
  other arithmetic  2.76 us (2%)
  between operations  1.48 us (1%)
    ppermute x16, starting transfers between devices, paired(): return lax.ppermute(value, axes, pairs)  29.4 us
    all_to_all x5, starting transfers between devices, exchange(): return lax.all_to_all(value, axes, 0, 0, tiled=True)  23.2 us
    all_to_all x5, waiting for transfers between devices, exchange(): return lax.all_to_all(value, axes, 0, 0, tiled=True)  21.1 us
    all_to_all x1, blocking collectives, exchange(): return lax.all_to_all(value, axes, 0, 0, tiled=True)  16.9 us
    ppermute x16, waiting for transfers between devices, paired(): return lax.ppermute(value, axes, pairs)  14.1 us
    pallas_call x2, Pallas kernels, gradients(): pl.pallas_call(functools.partial(gradient_kernel, first), out_shape=(stri...  12.5 us
    ppermute x4, starting transfers between devices, core_swap(): return lax.ppermute(value, 'core', [(0, 1), (1, 0)])  9.83 us
    ppermute x4, waiting for transfers between devices, core_swap(): return lax.ppermute(value, 'core', [(0, 1), (1, 0)])  3.83 us
  transfers between devices with their start and end apart: 25, of which 15 were waited for; matrix products, arithmetic and copies ran while one was open for 3% of the time, Pallas kernels for 0%

profile of v13, /device:TPU:1, one launch (start us, length us, event | category | flops | bytes accessed | tf_op | source)
XLA Modules:
  0.0 139.7 jit_solution(12275559234512328705)
XLA Ops:
  0.6 8.7 %collective-permute-start.1 = (f32[2,16,8,128]{3,2,1,0:T(8,128)}, f32[2,16,8,128]{3,2,1,0:T(8,128)S(1)}, u32[]{:S(2)}, u32[]{:S(2)}) collective-permute-start(f32[2,16,8,128]{3,2,1,0:T(8,128)} %bitcast.62), channel_id=1, source_target_pairs={{0,31},{1,2},{2,1},{3,4},{4,3},{5,6},{6,5},{7,8},{8,7},{9,10},{10,... | collective-permute-start | bytes 393224 | tf_op jit(solution)/shard_map/ppermute | solution.py:42
  9.3 3.4 %collective-permute-done.1 = f32[2,16,8,128]{3,2,1,0:T(8,128)S(1)} collective-permute-done((f32[2,16,8,128]{3,2,1,0:T(8,128)}, f32[2,16,8,128]{3,2,1,0:T(8,128)S(1)}, u32[]{:S(2)}, u32[]{:S(2)}) %collective-permute-start.1) | collective-permute-done | bytes 131104 | tf_op jit(solution)/shard_map/ppermute | solution.py:42
  14.5 3.1 %collective-permute-start.3 = (f32[3,2,16,8,128]{4,3,2,1,0:T(8,128)S(1)}, f32[3,2,16,8,128]{4,3,2,1,0:T(8,128)S(1)}, u32[]{:S(2)}, u32[]{:S(2)}) collective-permute-start(f32[3,2,16,8,128]{4,3,2,1,0:T(8,128)S(1)} %pad_maximum_fusion.refs_5_), channel_id=1, source_target_pairs={{0,224},{32,64},{64,32},{96,128},{128,96},{160,192},{192,160},{224... | collective-permute-start | bytes 1179656 | tf_op jit(solution)/shard_map/ppermute | solution.py:42
  19.1 4.3 %collective-permute-done.3.refs_7_ = f32[3,2,16,8,128]{4,3,2,1,0:T(8,128)S(1)} collective-permute-done((f32[3,2,16,8,128]{4,3,2,1,0:T(8,128)S(1)}, f32[3,2,16,8,128]{4,3,2,1,0:T(8,128)S(1)}, u32[]{:S(2)}, u32[]{:S(2)}) %collective-permute-start.3) | collective-permute-done | bytes 393248 | tf_op jit(solution)/shard_map/ppermute | solution.py:42
  23.4 5.9 %shard_map.86 = (f32[3,2,16,8,128]{4,3,2,1,0:T(8,128)S(1)}, f32[3,2,16,8,128]{4,3,2,1,0:T(8,128)S(1)}, f32[3,2,16,8,128]{4,3,2,1,0:T(8,128)S(1)}, f32[2,256,128]...) custom-call(s32[3,8]{1,0:T(4,128)S(1)} %concatenate.3.refs_0_, f32[8,256,256]{2,1,0:T(8,128)} %bitcast.58, ...), custom_call_target="tpu_custom_call" | custom-call | tf_op jit(solution)/shard_map/pallas_call | solution.py:241
  29.4 1.6 %collective-permute-start.4 = (f32[2,256,128]{2,1,0:T(8,128)S(1)}, f32[2,256,128]{2,1,0:T(8,128)S(1)}, u32[]{:S(2)}, u32[]{:S(2)}) collective-permute-start(f32[2,256,128]{2,1,0:T(8,128)S(1)} %get-tuple-element.27), channel_id=1, source_target_pairs={{0,32},{32,0},{1,33},{33,1},{2,34},{34,2},{3,35},{35,3},{4,36},{36... | collective-permute-start | bytes 786440 | tf_op jit(solution)/shard_map/ppermute | solution.py:266
  30.9 1.2 collective-permute-done.4
  33.2 3.8 %collective-permute-start.6 = (f32[3,2,16,8,128]{4,3,2,1,0:T(8,128)S(1)}, f32[3,2,16,8,128]{4,3,2,1,0:T(8,128)S(1)}, u32[]{:S(2)}, u32[]{:S(2)}) collective-permute-start(f32[3,2,16,8,128]{4,3,2,1,0:T(8,128)S(1)} %get-tuple-element.29), channel_id=1, source_target_pairs={{0,224},{32,64},{64,32},{96,128},{128,96},{160,192},{192,160},{224... | collective-permute-start | bytes 1179656 | tf_op jit(solution)/shard_map/ppermute | solution.py:42
  37.0 3.8 %all-to-all-start = ((f32[16,32,128]{2,1,0:T(8,128)}), f32[16,32,128]{2,1,0:T(8,128)S(1)}, u32[]{:S(2)}, u32[]{:S(2)}) async-start(f32[16,32,128]{2,1,0:T(8,128)} %bitcast.14), calls=%async_computation | async-start | bytes 524288 | tf_op jit(solution)/shard_map/all_to_all | solution.py:262
  40.8 1.9 %collective-permute-done.6 = f32[3,2,16,8,128]{4,3,2,1,0:T(8,128)S(1)} collective-permute-done((f32[3,2,16,8,128]{4,3,2,1,0:T(8,128)S(1)}, f32[3,2,16,8,128]{4,3,2,1,0:T(8,128)S(1)}, u32[]{:S(2)}, u32[]{:S(2)}) %collective-permute-start.6) | collective-permute-done | bytes 393248 | tf_op jit(solution)/shard_map/ppermute | solution.py:42
  42.9 3.2 %collective-permute-start.8 = (f32[2,16,8,128]{3,2,1,0:T(8,128)S(1)}, f32[2,16,8,128]{3,2,1,0:T(8,128)S(1)}, u32[]{:S(2)}, u32[]{:S(2)}) collective-permute-start(f32[2,16,8,128]{3,2,1,0:T(8,128)S(1)} %get-tuple-element.46), channel_id=1, source_target_pairs={{0,31},{1,2},{2,1},{3,4},{4,3},{5,6},{6,5},{7,8},{8,7},{9,10},{10,... | collective-permute-start | bytes 393224 | tf_op jit(solution)/shard_map/ppermute | solution.py:42
  46.1 2.3 %all-to-all-done = f32[16,32,128]{2,1,0:T(8,128)S(1)} async-done(((f32[16,32,128]{2,1,0:T(8,128)}), f32[16,32,128]{2,1,0:T(8,128)S(1)}, u32[]{:S(2)}, u32[]{:S(2)}) %all-to-all-start) | async-done | bytes 262176 | tf_op jit(solution)/shard_map/all_to_all | solution.py:262
  49.1 6.9 %all-to-all-start.1 = ((f32[8,32,128]{2,1,0:T(8,128)}), f32[8,32,128]{2,1,0:T(8,128)S(1)}, u32[]{:S(2)}, u32[]{:S(2)}) async-start(f32[8,32,128]{2,1,0:T(8,128)} %broadcast_in_dim.34), calls=%async_computation.1 | async-start | bytes 262144 | tf_op jit(solution)/shard_map/all_to_all | solution.py:262
  56.0 1.8 %collective-permute-start.10 = (f32[2,16,8,128]{3,2,1,0:T(8,128)S(1)}, f32[2,16,8,128]{3,2,1,0:T(8,128)S(1)}, u32[]{:S(2)}, u32[]{:S(2)}) collective-permute-start(f32[2,16,8,128]{3,2,1,0:T(8,128)S(1)} %fusion.8), channel_id=1, source_target_pairs={{0,31},{1,2},{2,1},{3,4},{4,3},{5,6},{6,5},{7,8},{8,7},{9,10},{10,... | collective-permute-start | bytes 393224 | tf_op jit(solution)/shard_map/ppermute | solution.py:42
  57.8 6.1 %all-to-all-done.1 = f32[8,32,128]{2,1,0:T(8,128)S(1)} async-done(((f32[8,32,128]{2,1,0:T(8,128)}), f32[8,32,128]{2,1,0:T(8,128)S(1)}, u32[]{:S(2)}, u32[]{:S(2)}) %all-to-all-start.1) | async-done | bytes 131104 | tf_op jit(solution)/shard_map/all_to_all | solution.py:262
  64.7 3.5 %all-to-all-start.2 = ((f32[16,32,128]{2,1,0:T(8,128)}), f32[16,32,128]{2,1,0:T(8,128)S(1)}, u32[]{:S(2)}, u32[]{:S(2)}) async-start(f32[16,32,128]{2,1,0:T(8,128)} %broadcast_in_dim.35), calls=%async_computation.2 | async-start | bytes 524288 | tf_op jit(solution)/shard_map/all_to_all | solution.py:262
  68.3 4.5 %collective-permute-start.12 = (f32[3,2,16,8,128]{4,3,2,1,0:T(8,128)S(1)}, f32[3,2,16,8,128]{4,3,2,1,0:T(8,128)S(1)}, u32[]{:S(2)}, u32[]{:S(2)}) collective-permute-start(f32[3,2,16,8,128]{4,3,2,1,0:T(8,128)S(1)} %pad_maximum_fusion.1.refs_5_), channel_id=1, source_target_pairs={{0,224},{32,64},{64,32},{96,128},{128,96},{160,192},{192,160},{224... | collective-permute-start | bytes 1179656 | tf_op jit(solution)/shard_map/ppermute | solution.py:42
  72.9 3.0 %all-to-all-done.2 = f32[16,32,128]{2,1,0:T(8,128)S(1)} async-done(((f32[16,32,128]{2,1,0:T(8,128)}), f32[16,32,128]{2,1,0:T(8,128)S(1)}, u32[]{:S(2)}, u32[]{:S(2)}) %all-to-all-start.2) | async-done | bytes 262176 | tf_op jit(solution)/shard_map/all_to_all | solution.py:262
  75.9 4.1 %collective-permute-start.13 = (f32[2,256,128]{2,1,0:T(8,128)S(1)}, f32[2,256,128]{2,1,0:T(8,128)S(1)}, u32[]{:S(2)}, u32[]{:S(2)}) collective-permute-start(f32[2,256,128]{2,1,0:T(8,128)S(1)} %bitcast.54), channel_id=1, source_target_pairs={{0,32},{32,0},{1,33},{33,1},{2,34},{34,2},{3,35},{35,3},{4,36},{36... | collective-permute-start | bytes 786440 | tf_op jit(solution)/shard_map/ppermute | solution.py:266
  81.1 6.6 %shard_map.87 = (f32[3,2,16,8,128]{4,3,2,1,0:T(8,128)S(1)}, f32[3,2,16,8,128]{4,3,2,1,0:T(8,128)S(1)}, f32[3,2,16,8,128]{4,3,2,1,0:T(8,128)S(1)}, f32[2,256,128]...) custom-call(s32[3,8]{1,0:T(4,128)S(1)} %concatenate.3.refs_0_, ...), custom_call_target="tpu_custom_call" | custom-call | tf_op jit(solution)/shard_map/pallas_call | solution.py:241
  88.9 1.2 collective-permute-done.14
  90.0 16.9 %all_to_all.30 = f32[16,32,128]{2,1,0:T(8,128)S(1)} all-to-all(f32[16,32,128]{2,1,0:T(8,128)S(1)} %bitcast.61), channel_id=1, replica_groups=mesh['y'=4,'core'=2,'z'=8,'x'=4] {'y','x'}, dimensions={0} | all-to-all | bytes 524288 | tf_op jit(solution)/shard_map/all_to_all | solution.py:262
  106.9 1.3 collective-permute-start.15
  108.9 3.4 %all-to-all-start.4 = ((f32[8,32,128]{2,1,0:T(8,128)}), f32[8,32,128]{2,1,0:T(8,128)S(1)}, u32[]{:S(2)}, u32[]{:S(2)}) async-start(f32[8,32,128]{2,1,0:T(8,128)} %broadcast_in_dim.36), calls=%async_computation.4 | async-start | bytes 262144 | tf_op jit(solution)/shard_map/all_to_all | solution.py:262
  112.3 3.4 %collective-permute-done.16 = f32[3,2,16,8,128]{4,3,2,1,0:T(8,128)S(1)} collective-permute-done((f32[3,2,16,8,128]{4,3,2,1,0:T(8,128)S(1)}, f32[3,2,16,8,128]{4,3,2,1,0:T(8,128)S(1)}, u32[]{:S(2)}, u32[]{:S(2)}) %collective-permute-start.16) | collective-permute-done | bytes 393248 | tf_op jit(solution)/shard_map/ppermute | solution.py:42
  115.8 4.2 %all-to-all-done.4 = f32[8,32,128]{2,1,0:T(8,128)S(1)} async-done(((f32[8,32,128]{2,1,0:T(8,128)}), f32[8,32,128]{2,1,0:T(8,128)S(1)}, u32[]{:S(2)}, u32[]{:S(2)}) %all-to-all-start.4) | async-done | bytes 131104 | tf_op jit(solution)/shard_map/all_to_all | solution.py:262
  120.7 5.5 %all-to-all-start.5 = ((f32[16,32,128]{2,1,0:T(8,128)}), f32[16,32,128]{2,1,0:T(8,128)S(1)}, u32[]{:S(2)}, u32[]{:S(2)}) async-start(f32[16,32,128]{2,1,0:T(8,128)} %broadcast_in_dim.37), calls=%async_computation.5 | async-start | bytes 524288 | tf_op jit(solution)/shard_map/all_to_all | solution.py:262
  126.2 1.2 collective-permute-start.18
  127.4 1.4 collective-permute-start.17
  128.8 5.5 %all-to-all-done.5 = f32[16,32,128]{2,1,0:T(8,128)S(1)} async-done(((f32[16,32,128]{2,1,0:T(8,128)}), f32[16,32,128]{2,1,0:T(8,128)S(1)}, u32[]{:S(2)}, u32[]{:S(2)}) %all-to-all-start.5) | async-done | bytes 262176 | tf_op jit(solution)/shard_map/all_to_all | solution.py:262
  134.3 3.1 %collective-permute-start.19 = (f32[2,256,128]{2,1,0:T(8,128)S(1)}, f32[2,256,128]{2,1,0:T(8,128)S(1)}, u32[]{:S(2)}, u32[]{:S(2)}) collective-permute-start(f32[2,256,128]{2,1,0:T(8,128)S(1)} %bitcast.56), channel_id=1, source_target_pairs={{0,32},{32,0},{1,33},{33,1},{2,34},{34,2},{3,35},{35,3},{4,36},{36... | collective-permute-start | bytes 786440 | tf_op jit(solution)/shard_map/ppermute | solution.py:266
  138.5 1.2 shard_map.88
  (49 shorter events, 10.3 us)
Async XLA Ops:
  0.6 12.1 %collective-permute-start.1 = (f32[2,16,8,128]{3,2,1,0:T(8,128)}, f32[2,16,8,128]{3,2,1,0:T(8,128)S(1)}, u32[]{:S(2)}, u32[]{:S(2)}) collective-permute-start(f32[2,16,8,128]{3,2,1,0:T(8,128)} %bitcast.62), channel_id=1, source_target_pairs={{0,31},{1,2},{2,1},{3,4},{4,3},{5,6},{6,5},{7,8},{8,7},{9,10},{10,... | collective-permute-start | bytes 393224 | tf_op jit(solution)/shard_map/ppermute | solution.py:42
  9.3 4.3 %collective-permute-start = (f32[2,16,8,128]{3,2,1,0:T(8,128)}, f32[2,16,8,128]{3,2,1,0:T(8,128)S(1)}, u32[]{:S(2)}, u32[]{:S(2)}) collective-permute-start(f32[2,16,8,128]{3,2,1,0:T(8,128)} %bitcast.63), channel_id=1, source_target_pairs={{0,1},{1,0},{2,3},{3,2},{4,5},{5,4},{6,7},{7,6},{8,9},{9,8},{10,11... | collective-permute-start | bytes 393224 | tf_op jit(solution)/shard_map/ppermute | solution.py:42
  14.5 8.9 %collective-permute-start.3 = (f32[3,2,16,8,128]{4,3,2,1,0:T(8,128)S(1)}, f32[3,2,16,8,128]{4,3,2,1,0:T(8,128)S(1)}, u32[]{:S(2)}, u32[]{:S(2)}) collective-permute-start(f32[3,2,16,8,128]{4,3,2,1,0:T(8,128)S(1)} %pad_maximum_fusion.refs_5_), channel_id=1, source_target_pairs={{0,224},{32,64},{64,32},{96,128},{128,96},{160,192},{192,160},{224... | collective-permute-start | bytes 1179656 | tf_op jit(solution)/shard_map/ppermute | solution.py:42
  17.7 5.8 %collective-permute-start.2 = (f32[3,2,16,8,128]{4,3,2,1,0:T(8,128)S(1)}, f32[3,2,16,8,128]{4,3,2,1,0:T(8,128)S(1)}, u32[]{:S(2)}, u32[]{:S(2)}) collective-permute-start(f32[3,2,16,8,128]{4,3,2,1,0:T(8,128)S(1)} %pad_maximum_fusion.refs_5_), channel_id=1, source_target_pairs={{0,32},{32,0},{64,96},{96,64},{128,160},{160,128},{192,224},{224,1... | collective-permute-start | bytes 1179656 | tf_op jit(solution)/shard_map/ppermute | solution.py:42
  29.3 26.6 %copy-start.1 = (f32[2,128,128]{2,1,0:T(8,128)S(1)}, f32[2,128,128]{2,1,0:T(8,128)}, u32[]{:S(2)}) copy-start(f32[2,128,128]{2,1,0:T(8,128)} %param.7) | copy-start | bytes 393220
  29.4 2.7 %collective-permute-start.4 = (f32[2,256,128]{2,1,0:T(8,128)S(1)}, f32[2,256,128]{2,1,0:T(8,128)S(1)}, u32[]{:S(2)}, u32[]{:S(2)}) collective-permute-start(f32[2,256,128]{2,1,0:T(8,128)S(1)} %get-tuple-element.27), channel_id=1, source_target_pairs={{0,32},{32,0},{1,33},{33,1},{2,34},{34,2},{3,35},{35,3},{4,36},{36... | collective-permute-start | bytes 786440 | tf_op jit(solution)/shard_map/ppermute | solution.py:266
  32.8 8.0 %collective-permute-start.5 = (f32[3,2,16,8,128]{4,3,2,1,0:T(8,128)S(1)}, f32[3,2,16,8,128]{4,3,2,1,0:T(8,128)S(1)}, u32[]{:S(2)}, u32[]{:S(2)}) collective-permute-start(f32[3,2,16,8,128]{4,3,2,1,0:T(8,128)S(1)} %get-tuple-element.28), channel_id=1, source_target_pairs={{0,32},{32,0},{64,96},{96,64},{128,160},{160,128},{192,224},{224,1... | collective-permute-start | bytes 1179656 | tf_op jit(solution)/shard_map/ppermute | solution.py:42
  33.2 9.6 %collective-permute-start.6 = (f32[3,2,16,8,128]{4,3,2,1,0:T(8,128)S(1)}, f32[3,2,16,8,128]{4,3,2,1,0:T(8,128)S(1)}, u32[]{:S(2)}, u32[]{:S(2)}) collective-permute-start(f32[3,2,16,8,128]{4,3,2,1,0:T(8,128)S(1)} %get-tuple-element.29), channel_id=1, source_target_pairs={{0,224},{32,64},{64,32},{96,128},{128,96},{160,192},{192,160},{224... | collective-permute-start | bytes 1179656 | tf_op jit(solution)/shard_map/ppermute | solution.py:42
  37.0 11.4 %all-to-all-start = ((f32[16,32,128]{2,1,0:T(8,128)}), f32[16,32,128]{2,1,0:T(8,128)S(1)}, u32[]{:S(2)}, u32[]{:S(2)}) async-start(f32[16,32,128]{2,1,0:T(8,128)} %bitcast.14), calls=%async_computation | async-start | bytes 524288 | tf_op jit(solution)/shard_map/all_to_all | solution.py:262
  42.9 13.1 %collective-permute-start.8 = (f32[2,16,8,128]{3,2,1,0:T(8,128)S(1)}, f32[2,16,8,128]{3,2,1,0:T(8,128)S(1)}, u32[]{:S(2)}, u32[]{:S(2)}) collective-permute-start(f32[2,16,8,128]{3,2,1,0:T(8,128)S(1)} %get-tuple-element.46), channel_id=1, source_target_pairs={{0,31},{1,2},{2,1},{3,4},{4,3},{5,6},{6,5},{7,8},{8,7},{9,10},{10,... | collective-permute-start | bytes 393224 | tf_op jit(solution)/shard_map/ppermute | solution.py:42
  46.1 9.9 %collective-permute-start.7 = (f32[2,16,8,128]{3,2,1,0:T(8,128)S(1)}, f32[2,16,8,128]{3,2,1,0:T(8,128)S(1)}, u32[]{:S(2)}, u32[]{:S(2)}) collective-permute-start(f32[2,16,8,128]{3,2,1,0:T(8,128)S(1)} %get-tuple-element.47), channel_id=1, source_target_pairs={{0,1},{1,0},{2,3},{3,2},{4,5},{5,4},{6,7},{7,6},{8,9},{9,8},{10,11... | collective-permute-start | bytes 393224 | tf_op jit(solution)/shard_map/ppermute | solution.py:42
  49.1 14.9 %all-to-all-start.1 = ((f32[8,32,128]{2,1,0:T(8,128)}), f32[8,32,128]{2,1,0:T(8,128)S(1)}, u32[]{:S(2)}, u32[]{:S(2)}) async-start(f32[8,32,128]{2,1,0:T(8,128)} %broadcast_in_dim.34), calls=%async_computation.1 | async-start | bytes 262144 | tf_op jit(solution)/shard_map/all_to_all | solution.py:262
  56.0 12.2 %collective-permute-start.10 = (f32[2,16,8,128]{3,2,1,0:T(8,128)S(1)}, f32[2,16,8,128]{3,2,1,0:T(8,128)S(1)}, u32[]{:S(2)}, u32[]{:S(2)}) collective-permute-start(f32[2,16,8,128]{3,2,1,0:T(8,128)S(1)} %fusion.8), channel_id=1, source_target_pairs={{0,31},{1,2},{2,1},{3,4},{4,3},{5,6},{6,5},{7,8},{8,7},{9,10},{10,... | collective-permute-start | bytes 393224 | tf_op jit(solution)/shard_map/ppermute | solution.py:42
  57.8 10.4 %collective-permute-start.9 = (f32[2,16,8,128]{3,2,1,0:T(8,128)S(1)}, f32[2,16,8,128]{3,2,1,0:T(8,128)S(1)}, u32[]{:S(2)}, u32[]{:S(2)}) collective-permute-start(f32[2,16,8,128]{3,2,1,0:T(8,128)S(1)} %fusion.8), channel_id=1, source_target_pairs={{0,1},{1,0},{2,3},{3,2},{4,5},{5,4},{6,7},{7,6},{8,9},{9,8},{10,11... | collective-permute-start | bytes 393224 | tf_op jit(solution)/shard_map/ppermute | solution.py:42
  64.7 11.2 %all-to-all-start.2 = ((f32[16,32,128]{2,1,0:T(8,128)}), f32[16,32,128]{2,1,0:T(8,128)S(1)}, u32[]{:S(2)}, u32[]{:S(2)}) async-start(f32[16,32,128]{2,1,0:T(8,128)} %broadcast_in_dim.35), calls=%async_computation.2 | async-start | bytes 524288 | tf_op jit(solution)/shard_map/all_to_all | solution.py:262
  68.3 11.7 %collective-permute-start.12 = (f32[3,2,16,8,128]{4,3,2,1,0:T(8,128)S(1)}, f32[3,2,16,8,128]{4,3,2,1,0:T(8,128)S(1)}, u32[]{:S(2)}, u32[]{:S(2)}) collective-permute-start(f32[3,2,16,8,128]{4,3,2,1,0:T(8,128)S(1)} %pad_maximum_fusion.1.refs_5_), channel_id=1, source_target_pairs={{0,224},{32,64},{64,32},{96,128},{128,96},{160,192},{192,160},{224... | collective-permute-start | bytes 1179656 | tf_op jit(solution)/shard_map/ppermute | solution.py:42
  72.9 7.2 %collective-permute-start.11 = (f32[3,2,16,8,128]{4,3,2,1,0:T(8,128)S(1)}, f32[3,2,16,8,128]{4,3,2,1,0:T(8,128)S(1)}, u32[]{:S(2)}, u32[]{:S(2)}) collective-permute-start(f32[3,2,16,8,128]{4,3,2,1,0:T(8,128)S(1)} %pad_maximum_fusion.1.refs_5_), channel_id=1, source_target_pairs={{0,32},{32,0},{64,96},{96,64},{128,160},{160,128},{192,224},{224,1... | collective-permute-start | bytes 1179656 | tf_op jit(solution)/shard_map/ppermute | solution.py:42
  75.9 5.2 %collective-permute-start.13 = (f32[2,256,128]{2,1,0:T(8,128)S(1)}, f32[2,256,128]{2,1,0:T(8,128)S(1)}, u32[]{:S(2)}, u32[]{:S(2)}) collective-permute-start(f32[2,256,128]{2,1,0:T(8,128)S(1)} %bitcast.54), channel_id=1, source_target_pairs={{0,32},{32,0},{1,33},{33,1},{2,34},{34,2},{3,35},{35,3},{4,36},{36... | collective-permute-start | bytes 786440 | tf_op jit(solution)/shard_map/ppermute | solution.py:266
  80.1 1.0 copy-start.2
  87.7 2.3 %collective-permute-start.14 = (f32[2,256,128]{2,1,0:T(8,128)S(1)}, f32[2,256,128]{2,1,0:T(8,128)S(1)}, u32[]{:S(2)}, u32[]{:S(2)}) collective-permute-start(f32[2,256,128]{2,1,0:T(8,128)S(1)} %get-tuple-element.35), channel_id=1, source_target_pairs={{0,32},{32,0},{1,33},{33,1},{2,34},{34,2},{3,35},{35,3},{4,36},{36... | collective-permute-start | bytes 786440 | tf_op jit(solution)/shard_map/ppermute | solution.py:266
  106.9 5.4 %collective-permute-start.15 = (f32[3,2,16,8,128]{4,3,2,1,0:T(8,128)S(1)}, f32[3,2,16,8,128]{4,3,2,1,0:T(8,128)S(1)}, u32[]{:S(2)}, u32[]{:S(2)}) collective-permute-start(f32[3,2,16,8,128]{4,3,2,1,0:T(8,128)S(1)} %get-tuple-element.38), channel_id=1, source_target_pairs={{0,32},{32,0},{64,96},{96,64},{128,160},{160,128},{192,224},{224,1... | collective-permute-start | bytes 1179656 | tf_op jit(solution)/shard_map/ppermute | solution.py:42
  108.2 7.5 %collective-permute-start.16 = (f32[3,2,16,8,128]{4,3,2,1,0:T(8,128)S(1)}, f32[3,2,16,8,128]{4,3,2,1,0:T(8,128)S(1)}, u32[]{:S(2)}, u32[]{:S(2)}) collective-permute-start(f32[3,2,16,8,128]{4,3,2,1,0:T(8,128)S(1)} %get-tuple-element.39), channel_id=1, source_target_pairs={{0,224},{32,64},{64,32},{96,128},{128,96},{160,192},{192,160},{224... | collective-permute-start | bytes 1179656 | tf_op jit(solution)/shard_map/ppermute | solution.py:42
  108.2 30.3 %copy-start = (f32[2,2,256,128]{3,2,1,0:T(8,128)S(1)}, f32[2,2,256,128]{3,2,1,0:T(8,128)}, u32[]{:S(2)}) copy-start(f32[2,2,256,128]{3,2,1,0:T(8,128)} %get-tuple-element.41.probe_ref) | copy-start | bytes 1572868
  108.9 11.1 %all-to-all-start.4 = ((f32[8,32,128]{2,1,0:T(8,128)}), f32[8,32,128]{2,1,0:T(8,128)S(1)}, u32[]{:S(2)}, u32[]{:S(2)}) async-start(f32[8,32,128]{2,1,0:T(8,128)} %broadcast_in_dim.36), calls=%async_computation.4 | async-start | bytes 262144 | tf_op jit(solution)/shard_map/all_to_all | solution.py:262
  120.7 13.6 %all-to-all-start.5 = ((f32[16,32,128]{2,1,0:T(8,128)}), f32[16,32,128]{2,1,0:T(8,128)S(1)}, u32[]{:S(2)}, u32[]{:S(2)}) async-start(f32[16,32,128]{2,1,0:T(8,128)} %broadcast_in_dim.37), calls=%async_computation.5 | async-start | bytes 524288 | tf_op jit(solution)/shard_map/all_to_all | solution.py:262
  126.2 11.1 %collective-permute-start.18 = (f32[2,16,8,128]{3,2,1,0:T(8,128)S(1)}, f32[2,16,8,128]{3,2,1,0:T(8,128)S(1)}, u32[]{:S(2)}, u32[]{:S(2)}) collective-permute-start(f32[2,16,8,128]{3,2,1,0:T(8,128)S(1)} %get-tuple-element.44), channel_id=1, source_target_pairs={{0,31},{1,2},{2,1},{3,4},{4,3},{5,6},{6,5},{7,8},{8,7},{9,10},{10,... | collective-permute-start | bytes 393224 | tf_op jit(solution)/shard_map/ppermute | solution.py:42
  127.4 10.0 %collective-permute-start.17 = (f32[2,16,8,128]{3,2,1,0:T(8,128)S(1)}, f32[2,16,8,128]{3,2,1,0:T(8,128)S(1)}, u32[]{:S(2)}, u32[]{:S(2)}) collective-permute-start(f32[2,16,8,128]{3,2,1,0:T(8,128)S(1)} %get-tuple-element.45), channel_id=1, source_target_pairs={{0,1},{1,0},{2,3},{3,2},{4,5},{5,4},{6,7},{7,6},{8,9},{9,8},{10,11... | collective-permute-start | bytes 393224 | tf_op jit(solution)/shard_map/ppermute | solution.py:42
  134.3 4.2 %collective-permute-start.19 = (f32[2,256,128]{2,1,0:T(8,128)S(1)}, f32[2,256,128]{2,1,0:T(8,128)S(1)}, u32[]{:S(2)}, u32[]{:S(2)}) collective-permute-start(f32[2,256,128]{2,1,0:T(8,128)S(1)} %bitcast.56), channel_id=1, source_target_pairs={{0,32},{32,0},{1,33},{33,1},{2,34},{34,2},{3,35},{35,3},{4,36},{36... | collective-permute-start | bytes 786440 | tf_op jit(solution)/shard_map/ppermute | solution.py:266

commit v14 on v12

--- a/solution.py
+++ b/solution.py
@@ -338,7 +338,7 @@
     strips = (strip, paired(strip, ROW, 0), paired(strip, ROW, 2))
     row0, row1, row2, keep, send, peak = gradients(True, live_slots, patterns, tables, probe_field, *strips)
     half = keep + core_swap(send)
-    row2 = after(row2, half)
+    row0 = after(row0, half)
     sums = side_sum(row1, paired(row0, ROW, 0), paired(row2, ROW, 2), row_end)
     payloads = to_sides(sums)
     shares = after(plane_shares(half), *payloads)

time: 141 us -> 140 us (level)
  starting transfers between devices: 65.9 us -> 58 us
  Pallas kernels: 13.5 us -> 21.1 us
    pallas_call x2, Pallas kernels: 12.3 us -> 20 us  [gradients(): pl.pallas_call(functools.partial(gradient_kernel, first), out_shape=(stri...]
    ppermute x4, starting transfers between devices: 17.1 us -> 10.6 us  [core_swap(): return lax.ppermute(value, 'core', [(0, 1), (1, 0)])]
    all_to_all x5, starting transfers between devices: 24.3 us -> 20.7 us  [exchange(): return lax.all_to_all(value, axes, 0, 0, tiled=True)]
    ppermute x16, waiting for transfers between devices: 15.6 us -> 13.4 us  [paired(): return lax.ppermute(value, axes, pairs)]
    ppermute x16, starting transfers between devices: 24.4 us -> 26.6 us  [paired(): return lax.ppermute(value, axes, pairs)]
where the time goes in v14:
time: 140 us; the launch traced here: 139 us
  starting transfers between devices  58 us (41%)
  waiting for transfers between devices  39.3 us (28%)
  Pallas kernels  21.1 us (15%)
  blocking collectives  13.2 us (9%)
  local copies, waits for them, and re-layouts  3.48 us (2%)
  other arithmetic  2.76 us (2%)
  between operations  1.48 us (1%)
    ppermute x16, starting transfers between devices, paired(): return lax.ppermute(value, axes, pairs)  26.6 us
    all_to_all x5, waiting for transfers between devices, exchange(): return lax.all_to_all(value, axes, 0, 0, tiled=True)  22.1 us
    all_to_all x5, starting transfers between devices, exchange(): return lax.all_to_all(value, axes, 0, 0, tiled=True)  20.7 us
    pallas_call x2, Pallas kernels, gradients(): pl.pallas_call(functools.partial(gradient_kernel, first), out_shape=(stri...  20 us
    ppermute x16, waiting for transfers between devices, paired(): return lax.ppermute(value, axes, pairs)  13.4 us
    all_to_all x1, blocking collectives, exchange(): return lax.all_to_all(value, axes, 0, 0, tiled=True)  13.2 us
    ppermute x4, starting transfers between devices, core_swap(): return lax.ppermute(value, 'core', [(0, 1), (1, 0)])  10.6 us
    ppermute x4, waiting for transfers between devices, core_swap(): return lax.ppermute(value, 'core', [(0, 1), (1, 0)])  3.75 us
  transfers between devices with their start and end apart: 25, of which 15 were waited for; matrix products, arithmetic and copies ran while one was open for 3% of the time, Pallas kernels for 0%

profile of v14, /device:TPU:1, one launch (start us, length us, event | category | flops | bytes accessed | tf_op | source)
XLA Modules:
  0.0 139.3 jit_solution(12287057829610223078)
XLA Ops:
  0.6 8.7 %collective-permute-start.1 = (f32[2,16,8,128]{3,2,1,0:T(8,128)}, f32[2,16,8,128]{3,2,1,0:T(8,128)S(1)}, u32[]{:S(2)}, u32[]{:S(2)}) collective-permute-start(f32[2,16,8,128]{3,2,1,0:T(8,128)} %bitcast.62), channel_id=1, source_target_pairs={{0,31},{1,2},{2,1},{3,4},{4,3},{5,6},{6,5},{7,8},{8,7},{9,10},{10,... | collective-permute-start | bytes 393224 | tf_op jit(solution)/shard_map/ppermute | solution.py:42
  9.3 3.4 %collective-permute-done.1 = f32[2,16,8,128]{3,2,1,0:T(8,128)S(1)} collective-permute-done((f32[2,16,8,128]{3,2,1,0:T(8,128)}, f32[2,16,8,128]{3,2,1,0:T(8,128)S(1)}, u32[]{:S(2)}, u32[]{:S(2)}) %collective-permute-start.1) | collective-permute-done | bytes 131104 | tf_op jit(solution)/shard_map/ppermute | solution.py:42
  14.5 3.1 %collective-permute-start.3 = (f32[3,2,16,8,128]{4,3,2,1,0:T(8,128)S(1)}, f32[3,2,16,8,128]{4,3,2,1,0:T(8,128)S(1)}, u32[]{:S(2)}, u32[]{:S(2)}) collective-permute-start(f32[3,2,16,8,128]{4,3,2,1,0:T(8,128)S(1)} %pad_maximum_fusion.refs_5_), channel_id=1, source_target_pairs={{0,224},{32,64},{64,32},{96,128},{128,96},{160,192},{192,160},{224... | collective-permute-start | bytes 1179656 | tf_op jit(solution)/shard_map/ppermute | solution.py:42
  19.1 4.3 %collective-permute-done.3.refs_7_ = f32[3,2,16,8,128]{4,3,2,1,0:T(8,128)S(1)} collective-permute-done((f32[3,2,16,8,128]{4,3,2,1,0:T(8,128)S(1)}, f32[3,2,16,8,128]{4,3,2,1,0:T(8,128)S(1)}, u32[]{:S(2)}, u32[]{:S(2)}) %collective-permute-start.3) | collective-permute-done | bytes 393248 | tf_op jit(solution)/shard_map/ppermute | solution.py:42
  23.4 9.6 %shard_map.86 = (f32[3,2,16,8,128]{4,3,2,1,0:T(8,128)S(1)}, f32[3,2,16,8,128]{4,3,2,1,0:T(8,128)S(1)}, f32[3,2,16,8,128]{4,3,2,1,0:T(8,128)S(1)}, f32[2,256,128]...) custom-call(s32[3,8]{1,0:T(4,128)S(1)} %concatenate.3.refs_0_, f32[8,256,256]{2,1,0:T(8,128)} %bitcast.58, ...), custom_call_target="tpu_custom_call" | custom-call | tf_op jit(solution)/shard_map/pallas_call | solution.py:241
  33.1 1.6 %collective-permute-start.4 = (f32[2,256,128]{2,1,0:T(8,128)S(1)}, f32[2,256,128]{2,1,0:T(8,128)S(1)}, u32[]{:S(2)}, u32[]{:S(2)}) collective-permute-start(f32[2,256,128]{2,1,0:T(8,128)S(1)} %get-tuple-element.25), channel_id=1, source_target_pairs={{0,32},{32,0},{1,33},{33,1},{2,34},{34,2},{3,35},{35,3},{4,36},{36... | collective-permute-start | bytes 786440 | tf_op jit(solution)/shard_map/ppermute | solution.py:266
  34.7 1.1 collective-permute-done.4
  37.4 3.5 %all-to-all-start = ((f32[16,32,128]{2,1,0:T(8,128)}), f32[16,32,128]{2,1,0:T(8,128)S(1)}, u32[]{:S(2)}, u32[]{:S(2)}) async-start(f32[16,32,128]{2,1,0:T(8,128)} %bitcast.14), calls=%async_computation | async-start | bytes 524288 | tf_op jit(solution)/shard_map/all_to_all | solution.py:262
  40.9 1.3 collective-permute-done.6
  42.3 3.4 %collective-permute-start.8 = (f32[2,16,8,128]{3,2,1,0:T(8,128)S(1)}, f32[2,16,8,128]{3,2,1,0:T(8,128)S(1)}, u32[]{:S(2)}, u32[]{:S(2)}) collective-permute-start(f32[2,16,8,128]{3,2,1,0:T(8,128)S(1)} %get-tuple-element.44), channel_id=1, source_target_pairs={{0,31},{1,2},{2,1},{3,4},{4,3},{5,6},{6,5},{7,8},{8,7},{9,10},{10,... | collective-permute-start | bytes 393224 | tf_op jit(solution)/shard_map/ppermute | solution.py:42
  45.7 3.8 %all-to-all-done = f32[16,32,128]{2,1,0:T(8,128)S(1)} async-done(((f32[16,32,128]{2,1,0:T(8,128)}), f32[16,32,128]{2,1,0:T(8,128)S(1)}, u32[]{:S(2)}, u32[]{:S(2)}) %all-to-all-start) | async-done | bytes 262176 | tf_op jit(solution)/shard_map/all_to_all | solution.py:262
  50.1 4.6 %all-to-all-start.1 = ((f32[8,32,128]{2,1,0:T(8,128)}), f32[8,32,128]{2,1,0:T(8,128)S(1)}, u32[]{:S(2)}, u32[]{:S(2)}) async-start(f32[8,32,128]{2,1,0:T(8,128)} %broadcast_in_dim.34), calls=%async_computation.1 | async-start | bytes 262144 | tf_op jit(solution)/shard_map/all_to_all | solution.py:262
  54.8 1.3 collective-permute-start.10
  56.1 6.5 %all-to-all-done.1 = f32[8,32,128]{2,1,0:T(8,128)S(1)} async-done(((f32[8,32,128]{2,1,0:T(8,128)}), f32[8,32,128]{2,1,0:T(8,128)S(1)}, u32[]{:S(2)}, u32[]{:S(2)}) %all-to-all-start.1) | async-done | bytes 131104 | tf_op jit(solution)/shard_map/all_to_all | solution.py:262
  63.4 3.7 %all-to-all-start.2 = ((f32[16,32,128]{2,1,0:T(8,128)}), f32[16,32,128]{2,1,0:T(8,128)S(1)}, u32[]{:S(2)}, u32[]{:S(2)}) async-start(f32[16,32,128]{2,1,0:T(8,128)} %broadcast_in_dim.35), calls=%async_computation.2 | async-start | bytes 524288 | tf_op jit(solution)/shard_map/all_to_all | solution.py:262
  67.2 5.3 %collective-permute-start.12 = (f32[3,2,16,8,128]{4,3,2,1,0:T(8,128)S(1)}, f32[3,2,16,8,128]{4,3,2,1,0:T(8,128)S(1)}, u32[]{:S(2)}, u32[]{:S(2)}) collective-permute-start(f32[3,2,16,8,128]{4,3,2,1,0:T(8,128)S(1)} %pad_maximum_fusion.1.refs_5_), channel_id=1, source_target_pairs={{0,224},{32,64},{64,32},{96,128},{128,96},{160,192},{192,160},{224... | collective-permute-start | bytes 1179656 | tf_op jit(solution)/shard_map/ppermute | solution.py:42
  72.4 2.2 %all-to-all-done.2 = f32[16,32,128]{2,1,0:T(8,128)S(1)} async-done(((f32[16,32,128]{2,1,0:T(8,128)}), f32[16,32,128]{2,1,0:T(8,128)S(1)}, u32[]{:S(2)}, u32[]{:S(2)}) %all-to-all-start.2) | async-done | bytes 262176 | tf_op jit(solution)/shard_map/all_to_all | solution.py:262
  74.6 4.9 %collective-permute-start.13 = (f32[2,256,128]{2,1,0:T(8,128)S(1)}, f32[2,256,128]{2,1,0:T(8,128)S(1)}, u32[]{:S(2)}, u32[]{:S(2)}) collective-permute-start(f32[2,256,128]{2,1,0:T(8,128)S(1)} %bitcast.54), channel_id=1, source_target_pairs={{0,32},{32,0},{1,33},{33,1},{2,34},{34,2},{3,35},{35,3},{4,36},{36... | collective-permute-start | bytes 786440 | tf_op jit(solution)/shard_map/ppermute | solution.py:266
  80.7 10.3 %shard_map.87 = (f32[3,2,16,8,128]{4,3,2,1,0:T(8,128)S(1)}, f32[3,2,16,8,128]{4,3,2,1,0:T(8,128)S(1)}, f32[3,2,16,8,128]{4,3,2,1,0:T(8,128)S(1)}, f32[2,256,128]...) custom-call(s32[3,8]{1,0:T(4,128)S(1)} %concatenate.3.refs_0_, ...), custom_call_target="tpu_custom_call" | custom-call | tf_op jit(solution)/shard_map/pallas_call | solution.py:241
  91.0 1.1 collective-permute-start.14
  92.1 1.2 collective-permute-done.14
  93.3 13.2 %all_to_all.30 = f32[16,32,128]{2,1,0:T(8,128)S(1)} all-to-all(f32[16,32,128]{2,1,0:T(8,128)S(1)} %bitcast.61), channel_id=1, replica_groups=mesh['y'=4,'core'=2,'z'=8,'x'=4] {'y','x'}, dimensions={0} | all-to-all | bytes 524288 | tf_op jit(solution)/shard_map/all_to_all | solution.py:262
  106.5 1.3 collective-permute-start.15
  108.5 3.4 %all-to-all-start.4 = ((f32[8,32,128]{2,1,0:T(8,128)}), f32[8,32,128]{2,1,0:T(8,128)S(1)}, u32[]{:S(2)}, u32[]{:S(2)}) async-start(f32[8,32,128]{2,1,0:T(8,128)} %broadcast_in_dim.36), calls=%async_computation.4 | async-start | bytes 262144 | tf_op jit(solution)/shard_map/all_to_all | solution.py:262
  111.8 3.4 %collective-permute-done.16 = f32[3,2,16,8,128]{4,3,2,1,0:T(8,128)S(1)} collective-permute-done((f32[3,2,16,8,128]{4,3,2,1,0:T(8,128)S(1)}, f32[3,2,16,8,128]{4,3,2,1,0:T(8,128)S(1)}, u32[]{:S(2)}, u32[]{:S(2)}) %collective-permute-start.16) | collective-permute-done | bytes 393248 | tf_op jit(solution)/shard_map/ppermute | solution.py:42
  115.4 4.2 %all-to-all-done.4 = f32[8,32,128]{2,1,0:T(8,128)S(1)} async-done(((f32[8,32,128]{2,1,0:T(8,128)}), f32[8,32,128]{2,1,0:T(8,128)S(1)}, u32[]{:S(2)}, u32[]{:S(2)}) %all-to-all-start.4) | async-done | bytes 131104 | tf_op jit(solution)/shard_map/all_to_all | solution.py:262
  120.2 5.5 %all-to-all-start.5 = ((f32[16,32,128]{2,1,0:T(8,128)}), f32[16,32,128]{2,1,0:T(8,128)S(1)}, u32[]{:S(2)}, u32[]{:S(2)}) async-start(f32[16,32,128]{2,1,0:T(8,128)} %broadcast_in_dim.37), calls=%async_computation.5 | async-start | bytes 524288 | tf_op jit(solution)/shard_map/all_to_all | solution.py:262
  125.8 1.2 collective-permute-start.18
  127.0 1.4 collective-permute-start.17
  128.3 5.5 %all-to-all-done.5 = f32[16,32,128]{2,1,0:T(8,128)S(1)} async-done(((f32[16,32,128]{2,1,0:T(8,128)}), f32[16,32,128]{2,1,0:T(8,128)S(1)}, u32[]{:S(2)}, u32[]{:S(2)}) %all-to-all-start.5) | async-done | bytes 262176 | tf_op jit(solution)/shard_map/all_to_all | solution.py:262
  133.9 3.1 %collective-permute-start.19 = (f32[2,256,128]{2,1,0:T(8,128)S(1)}, f32[2,256,128]{2,1,0:T(8,128)S(1)}, u32[]{:S(2)}, u32[]{:S(2)}) collective-permute-start(f32[2,256,128]{2,1,0:T(8,128)S(1)} %bitcast.56), channel_id=1, source_target_pairs={{0,32},{32,0},{1,33},{33,1},{2,34},{34,2},{3,35},{35,3},{4,36},{36... | collective-permute-start | bytes 786440 | tf_op jit(solution)/shard_map/ppermute | solution.py:266
  138.1 1.2 shard_map.88
  (49 shorter events, 9.7 us)
Async XLA Ops:
  0.6 12.1 %collective-permute-start.1 = (f32[2,16,8,128]{3,2,1,0:T(8,128)}, f32[2,16,8,128]{3,2,1,0:T(8,128)S(1)}, u32[]{:S(2)}, u32[]{:S(2)}) collective-permute-start(f32[2,16,8,128]{3,2,1,0:T(8,128)} %bitcast.62), channel_id=1, source_target_pairs={{0,31},{1,2},{2,1},{3,4},{4,3},{5,6},{6,5},{7,8},{8,7},{9,10},{10,... | collective-permute-start | bytes 393224 | tf_op jit(solution)/shard_map/ppermute | solution.py:42
  9.3 4.3 %collective-permute-start = (f32[2,16,8,128]{3,2,1,0:T(8,128)}, f32[2,16,8,128]{3,2,1,0:T(8,128)S(1)}, u32[]{:S(2)}, u32[]{:S(2)}) collective-permute-start(f32[2,16,8,128]{3,2,1,0:T(8,128)} %bitcast.63), channel_id=1, source_target_pairs={{0,1},{1,0},{2,3},{3,2},{4,5},{5,4},{6,7},{7,6},{8,9},{9,8},{10,11... | collective-permute-start | bytes 393224 | tf_op jit(solution)/shard_map/ppermute | solution.py:42
  14.5 8.9 %collective-permute-start.3 = (f32[3,2,16,8,128]{4,3,2,1,0:T(8,128)S(1)}, f32[3,2,16,8,128]{4,3,2,1,0:T(8,128)S(1)}, u32[]{:S(2)}, u32[]{:S(2)}) collective-permute-start(f32[3,2,16,8,128]{4,3,2,1,0:T(8,128)S(1)} %pad_maximum_fusion.refs_5_), channel_id=1, source_target_pairs={{0,224},{32,64},{64,32},{96,128},{128,96},{160,192},{192,160},{224... | collective-permute-start | bytes 1179656 | tf_op jit(solution)/shard_map/ppermute | solution.py:42
  17.7 5.8 %collective-permute-start.2 = (f32[3,2,16,8,128]{4,3,2,1,0:T(8,128)S(1)}, f32[3,2,16,8,128]{4,3,2,1,0:T(8,128)S(1)}, u32[]{:S(2)}, u32[]{:S(2)}) collective-permute-start(f32[3,2,16,8,128]{4,3,2,1,0:T(8,128)S(1)} %pad_maximum_fusion.refs_5_), channel_id=1, source_target_pairs={{0,32},{32,0},{64,96},{96,64},{128,160},{160,128},{192,224},{224,1... | collective-permute-start | bytes 1179656 | tf_op jit(solution)/shard_map/ppermute | solution.py:42
  33.1 21.6 %copy-start.1 = (f32[2,128,128]{2,1,0:T(8,128)S(1)}, f32[2,128,128]{2,1,0:T(8,128)}, u32[]{:S(2)}) copy-start(f32[2,128,128]{2,1,0:T(8,128)} %param.7) | copy-start | bytes 393220
  33.1 2.7 %collective-permute-start.4 = (f32[2,256,128]{2,1,0:T(8,128)S(1)}, f32[2,256,128]{2,1,0:T(8,128)S(1)}, u32[]{:S(2)}, u32[]{:S(2)}) collective-permute-start(f32[2,256,128]{2,1,0:T(8,128)S(1)} %get-tuple-element.25), channel_id=1, source_target_pairs={{0,32},{32,0},{1,33},{33,1},{2,34},{34,2},{3,35},{35,3},{4,36},{36... | collective-permute-start | bytes 786440 | tf_op jit(solution)/shard_map/ppermute | solution.py:266
  34.7 7.5 %collective-permute-start.6 = (f32[3,2,16,8,128]{4,3,2,1,0:T(8,128)S(1)}, f32[3,2,16,8,128]{4,3,2,1,0:T(8,128)S(1)}, u32[]{:S(2)}, u32[]{:S(2)}) collective-permute-start(f32[3,2,16,8,128]{4,3,2,1,0:T(8,128)S(1)} %get-tuple-element.27), channel_id=1, source_target_pairs={{0,224},{32,64},{64,32},{96,128},{128,96},{160,192},{192,160},{224... | collective-permute-start | bytes 1179656 | tf_op jit(solution)/shard_map/ppermute | solution.py:42
  36.6 5.6 %collective-permute-start.5 = (f32[3,2,16,8,128]{4,3,2,1,0:T(8,128)S(1)}, f32[3,2,16,8,128]{4,3,2,1,0:T(8,128)S(1)}, u32[]{:S(2)}, u32[]{:S(2)}) collective-permute-start(f32[3,2,16,8,128]{4,3,2,1,0:T(8,128)S(1)} %get-tuple-element.26), channel_id=1, source_target_pairs={{0,32},{32,0},{64,96},{96,64},{128,160},{160,128},{192,224},{224,1... | collective-permute-start | bytes 1179656 | tf_op jit(solution)/shard_map/ppermute | solution.py:42
  37.4 12.1 %all-to-all-start = ((f32[16,32,128]{2,1,0:T(8,128)}), f32[16,32,128]{2,1,0:T(8,128)S(1)}, u32[]{:S(2)}, u32[]{:S(2)}) async-start(f32[16,32,128]{2,1,0:T(8,128)} %bitcast.14), calls=%async_computation | async-start | bytes 524288 | tf_op jit(solution)/shard_map/all_to_all | solution.py:262
  42.3 12.4 %collective-permute-start.8 = (f32[2,16,8,128]{3,2,1,0:T(8,128)S(1)}, f32[2,16,8,128]{3,2,1,0:T(8,128)S(1)}, u32[]{:S(2)}, u32[]{:S(2)}) collective-permute-start(f32[2,16,8,128]{3,2,1,0:T(8,128)S(1)} %get-tuple-element.44), channel_id=1, source_target_pairs={{0,31},{1,2},{2,1},{3,4},{4,3},{5,6},{6,5},{7,8},{8,7},{9,10},{10,... | collective-permute-start | bytes 393224 | tf_op jit(solution)/shard_map/ppermute | solution.py:42
  45.7 9.1 %collective-permute-start.7 = (f32[2,16,8,128]{3,2,1,0:T(8,128)S(1)}, f32[2,16,8,128]{3,2,1,0:T(8,128)S(1)}, u32[]{:S(2)}, u32[]{:S(2)}) collective-permute-start(f32[2,16,8,128]{3,2,1,0:T(8,128)S(1)} %get-tuple-element.45), channel_id=1, source_target_pairs={{0,1},{1,0},{2,3},{3,2},{4,5},{5,4},{6,7},{7,6},{8,9},{9,8},{10,11... | collective-permute-start | bytes 393224 | tf_op jit(solution)/shard_map/ppermute | solution.py:42
  50.1 12.5 %all-to-all-start.1 = ((f32[8,32,128]{2,1,0:T(8,128)}), f32[8,32,128]{2,1,0:T(8,128)S(1)}, u32[]{:S(2)}, u32[]{:S(2)}) async-start(f32[8,32,128]{2,1,0:T(8,128)} %broadcast_in_dim.34), calls=%async_computation.1 | async-start | bytes 262144 | tf_op jit(solution)/shard_map/all_to_all | solution.py:262
  54.8 12.3 %collective-permute-start.10 = (f32[2,16,8,128]{3,2,1,0:T(8,128)S(1)}, f32[2,16,8,128]{3,2,1,0:T(8,128)S(1)}, u32[]{:S(2)}, u32[]{:S(2)}) collective-permute-start(f32[2,16,8,128]{3,2,1,0:T(8,128)S(1)} %fusion.8), channel_id=1, source_target_pairs={{0,31},{1,2},{2,1},{3,4},{4,3},{5,6},{6,5},{7,8},{8,7},{9,10},{10,... | collective-permute-start | bytes 393224 | tf_op jit(solution)/shard_map/ppermute | solution.py:42
  56.1 11.0 %collective-permute-start.9 = (f32[2,16,8,128]{3,2,1,0:T(8,128)S(1)}, f32[2,16,8,128]{3,2,1,0:T(8,128)S(1)}, u32[]{:S(2)}, u32[]{:S(2)}) collective-permute-start(f32[2,16,8,128]{3,2,1,0:T(8,128)S(1)} %fusion.8), channel_id=1, source_target_pairs={{0,1},{1,0},{2,3},{3,2},{4,5},{5,4},{6,7},{7,6},{8,9},{9,8},{10,11... | collective-permute-start | bytes 393224 | tf_op jit(solution)/shard_map/ppermute | solution.py:42
  63.4 11.2 %all-to-all-start.2 = ((f32[16,32,128]{2,1,0:T(8,128)}), f32[16,32,128]{2,1,0:T(8,128)S(1)}, u32[]{:S(2)}, u32[]{:S(2)}) async-start(f32[16,32,128]{2,1,0:T(8,128)} %broadcast_in_dim.35), calls=%async_computation.2 | async-start | bytes 524288 | tf_op jit(solution)/shard_map/all_to_all | solution.py:262
  67.2 12.5 %collective-permute-start.12 = (f32[3,2,16,8,128]{4,3,2,1,0:T(8,128)S(1)}, f32[3,2,16,8,128]{4,3,2,1,0:T(8,128)S(1)}, u32[]{:S(2)}, u32[]{:S(2)}) collective-permute-start(f32[3,2,16,8,128]{4,3,2,1,0:T(8,128)S(1)} %pad_maximum_fusion.1.refs_5_), channel_id=1, source_target_pairs={{0,224},{32,64},{64,32},{96,128},{128,96},{160,192},{192,160},{224... | collective-permute-start | bytes 1179656 | tf_op jit(solution)/shard_map/ppermute | solution.py:42
  72.4 7.2 %collective-permute-start.11 = (f32[3,2,16,8,128]{4,3,2,1,0:T(8,128)S(1)}, f32[3,2,16,8,128]{4,3,2,1,0:T(8,128)S(1)}, u32[]{:S(2)}, u32[]{:S(2)}) collective-permute-start(f32[3,2,16,8,128]{4,3,2,1,0:T(8,128)S(1)} %pad_maximum_fusion.1.refs_5_), channel_id=1, source_target_pairs={{0,32},{32,0},{64,96},{96,64},{128,160},{160,128},{192,224},{224,1... | collective-permute-start | bytes 1179656 | tf_op jit(solution)/shard_map/ppermute | solution.py:42
  74.6 6.0 %collective-permute-start.13 = (f32[2,256,128]{2,1,0:T(8,128)S(1)}, f32[2,256,128]{2,1,0:T(8,128)S(1)}, u32[]{:S(2)}, u32[]{:S(2)}) collective-permute-start(f32[2,256,128]{2,1,0:T(8,128)S(1)} %bitcast.54), channel_id=1, source_target_pairs={{0,32},{32,0},{1,33},{33,1},{2,34},{34,2},{3,35},{35,3},{4,36},{36... | collective-permute-start | bytes 786440 | tf_op jit(solution)/shard_map/ppermute | solution.py:266
  79.6 1.0 copy-start.2
  91.0 2.3 %collective-permute-start.14 = (f32[2,256,128]{2,1,0:T(8,128)S(1)}, f32[2,256,128]{2,1,0:T(8,128)S(1)}, u32[]{:S(2)}, u32[]{:S(2)}) collective-permute-start(f32[2,256,128]{2,1,0:T(8,128)S(1)} %get-tuple-element.33), channel_id=1, source_target_pairs={{0,32},{32,0},{1,33},{33,1},{2,34},{34,2},{3,35},{35,3},{4,36},{36... | collective-permute-start | bytes 786440 | tf_op jit(solution)/shard_map/ppermute | solution.py:266
  106.5 5.4 %collective-permute-start.15 = (f32[3,2,16,8,128]{4,3,2,1,0:T(8,128)S(1)}, f32[3,2,16,8,128]{4,3,2,1,0:T(8,128)S(1)}, u32[]{:S(2)}, u32[]{:S(2)}) collective-permute-start(f32[3,2,16,8,128]{4,3,2,1,0:T(8,128)S(1)} %get-tuple-element.36), channel_id=1, source_target_pairs={{0,32},{32,0},{64,96},{96,64},{128,160},{160,128},{192,224},{224,1... | collective-permute-start | bytes 1179656 | tf_op jit(solution)/shard_map/ppermute | solution.py:42
  107.7 7.5 %collective-permute-start.16 = (f32[3,2,16,8,128]{4,3,2,1,0:T(8,128)S(1)}, f32[3,2,16,8,128]{4,3,2,1,0:T(8,128)S(1)}, u32[]{:S(2)}, u32[]{:S(2)}) collective-permute-start(f32[3,2,16,8,128]{4,3,2,1,0:T(8,128)S(1)} %get-tuple-element.37), channel_id=1, source_target_pairs={{0,224},{32,64},{64,32},{96,128},{128,96},{160,192},{192,160},{224... | collective-permute-start | bytes 1179656 | tf_op jit(solution)/shard_map/ppermute | solution.py:42
  107.8 30.3 %copy-start = (f32[2,2,256,128]{3,2,1,0:T(8,128)S(1)}, f32[2,2,256,128]{3,2,1,0:T(8,128)}, u32[]{:S(2)}) copy-start(f32[2,2,256,128]{3,2,1,0:T(8,128)} %get-tuple-element.39.probe_ref) | copy-start | bytes 1572868
  108.5 11.1 %all-to-all-start.4 = ((f32[8,32,128]{2,1,0:T(8,128)}), f32[8,32,128]{2,1,0:T(8,128)S(1)}, u32[]{:S(2)}, u32[]{:S(2)}) async-start(f32[8,32,128]{2,1,0:T(8,128)} %broadcast_in_dim.36), calls=%async_computation.4 | async-start | bytes 262144 | tf_op jit(solution)/shard_map/all_to_all | solution.py:262
  120.2 13.6 %all-to-all-start.5 = ((f32[16,32,128]{2,1,0:T(8,128)}), f32[16,32,128]{2,1,0:T(8,128)S(1)}, u32[]{:S(2)}, u32[]{:S(2)}) async-start(f32[16,32,128]{2,1,0:T(8,128)} %broadcast_in_dim.37), calls=%async_computation.5 | async-start | bytes 524288 | tf_op jit(solution)/shard_map/all_to_all | solution.py:262
  125.8 11.1 %collective-permute-start.18 = (f32[2,16,8,128]{3,2,1,0:T(8,128)S(1)}, f32[2,16,8,128]{3,2,1,0:T(8,128)S(1)}, u32[]{:S(2)}, u32[]{:S(2)}) collective-permute-start(f32[2,16,8,128]{3,2,1,0:T(8,128)S(1)} %get-tuple-element.42), channel_id=1, source_target_pairs={{0,31},{1,2},{2,1},{3,4},{4,3},{5,6},{6,5},{7,8},{8,7},{9,10},{10,... | collective-permute-start | bytes 393224 | tf_op jit(solution)/shard_map/ppermute | solution.py:42
  127.0 10.0 %collective-permute-start.17 = (f32[2,16,8,128]{3,2,1,0:T(8,128)S(1)}, f32[2,16,8,128]{3,2,1,0:T(8,128)S(1)}, u32[]{:S(2)}, u32[]{:S(2)}) collective-permute-start(f32[2,16,8,128]{3,2,1,0:T(8,128)S(1)} %get-tuple-element.43), channel_id=1, source_target_pairs={{0,1},{1,0},{2,3},{3,2},{4,5},{5,4},{6,7},{7,6},{8,9},{9,8},{10,11... | collective-permute-start | bytes 393224 | tf_op jit(solution)/shard_map/ppermute | solution.py:42
  133.9 4.2 %collective-permute-start.19 = (f32[2,256,128]{2,1,0:T(8,128)S(1)}, f32[2,256,128]{2,1,0:T(8,128)S(1)}, u32[]{:S(2)}, u32[]{:S(2)}) collective-permute-start(f32[2,256,128]{2,1,0:T(8,128)S(1)} %bitcast.56), channel_id=1, source_target_pairs={{0,32},{32,0},{1,33},{33,1},{2,34},{34,2},{3,35},{35,3},{4,36},{36... | collective-permute-start | bytes 786440 | tf_op jit(solution)/shard_map/ppermute | solution.py:266
